TPU v7x, 32 devices: a whole 2x2x4 slice. The times are simulated.
32 devices in a mesh: row: 4 (over y, x), col: 8 (over z, core).
Axes of the slice: x: 2, y: 2, z: 4, core: 2. Of those that a mesh axis runs over, the one named last changes fastest.
Arguments:
- features: bfloat16 [8, 128, 64, 1024], P('row', 'col'), may hold values from -6 to 6
- tissue: int32 [8, 128, 64], P('row', 'col'), may hold values 0 or 1
- probe: float32 [8, 128, 4096], P('row', 'col'), may hold values from -6 to 6
Outputs:
- basis: float32 [8, 128, 4096], P('row', 'col')
All inputs are finite; a program needn't handle non-finite values. No bound on the sum of `tissue` on one device may be relied on, other than what follows from the above.
Results may differ from a plain program's by a relative error of at most 0.00091.
Values may be sent and summed in bfloat16 or wider, within the bound.
No kernel may reach another device: no remote copies, remote signals or barrier semaphores. Data moves between devices by JAX's collectives and lax.ppermute only.
A program may use at most 128 MiB of HBM per device.

v0:
```python
import math

import jax
import jax.numpy as jnp
from jax import lax
from jax.sharding import PartitionSpec as P

RANK = 64
ITERS = 3


AFFINITY_TEMP = 4.0


def passed_along(shard, axis, by):
    count = lax.axis_size(axis)
    pairs = [(i, i + by) for i in range(count) if 0 <= i + by < count]
    return lax.ppermute(shard, axis, pairs)


def shortened(shard):

    def short(part):
        return part.astype(jnp.bfloat16) if part.dtype == jnp.float32 else part

    return jax.tree.map(short, shard)


def with_halo(shard, sides, width):
    for axis, dim in sides:
        count, length = (lax.axis_size(axis), shard.shape[dim])
        up = [(i, (i + 1) % count) for i in range(count - 1)]
        down = [(j, i) for i, j in up]
        last = lax.slice_in_dim(shard, length - width, length, axis=dim)
        leading = lax.slice_in_dim(shard, 0, width, axis=dim)
        before = lax.ppermute(last, axis, up)
        after = lax.ppermute(leading, axis, down)
        shard = jnp.concatenate([before, shard, after], axis=dim)
    return shard


def normalized(features):
    values = features.astype(jnp.float32)
    scaled = values * lax.rsqrt(jnp.sum(values * values, axis=-1, keepdims=True) + 1e-06)
    return scaled.astype(jnp.bfloat16)


def tissue_of(masked_unit):
    values = masked_unit.astype(jnp.float32)
    return (jnp.sum(values * values, axis=-1) > 0.5).astype(jnp.float32)


def pair_weights(left_unit, leftward_mask, right_unit, rightward_mask):
    affinity_scores = jnp.einsum(
        "abpd,abqd->abpq", left_unit, right_unit, preferred_element_type=jnp.float32
    )
    return (
        leftward_mask[..., :, None]
        * rightward_mask[..., None, :]
        * jnp.exp(AFFINITY_TEMP * (affinity_scores - 1.0))
    )


def flipped(blocks):
    return jnp.swapaxes(blocks, 2, 3)


def forward_affinity(masked_unit, central_mask):
    tile_rows, tile_cols = (masked_unit.shape[0], masked_unit.shape[1])
    right_unit = passed_along(masked_unit[:, :1], "col", -1)
    ext_unit = jnp.concatenate([masked_unit, right_unit], axis=1)
    below_unit = passed_along(ext_unit[:1], "row", -1)
    ext_unit = jnp.concatenate([ext_unit, below_unit], axis=0)
    ext_mask = tissue_of(ext_unit)
    own_unit = ext_unit[:tile_rows, :tile_cols]
    own_mask = ext_mask[:tile_rows, :tile_cols]
    across = pair_weights(own_unit, own_mask, ext_unit[:tile_rows, 1:], ext_mask[:tile_rows, 1:])
    downward = pair_weights(own_unit, own_mask, ext_unit[1:, :tile_cols], ext_mask[1:, :tile_cols])
    diagonal = pair_weights(own_unit, own_mask, ext_unit[1:, 1:], ext_mask[1:, 1:])
    antidiag = pair_weights(
        ext_unit[:tile_rows, 1:],
        ext_mask[:tile_rows, 1:],
        ext_unit[1:, :tile_cols],
        ext_mask[1:, :tile_cols],
    )
    own_block = pair_weights(masked_unit, central_mask, masked_unit, central_mask)
    leftward = passed_along(
        jnp.stack([across[:, -1:], diagonal[:, -1:], antidiag[:, -1:]]).astype(jnp.bfloat16),
        "col",
        1,
    ).astype(jnp.float32)
    across_wide = jnp.concatenate([leftward[0], across], axis=1)
    diagonal_cols = jnp.concatenate([leftward[1], diagonal], axis=1)
    antidiag_cols = jnp.concatenate([leftward[2], antidiag], axis=1)
    upward = passed_along(
        shortened(jnp.concatenate([downward[-1:], diagonal_cols[-1:], antidiag_cols[-1:]], axis=1)),
        "row",
        1,
    )
    upper_down = upward[:, :tile_cols]
    upper_diagonal = upward[:, tile_cols : 2 * tile_cols + 1]
    upper_antidiag = upward[:, 2 * tile_cols + 1 :]
    downward_wide = jnp.concatenate([upper_down, downward], axis=0)
    diagonal_wide = jnp.concatenate([upper_diagonal, diagonal_cols], axis=0)
    antidiag_wide = jnp.concatenate([upper_antidiag, antidiag_cols], axis=0)
    blocks = [
        flipped(diagonal_wide[:tile_rows, :tile_cols]),
        flipped(downward_wide[:tile_rows]),
        flipped(antidiag_wide[:tile_rows, 1:]),
        flipped(across_wide[:, :tile_cols]),
        own_block,
        across,
        antidiag_wide[1:, :tile_cols],
        downward,
        diagonal,
    ]
    return jnp.concatenate(blocks, axis=3)


def panel_context(carried):
    return with_halo(carried, (("row", 0), ("col", 1)), 1)


def local(features, tissue, probe):
    tile_rows, tile_cols, patches, width = features.shape
    unit = normalized(features)
    masked_unit = unit * tissue.astype(jnp.bfloat16)[..., None]
    central_mask = tissue.astype(jnp.float32)
    affinity = forward_affinity(masked_unit, central_mask)
    degree = 1.0 + jnp.sum(affinity, axis=-1)
    inverse_root = lax.rsqrt(degree)
    panel = probe.reshape(tile_rows, tile_cols, patches, RANK)
    for step in range(ITERS):
        carried = (inverse_root[..., None] * panel).reshape(tile_rows, tile_cols, patches * RANK)
        wide_panel = panel_context(carried)
        summed = jnp.zeros((tile_rows, tile_cols, patches, RANK), jnp.float32)
        for shift_row in range(3):
            for shift_col in range(3):
                which = 3 * shift_row + shift_col
                block = affinity[:, :, :, which * patches : (which + 1) * patches]
                source = wide_panel[
                    shift_row : shift_row + tile_rows, shift_col : shift_col + tile_cols
                ]
                source = source.reshape(tile_rows, tile_cols, patches, RANK)
                summed = summed + jnp.einsum(
                    "abpq,abqk->abpk", block, source, precision=lax.Precision.HIGHEST
                )
        image = panel + inverse_root[..., None] * summed
        flat = image.reshape(-1, RANK)
        local_gram = jnp.dot(
            flat.T, flat, precision=lax.Precision.HIGHEST, preferred_element_type=jnp.float32
        )
        gram_matrix = lax.psum(local_gram, ("row", "col"))
        lower = jnp.linalg.cholesky(gram_matrix)
        solved = jax.scipy.linalg.solve_triangular(lower, flat.T, lower=True)
        panel = solved.T.reshape(tile_rows, tile_cols, patches, RANK)
    total = tile_rows * lax.axis_size("row") * tile_cols * lax.axis_size("col") * patches
    factor = math.sqrt(float(total))
    return (factor * panel).reshape(tile_rows, tile_cols, patches * RANK)


def solution(mesh):
    placed = (P("row", "col", None, None), P("row", "col", None), P("row", "col", None))
    return jax.shard_map(
        local, mesh=mesh, in_specs=placed, out_specs=P("row", "col", None), check_vma=False
    )
```

profile of v0, /device:TPU:0, one launch (start us, length us, event | category | flops | bytes accessed | tf_op | source)
XLA Modules:
  0.0 544.7 jit_solution(90075870347767727)
XLA Ops:
  0.8 3.2 fusion
  10.4 49.0 %collective-permute-done.1 = bf16[1,17,64,1024]{3,2,1,0:T(8,128)(2,1)S(1)} collective-permute-done((bf16[1,17,64,1024]{3,2,1,0:T(8,128)(2,1)S(1)}, bf16[1,17,64,1024]{3,2,1,0:T(8,128)(2,1)S(1)}, u32[]{:S(2)}, u32[]{:S(2)}) %collective-permute-start.1) | collective-permute-done | bytes 2228256 | tf_op jit(solution)/shard_map/ppermute | solution.py:18
  59.3 4.3 multiply_reduce_fusion
  70.4 5.6 %collective-permute-start.2 = (bf16[3,2,1,64,64]{4,3,1,2,0:T(8,128)(2,1)S(1)}, bf16[3,2,1,64,64]{4,3,1,2,0:T(8,128)(2,1)S(1)}, u32[]{:S(2)}, u32[]{:S(2)}) collective-permute-start(bf16[3,2,1,64,64]{4,3,1,2,0:T(8,128)(2,1)S(1)} %pad_maximum_fusion.24), channel_id=1, source_target_pairs={{0,1},{1,2},{2,3},{3,4},{4,5},{5,6},{6,7},{8,9},{9,10},{10,11},{11... | collective-permute-start | bytes 147464 | tf_op jit(solution)/shard_map/ppermute | solution.py:18
  78.5 5.9 %collective-permute-start.3 = (bf16[1,50,64,64]{3,2,1,0:T(8,128)(2,1)}, bf16[1,50,64,64]{3,2,1,0:T(8,128)(2,1)}, u32[]{:S(2)}, u32[]{:S(2)}) collective-permute-start(bf16[1,50,64,64]{3,2,1,0:T(8,128)(2,1)} %pad_maximum_fusion.13), channel_id=1, source_target_pairs={{0,8},{8,16},{16,24},{1,9},{9,17},{17,25},{2,10},{10,18},{18,26},{... | collective-permute-start | bytes 1228808 | tf_op jit(solution)/shard_map/ppermute | solution.py:18
  86.8 2.5 reshape.258
  90.7 8.8 %collective-permute-done.3 = bf16[1,50,64,64]{3,2,1,0:T(8,128)(2,1)} collective-permute-done((bf16[1,50,64,64]{3,2,1,0:T(8,128)(2,1)}, bf16[1,50,64,64]{3,2,1,0:T(8,128)(2,1)}, u32[]{:S(2)}, u32[]{:S(2)}) %collective-permute-start.3) | collective-permute-done | bytes 409632 | tf_op jit(solution)/shard_map/ppermute | solution.py:18
  109.2 4.4 collective-permute-start.4
  122.1 3.4 fusion.137
  129.1 2.4 reshape.260
  133.5 2.9 collective-permute-start.6
  138.0 2.4 reshape.265
  140.5 3.6 fusion.196
  144.0 2.8 fusion.113
  146.9 2.5 maximum_maximum_fusion.1
  153.1 4.5 fusion.143
  163.7 2.5 reshape.264
  166.2 3.7 fusion.139
  169.9 2.4 reshape.266
  172.3 3.4 fusion.128
  175.7 2.4 reshape.263
  178.2 3.7 fusion.119
  181.9 3.7 fusion.23
  190.2 46.3 %psum.21 = f32[64,64]{0,1:T(8,128)S(1)} all-reduce(f32[64,64]{0,1:T(8,128)S(1)} %convolution_bitcast_fusion.4), channel_id=1, replica_groups=mesh['row'=4,'col'=8] {'row','col'}, use_global_device_ids=true, to_apply=%region_11.12 | all-reduce | flops 4096 | bytes 32768 | tf_op jit(solution)/shard_map/psum | solution.py:153
  236.6 5.8 %cholesky.59 = f32[64,64]{1,0:T(8,128)S(1)} custom-call(f32[64,64]{1,0:T(8,128)S(1)} %fusion.161), custom_call_target="Cholesky" | custom-call | tf_op jit(solution)/shard_map/jit(cholesky)/cholesky | solution.py:154
  243.8 4.9 custom-call.7
  248.7 3.3 convolution_bitcast_fusion.1
  263.3 4.1 collective-permute-start.8
  270.8 3.7 fusion.135
  274.5 6.0 %collective-permute-done.9 = f32[1,16,4096]{2,1,0:T(8,128)S(1)} collective-permute-done((f32[1,16,4096]{2,1,0:T(8,128)}, f32[1,16,4096]{2,1,0:T(8,128)S(1)}, u32[]{:S(2)}, u32[]{:S(2)}) %collective-permute-start.9) | collective-permute-done | bytes 262176 | tf_op jit(solution)/shard_map/ppermute | solution.py:37
  281.7 2.4 reshape.271
  289.0 2.4 reshape.276
  291.5 3.5 fusion.197
  295.0 2.8 fusion.112
  303.9 4.5 fusion.142
  312.0 4.3 fusion.117
  318.8 2.5 reshape.275
  321.3 3.7 fusion.141
  325.0 2.4 reshape.277
  327.4 3.6 fusion.126
  331.0 2.4 reshape.274
  333.5 4.9 fusion.28
  342.9 40.8 %psum.22 = f32[64,64]{0,1:T(8,128)S(1)} all-reduce(f32[64,64]{0,1:T(8,128)S(1)} %convolution_bitcast_fusion.3), channel_id=1, replica_groups=mesh['row'=4,'col'=8] {'row','col'}, use_global_device_ids=true, to_apply=%region_14.17 | all-reduce | flops 4096 | bytes 32768 | tf_op jit(solution)/shard_map/psum | solution.py:153
  383.8 5.8 %cholesky.70 = f32[64,64]{1,0:T(8,128)S(1)} custom-call(f32[64,64]{1,0:T(8,128)S(1)} %fusion.159), custom_call_target="Cholesky" | custom-call | tf_op jit(solution)/shard_map/jit(cholesky)/cholesky | solution.py:154
  391.0 4.9 custom-call.8
  395.9 3.3 convolution_bitcast_fusion
  410.5 4.2 collective-permute-start.12
  418.0 3.7 fusion.133
  421.7 5.1 collective-permute-done.13
  427.9 2.5 reshape.282
  435.1 2.5 reshape.287
  437.5 3.5 fusion.198
  441.1 2.9 fusion.114
  447.4 2.5 reshape.283
  449.9 4.3 fusion.144
  455.4 2.4 reshape.284
  457.8 4.0 fusion.115
  461.9 2.5 reshape.281
  466.8 3.4 fusion.140
  472.7 3.7 fusion.124
  478.9 4.5 fusion.33
  487.0 42.2 %psum.23 = f32[64,64]{0,1:T(8,128)S(1)} all-reduce(f32[64,64]{0,1:T(8,128)S(1)} %convolution_bitcast_fusion.2), channel_id=1, replica_groups=mesh['row'=4,'col'=8] {'row','col'}, use_global_device_ids=true, to_apply=%region_15.18 | all-reduce | flops 4096 | bytes 32768 | tf_op jit(solution)/shard_map/psum | solution.py:153
  529.3 5.8 %cholesky.81 = f32[64,64]{1,0:T(8,128)S(1)} custom-call(f32[64,64]{1,0:T(8,128)S(1)} %fusion.157), custom_call_target="Cholesky" | custom-call | tf_op jit(solution)/shard_map/jit(cholesky)/cholesky | solution.py:154
  536.5 4.9 custom-call.9
  (236 shorter events, 140.1 us)
Async XLA Ops:
  0.8 3.4 copy-start.3
  5.4 3.4 collective-permute-start
  9.0 50.3 %collective-permute-start.1 = (bf16[1,17,64,1024]{3,2,1,0:T(8,128)(2,1)S(1)}, bf16[1,17,64,1024]{3,2,1,0:T(8,128)(2,1)S(1)}, u32[]{:S(2)}, u32[]{:S(2)}) collective-permute-start(bf16[1,17,64,1024]{3,2,1,0:T(8,128)(2,1)S(1)} %fusion.15), channel_id=1, source_target_pairs={{8,0},{16,8},{24,16},{9,1},{17,9},{25,17},{10,2},{18,10},{26,18},{... | collective-permute-start | bytes 6684680 | tf_op jit(solution)/shard_map/ppermute | solution.py:18
  67.4 10.0 %copy-start.14 = (f32[2,16,64,64]{3,2,1,0:T(8,128)}, f32[2,16,64,64]{3,2,1,0:T(8,128)S(1)}, u32[]{:S(2)}) copy-start(f32[2,16,64,64]{3,2,1,0:T(8,128)S(1)} %copy_multiply_fusion) | copy-start | bytes 1572868
  70.4 6.9 %collective-permute-start.2 = (bf16[3,2,1,64,64]{4,3,1,2,0:T(8,128)(2,1)S(1)}, bf16[3,2,1,64,64]{4,3,1,2,0:T(8,128)(2,1)S(1)}, u32[]{:S(2)}, u32[]{:S(2)}) collective-permute-start(bf16[3,2,1,64,64]{4,3,1,2,0:T(8,128)(2,1)S(1)} %pad_maximum_fusion.24), channel_id=1, source_target_pairs={{0,1},{1,2},{2,3},{3,4},{4,5},{5,6},{6,7},{8,9},{9,10},{10,11},{11... | collective-permute-start | bytes 147464 | tf_op jit(solution)/shard_map/ppermute | solution.py:18
  78.5 21.0 %collective-permute-start.3 = (bf16[1,50,64,64]{3,2,1,0:T(8,128)(2,1)}, bf16[1,50,64,64]{3,2,1,0:T(8,128)(2,1)}, u32[]{:S(2)}, u32[]{:S(2)}) collective-permute-start(bf16[1,50,64,64]{3,2,1,0:T(8,128)(2,1)} %pad_maximum_fusion.13), channel_id=1, source_target_pairs={{0,8},{8,16},{16,24},{1,9},{9,17},{17,25},{2,10},{10,18},{18,26},{... | collective-permute-start | bytes 1228808 | tf_op jit(solution)/shard_map/ppermute | solution.py:18
  89.3 11.4 %copy-start.15 = (f32[2,16,64,64]{3,2,1,0:T(8,128)S(1)}, f32[2,16,64,64]{3,2,1,0:T(8,128)}, u32[]{:S(2)}) copy-start(f32[2,16,64,64]{3,2,1,0:T(8,128)} %copy-done.14) | copy-start | bytes 1572868
  100.7 1.5 copy-start.51
  103.4 1.5 copy-start.22
  109.2 16.2 %collective-permute-start.4 = (f32[1,16,4096]{2,1,0:T(8,128)}, f32[1,16,4096]{2,1,0:T(8,128)S(1)}, u32[]{:S(2)}, u32[]{:S(2)}) collective-permute-start(f32[1,16,4096]{2,1,0:T(8,128)} %slice.273), channel_id=1, source_target_pairs={{0,8},{8,16},{16,24},{1,9},{9,17},{17,25},{2,10},{10,18},{18,26},{... | collective-permute-start | bytes 786440 | tf_op jit(solution)/shard_map/ppermute | solution.py:36
  115.6 11.4 %collective-permute-start.5 = (f32[1,16,4096]{2,1,0:T(8,128)}, f32[1,16,4096]{2,1,0:T(8,128)}, u32[]{:S(2)}, u32[]{:S(2)}) collective-permute-start(f32[1,16,4096]{2,1,0:T(8,128)} %slice.275), channel_id=1, source_target_pairs={{8,0},{16,8},{24,16},{9,1},{17,9},{25,17},{10,2},{18,10},{26,18},{... | collective-permute-start | bytes 786440 | tf_op jit(solution)/shard_map/ppermute | solution.py:37
  120.6 1.5 copy-start.18
  121.9 7.2 %copy-start.28 = (f32[2,16,4096]{2,1,0:T(8,128)}, f32[2,16,4096]{2,1,0:T(8,128)S(1)}, u32[]{:S(2)}) copy-start(f32[2,16,4096]{2,1,0:T(8,128)S(1)} %mul.204) | copy-start | bytes 1572868
  133.5 13.4 %collective-permute-start.6 = (f32[4,1,4096]{2,1,0:T(1,128)}, f32[4,1,4096]{2,1,0:T(1,128)S(1)}, u32[]{:S(2)}, u32[]{:S(2)}) collective-permute-start(f32[4,1,4096]{2,1,0:T(1,128)} %get-tuple-element.51), channel_id=1, source_target_pairs={{0,1},{1,2},{2,3},{3,4},{4,5},{5,6},{6,7},{8,9},{9,10},{10,11},{11... | collective-permute-start | bytes 196616 | tf_op jit(solution)/shard_map/ppermute | solution.py:36
  136.3 10.6 %collective-permute-start.7 = (f32[4,1,4096]{2,1,0:T(1,128)}, f32[4,1,4096]{2,1,0:T(1,128)}, u32[]{:S(2)}, u32[]{:S(2)}) collective-permute-start(f32[4,1,4096]{2,1,0:T(1,128)} %get-tuple-element.52), channel_id=1, source_target_pairs={{1,0},{2,1},{3,2},{4,3},{5,4},{6,5},{7,6},{9,8},{10,9},{11,10},{12... | collective-permute-start | bytes 196616 | tf_op jit(solution)/shard_map/ppermute | solution.py:37
  140.5 3.6 copy-start.11
  140.5 3.6 copy-start.36
  144.0 2.9 copy-start.29
  153.1 4.5 copy-start.31
  178.1 3.7 copy-start.1
  178.2 3.7 copy-start.33
  178.2 3.7 copy-start.34
  181.9 3.7 copy-start.23
  181.9 3.7 copy-start.39
  181.9 3.7 copy-start.41
  181.9 3.7 copy-start.44
  181.9 3.7 copy-start.53
  256.8 2.2 copy-start.6
  263.3 11.2 %collective-permute-start.8 = (f32[1,16,4096]{2,1,0:T(8,128)}, f32[1,16,4096]{2,1,0:T(8,128)S(1)}, u32[]{:S(2)}, u32[]{:S(2)}) collective-permute-start(f32[1,16,4096]{2,1,0:T(8,128)} %slice.287), channel_id=1, source_target_pairs={{0,8},{8,16},{16,24},{1,9},{9,17},{17,25},{2,10},{10,18},{18,26},{... | collective-permute-start | bytes 786440 | tf_op jit(solution)/shard_map/ppermute | solution.py:36
  269.4 11.1 %copy-start.26 = (f32[2,16,4096]{2,1,0:T(8,128)S(1)}, f32[2,16,4096]{2,1,0:T(8,128)}, u32[]{:S(2)}) copy-start(f32[2,16,4096]{2,1,0:T(8,128)} %mul.207) | copy-start | bytes 1572868
  269.4 11.1 %collective-permute-start.9 = (f32[1,16,4096]{2,1,0:T(8,128)}, f32[1,16,4096]{2,1,0:T(8,128)S(1)}, u32[]{:S(2)}, u32[]{:S(2)}) collective-permute-start(f32[1,16,4096]{2,1,0:T(8,128)} %slice.289), channel_id=1, source_target_pairs={{8,0},{16,8},{24,16},{9,1},{17,9},{25,17},{10,2},{18,10},{26,18},{... | collective-permute-start | bytes 786440 | tf_op jit(solution)/shard_map/ppermute | solution.py:37
  280.5 1.2 copy-start.49
  286.0 11.9 %collective-permute-start.10 = (f32[4,1,4096]{2,1,0:T(1,128)}, f32[4,1,4096]{2,1,0:T(1,128)S(1)}, u32[]{:S(2)}, u32[]{:S(2)}) collective-permute-start(f32[4,1,4096]{2,1,0:T(1,128)} %get-tuple-element.45), channel_id=1, source_target_pairs={{0,1},{1,2},{2,3},{3,4},{4,5},{5,6},{6,7},{8,9},{9,10},{10,11},{11... | collective-permute-start | bytes 196616 | tf_op jit(solution)/shard_map/ppermute | solution.py:36
  287.3 10.6 %collective-permute-start.11 = (f32[4,1,4096]{2,1,0:T(1,128)}, f32[4,1,4096]{2,1,0:T(1,128)}, u32[]{:S(2)}, u32[]{:S(2)}) collective-permute-start(f32[4,1,4096]{2,1,0:T(1,128)} %get-tuple-element.46), channel_id=1, source_target_pairs={{1,0},{2,1},{3,2},{4,3},{5,4},{6,5},{7,6},{9,8},{10,9},{11,10},{12... | collective-permute-start | bytes 196616 | tf_op jit(solution)/shard_map/ppermute | solution.py:37
  291.5 3.6 copy-start.12
  291.5 3.6 copy-start.37
  295.0 2.9 copy-start.27
  295.0 2.9 copy-start.50
  303.9 4.5 copy-start.32
  333.5 4.9 copy-start.7
  333.5 4.9 copy-start.40
  333.5 4.9 copy-start.43
  333.5 4.9 copy-start.46
  333.5 4.9 copy-start.54
  404.0 2.2 copy-start.4
  410.5 11.2 %collective-permute-start.12 = (f32[1,16,4096]{2,1,0:T(8,128)}, f32[1,16,4096]{2,1,0:T(8,128)S(1)}, u32[]{:S(2)}, u32[]{:S(2)}) collective-permute-start(f32[1,16,4096]{2,1,0:T(8,128)} %slice.301), channel_id=1, source_target_pairs={{0,8},{8,16},{16,24},{1,9},{9,17},{17,25},{2,10},{10,18},{18,26},{... | collective-permute-start | bytes 786440 | tf_op jit(solution)/shard_map/ppermute | solution.py:36
  416.6 10.2 %copy-start.24 = (f32[2,16,4096]{2,1,0:T(8,128)S(1)}, f32[2,16,4096]{2,1,0:T(8,128)}, u32[]{:S(2)}) copy-start(f32[2,16,4096]{2,1,0:T(8,128)} %mul.210) | copy-start | bytes 1572868
  416.6 10.2 %collective-permute-start.13 = (f32[1,16,4096]{2,1,0:T(8,128)}, f32[1,16,4096]{2,1,0:T(8,128)S(1)}, u32[]{:S(2)}, u32[]{:S(2)}) collective-permute-start(f32[1,16,4096]{2,1,0:T(8,128)} %slice.303), channel_id=1, source_target_pairs={{8,0},{16,8},{24,16},{9,1},{17,9},{25,17},{10,2},{18,10},{26,18},{... | collective-permute-start | bytes 786440 | tf_op jit(solution)/shard_map/ppermute | solution.py:37
  432.3 11.7 %collective-permute-start.14 = (f32[4,1,4096]{2,1,0:T(1,128)}, f32[4,1,4096]{2,1,0:T(1,128)S(1)}, u32[]{:S(2)}, u32[]{:S(2)}) collective-permute-start(f32[4,1,4096]{2,1,0:T(1,128)} %get-tuple-element.39), channel_id=1, source_target_pairs={{0,1},{1,2},{2,3},{3,4},{4,5},{5,6},{6,7},{8,9},{9,10},{10,11},{11... | collective-permute-start | bytes 196616 | tf_op jit(solution)/shard_map/ppermute | solution.py:36
  433.6 10.4 %collective-permute-start.15 = (f32[4,1,4096]{2,1,0:T(1,128)}, f32[4,1,4096]{2,1,0:T(1,128)}, u32[]{:S(2)}, u32[]{:S(2)}) collective-permute-start(f32[4,1,4096]{2,1,0:T(1,128)} %get-tuple-element.40), channel_id=1, source_target_pairs={{1,0},{2,1},{3,2},{4,3},{5,4},{6,5},{7,6},{9,8},{10,9},{11,10},{12... | collective-permute-start | bytes 196616 | tf_op jit(solution)/shard_map/ppermute | solution.py:37
  437.5 3.5 copy-start.13
  437.5 3.5 copy-start.35
  441.1 2.9 copy-start.25
  441.1 2.9 copy-start.48
  446.2 3.6 copy-start.16
  449.9 4.3 copy-start.30
  454.2 3.6 copy-start
  461.9 5.0 copy-start.17
  472.7 6.2 %copy-start.2 = (f32[2,16,64,64]{3,2,0,1:T(8,128)S(1)}, f32[2,16,64,64]{3,2,0,1:T(8,128)}, u32[]{:S(2)}) copy-start(f32[2,16,64,64]{3,2,0,1:T(8,128)} %get-tuple-element.12) | copy-start | bytes 1572868
  478.8 4.6 copy-start.5
  478.8 4.6 copy-start.38
  478.8 4.6 copy-start.42
  478.8 4.6 copy-start.45
  478.9 4.6 copy-start.52
  (7 other events, 7.0 us)
where the time goes:
time: 554 us; the launch traced here: 545 us
  blocking collectives  129 us (23%)
  matrix products  116 us (21%)
  local copies, waits for them, and re-layouts  106 us (19%)
  other arithmetic  77.6 us (14%)
  waiting for transfers between devices  72.5 us (13%)
  starting transfers between devices  41.2 us (7%)
    psum x3, blocking collectives, local(): gram_matrix = lax.psum(local_gram, ('row', 'col'))  129 us
    dot_general x27, matrix products, local(): jnp.einsum('abpq,abqk->abpk', block, source, precision=lax.Precision.HIGH...  94.6 us
    ppermute x4, waiting for transfers between devices, passed_along(): return lax.ppermute(shard, axis, pairs)  59.9 us
    reshape x24, local copies, waits for them, and re-layouts, local(): source = source.reshape(tile_rows, tile_cols, patches, RANK)  58.8 us
    another operation x9, other arithmetic, local(): lower = jnp.linalg.cholesky(gram_matrix)  19.6 us
    ppermute x6, starting transfers between devices, with_halo(): before = lax.ppermute(last, axis, up)  18.1 us
    another operation x6, other arithmetic, local(): solved = jax.scipy.linalg.solve_triangular(lower, flat.T, lower=True)  16.6 us
    ppermute x4, starting transfers between devices, passed_along(): return lax.ppermute(shard, axis, pairs)  14.1 us
  transfers between devices with their start and end apart: 16, of which 6 were waited for; matrix products, arithmetic and copies ran while one was open for 10% of the time, Pallas kernels for 0%

commit v1 on v0

v1 whole, which is shorter than its diff:
```python
import functools
import math

import jax
import jax.numpy as jnp
from jax import lax
from jax.experimental import pallas as pl
from jax.experimental.pallas import tpu as pltpu
from jax.sharding import PartitionSpec as P

RANK = 64
ITERS = 3
AFFINITY_TEMP = 4.0

GHOST = ITERS + 1
TINY = 1e-30
VMEM_BYTES = 56 * 1024 * 1024
FLOOR = math.exp(-AFFINITY_TEMP)
ABT = (((1,), (1,)), ((), ()))
ATB = (((0,), (0,)), ((), ()))

f32 = jnp.float32
bf16 = jnp.bfloat16


def kernel_call(body, out_shape, scratch=(), cost=0):
    return pl.pallas_call(
        body,
        out_shape=out_shape,
        scratch_shapes=list(scratch),
        compiler_params=pltpu.CompilerParams(vmem_limit_bytes=VMEM_BYTES),
        cost_estimate=pl.CostEstimate(flops=cost, bytes_accessed=1 << 20, transcendentals=0),
    )


def sds(shape, dtype):
    return jax.ShapeDtypeStruct(shape, dtype)


def iota(shape, dim):
    return lax.broadcasted_iota(jnp.int32, shape, dim)


def identity(n):
    return iota((n, n), 0) == iota((n, n), 1)


def to_lanes(column, eye):
    return jnp.sum(jnp.where(eye, column, 0.0), axis=0, keepdims=True)


def to_sublanes(row, eye):
    return jnp.sum(jnp.where(eye, row, 0.0), axis=1, keepdims=True)


def unit_and_mask(block):
    values = block.astype(f32)
    scaled = values * lax.rsqrt(jnp.sum(values * values, axis=-1, keepdims=True) + 1e-06)
    return scaled.astype(bf16), (values[:, :1] != 0.0).astype(f32)


def affinity_of(left, right):
    scores = lax.dot_general(left, right, ABT, preferred_element_type=f32)
    return jnp.exp(AFFINITY_TEMP * scores - AFFINITY_TEMP)


def masked_sum(weights, mask):
    absent = mask.shape[0] - jnp.sum(mask, axis=0, keepdims=True)
    return jnp.sum(weights, axis=1, keepdims=True) - FLOOR * absent


def packed(block):
    half = block.shape[0] // 2
    return jnp.concatenate([block[:half], block[half:]], axis=1)


def unpacked(block):
    return jnp.concatenate([block[:, :RANK], block[:, RANK:]], axis=0)


def pair_of(values):
    high = values.astype(bf16)
    return high, (values - high.astype(f32)).astype(bf16)


def own_kernel(n, x_ref, xl_ref, xr_ref, p_ref, m_ref, u1_ref, stat_ref, pay_ref, unit_ref, mask_ref):
    rows, cols, patch, width = x_ref.shape
    both = rows * patch
    eye = identity(both)
    small_eye = identity(patch)

    def normalise(ref, index, e):
        for row in range(rows):
            unit, mask = unit_and_mask(ref[row, index])
            start = pl.multiple_of(e * both + row * patch, patch)
            unit_ref[pl.ds(start, patch), :] = unit
            mask_ref[pl.ds(start, patch), :] = mask
            if row == rows - 1:
                u1_ref[e] = unit

    def loop(ref, count, first):
        def step(i, carry):
            normalise(ref, i, first + i)
            return carry

        lax.fori_loop(0, count, step, 0)

    loop(xl_ref, GHOST, 0)
    loop(x_ref, cols, GHOST)
    loop(xr_ref, GHOST, GHOST + cols)
    tail = (n - 2) * patch // 2
    pay_ref[tail:, :] = jnp.zeros((pay_ref.shape[0] - tail, 2 * RANK), bf16)

    def band(e, carry):
        around = pl.ds(pl.multiple_of((e - 1) * both, both), 3 * both)
        here = pl.ds(pl.multiple_of(e * both, both), both)
        weights = affinity_of(unit_ref[here, :], unit_ref[around, :])
        degree = masked_sum(weights, mask_ref[around, :])
        centre = weights[:, both : 2 * both]
        diagonal = jnp.sum(jnp.where(eye, centre, 0.0), axis=1, keepdims=True)
        m_ref[e, :, :both] = weights[:, :both].astype(bf16)
        m_ref[e, :, both : 2 * both] = jnp.where(eye, 0.0, centre).astype(bf16)
        m_ref[e, :, 2 * both :] = weights[:, 2 * both :].astype(bf16)
        stat_ref[e, :, 0:1] = degree
        stat_ref[e, :, 1:2] = diagonal
        stat_ref[e, :, 2:3] = mask_ref[here, :]
        return carry

    lax.fori_loop(1, n - 1, band, 0)
    for e in range(1, n - 1):
        high, low = pair_of(to_lanes(stat_ref[e, :patch, 0:1], small_eye))
        pay_ref[tail + e : tail + e + 1, :patch] = high
        pay_ref[tail + 32 + e : tail + 33 + e, :patch] = low
        at = (e - 1) * patch // 2
        pay_ref[at : at + patch // 2, :] = packed(p_ref[0, e]).astype(bf16)


def payload_rows(n, patch):
    return (n - 2) * patch // 2 + 64


def own_affinity(x, xl, xr, panel):
    rows, cols, patch, width = x.shape
    n = cols + 2 * GHOST
    both = rows * patch
    return kernel_call(
        functools.partial(own_kernel, n),
        (
            sds((n, both, 3 * both), bf16),
            sds((n, patch, width), bf16),
            sds((n, both, 128), f32),
            sds((payload_rows(n, patch), 2 * RANK), bf16),
        ),
        [pltpu.VMEM((n * both, width), bf16), pltpu.VMEM((n * both, 1), f32)],
        cost=2 * n * both * 3 * both * width,
    )(x, xl, xr, panel)


def cross_columns(columns, sources, u1_ref, unit_ref, mask_ref, v_ref, w_ref, stat_ref):
    patch = u1_ref.shape[1]
    needed = sorted({c for e in columns for c in (e - 1, e, e + 1)})
    for c in needed:
        ref, index = sources[c]
        unit, mask = unit_and_mask(ref[index])
        unit_ref[c * patch : (c + 1) * patch, :] = unit
        mask_ref[c * patch : (c + 1) * patch, :] = mask
    for place, e in enumerate(columns):
        around = slice((e - 1) * patch, (e + 2) * patch)
        here = slice(e * patch, (e + 1) * patch)
        above = u1_ref[e - 1 : e + 2].reshape(3 * patch, u1_ref.shape[2])
        down = affinity_of(u1_ref[e], unit_ref[around, :])
        up = affinity_of(unit_ref[here, :], above)
        v_ref[place] = down.astype(bf16)
        w_ref[place] = up.astype(bf16)
        stat_ref[place, :, 0:1] = masked_sum(down, mask_ref[around, :])
        stat_ref[place, :, 1:2] = jnp.sum(up, axis=1, keepdims=True)
        stat_ref[place, :, 2:3] = mask_ref[here, :]


def edge_columns(n):
    return list(range(1, 2 * GHOST - 1)) + list(range(n - 2 * GHOST + 1, n - 1))


def middle_columns(n):
    return list(range(2 * GHOST - 1, n - 2 * GHOST + 1))


def below_sources(n, bl_ref, be_ref, bm_ref, br_ref):
    sources = {}
    for c in range(n):
        if c < GHOST:
            sources[c] = (bl_ref, c)
        elif c < 2 * GHOST:
            sources[c] = (be_ref, c - GHOST)
        elif c < n - 2 * GHOST:
            sources[c] = (bm_ref, c - 2 * GHOST)
        elif c < n - GHOST:
            sources[c] = (be_ref, c - (n - 2 * GHOST) + GHOST)
        else:
            sources[c] = (br_ref, c - (n - GHOST))
    return sources


def edge_kernel(n, bl_ref, be_ref, br_ref, u1_ref, v_ref, w_ref, stat_ref, unit_ref, mask_ref):
    sources = below_sources(n, bl_ref, be_ref, None, br_ref)
    cross_columns(edge_columns(n), sources, u1_ref, unit_ref, mask_ref, v_ref, w_ref, stat_ref)


def cross_shapes(count, patch):
    return (
        sds((count, patch, 3 * patch), bf16),
        sds((count, patch, 3 * patch), bf16),
        sds((count, patch, 128), f32),
    )


def cross_scratch(n, patch, width):
    return [pltpu.VMEM((n * patch, width), bf16), pltpu.VMEM((n * patch, 1), f32)]


def edge_affinity(bl, be, br, u1):
    n, patch, width = u1.shape
    count = len(edge_columns(n))
    return kernel_call(
        functools.partial(edge_kernel, n),
        cross_shapes(count, patch),
        cross_scratch(n, patch, width),
        cost=4 * count * patch * 3 * patch * width,
    )(bl, be, br, u1)


def place_of(n):
    edge, middle = edge_columns(n), middle_columns(n)
    return {e: (0, i) for i, e in enumerate(edge)} | {e: (1, i) for i, e in enumerate(middle)}


def middle_kernel(
    n,
    be_ref, bm_ref, u1_ref, va_ref, wa_ref, sa_ref, stat_ref, p_ref, got_ref,
    v_ref, w_ref, u0_ref, u2_ref, t_ref, pay_ref,
    unit_ref, mask_ref, sb_ref,
):
    patch = u1_ref.shape[1]
    both = 2 * patch
    half = patch // 2
    sources = below_sources(n, None, be_ref, bm_ref, None)
    cross_columns(middle_columns(n), sources, u1_ref, unit_ref, mask_ref, v_ref, w_ref, sb_ref)
    where = place_of(n)
    stats, ups = (sa_ref, sb_ref), (wa_ref, w_ref)
    eye = identity(patch)
    tail = (n - 2) * half
    got_tail = (n - 2) * half
    pay_ref[...] = jnp.zeros(pay_ref.shape, bf16)
    for e in range(1, n - 1):
        which, i = where[e]
        own_mask = stat_ref[e - 1 : e + 2, patch:, 2:3].reshape(3 * patch, 1)
        absent = 3 * patch - jnp.sum(own_mask, axis=0, keepdims=True)
        shared = stats[which][i, :, 1:2] - FLOOR * absent
        scale = lax.rsqrt(1.0 + stat_ref[e, patch:, 0:1] + stats[which][i, :, 0:1])
        t_own = stat_ref[e, patch:, 2:3] * scale
        t_ref[e, :, 0:1] = t_own
        u0_ref[e] = (t_own * p_ref[1, e]).astype(bf16)
        high = got_ref[got_tail + e : got_tail + e + 1, :patch].astype(f32)
        low = got_ref[got_tail + 32 + e : got_tail + 33 + e, :patch].astype(f32)
        partial = to_sublanes(high + low, eye)
        t_below = stats[which][i, :, 2:3] * lax.rsqrt(1.0 + partial + shared)
        theirs = unpacked(got_ref[(e - 1) * half : e * half, :].astype(f32))
        u2_ref[e] = (t_below * theirs).astype(bf16)
        high, low = pair_of(to_lanes(shared, eye))
        pay_ref[tail + e : tail + e + 1, :patch] = high
        pay_ref[tail + 32 + e : tail + 33 + e, :patch] = low
    for e in range(2, n - 2):
        which, i = where[e]
        source = u0_ref[e - 1 : e + 2].reshape(3 * patch, RANK)
        product = jnp.dot(ups[which][i], source, preferred_element_type=f32)
        pay_ref[(e - 1) * half : e * half, :] = packed(product).astype(bf16)


def middle_affinity(be, bm, u1, va, wa, sa, stat, panel, got):
    n, patch, width = u1.shape
    count = len(middle_columns(n))
    v, w, s = cross_shapes(count, patch)
    return kernel_call(
        functools.partial(middle_kernel, n),
        (
            v,
            w,
            sds((n, patch, RANK), bf16),
            sds((n, patch, RANK), bf16),
            sds((n, patch, 128), f32),
            sds((payload_rows(n, patch), 2 * RANK), bf16),
        ),
        cross_scratch(n, patch, width) + [pltpu.VMEM(s.shape, f32)],
        cost=4 * count * patch * 3 * patch * width,
    )(be, bm, u1, va, wa, sa, stat, panel, got)


def send_products(payload_ref, u_ref, ups, where, low, high, first):
    patch = u_ref.shape[1] // 2
    half = patch // 2
    for e in range(low, high):
        which, i = where[e]
        source = u_ref[e - 1 : e + 2, patch:, :].reshape(3 * patch, RANK)
        product = jnp.dot(ups[which][i], source, preferred_element_type=f32)
        payload_ref[(e - first) * half : (e - first + 1) * half, :] = packed(product).astype(bf16)


def first_kernel(
    n,
    got_ref, stat_ref, t_ref, u0_ref, u2_ref, p_ref, m_ref, va_ref, wa_ref, vb_ref, wb_ref,
    y_ref, u_ref, tt_ref, up_ref, down_ref,
    start_ref,
):
    patch = u0_ref.shape[1]
    half = patch // 2
    both = 2 * patch
    eye = identity(patch)
    where = place_of(n)
    downs, ups = (va_ref, vb_ref), (wa_ref, wb_ref)
    tail = (n - 2) * half
    for e in range(1, n - 1):
        high = got_ref[tail + e : tail + e + 1, :patch].astype(f32)
        low = got_ref[tail + 32 + e : tail + 33 + e, :patch].astype(f32)
        degree = 1.0 + stat_ref[e, :patch, 0:1] + to_sublanes(high + low, eye)
        t_own = stat_ref[e, :patch, 2:3] * lax.rsqrt(degree)
        tt_ref[e, :patch, 0:1] = t_own
        tt_ref[e, patch:, 0:1] = t_ref[e, :, 0:1]
        tt_ref[e, :, 1:2] = stat_ref[e, :, 1:2]
        start_ref[e, :patch, :] = (t_own * p_ref[0, e]).astype(bf16)
        start_ref[e, patch:, :] = u0_ref[e]
    for e in range(2, n - 2):
        which, i = where[e]
        source = start_ref[e - 1 : e + 2].reshape(3 * both, RANK)
        total = jnp.dot(m_ref[e], source, preferred_element_type=f32)
        below = u2_ref[e - 1 : e + 2].reshape(3 * patch, RANK)
        lower = jnp.dot(downs[which][i], below, preferred_element_type=f32)
        upper = unpacked(got_ref[(e - 1) * half : e * half, :].astype(f32))
        total = total + jnp.concatenate([upper, lower], axis=0)
        old = jnp.concatenate([p_ref[0, e], p_ref[1, e]], axis=0)
        scale, diagonal = tt_ref[e, :, 0:1], tt_ref[e, :, 1:2]
        image = old * (1.0 + scale * scale * diagonal) + scale * total
        y_ref[e] = image
        u_ref[e] = (scale * image).astype(bf16)
        up_ref[(e - 2) * half : (e - 1) * half, :] = packed(scale[:patch] * image[:patch]).astype(bf16)
    send_products(down_ref, u_ref, ups, where, 3, n - 3, 3)


def first_iteration(got, stat, t, u0, u2, panel, m, va, wa, vb, wb):
    n, patch, _ = u0.shape
    both = 2 * patch
    half = patch // 2
    return kernel_call(
        functools.partial(first_kernel, n),
        (
            sds((n, both, RANK), f32),
            sds((n, both, RANK), bf16),
            sds((n, both, 128), f32),
            sds(((n - 4) * half, 2 * RANK), bf16),
            sds(((n - 6) * half, 2 * RANK), bf16),
        ),
        [pltpu.VMEM((n, both, RANK), bf16)],
        cost=2 * n * both * 3 * both * RANK,
    )(got, stat, t, u0, u2, panel, m, va, wa, vb, wb)


def local_kernel(low, high, m_ref, u_ref, z_ref):
    both = m_ref.shape[1]
    for e in range(low, high):
        source = u_ref[e - 1 : e + 2].reshape(3 * both, RANK)
        z_ref[e] = jnp.dot(m_ref[e], source, preferred_element_type=f32)


def local_products(low, high, m, u):
    n, both, _ = m.shape
    return kernel_call(
        functools.partial(local_kernel, low, high),
        sds((n, both, RANK), f32),
        cost=2 * n * both * 3 * both * RANK,
    )(m, u)


def joined(e, low, where, downs, z_ref, below_ref, above_ref, y_ref, tt_ref):
    both = y_ref.shape[1]
    patch = both // 2
    half = patch // 2
    which, i = where[e]
    near = [unpacked(below_ref[(c - low + 1) * half : (c - low + 2) * half, :]) for c in (e - 1, e, e + 1)]
    lower = jnp.dot(downs[which][i], jnp.concatenate(near, axis=0), preferred_element_type=f32)
    upper = unpacked(above_ref[(e - low) * half : (e - low + 1) * half, :].astype(f32))
    total = z_ref[e] + jnp.concatenate([upper, lower], axis=0)
    scale, diagonal = tt_ref[e, :, 0:1], tt_ref[e, :, 1:2]
    return y_ref[e] * (1.0 + scale * scale * diagonal) + scale * total, scale


def middle_step_kernel(
    n, low,
    below_ref, above_ref, z_ref, y_ref, tt_ref, va_ref, wa_ref, vb_ref, wb_ref,
    new_ref, u_ref, up_ref, down_ref,
):
    patch = y_ref.shape[1] // 2
    half = patch // 2
    where = place_of(n)
    for e in range(low, n - low):
        image, scale = joined(e, low, where, (va_ref, vb_ref), z_ref, below_ref, above_ref, y_ref, tt_ref)
        new_ref[e] = image
        u_ref[e] = (scale * image).astype(bf16)
        up_ref[(e - low) * half : (e - low + 1) * half, :] = packed(scale[:patch] * image[:patch]).astype(bf16)
    send_products(down_ref, u_ref, (wa_ref, wb_ref), where, low + 1, n - low - 1, low + 1)


def middle_step(low, below, above, z, y, tt, va, wa, vb, wb):
    n, both, _ = y.shape
    half = both // 4
    return kernel_call(
        functools.partial(middle_step_kernel, n, low),
        (
            sds((n, both, RANK), f32),
            sds((n, both, RANK), bf16),
            sds(((n - 2 * low) * half, 2 * RANK), bf16),
            sds(((n - 2 * low - 2) * half, 2 * RANK), bf16),
        ),
        cost=2 * n * both * both * RANK,
    )(below, above, z, y, tt, va, wa, vb, wb)


def last_step_kernel(n, low, below_ref, above_ref, z_ref, y_ref, tt_ref, va_ref, vb_ref, new_ref, gram_ref, side_ref):
    patch = y_ref.shape[1] // 2
    where = place_of(n)
    for e in range(low, n - low):
        image, _ = joined(e, low, where, (va_ref, vb_ref), z_ref, below_ref, above_ref, y_ref, tt_ref)
        new_ref[0, e - low] = image[:patch]
        new_ref[1, e - low] = image[patch:]
        side_ref[(e - low) * patch : (e - low + 1) * patch, :] = jnp.concatenate(
            [image[:patch], image[patch:]], axis=1
        )
    side = side_ref[...]
    gram = lax.dot_general(side, side, ATB, precision=lax.Precision.HIGHEST, preferred_element_type=f32)
    gram_ref[...] = packed(gram[:RANK, :RANK] + gram[RANK:, RANK:])


def last_step(low, below, above, z, y, tt, va, vb):
    n, both, _ = y.shape
    patch = both // 2
    cols = n - 2 * low
    return kernel_call(
        functools.partial(last_step_kernel, n, low),
        (sds((2, cols, patch, RANK), f32), sds((RANK // 2, 2 * RANK), f32)),
        [pltpu.VMEM((cols * patch, 2 * RANK), f32)],
        cost=2 * n * both * both * RANK,
    )(below, above, z, y, tt, va, vb)


def inverse_factor(gram):
    size = gram.shape[0]
    step = 4
    row = iota((size, 2 * size), 0)
    lane = iota((size, 2 * size), 1)
    table = jnp.concatenate([gram, identity(size).astype(f32)], axis=1)
    for k in range(0, size, step):
        cols = [jnp.broadcast_to(table[:, k + i : k + i + 1], table.shape) for i in range(step)]
        lines = [table[k + i : k + i + 1, :] for i in range(step)]
        for i in range(step):
            inverse = 1.0 / cols[i][k + i : k + i + 1, :]
            for j in range(i + 1, step):
                lines[j] = lines[j] - lines[i] * (cols[i][k + j : k + j + 1, :] * inverse)
                cols[j] = cols[j] - cols[i] * (cols[j][k + i : k + i + 1, :] * inverse)
            table = table - jnp.where(row > k + i, cols[i], 0.0) * (lines[i] * inverse)
    pivots = jnp.sum(jnp.where(row == lane, table, 0.0), axis=1, keepdims=True)
    return table[:, size:] * lax.rsqrt(pivots)


def finish_kernel(factor, count, *refs):
    parts, y_ref, out_ref = refs[:count], refs[count], refs[count + 1]
    total = parts[0][...]
    for part in parts[1:]:
        total = total + part[...]
    inverse = factor * inverse_factor(unpacked(total))
    zero = jnp.zeros_like(inverse)
    wide = jnp.concatenate(
        [jnp.concatenate([inverse, zero], axis=1), jnp.concatenate([zero, inverse], axis=1)], axis=0
    )
    for q in range(y_ref.shape[1] // (2 * RANK)):
        span = slice(q * 2 * RANK, (q + 1) * 2 * RANK)
        out_ref[:, span] = lax.dot_general(
            y_ref[:, span], wide, ABT, precision=lax.Precision.HIGHEST, preferred_element_type=f32
        )


def finish(factor, parts, y):
    return kernel_call(
        functools.partial(finish_kernel, factor, len(parts)),
        sds(y.shape, f32),
        cost=2 * y.shape[0] * y.shape[1] * RANK,
    )(*parts, y)


def exchange_stages():
    stages = []
    for axis in ("col", "row"):
        size = lax.axis_size(axis)
        bit = 1
        if axis == "col":
            stages.append((axis, size, [1]))
            bit = 2
        while bit < size:
            if 2 * bit < size:
                stages.append((axis, size, [bit, 2 * bit, 3 * bit]))
                bit *= 4
            else:
                stages.append((axis, size, [bit]))
                bit *= 2
    return stages


def summed_parts(gram):
    stages = exchange_stages()
    for place, (axis, size, partners) in enumerate(stages):
        parts = [gram] + [
            lax.ppermute(gram, axis, [(i, i ^ p) for i in range(size)]) for p in partners
        ]
        if place == len(stages) - 1:
            return parts
        gram = parts[0]
        for part in parts[1:]:
            gram = gram + part


def passed_along(shard, axis, by):
    count = lax.axis_size(axis)
    pairs = [(i, i + by) for i in range(count) if 0 <= i + by < count]
    return lax.ppermute(shard, axis, pairs)


def local(features, tissue, probe):
    tile_rows, tile_cols, patches, width = features.shape
    first = iota(features.shape, 3) == 0
    marked = jnp.where(first & (features == 0), jnp.asarray(TINY, bf16), features)
    marked = jnp.where(tissue[..., None] != 0, marked, jnp.zeros((), bf16))
    edges = jnp.concatenate([marked[0, :GHOST], marked[0, -GHOST:]], axis=0)
    below_edges = passed_along(edges, "row", -1)
    from_left = passed_along(marked[:, -GHOST:], "col", 1)
    from_right = passed_along(marked[:, :GHOST], "col", -1)
    below_middle = passed_along(marked[0, GHOST:-GHOST], "row", -1)
    probe_left = passed_along(probe[:, -GHOST:], "col", 1)
    probe_right = passed_along(probe[:, :GHOST], "col", -1)
    panel = jnp.concatenate([probe_left, probe, probe_right], axis=1)
    n = panel.shape[1]
    panel = panel.reshape(tile_rows, n, patches, RANK)

    m, u1, stat, payload = own_affinity(marked, from_left, from_right, panel)
    got_below = passed_along(payload, "row", -1)
    below_left = passed_along(below_edges[GHOST:], "col", 1)
    below_right = passed_along(below_edges[:GHOST], "col", -1)
    va, wa, sa = edge_affinity(below_left, below_edges, below_right, u1)
    vb, wb, u0, u2, t, payload = middle_affinity(
        below_edges, below_middle, u1, va, wa, sa, stat, panel, got_below
    )
    got_above = passed_along(payload, "row", 1)
    y, u, tt, up, down = first_iteration(got_above, stat, t, u0, u2, panel, m, va, wa, vb, wb)
    below, above = passed_along(up, "row", -1), passed_along(down, "row", 1)
    z = local_products(3, n - 3, m, u)
    y, u, up, down = middle_step(3, below, above, z, y, tt, va, wa, vb, wb)
    below, above = passed_along(up, "row", -1), passed_along(down, "row", 1)
    z = local_products(4, n - 4, m, u)
    y, gram = last_step(4, below, above, z, y, tt, va, vb)

    parts = summed_parts(gram)
    flat = y.reshape(tile_rows * tile_cols, patches * RANK)
    total = tile_rows * lax.axis_size("row") * tile_cols * lax.axis_size("col") * patches
    out = finish(math.sqrt(float(total)), parts, flat)
    return out.reshape(tile_rows, tile_cols, patches * RANK)


def solution(mesh):
    placed = (P("row", "col", None, None), P("row", "col", None), P("row", "col", None))
    return jax.shard_map(
        local, mesh=mesh, in_specs=placed, out_specs=P("row", "col", None), check_vma=False
    )
```

time: 554 us -> 183 us (0.33); the launches traced: 545 us -> 182 us
  blocking collectives: 129 us -> 0 us
  matrix products: 116 us -> 0 us
  local copies, waits for them, and re-layouts: 106 us -> 12.5 us
  Pallas kernels: 0 us -> 79.3 us
  other arithmetic: 77.6 us -> 7.31 us
  waiting for transfers between devices: 72.5 us -> 30.5 us
  starting transfers between devices: 41.2 us -> 52.2 us
    psum x3 -> x0, blocking collectives: 129 us -> none  [local(): gram_matrix = lax.psum(local_gram, ('row', 'col'))]
    dot_general x35 -> x0, matrix products: 108 us -> none  [the longest x27 94.6 us: local(): jnp.einsum('abpq,abqk->abpk', block, source, precision=lax.Precision.HIGH...]
    pallas_call x0 -> x9, Pallas kernels: none -> 79.3 us  [the longest x1 19.7 us: own_affinity(): kernel_call(functools.partial(own_kernel, n), (sds((n, both, 3 * both), b...]
    reshape x27 -> x2, local copies, waits for them, and re-layouts: 66.1 us -> 4.14 us  [the longest x1 2.37 us: local(): flat = y.reshape(tile_rows * tile_cols, patches * RANK)]
    ppermute x4 -> x14, waiting for transfers between devices: 59.9 us -> 22.8 us  [passed_along(): return lax.ppermute(shard, axis, pairs)]
    another operation x17 -> x0, other arithmetic: 36.3 us -> none  [the longest x9 19.6 us: local(): lower = jnp.linalg.cholesky(gram_matrix)]
    ppermute x4 -> x14, starting transfers between devices: 14.1 us -> 38.3 us  [passed_along(): return lax.ppermute(shard, axis, pairs)]
    slice x23 -> x3, local copies, waits for them, and re-layouts: 23.6 us -> 2.9 us  [the longest x1 1.75 us: local(): from_right = passed_along(marked[:, :GHOST], 'col', -1)]
  transfers between devices with their start and end apart: 16 -> 21, of which waited for: 6 -> 7; matrix products, arithmetic and copies ran while one was open for 10% -> 4% of each run, Pallas kernels for 0% -> 19%
where the time goes in v1:
time: 183 us; the launch traced here: 182 us
  Pallas kernels  79.3 us (43%)
  starting transfers between devices  52.2 us (29%)
  waiting for transfers between devices  30.5 us (17%)
  local copies, waits for them, and re-layouts  12.5 us (7%)
  other arithmetic  7.31 us (4%)
    ppermute x14, starting transfers between devices, passed_along(): return lax.ppermute(shard, axis, pairs)  38.3 us
    ppermute x14, waiting for transfers between devices, passed_along(): return lax.ppermute(shard, axis, pairs)  22.8 us
    pallas_call x1, Pallas kernels, own_affinity(): kernel_call(functools.partial(own_kernel, n), (sds((n, both, 3 * both), b...  19.7 us
    ppermute x7, starting transfers between devices, summed_parts(): lax.ppermute(gram, axis, [(i, i ^ p) for i in range(size)])  13.9 us
    pallas_call x1, Pallas kernels, first_iteration(): kernel_call(functools.partial(first_kernel, n), (sds((n, both, RANK), f32...  12.6 us
    pallas_call x1, Pallas kernels, middle_affinity(): kernel_call(functools.partial(middle_kernel, n), (v, w, sds((n, patch, RA...  11.3 us
    ppermute x7, waiting for transfers between devices, summed_parts(): lax.ppermute(gram, axis, [(i, i ^ p) for i in range(size)])  7.76 us
    pallas_call x1, Pallas kernels, finish(): kernel_call(functools.partial(finish_kernel, factor, len(parts)), sds(y.s...  7.59 us
  transfers between devices with their start and end apart: 21, of which 7 were waited for; matrix products, arithmetic and copies ran while one was open for 4% of the time, Pallas kernels for 19%

profile of v1, /device:TPU:0, one launch (start us, length us, event | category | flops | bytes accessed | tf_op | source)
XLA Modules:
  0.0 182.1 jit_solution(2122185132056652315)
XLA Ops:
  0.0 0.7 broadcast_compare_fusion
  0.7 5.6 %fusion.x_ref = bf16[2,16,64,1024]{3,2,1,0:T(8,128)(2,1)S(1)} fusion(bf16[2,16,64,1024]{3,2,1,0:T(8,128)(2,1)} %param.3, pred[1024]{0:T(1024)(128)(4,1)S(1)} %iota_compare_fusion, pred[2,16,64]{2,1,0:T(8,128)(4,1)S(1)} %broadcast_compare_fusion), kind=kLoop, calls=%fused_computation.1 | loop fusion | flops 12582912 | bytes 8391680 | tf_op jit(solution)/shard_map/jit(_where)/select_n | solution.py:538
  6.4 1.8 fusion.1
  8.1 3.5 %collective-permute-start.2 = (bf16[2,4,64,1024]{3,2,1,0:T(8,128)(2,1)}, bf16[2,4,64,1024]{3,2,1,0:T(8,128)(2,1)}, u32[]{:S(2)}, u32[]{:S(2)}) collective-permute-start(bf16[2,4,64,1024]{3,2,1,0:T(8,128)(2,1)} %get-tuple-element.54), channel_id=1, source_target_pairs={{0,1},{1,2},{2,3},{3,4},{4,5},{5,6},{6,7},{8,9},{9,10},{10,11},{11... | collective-permute-start | bytes 3145736 | tf_op jit(solution)/shard_map/ppermute | solution.py:531
  11.6 1.3 collective-permute-start.3
  12.9 0.1 slice_bitcast_fusion.2
  13.0 0.1 pad_maximum_fusion
  13.1 1.3 collective-permute-start
  14.5 4.2 %collective-permute-start.4 = (f32[2,4,4096]{2,1,0:T(4,128)S(1)}, f32[2,4,4096]{2,1,0:T(4,128)S(1)}, u32[]{:S(2)}, u32[]{:S(2)}) collective-permute-start(f32[2,4,4096]{2,1,0:T(4,128)S(1)} %get-tuple-element.59), channel_id=1, source_target_pairs={{0,1},{1,2},{2,3},{3,4},{4,5},{5,6},{6,7},{8,9},{9,10},{10,11},{11... | collective-permute-start | bytes 393224 | tf_op jit(solution)/shard_map/ppermute | solution.py:531
  18.7 1.3 collective-permute-start.5
  20.0 1.1 slice_bitcast_fusion
  21.1 19.2 %collective-permute-done.be_ref = bf16[8,64,1024]{2,1,0:T(8,128)(2,1)S(1)} collective-permute-done((bf16[8,64,1024]{2,1,0:T(8,128)(2,1)S(1)}, bf16[8,64,1024]{2,1,0:T(8,128)(2,1)S(1)}, u32[]{:S(2)}, u32[]{:S(2)}) %collective-permute-start) | collective-permute-done | bytes 1048608 | tf_op jit(solution)/shard_map/ppermute | solution.py:531
  40.3 1.3 collective-permute-start.1
  41.6 1.1 fusion.2
  42.7 2.8 %collective-permute-start.6 = (bf16[4,64,1024]{2,1,0:T(8,128)(2,1)}, bf16[4,64,1024]{2,1,0:T(8,128)(2,1)S(1)}, u32[]{:S(2)}, u32[]{:S(2)}) collective-permute-start(bf16[4,64,1024]{2,1,0:T(8,128)(2,1)} %get-tuple-element.58), channel_id=1, source_target_pairs={{0,1},{1,2},{2,3},{3,4},{4,5},{5,6},{6,7},{8,9},{9,10},{10,11},{11... | collective-permute-start | bytes 1572872 | tf_op jit(solution)/shard_map/ppermute | solution.py:531
  45.5 1.3 collective-permute-start.7
  46.8 0.1 pad_maximum_fusion.1
  46.9 1.8 reshape.11.p_ref
  48.7 0.0 collective-permute-done.2.xl_ref
  48.7 0.0 collective-permute-done.3.xr_ref
  48.7 19.7 %shard_map.37 = (bf16[24,128,384]{2,1,0:T(8,128)(2,1)}, bf16[24,64,1024]{2,1,0:T(8,128)(2,1)}, f32[24,128,128]{2,1,0:T(8,128)}, bf16[768,128]{1,0:T(8,128)(2,1)}) custom-call(bf16[2,16,64,1024]{3,2,1,0:T(8,128)(2,1)} %copy-done, bf16[2,4,64,1024]{3,2,1,0:T(8,128)(2,1)} %collective-permute-done.2.xl_ref, ...), custom_call_target="tpu_custom_call" | custom-call | flops 2415919104 | bytes 1048576 | tf_op jit(solution)/shard_map/pallas_call | solution.py:146
  68.4 1.3 collective-permute-start.8
  69.7 0.8 copy-done.4
  70.4 7.0 %shard_map.38 = (bf16[12,64,192]{2,1,0:T(8,128)(2,1)}, bf16[12,64,192]{2,1,0:T(8,128)(2,1)}, f32[12,64,128]{2,1,0:T(8,128)}) custom-call(bf16[4,64,1024]{2,1,0:T(8,128)(2,1)} %copy-done.4, bf16[8,64,1024]{2,1,0:T(8,128)(2,1)} %copy-done.1, bf16[4,64,1024]{2,1,0:T(8,128)(2,1)} %collective-permute-done.7.br_ref, bf16[24,64,1024]{2,1,0:T(8,128)(2,1)} %get-tuple-element.29.u1_ref), custom_call_target="tpu_custom_call" | custom-call | flops 603979776 | bytes 1048576 | tf_op jit(solution)/shard_map/pallas_call | solution.py:224
  77.4 0.2 collective-permute-done.8.got_ref
  77.7 0.8 copy-done.3
  78.4 0.1 copy-done.5
  78.5 11.3 %shard_map.39 = (bf16[10,64,192]{2,1,0:T(8,128)(2,1)}, bf16[10,64,192]{2,1,0:T(8,128)(2,1)}, bf16[24,64,64]{2,1,0:T(8,128)(2,1)}, bf16[24,64,64]{2,1,0:T(8,128)(...) custom-call(bf16[8,64,1024]{2,1,0:T(8,128)(2,1)} %copy-done.1, bf16[8,64,1024]{2,1,0:T(8,128)(2,1)} %copy-done.3, ...), custom_call_target="tpu_custom_call" | custom-call | flops 503316480 | bytes 1048576 | tf_op jit(solution)/shard_map/pallas_call | solution.py:283
  89.8 6.3 %collective-permute-start.9 = (bf16[768,128]{1,0:T(8,128)(2,1)}, bf16[768,128]{1,0:T(8,128)(2,1)S(1)}, u32[]{:S(2)}, u32[]{:S(2)}) collective-permute-start(bf16[768,128]{1,0:T(8,128)(2,1)} %get-tuple-element.35), channel_id=1, source_target_pairs={{0,8},{8,16},{16,24},{1,9},{9,17},{17,25},{2,10},{10,18},{18,26},{... | collective-permute-start | bytes 589832 | tf_op jit(solution)/shard_map/ppermute | solution.py:531
  96.1 3.3 %collective-permute-done.9.got_ref = bf16[768,128]{1,0:T(8,128)(2,1)S(1)} collective-permute-done((bf16[768,128]{1,0:T(8,128)(2,1)}, bf16[768,128]{1,0:T(8,128)(2,1)S(1)}, u32[]{:S(2)}, u32[]{:S(2)}) %collective-permute-start.9) | collective-permute-done | bytes 196640 | tf_op jit(solution)/shard_map/ppermute | solution.py:531
  99.4 0.7 copy-done.6
  100.1 12.6 %shard_map.40 = (f32[24,128,64]{2,1,0:T(8,128)}, bf16[24,128,64]{2,1,0:T(8,128)(2,1)}, f32[24,128,128]{2,1,0:T(8,128)}, bf16[640,128]{1,0:T(8,128)(2,1)}, bf16[576,128]{1,0:T(8,128)(2,1)}) custom-call(bf16[768,128]{1,0:T(8,128)(2,1)} %copy-done.6, f32[24,128,128]{2,1,0:T(8,128)} %get-tuple-element.33.stat_ref, f32[24,64,128]{2,1,0:T(8,128)} %get-tuple-element.36.t_ref, ...), custom_call_target="tpu_custom_call" | custom-call | flops 150994944 | bytes 1048576 | tf_op jit(solution)/shard_map/pallas_call | solution.py:352
  112.7 1.3 collective-permute-start.10
  113.9 5.4 %collective-permute-start.11 = (bf16[576,128]{1,0:T(8,128)(2,1)}, bf16[576,128]{1,0:T(8,128)(2,1)S(1)}, u32[]{:S(2)}, u32[]{:S(2)}) collective-permute-start(bf16[576,128]{1,0:T(8,128)(2,1)} %get-tuple-element.43), channel_id=1, source_target_pairs={{0,8},{8,16},{16,24},{1,9},{9,17},{17,25},{2,10},{10,18},{18,26},{... | collective-permute-start | bytes 442376 | tf_op jit(solution)/shard_map/ppermute | solution.py:531
  119.4 3.7 %shard_map.41.z_ref = f32[24,128,64]{2,1,0:T(8,128)} custom-call(bf16[24,128,384]{2,1,0:T(8,128)(2,1)} %get-tuple-element.39.m_ref, bf16[24,128,64]{2,1,0:T(8,128)(2,1)} %get-tuple-element.44.u_ref), custom_call_target="tpu_custom_call" | custom-call | flops 150994944 | bytes 1048576 | tf_op jit(solution)/shard_map/pallas_call | solution.py:375
  123.1 0.0 collective-permute-done.11.above_ref
  123.1 0.0 collective-permute-done.10.below_ref
  123.1 0.6 copy-done.9
  123.7 0.1 copy-done.7
  123.8 7.5 %shard_map.42 = (f32[24,128,64]{2,1,0:T(8,128)}, bf16[24,128,64]{2,1,0:T(8,128)(2,1)}, bf16[576,128]{1,0:T(8,128)(2,1)}, bf16[512,128]{1,0:T(8,128)(2,1)}) custom-call(bf16[640,128]{1,0:T(8,128)(2,1)} %copy-done.7, bf16[576,128]{1,0:T(8,128)(2,1)} %copy-done.9, f32[24,128,64]{2,1,0:T(8,128)} %shard_map.41.z_ref, f32[24,128,64]{2,1,0:T(8,128)} %get-tuple-element.45.y_ref, ...), custom_call_target="tpu_custom_call" | custom-call | flops 50331648 | bytes 1048576 | tf_op jit(solution)/shard_map/pallas_call | solution.py:414
  131.2 1.3 collective-permute-start.12
  132.5 5.8 %collective-permute-start.13 = (bf16[512,128]{1,0:T(8,128)(2,1)}, bf16[512,128]{1,0:T(8,128)(2,1)S(1)}, u32[]{:S(2)}, u32[]{:S(2)}) collective-permute-start(bf16[512,128]{1,0:T(8,128)(2,1)} %get-tuple-element.48), channel_id=1, source_target_pairs={{0,8},{8,16},{16,24},{1,9},{9,17},{17,25},{2,10},{10,18},{18,26},{... | collective-permute-start | bytes 393224 | tf_op jit(solution)/shard_map/ppermute | solution.py:531
  138.4 3.6 %shard_map.43.z_ref = f32[24,128,64]{2,1,0:T(8,128)} custom-call(bf16[24,128,384]{2,1,0:T(8,128)(2,1)} %get-tuple-element.39.m_ref, bf16[24,128,64]{2,1,0:T(8,128)(2,1)} %get-tuple-element.49.u_ref), custom_call_target="tpu_custom_call" | custom-call | flops 150994944 | bytes 1048576 | tf_op jit(solution)/shard_map/pallas_call | solution.py:375
  141.9 0.0 collective-permute-done.13.above_ref
  141.9 0.0 collective-permute-done.12.below_ref
  142.0 0.6 copy-done.10
  142.6 0.1 copy-done.8
  142.6 6.4 %shard_map.44 = (f32[2,16,64,64]{3,2,1,0:T(8,128)}, f32[32,128]{1,0:T(8,128)}) custom-call(bf16[576,128]{1,0:T(8,128)(2,1)} %copy-done.8, bf16[512,128]{1,0:T(8,128)(2,1)} %copy-done.10, f32[24,128,64]{2,1,0:T(8,128)} %shard_map.43.z_ref, f32[24,128,64]{2,1,0:T(8,128)} %get-tuple-element.50.y_ref, f32[24,128,128]{2,1,0:T(8,128)} %get-tuple-element.46.tt_ref, ...), custom_call_target="tpu_custom_call" | custom-call | flops 50331648 | bytes 1048576 | tf_op jit(solution)/shard_map/pallas_call | solution.py:445
  149.1 1.4 collective-permute-start.14
  150.5 1.0 collective-permute-done.14
  151.5 0.7 add.12
  152.2 4.7 %collective-permute-start.15 = (f32[32,128]{1,0:T(8,128)S(1)}, f32[32,128]{1,0:T(8,128)S(1)}, u32[]{:S(2)}, u32[]{:S(2)}) collective-permute-start(f32[32,128]{1,0:T(8,128)S(1)} %add.12), channel_id=1, source_target_pairs={{0,2},{1,3},{2,0},{3,1},{4,6},{5,7},{6,4},{7,5},{8,10},{9,11},{10,... | collective-permute-start | bytes 49160 | tf_op jit(solution)/shard_map/ppermute | solution.py:519
  156.9 2.0 %collective-permute-start.16 = (f32[32,128]{1,0:T(8,128)S(1)}, f32[32,128]{1,0:T(8,128)S(1)}, u32[]{:S(2)}, u32[]{:S(2)}) collective-permute-start(f32[32,128]{1,0:T(8,128)S(1)} %add.12), channel_id=1, source_target_pairs={{0,4},{1,5},{2,6},{3,7},{4,0},{5,1},{6,2},{7,3},{8,12},{9,13},{10,... | collective-permute-start | bytes 49160 | tf_op jit(solution)/shard_map/ppermute | solution.py:519
  158.9 0.4 collective-permute-start.17
  159.3 2.3 %collective-permute-done.16 = f32[32,128]{1,0:T(8,128)S(1)} collective-permute-done((f32[32,128]{1,0:T(8,128)S(1)}, f32[32,128]{1,0:T(8,128)S(1)}, u32[]{:S(2)}, u32[]{:S(2)}) %collective-permute-start.16) | collective-permute-done | bytes 16416 | tf_op jit(solution)/shard_map/ppermute | solution.py:519
  161.6 2.9 %collective-permute-done.17 = f32[32,128]{1,0:T(8,128)S(1)} collective-permute-done((f32[32,128]{1,0:T(8,128)S(1)}, f32[32,128]{1,0:T(8,128)S(1)}, u32[]{:S(2)}, u32[]{:S(2)}) %collective-permute-start.17) | collective-permute-done | bytes 16416 | tf_op jit(solution)/shard_map/ppermute | solution.py:519
  164.5 3.0 %collective-permute-start.18 = (f32[32,128]{1,0:T(8,128)S(1)}, f32[32,128]{1,0:T(8,128)S(1)}, u32[]{:S(2)}, u32[]{:S(2)}) collective-permute-start(f32[32,128]{1,0:T(8,128)S(1)} %add_add_fusion.refs_0_), channel_id=1, source_target_pairs={{0,8},{8,0},{16,24},{24,16},{1,9},{9,1},{17,25},{25,17},{2,10},{10... | collective-permute-start | bytes 49160 | tf_op jit(solution)/shard_map/ppermute | solution.py:519
  167.5 1.8 collective-permute-start.19
  169.2 0.7 collective-permute-start.20
  169.9 2.4 %reshape.12.refs_4_ = f32[32,4096]{1,0:T(8,128)} reshape(f32[2,16,64,64]{3,2,1,0:T(8,128)} %get-tuple-element.52) | data formatting | bytes 1048576 | tf_op jit(solution)/shard_map/reshape | solution.py:568
  172.3 0.0 collective-permute-done.18.refs_1_
  172.3 1.6 collective-permute-done.20.refs_3_
  173.9 0.6 copy-done.14
  174.5 7.6 %shard_map.45 = f32[32,4096]{1,0:T(8,128)} custom-call(f32[32,128]{1,0:T(8,128)} %copy-done.11, f32[32,128]{1,0:T(8,128)} %copy-done.12, f32[32,128]{1,0:T(8,128)} %copy-done.13, f32[32,128]{1,0:T(8,128)} %copy-done.14, f32[32,4096]{1,0:T(8,128)} %reshape.12.refs_4_), custom_call_target="tpu_custom_call" | custom-call | flops 16777216 | bytes 1048576 | tf_op jit(solution)/shard_map/pallas_call | solution.py:490
  (31 shorter events, 0.1 us)
Async XLA Ops:
  6.4 13.6 %copy-start = (bf16[2,16,64,1024]{3,2,1,0:T(8,128)(2,1)}, bf16[2,16,64,1024]{3,2,1,0:T(8,128)(2,1)S(1)}, u32[]{:S(2)}) copy-start(bf16[2,16,64,1024]{3,2,1,0:T(8,128)(2,1)S(1)} %fusion.x_ref) | copy-start | bytes 12582916
  8.1 6.3 %copy-start.2 = (f32[2,16,4096]{2,1,0:T(8,128)S(1)}, f32[2,16,4096]{2,1,0:T(8,128)}, u32[]{:S(2)}) copy-start(f32[2,16,4096]{2,1,0:T(8,128)} %param.5) | copy-start | bytes 1572868
  8.1 40.6 %collective-permute-start.2 = (bf16[2,4,64,1024]{3,2,1,0:T(8,128)(2,1)}, bf16[2,4,64,1024]{3,2,1,0:T(8,128)(2,1)}, u32[]{:S(2)}, u32[]{:S(2)}) collective-permute-start(bf16[2,4,64,1024]{3,2,1,0:T(8,128)(2,1)} %get-tuple-element.54), channel_id=1, source_target_pairs={{0,1},{1,2},{2,3},{3,4},{4,5},{5,6},{6,7},{8,9},{9,10},{10,11},{11... | collective-permute-start | bytes 3145736 | tf_op jit(solution)/shard_map/ppermute | solution.py:531
  11.6 37.1 %collective-permute-start.3 = (bf16[2,4,64,1024]{3,2,1,0:T(8,128)(2,1)}, bf16[2,4,64,1024]{3,2,1,0:T(8,128)(2,1)}, u32[]{:S(2)}, u32[]{:S(2)}) collective-permute-start(bf16[2,4,64,1024]{3,2,1,0:T(8,128)(2,1)} %get-tuple-element.53), channel_id=1, source_target_pairs={{1,0},{2,1},{3,2},{4,3},{5,4},{6,5},{7,6},{9,8},{10,9},{11,10},{12... | collective-permute-start | bytes 3145736 | tf_op jit(solution)/shard_map/ppermute | solution.py:531
  13.1 27.2 %collective-permute-start = (bf16[8,64,1024]{2,1,0:T(8,128)(2,1)S(1)}, bf16[8,64,1024]{2,1,0:T(8,128)(2,1)S(1)}, u32[]{:S(2)}, u32[]{:S(2)}) collective-permute-start(bf16[8,64,1024]{2,1,0:T(8,128)(2,1)S(1)} %pad_maximum_fusion), channel_id=1, source_target_pairs={{8,0},{16,8},{24,16},{9,1},{17,9},{25,17},{10,2},{18,10},{26,18},{... | collective-permute-start | bytes 3145736 | tf_op jit(solution)/shard_map/ppermute | solution.py:531
  14.5 28.2 %collective-permute-start.4 = (f32[2,4,4096]{2,1,0:T(4,128)S(1)}, f32[2,4,4096]{2,1,0:T(4,128)S(1)}, u32[]{:S(2)}, u32[]{:S(2)}) collective-permute-start(f32[2,4,4096]{2,1,0:T(4,128)S(1)} %get-tuple-element.59), channel_id=1, source_target_pairs={{0,1},{1,2},{2,3},{3,4},{4,5},{5,6},{6,7},{8,9},{9,10},{10,11},{11... | collective-permute-start | bytes 393224 | tf_op jit(solution)/shard_map/ppermute | solution.py:531
  18.7 26.8 %collective-permute-start.5 = (f32[2,4,4096]{2,1,0:T(4,128)S(1)}, f32[2,4,4096]{2,1,0:T(4,128)S(1)}, u32[]{:S(2)}, u32[]{:S(2)}) collective-permute-start(f32[2,4,4096]{2,1,0:T(4,128)S(1)} %get-tuple-element.60), channel_id=1, source_target_pairs={{1,0},{2,1},{3,2},{4,3},{5,4},{6,5},{7,6},{9,8},{10,9},{11,10},{12... | collective-permute-start | bytes 393224 | tf_op jit(solution)/shard_map/ppermute | solution.py:531
  40.3 28.1 %copy-start.1 = (bf16[8,64,1024]{2,1,0:T(8,128)(2,1)}, bf16[8,64,1024]{2,1,0:T(8,128)(2,1)S(1)}, u32[]{:S(2)}) copy-start(bf16[8,64,1024]{2,1,0:T(8,128)(2,1)S(1)} %collective-permute-done.be_ref) | copy-start | bytes 3145732
  40.3 37.1 %collective-permute-start.1 = (bf16[8,64,1024]{2,1,0:T(8,128)(2,1)}, bf16[8,64,1024]{2,1,0:T(8,128)(2,1)S(1)}, u32[]{:S(2)}, u32[]{:S(2)}) collective-permute-start(bf16[8,64,1024]{2,1,0:T(8,128)(2,1)} %slice_bitcast_fusion), channel_id=1, source_target_pairs={{8,0},{16,8},{24,16},{9,1},{17,9},{25,17},{10,2},{18,10},{26,18},{... | collective-permute-start | bytes 3145736 | tf_op jit(solution)/shard_map/ppermute | solution.py:531
  42.7 27.0 %collective-permute-start.6 = (bf16[4,64,1024]{2,1,0:T(8,128)(2,1)}, bf16[4,64,1024]{2,1,0:T(8,128)(2,1)S(1)}, u32[]{:S(2)}, u32[]{:S(2)}) collective-permute-start(bf16[4,64,1024]{2,1,0:T(8,128)(2,1)} %get-tuple-element.58), channel_id=1, source_target_pairs={{0,1},{1,2},{2,3},{3,4},{4,5},{5,6},{6,7},{8,9},{9,10},{10,11},{11... | collective-permute-start | bytes 1572872 | tf_op jit(solution)/shard_map/ppermute | solution.py:531
  45.5 24.2 %collective-permute-start.7 = (bf16[4,64,1024]{2,1,0:T(8,128)(2,1)}, bf16[4,64,1024]{2,1,0:T(8,128)(2,1)}, u32[]{:S(2)}, u32[]{:S(2)}) collective-permute-start(bf16[4,64,1024]{2,1,0:T(8,128)(2,1)} %get-tuple-element.57), channel_id=1, source_target_pairs={{1,0},{2,1},{3,2},{4,3},{5,4},{6,5},{7,6},{9,8},{10,9},{11,10},{12... | collective-permute-start | bytes 1572872 | tf_op jit(solution)/shard_map/ppermute | solution.py:531
  68.4 9.3 %collective-permute-start.8 = (bf16[768,128]{1,0:T(8,128)(2,1)}, bf16[768,128]{1,0:T(8,128)(2,1)S(1)}, u32[]{:S(2)}, u32[]{:S(2)}) collective-permute-start(bf16[768,128]{1,0:T(8,128)(2,1)} %get-tuple-element.34), channel_id=1, source_target_pairs={{8,0},{16,8},{24,16},{9,1},{17,9},{25,17},{10,2},{18,10},{26,18},{... | collective-permute-start | bytes 589832 | tf_op jit(solution)/shard_map/ppermute | solution.py:531
  69.7 0.8 copy-start.4
  77.4 1.0 copy-start.3
  77.7 0.9 copy-start.5
  89.8 9.6 %collective-permute-start.9 = (bf16[768,128]{1,0:T(8,128)(2,1)}, bf16[768,128]{1,0:T(8,128)(2,1)S(1)}, u32[]{:S(2)}, u32[]{:S(2)}) collective-permute-start(bf16[768,128]{1,0:T(8,128)(2,1)} %get-tuple-element.35), channel_id=1, source_target_pairs={{0,8},{8,16},{16,24},{1,9},{9,17},{17,25},{2,10},{10,18},{18,26},{... | collective-permute-start | bytes 589832 | tf_op jit(solution)/shard_map/ppermute | solution.py:531
  99.4 0.7 copy-start.6
  112.7 10.4 %collective-permute-start.10 = (bf16[640,128]{1,0:T(8,128)(2,1)}, bf16[640,128]{1,0:T(8,128)(2,1)S(1)}, u32[]{:S(2)}, u32[]{:S(2)}) collective-permute-start(bf16[640,128]{1,0:T(8,128)(2,1)} %get-tuple-element.42), channel_id=1, source_target_pairs={{8,0},{16,8},{24,16},{9,1},{17,9},{25,17},{10,2},{18,10},{26,18},{... | collective-permute-start | bytes 491528 | tf_op jit(solution)/shard_map/ppermute | solution.py:531
  113.9 9.1 %collective-permute-start.11 = (bf16[576,128]{1,0:T(8,128)(2,1)}, bf16[576,128]{1,0:T(8,128)(2,1)S(1)}, u32[]{:S(2)}, u32[]{:S(2)}) collective-permute-start(bf16[576,128]{1,0:T(8,128)(2,1)} %get-tuple-element.43), channel_id=1, source_target_pairs={{0,8},{8,16},{16,24},{1,9},{9,17},{17,25},{2,10},{10,18},{18,26},{... | collective-permute-start | bytes 442376 | tf_op jit(solution)/shard_map/ppermute | solution.py:531
  123.1 0.7 copy-start.9
  123.1 0.7 copy-start.7
  131.2 10.7 %collective-permute-start.12 = (bf16[576,128]{1,0:T(8,128)(2,1)}, bf16[576,128]{1,0:T(8,128)(2,1)S(1)}, u32[]{:S(2)}, u32[]{:S(2)}) collective-permute-start(bf16[576,128]{1,0:T(8,128)(2,1)} %get-tuple-element.47), channel_id=1, source_target_pairs={{8,0},{16,8},{24,16},{9,1},{17,9},{25,17},{10,2},{18,10},{26,18},{... | collective-permute-start | bytes 442376 | tf_op jit(solution)/shard_map/ppermute | solution.py:531
  132.5 9.4 %collective-permute-start.13 = (bf16[512,128]{1,0:T(8,128)(2,1)}, bf16[512,128]{1,0:T(8,128)(2,1)S(1)}, u32[]{:S(2)}, u32[]{:S(2)}) collective-permute-start(bf16[512,128]{1,0:T(8,128)(2,1)} %get-tuple-element.48), channel_id=1, source_target_pairs={{0,8},{8,16},{16,24},{1,9},{9,17},{17,25},{2,10},{10,18},{18,26},{... | collective-permute-start | bytes 393224 | tf_op jit(solution)/shard_map/ppermute | solution.py:531
  141.9 0.7 copy-start.10
  141.9 0.7 copy-start.8
  149.1 2.4 %collective-permute-start.14 = (f32[32,128]{1,0:T(8,128)}, f32[32,128]{1,0:T(8,128)S(1)}, u32[]{:S(2)}, u32[]{:S(2)}) collective-permute-start(f32[32,128]{1,0:T(8,128)} %get-tuple-element.51), channel_id=1, source_target_pairs={{0,1},{1,0},{2,3},{3,2},{4,5},{5,4},{6,7},{7,6},{8,9},{9,8},{10,11... | collective-permute-start | bytes 49160 | tf_op jit(solution)/shard_map/ppermute | solution.py:519
  152.2 7.1 %collective-permute-start.15 = (f32[32,128]{1,0:T(8,128)S(1)}, f32[32,128]{1,0:T(8,128)S(1)}, u32[]{:S(2)}, u32[]{:S(2)}) collective-permute-start(f32[32,128]{1,0:T(8,128)S(1)} %add.12), channel_id=1, source_target_pairs={{0,2},{1,3},{2,0},{3,1},{4,6},{5,7},{6,4},{7,5},{8,10},{9,11},{10,... | collective-permute-start | bytes 49160 | tf_op jit(solution)/shard_map/ppermute | solution.py:519
  156.9 4.7 %collective-permute-start.16 = (f32[32,128]{1,0:T(8,128)S(1)}, f32[32,128]{1,0:T(8,128)S(1)}, u32[]{:S(2)}, u32[]{:S(2)}) collective-permute-start(f32[32,128]{1,0:T(8,128)S(1)} %add.12), channel_id=1, source_target_pairs={{0,4},{1,5},{2,6},{3,7},{4,0},{5,1},{6,2},{7,3},{8,12},{9,13},{10,... | collective-permute-start | bytes 49160 | tf_op jit(solution)/shard_map/ppermute | solution.py:519
  158.9 5.5 %collective-permute-start.17 = (f32[32,128]{1,0:T(8,128)S(1)}, f32[32,128]{1,0:T(8,128)S(1)}, u32[]{:S(2)}, u32[]{:S(2)}) collective-permute-start(f32[32,128]{1,0:T(8,128)S(1)} %add.12), channel_id=1, source_target_pairs={{0,6},{1,7},{2,4},{3,5},{4,2},{5,3},{6,0},{7,1},{8,14},{9,15},{10,... | collective-permute-start | bytes 49160 | tf_op jit(solution)/shard_map/ppermute | solution.py:519
  164.5 9.4 %copy-start.11 = (f32[32,128]{1,0:T(8,128)}, f32[32,128]{1,0:T(8,128)S(1)}, u32[]{:S(2)}) copy-start(f32[32,128]{1,0:T(8,128)S(1)} %add_add_fusion.refs_0_) | copy-start | bytes 49156
  164.5 7.8 %collective-permute-start.18 = (f32[32,128]{1,0:T(8,128)S(1)}, f32[32,128]{1,0:T(8,128)S(1)}, u32[]{:S(2)}, u32[]{:S(2)}) collective-permute-start(f32[32,128]{1,0:T(8,128)S(1)} %add_add_fusion.refs_0_), channel_id=1, source_target_pairs={{0,8},{8,0},{16,24},{24,16},{1,9},{9,1},{17,25},{25,17},{2,10},{10... | collective-permute-start | bytes 49160 | tf_op jit(solution)/shard_map/ppermute | solution.py:519
  167.5 4.8 %collective-permute-start.19 = (f32[32,128]{1,0:T(8,128)S(1)}, f32[32,128]{1,0:T(8,128)S(1)}, u32[]{:S(2)}, u32[]{:S(2)}) collective-permute-start(f32[32,128]{1,0:T(8,128)S(1)} %add_add_fusion.refs_0_), channel_id=1, source_target_pairs={{0,16},{8,24},{16,0},{24,8},{1,17},{9,25},{17,1},{25,9},{2,18},{10... | collective-permute-start | bytes 49160 | tf_op jit(solution)/shard_map/ppermute | solution.py:519
  169.2 4.6 %collective-permute-start.20 = (f32[32,128]{1,0:T(8,128)S(1)}, f32[32,128]{1,0:T(8,128)S(1)}, u32[]{:S(2)}, u32[]{:S(2)}) collective-permute-start(f32[32,128]{1,0:T(8,128)S(1)} %add_add_fusion.refs_0_), channel_id=1, source_target_pairs={{0,24},{8,16},{16,8},{24,0},{1,25},{9,17},{17,9},{25,1},{2,26},{10... | collective-permute-start | bytes 49160 | tf_op jit(solution)/shard_map/ppermute | solution.py:519
  172.3 1.6 copy-start.12
  172.3 1.6 copy-start.13
  173.9 0.6 copy-start.14

commit v2 on v1

v2 whole, which is shorter than its diff:
```python
import functools
import math

import jax
import jax.numpy as jnp
from jax import lax
from jax.experimental import pallas as pl
from jax.experimental.pallas import tpu as pltpu
from jax.sharding import PartitionSpec as P

RANK = 64
ITERS = 3
AFFINITY_TEMP = 4.0

GHOST = ITERS + 1
EDGE = 5
TINY = 1e-30
VMEM_BYTES = 16 * 1024 * 1024
FLOOR = math.exp(-AFFINITY_TEMP)
ABT = (((1,), (1,)), ((), ()))
ATB = (((0,), (0,)), ((), ()))

f32 = jnp.float32
bf16 = jnp.bfloat16


def kernel_call(body, out_shape, scratch=(), cost=0):
    return pl.pallas_call(
        body,
        out_shape=out_shape,
        scratch_shapes=list(scratch),
        compiler_params=pltpu.CompilerParams(vmem_limit_bytes=VMEM_BYTES),
        cost_estimate=pl.CostEstimate(flops=cost, bytes_accessed=1 << 20, transcendentals=0),
    )


def sds(shape, dtype):
    return jax.ShapeDtypeStruct(shape, dtype)


def iota(shape, dim):
    return lax.broadcasted_iota(jnp.int32, shape, dim)


def identity(n):
    return iota((n, n), 0) == iota((n, n), 1)


def unit_and_mask(block):
    values = block.astype(f32)
    scaled = values * lax.rsqrt(jnp.sum(values * values, axis=-1, keepdims=True) + 1e-06)
    return scaled.astype(bf16), (values[:, :1] != 0.0).astype(f32)


def affinity_of(left, right):
    scores = lax.dot_general(left, right, ABT, preferred_element_type=f32)
    return jnp.exp(AFFINITY_TEMP * scores - AFFINITY_TEMP)


def at_lane(lane, e, column, table):
    return jnp.where(lane == e, column, table)


def absent_near(mask, width):
    count = jnp.sum(mask, axis=0, keepdims=True)
    return width - (pltpu.roll(count, 1, 1) + count + pltpu.roll(count, 127, 1))


def packed(block):
    half = block.shape[0] // 2
    return jnp.concatenate([block[:half], block[half:]], axis=1)


def unpacked(block):
    return jnp.concatenate([block[:, :RANK], block[:, RANK:]], axis=0)


def panel_at(panel, row, e):
    left_ref, own_ref, right_ref = panel
    own = own_ref.shape[1]
    if GHOST <= e < GHOST + own:
        return own_ref[row, e - GHOST]
    both = (left_ref[row, e] if e < GHOST else right_ref[row, e - GHOST - own]).astype(f32)
    return both[:, :RANK] + both[:, RANK:]


def pair_of(values):
    high = values.astype(bf16)
    return high, (values - high.astype(f32)).astype(bf16)


def by_sublane(tissue):
    mask = (tissue != 0).astype(bf16)
    return lax.dot_general(mask, identity(mask.shape[0]).astype(bf16), ATB, preferred_element_type=f32)


def marked(tile, column):
    zero = (iota(tile.shape, 1) == 0) & (tile == 0)
    return jnp.where(zero, jnp.asarray(TINY, bf16), tile) * column.astype(bf16)


def mark_row_kernel(x_ref, tissue_ref, edge_ref, middle_ref, tile_ref, mask_ref, sem_ref):
    cols = x_ref.shape[1]
    copies = [pltpu.make_async_copy(x_ref.at[0, c], tile_ref.at[c], sem_ref.at[c]) for c in range(cols)]
    mask_copy = pltpu.make_async_copy(tissue_ref.at[0], mask_ref, sem_ref.at[cols])
    mask_copy.start()
    for copy in copies:
        copy.start()
    mask_copy.wait()
    mask = by_sublane(mask_ref[...])
    for c in range(cols):
        copies[c].wait()
        tile = marked(tile_ref[c], mask[:, c : c + 1])
        if c < EDGE:
            edge_ref[c] = tile
        elif c < cols - EDGE:
            middle_ref[c - EDGE] = tile
        else:
            edge_ref[c - cols + 2 * EDGE] = tile


def mark_row(x, tissue):
    rows, cols, patch, width = x.shape
    vmem = pl.BlockSpec(memory_space=pltpu.VMEM)
    hbm = pl.BlockSpec(memory_space=pltpu.HBM)
    return pl.pallas_call(
        mark_row_kernel,
        in_specs=[hbm, hbm],
        out_specs=[vmem] * 2,
        out_shape=(
            sds((2 * EDGE, patch, width), bf16),
            sds((cols - 2 * EDGE, patch, width), bf16),
        ),
        scratch_shapes=[
            pltpu.VMEM((cols, patch, width), bf16),
            pltpu.VMEM((cols, patch), jnp.int32),
            pltpu.SemaphoreType.DMA((cols + 1,)),
        ],
        compiler_params=pltpu.CompilerParams(vmem_limit_bytes=VMEM_BYTES),
    )(pltpu.with_memory_space_constraint(x, pltpu.HBM), pltpu.with_memory_space_constraint(tissue, pltpu.HBM))


def mark_ends_kernel(first_ref, last_ref, tissue_ref, after_ref, left_ref, right_ref):
    rows, count, patch, width = first_ref.shape
    cols = tissue_ref.shape[1]
    for row in range(rows):
        mask = by_sublane(tissue_ref[row])
        for c in range(count):
            left_ref[row, c] = marked(first_ref[row, c], mask[:, c : c + 1])
            at = cols - count + c
            right_ref[row, c] = marked(last_ref[row, c], mask[:, at : at + 1])


def mark_ends(x, tissue, after):
    rows, cols, patch, width = x.shape
    shape = (rows, GHOST, patch, width)
    return pl.pallas_call(
        mark_ends_kernel,
        grid=(1,),
        in_specs=[
            pl.BlockSpec(shape, lambda i: (0, 0, 0, 0)),
            pl.BlockSpec(shape, lambda i: (0, cols // GHOST - 1, 0, 0)),
            pl.BlockSpec((rows, cols, patch), lambda i: (0, 0, 0)),
            pl.BlockSpec(memory_space=pl.ANY),
        ],
        out_specs=[pl.BlockSpec(shape, lambda i: (0, 0, 0, 0))] * 2,
        out_shape=(sds(shape, bf16), sds(shape, bf16)),
        compiler_params=pltpu.CompilerParams(vmem_limit_bytes=VMEM_BYTES),
    )(x, x, tissue, after)


def units_kernel(n, x_ref, tissue_ref, probe_ref, after_ref, unit0_ref, unit1_ref, left_ref, right_ref):
    rows, cols, patch, width = x_ref.shape
    for row, unit_ref in ((0, unit0_ref), (1, unit1_ref)):
        mask = by_sublane(tissue_ref[row]).astype(bf16)
        for c in range(cols):
            unit, _ = unit_and_mask(x_ref[row, c])
            at = (GHOST + c) * patch
            unit_ref[at : at + patch, :] = unit * mask[:, c : c + 1]
        for c in range(GHOST):
            left_ref[row, c] = jnp.concatenate(pair_of(probe_ref[row, c]), axis=1)
            right_ref[row, c] = jnp.concatenate(pair_of(probe_ref[row, cols - GHOST + c]), axis=1)


def own_units(x, tissue, probe, after):
    rows, cols, patch, width = x.shape
    n = cols + 2 * GHOST
    vmem = pl.BlockSpec(memory_space=pltpu.VMEM)
    side = sds((rows, GHOST, patch, 2 * RANK), bf16)
    unit = sds((n * patch, width), bf16)
    return pl.pallas_call(
        functools.partial(units_kernel, n),
        in_specs=[vmem, vmem, vmem, pl.BlockSpec(memory_space=pl.ANY)],
        out_specs=[vmem] * 4,
        out_shape=(unit, unit, side, side),
        compiler_params=pltpu.CompilerParams(vmem_limit_bytes=VMEM_BYTES),
    )(x, tissue, probe, after)


def bands(ranges, patch, unit0_ref, unit1_ref, m_ref, degree, diagonal):
    both = 2 * patch
    shape = (both, 3 * both)
    patch_of = iota(shape, 0)
    own = iota(shape, 1) == jnp.where(patch_of < patch, patch_of + patch, patch_of + 3 * patch)
    lane = iota((both, 128), 1)

    def band(e, carry):
        degree, diagonal = carry
        around = pl.ds(pl.multiple_of((e - 1) * patch, patch), 3 * patch)
        here = pl.ds(pl.multiple_of(e * patch, patch), patch)
        left = jnp.concatenate([unit0_ref[here, :], unit1_ref[here, :]], axis=0)
        right = jnp.concatenate([unit0_ref[around, :], unit1_ref[around, :]], axis=0)
        weights = affinity_of(left, right)
        others = jnp.where(own, 0.0, weights)
        m_ref[e] = others.astype(bf16)
        itself = jnp.sum(weights - others, axis=1, keepdims=True)
        degree = at_lane(lane, e, jnp.sum(weights, axis=1, keepdims=True), degree)
        diagonal = at_lane(lane, e, itself, diagonal)
        return degree, diagonal

    carry = (degree, diagonal)
    for low, high in ranges:
        carry = lax.fori_loop(low, high, band, carry)
    return carry


def inside_kernel(n, unit0_ref, unit1_ref, m_ref, sum_ref):
    patch = m_ref.shape[1] // 2
    empty = jnp.zeros((2 * patch, 128), f32)
    sum_ref[0], sum_ref[1] = bands([(GHOST + 1, n - GHOST - 1)], patch, unit0_ref, unit1_ref, m_ref, empty, empty)


def inside_affinity(unit0, unit1, patch):
    n = unit0.shape[0] // patch
    both = 2 * patch
    return pl.pallas_call(
        functools.partial(inside_kernel, n),
        out_shape=(sds((n, both, 3 * both), bf16), sds((2, both, 128), f32)),
        compiler_params=pltpu.CompilerParams(vmem_limit_bytes=VMEM_BYTES),
    )(unit0, unit1)


def outside_kernel(
    n,
    start0_ref, start1_ref, some_ref, xl_ref, xr_ref, tissue_ref, sum_ref, pl_ref, p_ref, pr_ref,
    unit0_ref, unit1_ref, m_ref, stat_ref, pay_ref,
):
    rows, count, patch, width = xl_ref.shape
    cols = n - 2 * count
    both = rows * patch
    lane = iota((patch, 128), 1)

    masks = []
    for row, unit_ref in ((0, unit0_ref), (1, unit1_ref)):
        own_mask = by_sublane(tissue_ref[row])
        mask = jnp.zeros((patch, 128), f32)
        for e in range(n):
            if e < count:
                unit, column = unit_and_mask(xl_ref[row, e])
            elif e < count + cols:
                unit, column = None, own_mask[:, e - count : e - count + 1]
            else:
                unit, column = unit_and_mask(xr_ref[row, e - count - cols])
            mask = at_lane(lane, e, column, mask)
            if unit is not None:
                unit_ref[e * patch : (e + 1) * patch, :] = unit
        masks.append(mask)
    mask = jnp.concatenate(masks, axis=0)
    ranges = [(1, GHOST + 1), (n - GHOST - 1, n - 1)]
    degree, diagonal = bands(ranges, patch, unit0_ref, unit1_ref, m_ref, sum_ref[0], sum_ref[1])
    degree = degree - FLOOR * absent_near(mask, 3 * both)
    stat_ref[0] = degree
    stat_ref[1] = diagonal
    stat_ref[2] = mask
    half = patch // 2
    tail = (n - 2) * half
    for e in range(1, n - 1):
        pay_ref[(e - 1) * half : e * half, :] = packed(panel_at((pl_ref, p_ref, pr_ref), 0, e)).astype(bf16)
    pay_ref[tail : tail + patch, :], pay_ref[tail + patch :, :] = pair_of(degree[:patch])


def payload_rows(columns, patch):
    return columns * patch // 2 + 2 * patch


def outside_affinity(unit0, unit1, m, xl, xr, tissue, sums, panel):
    n, both, _ = m.shape
    payload = sds((payload_rows(n - 2, both // 2), 2 * RANK), bf16)
    unit = sds(unit0.shape, bf16)
    return pl.pallas_call(
        functools.partial(outside_kernel, n),
        out_shape=(unit, unit, sds(m.shape, bf16), sds((3, both, 128), f32), payload),
        input_output_aliases={0: 0, 1: 1, 2: 2},
        compiler_params=pltpu.CompilerParams(vmem_limit_bytes=VMEM_BYTES),
    )(unit0, unit1, m, xl, xr, tissue, sums, *panel)


def cut_kernel(be_ref, after_ref, left_ref, right_ref):
    left_ref[...] = be_ref[:GHOST]
    right_ref[...] = be_ref[be_ref.shape[0] - GHOST :]


def cut(be, after):
    vmem = pl.BlockSpec(memory_space=pltpu.VMEM)
    side = sds((GHOST,) + be.shape[1:], be.dtype)
    return pl.pallas_call(
        cut_kernel,
        in_specs=[vmem, pl.BlockSpec(memory_space=pl.ANY)],
        out_specs=[vmem] * 2,
        out_shape=(side, side),
        compiler_params=pltpu.CompilerParams(vmem_limit_bytes=VMEM_BYTES),
    )(be, after)


def cross_columns(patch, columns, sources, own_ref, unit_ref, v_ref, w_ref, sums):
    lane = iota((patch, 128), 1)
    down_sum, up_sum, mask = sums
    needed = sorted({c for e in columns for c in (e - 1, e, e + 1)})
    for c in needed:
        ref, index = sources[c]
        unit, column = unit_and_mask(ref[index])
        unit_ref[c * patch : (c + 1) * patch, :] = unit
        mask = at_lane(lane, c, column, mask)
    for place, e in enumerate(columns):
        around = slice((e - 1) * patch, (e + 2) * patch)
        here = slice(e * patch, (e + 1) * patch)
        down = affinity_of(own_ref[here, :], unit_ref[around, :])
        up = affinity_of(unit_ref[here, :], own_ref[around, :])
        v_ref[place] = down.astype(bf16)
        w_ref[place] = up.astype(bf16)
        down_sum = at_lane(lane, e, jnp.sum(down, axis=1, keepdims=True), down_sum)
        up_sum = at_lane(lane, e, jnp.sum(up, axis=1, keepdims=True), up_sum)
    return down_sum, up_sum, mask


def edge_columns(n):
    return list(range(1, GHOST + EDGE - 1)) + list(range(n - GHOST - EDGE + 1, n - 1))


def middle_columns(n):
    return list(range(GHOST + EDGE - 1, n - GHOST - EDGE + 1))


def inner(columns, low, high):
    return [e for e in columns if low <= e < high and e - 1 in columns and e + 1 in columns]


def place_of(n):
    edge, middle = edge_columns(n), middle_columns(n)
    return {e: (0, i) for i, e in enumerate(edge)} | {e: (1, i) for i, e in enumerate(middle)}


def below_sources(n, bl_ref, be_ref, bm_ref, br_ref):
    sources = {}
    for c in range(n):
        if c < GHOST:
            sources[c] = (bl_ref, c)
        elif c < GHOST + EDGE:
            sources[c] = (be_ref, c - GHOST)
        elif c < n - GHOST - EDGE:
            sources[c] = (bm_ref, c - GHOST - EDGE)
        elif c < n - GHOST:
            sources[c] = (be_ref, c - (n - GHOST) + 2 * EDGE)
        else:
            sources[c] = (br_ref, c - (n - GHOST))
    return sources


def scale_of(stat_ref, sums):
    down_sum, _, mask = sums
    patch = mask.shape[0]
    degree = 1.0 + stat_ref[0, patch:] + down_sum - FLOOR * absent_near(mask, 3 * patch)
    return stat_ref[2, patch:] * lax.rsqrt(degree)


def products(columns, where, ups, u_ref, pay_ref, first):
    half = u_ref.shape[1] // 2
    for e in columns:
        which, i = where[e]
        source = u_ref[e - 1 : e + 2].reshape(3 * u_ref.shape[1], RANK)
        product = jnp.dot(ups[which][i], source, preferred_element_type=f32)
        pay_ref[(e - first) * half : (e - first + 1) * half, :] = packed(product).astype(bf16)


def edge_kernel(n, bl_ref, be_ref, br_ref, u1_ref, stat_ref, pl_ref, p_ref, pr_ref, v_ref, w_ref, sum_ref, u0_ref, pay_ref, unit_ref):
    patch = be_ref.shape[1]
    sources = below_sources(n, bl_ref, be_ref, None, br_ref)
    columns = edge_columns(n)
    empty = jnp.zeros((patch, 128), f32)
    sums = cross_columns(patch, columns, sources, u1_ref, unit_ref, v_ref, w_ref, (empty, empty, empty))
    for i in range(3):
        sum_ref[i] = sums[i]
    scale = scale_of(stat_ref, sums)
    for e in columns:
        u0_ref[e] = (scale[:, e : e + 1] * panel_at((pl_ref, p_ref, pr_ref), 1, e)).astype(bf16)
    products(inner(columns, 2, n - 2), place_of(n), (w_ref, None), u0_ref, pay_ref, 2)


def edge_affinity(bl, be, br, u1, stat, panel):
    _, patch, width = be.shape
    n = u1.shape[0] // patch
    count = len(edge_columns(n))
    return kernel_call(
        functools.partial(edge_kernel, n),
        (
            sds((count, patch, 3 * patch), bf16),
            sds((count, patch, 3 * patch), bf16),
            sds((3, patch, 128), f32),
            sds((n, patch, RANK), bf16),
            sds(((n - 4) * patch // 2, 2 * RANK), bf16),
        ),
        [pltpu.VMEM((n * patch, width), bf16)],
        cost=4 * count * patch * 3 * patch * width,
    )(bl, be, br, u1, stat, *panel)


def middle_kernel(
    n,
    be_ref, bm_ref, u1_ref, stat_ref, pl_ref, p_ref, pr_ref, sa_ref, ua_ref, wa_ref, paya_ref,
    v_ref, w_ref, sum_ref, u0_ref, t_ref, pay_ref,
    unit_ref,
):
    patch = be_ref.shape[1]
    half = patch // 2
    sources = below_sources(n, None, be_ref, bm_ref, None)
    columns = middle_columns(n)
    before = tuple(sa_ref[i] for i in range(3))
    sums = cross_columns(patch, columns, sources, u1_ref, unit_ref, v_ref, w_ref, before)
    scale = scale_of(stat_ref, sums)
    t_ref[...] = scale
    shared = sums[1] - FLOOR * absent_near(stat_ref[2, patch:], 3 * patch)
    sum_ref[0] = shared
    sum_ref[1] = sums[2]
    edges = edge_columns(n)
    for e in edges:
        u0_ref[e] = ua_ref[e]
    for e in columns:
        u0_ref[e] = (scale[:, e : e + 1] * panel_at((pl_ref, p_ref, pr_ref), 1, e)).astype(bf16)
    done = inner(edges, 2, n - 2)
    for e in done:
        pay_ref[(e - 2) * half : (e - 1) * half, :] = paya_ref[(e - 2) * half : (e - 1) * half, :]
    products([e for e in range(2, n - 2) if e not in done], place_of(n), (wa_ref, w_ref), u0_ref, pay_ref, 2)
    tail = (n - 4) * half
    pay_ref[tail : tail + patch, :], pay_ref[tail + patch :, :] = pair_of(shared)


def middle_affinity(be, bm, u1, stat, panel, sa, ua, wa, paya):
    _, patch, width = be.shape
    n = u1.shape[0] // patch
    count = len(middle_columns(n))
    return kernel_call(
        functools.partial(middle_kernel, n),
        (
            sds((count, patch, 3 * patch), bf16),
            sds((count, patch, 3 * patch), bf16),
            sds((2, patch, 128), f32),
            sds((n, patch, RANK), bf16),
            sds((patch, 128), f32),
            sds((payload_rows(n - 4, patch), 2 * RANK), bf16),
        ),
        [pltpu.VMEM((n * patch, width), bf16)],
        cost=4 * count * patch * 3 * patch * width,
    )(be, bm, u1, stat, *panel, sa, ua, wa, paya)


def before_first_kernel(n, got_ref, sum_ref, u0_ref, m_ref, va_ref, vb_ref, z_ref, u2_ref):
    patch = u0_ref.shape[1]
    half = patch // 2
    both = 2 * patch
    where = place_of(n)
    tail = (n - 2) * half
    partial = got_ref[tail : tail + patch, :].astype(f32) + got_ref[tail + patch :, :].astype(f32)
    scale = sum_ref[1] * lax.rsqrt(1.0 + partial + sum_ref[0])
    for e in range(1, n - 1):
        theirs = unpacked(got_ref[(e - 1) * half : e * half, :].astype(f32))
        u2_ref[e] = (scale[:, e : e + 1] * theirs).astype(bf16)
    for e in range(2, n - 2):
        which, i = where[e]
        own = u0_ref[e - 1 : e + 2].reshape(3 * patch, RANK)
        total = jnp.dot(m_ref[e, :, 3 * patch :], own, preferred_element_type=f32)
        below = u2_ref[e - 1 : e + 2].reshape(3 * patch, RANK)
        lower = jnp.dot((va_ref, vb_ref)[which][i], below, preferred_element_type=f32)
        z_ref[e, :patch] = total[:patch]
        z_ref[e, patch:] = total[patch:] + lower


def before_first(got, sums, u0, m, va, vb):
    n, patch, _ = u0.shape
    return kernel_call(
        functools.partial(before_first_kernel, n),
        sds((n, 2 * patch, RANK), f32),
        [pltpu.VMEM((n, patch, RANK), bf16)],
        cost=2 * n * 2 * patch * 3 * patch * RANK,
    )(got, sums, u0, m, va, vb)


def first_kernel(
    n,
    got_ref, stat_ref, t_ref, z_ref, pl_ref, p_ref, pr_ref, m_ref, wa_ref, wb_ref,
    y_ref, u_ref, tt_ref, up_ref, down_ref,
    start_ref,
):
    panel = (pl_ref, p_ref, pr_ref)
    patch = t_ref.shape[0]
    half = patch // 2
    tail = (n - 4) * half
    partial = got_ref[tail : tail + patch, :].astype(f32) + got_ref[tail + patch :, :].astype(f32)
    upper_scale = stat_ref[2, :patch] * lax.rsqrt(1.0 + stat_ref[0, :patch] + partial)
    scale = jnp.concatenate([upper_scale, t_ref[...]], axis=0)
    gain = 1.0 + scale * scale * stat_ref[1]
    tt_ref[0] = scale
    tt_ref[1] = gain
    for e in range(1, n - 1):
        start_ref[e] = (upper_scale[:, e : e + 1] * panel_at(panel, 0, e)).astype(bf16)
    for e in range(2, n - 2):
        own = start_ref[e - 1 : e + 2].reshape(3 * patch, RANK)
        total = z_ref[e] + jnp.dot(m_ref[e, :, : 3 * patch], own, preferred_element_type=f32)
        upper = unpacked(got_ref[(e - 2) * half : (e - 1) * half, :].astype(f32))
        for row in range(2):
            span = slice(row * patch, (row + 1) * patch)
            piece = total[span] + upper if row == 0 else total[span]
            t = scale[span, e : e + 1]
            image = panel_at(panel, row, e) * gain[span, e : e + 1] + t * piece
            y_ref[row, e] = image
            scaled = t * image
            u_ref[row, e] = scaled.astype(bf16)
            if row == 0:
                up_ref[(e - 2) * half : (e - 1) * half, :] = packed(scaled).astype(bf16)
    products(range(3, n - 3), place_of(n), (wa_ref, wb_ref), u_ref.at[1], down_ref, 3)


def first_iteration(got, stat, t, z, panel, m, wa, wb):
    n, both, _ = z.shape
    patch = both // 2
    half = patch // 2
    return kernel_call(
        functools.partial(first_kernel, n),
        (
            sds((2, n, patch, RANK), f32),
            sds((2, n, patch, RANK), bf16),
            sds((2, both, 128), f32),
            sds(((n - 4) * half, 2 * RANK), bf16),
            sds(((n - 6) * half, 2 * RANK), bf16),
        ),
        [pltpu.VMEM((n, patch, RANK), bf16)],
        cost=2 * n * both * 3 * patch * RANK,
    )(got, stat, t, z, *panel, m, wa, wb)


def local_kernel(low, high, m_ref, u_ref, z_ref):
    patch = u_ref.shape[2]
    for e in range(low, high):
        upper = u_ref[0, e - 1 : e + 2].reshape(3 * patch, RANK)
        lower = u_ref[1, e - 1 : e + 2].reshape(3 * patch, RANK)
        z_ref[e] = jnp.dot(m_ref[e], jnp.concatenate([upper, lower], axis=0), preferred_element_type=f32)


def local_products(low, high, m, u):
    n, both, _ = m.shape
    return kernel_call(
        functools.partial(local_kernel, low, high),
        sds((n, both, RANK), f32),
        cost=2 * n * both * 3 * both * RANK,
    )(m, u)


def joined(e, low, where, downs, near, z_ref, above_ref, y_ref, scale, gain):
    patch = y_ref.shape[2]
    half = patch // 2
    which, i = where[e]
    below = jnp.concatenate([near[e - 1], near[e], near[e + 1]], axis=0)
    lower = z_ref[e, patch:] + jnp.dot(downs[which][i], below, preferred_element_type=f32)
    upper = z_ref[e, :patch] + unpacked(above_ref[(e - low) * half : (e - low + 1) * half, :].astype(f32))
    images = []
    for row, piece in ((0, upper), (1, lower)):
        span = slice(row * patch, (row + 1) * patch)
        images.append(y_ref[row, e] * gain[span, e : e + 1] + scale[span, e : e + 1] * piece)
    return images


def halo(n, low, half, below_ref):
    return {
        e: unpacked(below_ref[(e - low + 1) * half : (e - low + 2) * half, :]) for e in range(low - 1, n - low + 1)
    }


def middle_step_kernel(
    n, low,
    below_ref, above_ref, z_ref, y_ref, tt_ref, va_ref, wa_ref, vb_ref, wb_ref,
    new_ref, u_ref, up_ref, down_ref,
):
    patch = y_ref.shape[2]
    half = patch // 2
    where = place_of(n)
    scale, gain = tt_ref[0], tt_ref[1]
    near = halo(n, low, half, below_ref)
    for e in range(low, n - low):
        images = joined(e, low, where, (va_ref, vb_ref), near, z_ref, above_ref, y_ref, scale, gain)
        for row in range(2):
            new_ref[row, e] = images[row]
            scaled = scale[row * patch : (row + 1) * patch, e : e + 1] * images[row]
            u_ref[row, e] = scaled.astype(bf16)
            if row == 0:
                up_ref[(e - low) * half : (e - low + 1) * half, :] = packed(scaled).astype(bf16)
    products(range(low + 1, n - low - 1), where, (wa_ref, wb_ref), u_ref.at[1], down_ref, low + 1)


def middle_step(low, below, above, z, y, tt, va, wa, vb, wb):
    _, n, patch, _ = y.shape
    half = patch // 2
    return kernel_call(
        functools.partial(middle_step_kernel, n, low),
        (
            sds((2, n, patch, RANK), f32),
            sds((2, n, patch, RANK), bf16),
            sds(((n - 2 * low) * half, 2 * RANK), bf16),
            sds(((n - 2 * low - 2) * half, 2 * RANK), bf16),
        ),
        cost=8 * n * patch * patch * RANK,
    )(below, above, z, y, tt, va, wa, vb, wb)


def last_step_kernel(n, low, below_ref, above_ref, z_ref, y_ref, tt_ref, va_ref, vb_ref, new_ref, gram_ref, side_ref):
    patch = y_ref.shape[2]
    where = place_of(n)
    scale, gain = tt_ref[0], tt_ref[1]
    near = halo(n, low, patch // 2, below_ref)
    wide = 2 * RANK
    for e in range(low, n - low):
        images = joined(e, low, where, (va_ref, vb_ref), near, z_ref, above_ref, y_ref, scale, gain)
        for row in range(2):
            new_ref[row, e - low] = images[row]
        span = slice((e - low) * patch, (e - low + 1) * patch)
        side_ref[span, :wide], side_ref[span, wide:] = pair_of(jnp.concatenate(images, axis=1))
    side = side_ref[...]
    gram = lax.dot_general(side, side, ATB, preferred_element_type=f32)
    gram = gram[:wide] + gram[wide:]
    gram = gram[:, :wide] + gram[:, wide:]
    gram_ref[...] = packed(gram[:RANK, :RANK] + gram[RANK:, RANK:])


def last_step(low, below, above, z, y, tt, va, vb):
    _, n, patch, _ = y.shape
    cols = n - 2 * low
    return kernel_call(
        functools.partial(last_step_kernel, n, low),
        (sds((2, cols, patch, RANK), f32), sds((RANK // 2, 2 * RANK), f32)),
        [pltpu.VMEM((cols * patch, 4 * RANK), bf16)],
        cost=8 * n * patch * patch * RANK,
    )(below, above, z, y, tt, va, vb)


def inverse_factor(gram):
    size = gram.shape[0]
    step = 4
    row = iota((size, 2 * size), 0)
    lane = iota((size, 2 * size), 1)
    table = jnp.concatenate([gram, identity(size).astype(f32)], axis=1)
    for k in range(0, size, step):
        cols = [jnp.broadcast_to(table[:, k + i : k + i + 1], table.shape) for i in range(step)]
        lines = [table[k + i : k + i + 1, :] for i in range(step)]
        for i in range(step):
            inverse = 1.0 / cols[i][k + i : k + i + 1, :]
            for j in range(i + 1, step):
                lines[j] = lines[j] - lines[i] * (cols[i][k + j : k + j + 1, :] * inverse)
                cols[j] = cols[j] - cols[i] * (cols[j][k + i : k + i + 1, :] * inverse)
            table = table - jnp.where(row > k + i, cols[i], 0.0) * (lines[i] * inverse)
    pivots = jnp.sum(jnp.where(row == lane, table, 0.0), axis=1, keepdims=True)
    return table[:, size:] * lax.rsqrt(pivots)


def finish_kernel(factor, count, *refs):
    parts, y_ref, out_ref = refs[:count], refs[count], refs[count + 1]
    total = parts[0][...]
    for part in parts[1:]:
        total = total + part[...]
    inverse = factor * inverse_factor(unpacked(total))
    zero = jnp.zeros_like(inverse)
    both = jnp.concatenate(
        [jnp.concatenate([inverse, zero], axis=1), jnp.concatenate([zero, inverse], axis=1)], axis=0
    )
    wide = 2 * RANK
    tiles, width = y_ref.shape
    pieces = [y_ref[:, q * wide : (q + 1) * wide] for q in range(width // wide)]
    y_high, y_low = pair_of(jnp.concatenate(pieces, axis=0))
    t_high, t_low = pair_of(both)

    def times(a, b):
        return lax.dot_general(a, b, ABT, preferred_element_type=f32)

    out = times(y_high, t_high) + (times(y_low, t_high) + times(y_high, t_low))
    for q in range(width // wide):
        out_ref[:, q * wide : (q + 1) * wide] = out[q * tiles : (q + 1) * tiles]


def finish(factor, parts, y):
    return kernel_call(
        functools.partial(finish_kernel, factor, len(parts)),
        sds(y.shape, f32),
        cost=2 * y.shape[0] * y.shape[1] * RANK,
    )(*parts, y)


def exchange_stages():
    stages = []
    for axis in ("col", "row"):
        size = lax.axis_size(axis)
        bit = 1
        if axis == "col":
            stages.append((axis, size, [1]))
            bit = 2
        while bit < size:
            if 2 * bit < size:
                stages.append((axis, size, [bit, 2 * bit, 3 * bit]))
                bit *= 4
            else:
                stages.append((axis, size, [bit]))
                bit *= 2
    return stages


def summed_parts(gram):
    stages = exchange_stages()
    for place, (axis, size, partners) in enumerate(stages):
        parts = [gram] + [
            lax.ppermute(gram, axis, [(i, i ^ p) for i in range(size)]) for p in partners
        ]
        if place == len(stages) - 1:
            return parts
        gram = parts[0]
        for part in parts[1:]:
            gram = gram + part


def passed_along(shard, axis, by):
    count = lax.axis_size(axis)
    pairs = [(i, i + by) for i in range(count) if 0 <= i + by < count]
    return lax.ppermute(shard, axis, pairs)


def local(features, tissue, probe):
    tile_rows, tile_cols, patches, width = features.shape
    edges, middle = mark_row(features, tissue)
    below_edges = passed_along(edges, "row", -1)
    below_middle = passed_along(middle, "row", -1)
    own_panel = probe.reshape(tile_rows, tile_cols, patches, RANK)
    unit0, unit1, probe_left, probe_right = own_units(features, tissue, own_panel, middle)
    left_end, right_end = mark_ends(features, tissue, edges)
    from_left = passed_along(right_end, "col", 1)
    from_right = passed_along(left_end, "col", -1)
    probe_left, probe_right = passed_along(probe_right, "col", 1), passed_along(probe_left, "col", -1)
    panel = (probe_left, own_panel, probe_right)
    m, sums = inside_affinity(unit0, unit1, patches)
    _, u1, m, stat, payload = outside_affinity(unit0, unit1, m, from_left, from_right, tissue, sums, panel)
    got_below = passed_along(payload, "row", -1)
    below_left, below_right = cut(below_edges, stat)
    below_left, below_right = passed_along(below_right, "col", 1), passed_along(below_left, "col", -1)
    va, wa, sa, ua, paya = edge_affinity(below_left, below_edges, below_right, u1, stat, panel)
    vb, wb, sums, u0, t, payload = middle_affinity(below_edges, below_middle, u1, stat, panel, sa, ua, wa, paya)
    got_above = passed_along(payload, "row", 1)
    z = before_first(got_below, sums, u0, m, va, vb)
    y, u, tt, up, down = first_iteration(got_above, stat, t, z, panel, m, wa, wb)
    below, above = passed_along(up, "row", -1), passed_along(down, "row", 1)
    n = tile_cols + 2 * GHOST
    z = local_products(3, n - 3, m, u)
    y, u, up, down = middle_step(3, below, above, z, y, tt, va, wa, vb, wb)
    below, above = passed_along(up, "row", -1), passed_along(down, "row", 1)
    z = local_products(4, n - 4, m, u)
    y, gram = last_step(4, below, above, z, y, tt, va, vb)

    parts = summed_parts(gram)
    flat = y.reshape(tile_rows * tile_cols, patches * RANK)
    total = tile_rows * lax.axis_size("row") * tile_cols * lax.axis_size("col") * patches
    out = finish(math.sqrt(float(total)), parts, flat)
    return out.reshape(tile_rows, tile_cols, patches * RANK)


def solution(mesh):
    placed = (P("row", "col", None, None), P("row", "col", None), P("row", "col", None))
    return jax.shard_map(
        local, mesh=mesh, in_specs=placed, out_specs=P("row", "col", None), check_vma=False
    )
```

time: 183 us -> 119 us (0.65)
  Pallas kernels: 79.3 us -> 39.9 us
  waiting for transfers between devices: 30.5 us -> 18.1 us
  local copies, waits for them, and re-layouts: 12.5 us -> 5.14 us
  other arithmetic: 7.31 us -> 0.01 us
  starting transfers between devices: 52.2 us -> 54.7 us
    pallas_call x5 -> x11, Pallas kernels: 58 us -> 33.2 us  [the longest x1 6.73 us: inside_affinity(): pl.pallas_call(functools.partial(inside_kernel, n), out_shape=(sds((n, bo...]
    ppermute x14, waiting for transfers between devices: 22.8 us -> 11.4 us  [passed_along(): return lax.ppermute(shard, axis, pairs)]
    pallas_call x2, Pallas kernels: 7.25 us -> 1.18 us  [local_products(): kernel_call(functools.partial(local_kernel, low, high), sds((n, both, RAN...]
    select_n x1 -> x0, other arithmetic: 5.64 us -> none  [local(): marked = jnp.where(tissue[..., None] != 0, marked, jnp.zeros((), bf16))]
    pallas_call x1, Pallas kernels: 6.45 us -> 2.04 us  [last_step(): kernel_call(functools.partial(last_step_kernel, n, low), (sds((2, cols, p...]
    pallas_call x1, Pallas kernels: 7.59 us -> 3.5 us  [finish(): kernel_call(functools.partial(finish_kernel, factor, len(parts)), sds(y.s...]
    slice x3 -> x0, local copies, waits for them, and re-layouts: 2.9 us -> none  [the longest x1 1.75 us: local(): from_right = passed_along(marked[:, :GHOST], 'col', -1)]
    ppermute x7, starting transfers between devices: 13.9 us -> 16.2 us  [summed_parts(): lax.ppermute(gram, axis, [(i, i ^ p) for i in range(size)])]
  transfers between devices with their start and end apart: 21 -> 21, of which waited for: 7 -> 12; matrix products, arithmetic and copies ran while one was open for 4% -> 2% of each run, Pallas kernels for 19% -> 22%
where the time goes in v2:
time: 119 us; the launch traced here: 118 us
  starting transfers between devices  54.7 us (46%)
  Pallas kernels  39.9 us (34%)
  waiting for transfers between devices  18.1 us (15%)
  local copies, waits for them, and re-layouts  5.14 us (4%)
    ppermute x14, starting transfers between devices, passed_along(): return lax.ppermute(shard, axis, pairs)  38.5 us
    ppermute x7, starting transfers between devices, summed_parts(): lax.ppermute(gram, axis, [(i, i ^ p) for i in range(size)])  16.2 us
    ppermute x14, waiting for transfers between devices, passed_along(): return lax.ppermute(shard, axis, pairs)  11.4 us
    pallas_call x1, Pallas kernels, inside_affinity(): pl.pallas_call(functools.partial(inside_kernel, n), out_shape=(sds((n, bo...  6.73 us
    ppermute x7, waiting for transfers between devices, summed_parts(): lax.ppermute(gram, axis, [(i, i ^ p) for i in range(size)])  6.7 us
    pallas_call x1, Pallas kernels, outside_affinity(): pl.pallas_call(functools.partial(outside_kernel, n), out_shape=(unit, uni...  6.23 us
    pallas_call x1, Pallas kernels, edge_affinity(): kernel_call(functools.partial(edge_kernel, n), (sds((count, patch, 3 * pa...  4.55 us
    pallas_call x1, Pallas kernels, mark_row(): pl.pallas_call(mark_row_kernel, in_specs=[hbm, hbm], out_specs=[vmem] * 2...  3.6 us
  transfers between devices with their start and end apart: 21, of which 12 were waited for; matrix products, arithmetic and copies ran while one was open for 2% of the time, Pallas kernels for 22%

profile of v2, /device:TPU:0, one launch (start us, length us, event | category | flops | bytes accessed | tf_op | source)
XLA Modules:
  0.0 118.2 jit_solution(5686669651964547532)
XLA Ops:
  0.0 3.6 %shard_map.37 = (bf16[10,64,1024]{2,1,0:T(8,128)(2,1)}, bf16[6,64,1024]{2,1,0:T(8,128)(2,1)S(1)}) custom-call(bf16[2,16,64,1024]{3,2,1,0:T(8,128)(2,1)} %last_ref.1, s32[2,16,64]{2,1,0:T(8,128)} %tissue_ref.7), custom_call_target="tpu_custom_call" | custom-call | tf_op jit(solution)/shard_map/pallas_call | solution.py:126
  3.6 0.0 copy-start.2
  3.6 1.3 %collective-permute-start = (bf16[10,64,1024]{2,1,0:T(8,128)(2,1)}, bf16[10,64,1024]{2,1,0:T(8,128)(2,1)S(1)}, u32[]{:S(2)}, u32[]{:S(2)}) collective-permute-start(bf16[10,64,1024]{2,1,0:T(8,128)(2,1)} %get-tuple-element.43.after_ref), channel_id=1, source_target_pairs={{8,0},{16,8},{24,16},{9,1},{17,9},{25,17},{10,2},{18,10},{26,18},{... | collective-permute-start | bytes 3932168 | tf_op jit(solution)/shard_map/ppermute | solution.py:738
  4.9 0.0 copy-done.4
  4.9 1.8 %shard_map.40 = (bf16[2,4,64,1024]{3,2,1,0:T(8,128)(2,1)}, bf16[2,4,64,1024]{3,2,1,0:T(8,128)(2,1)}) custom-call(bf16[2,16,64,1024]{3,2,1,0:T(8,128)(2,1)S(1)} %copy-done, bf16[2,16,64,1024]{3,2,1,0:T(8,128)(2,1)S(1)} %copy-done, s32[2,16,64]{2,1,0:T(8,128)S(1)} %copy-done.4, bf16[10,64,1024]{2,1,0:T(8,128)(2,1)} %get-tuple-element.43.after_ref), custom_call_target="tpu_custom_call" | custom-call | tf_op jit(solution)/shard_map/pallas_call | solution.py:157
  6.8 2.4 %collective-permute-start.2 = (bf16[2,4,64,1024]{3,2,1,0:T(8,128)(2,1)}, bf16[2,4,64,1024]{3,2,1,0:T(8,128)(2,1)S(1)}, u32[]{:S(2)}, u32[]{:S(2)}) collective-permute-start(bf16[2,4,64,1024]{3,2,1,0:T(8,128)(2,1)} %get-tuple-element.48), channel_id=1, source_target_pairs={{0,1},{1,2},{2,3},{3,4},{4,5},{5,6},{6,7},{8,9},{9,10},{10,11},{11... | collective-permute-start | bytes 3145736 | tf_op jit(solution)/shard_map/ppermute | solution.py:738
  9.2 1.3 %collective-permute-start.3 = (bf16[2,4,64,1024]{3,2,1,0:T(8,128)(2,1)}, bf16[2,4,64,1024]{3,2,1,0:T(8,128)(2,1)}, u32[]{:S(2)}, u32[]{:S(2)}) collective-permute-start(bf16[2,4,64,1024]{3,2,1,0:T(8,128)(2,1)} %get-tuple-element.49), channel_id=1, source_target_pairs={{1,0},{2,1},{3,2},{4,3},{5,4},{6,5},{7,6},{9,8},{10,9},{11,10},{12... | collective-permute-start | bytes 3145736 | tf_op jit(solution)/shard_map/ppermute | solution.py:738
  10.5 1.5 %reshape.9.probe_ref.p_ref = f32[2,16,64,64]{3,2,1,0:T(8,128)S(1)} reshape(f32[2,16,4096]{2,1,0:T(8,128)} %param.5) | data formatting | bytes 1048576 | tf_op jit(solution)/shard_map/reshape | solution.py:746
  11.9 0.0 copy-start.1
  12.0 2.2 %copy-done.1 = bf16[2,16,64,1024]{3,2,1,0:T(8,128)(2,1)S(1)} copy-done((bf16[2,16,64,1024]{3,2,1,0:T(8,128)(2,1)S(1)}, bf16[2,16,64,1024]{3,2,1,0:T(8,128)(2,1)}, u32[]{:S(2)}) %copy-start.1) | copy-done | bytes 4194328
  14.1 1.1 copy-done.3
  15.3 1.8 %shard_map.38 = (bf16[1536,1024]{1,0:T(8,128)(2,1)S(1)}, bf16[1536,1024]{1,0:T(8,128)(2,1)S(1)}, bf16[2,4,64,128]{3,2,1,0:T(8,128)(2,1)S(1)}, bf16[2,4,64,128]{3,2,1,0:T(8,128)(2,1)S(1)}) custom-call(bf16[2,16,64,1024]{3,2,1,0:T(8,128)(2,1)S(1)} %copy-done.1, s32[2,16,64]{2,1,0:T(8,128)S(1)} %copy-done.4, f32[2,16,64,64]{3,2,1,0:T(8,128)S(1)} %reshape.9.probe_ref.p_ref, ...), custom_call_target="tpu_custom_call" | custom-call | tf_op jit(solution)/shard_map/pallas_call | solution.py:191
  17.1 5.2 %collective-permute-start.4 = (bf16[2,4,64,128]{3,2,1,0:T(8,128)(2,1)S(1)}, bf16[2,4,64,128]{3,2,1,0:T(8,128)(2,1)S(1)}, u32[]{:S(2)}, u32[]{:S(2)}) collective-permute-start(bf16[2,4,64,128]{3,2,1,0:T(8,128)(2,1)S(1)} %get-tuple-element.51), channel_id=1, source_target_pairs={{0,1},{1,2},{2,3},{3,4},{4,5},{5,6},{6,7},{8,9},{9,10},{10,11},{11... | collective-permute-start | bytes 393224 | tf_op jit(solution)/shard_map/ppermute | solution.py:738
  22.3 1.3 %collective-permute-start.1 = (bf16[6,64,1024]{2,1,0:T(8,128)(2,1)S(1)}, bf16[6,64,1024]{2,1,0:T(8,128)(2,1)S(1)}, u32[]{:S(2)}, u32[]{:S(2)}) collective-permute-start(bf16[6,64,1024]{2,1,0:T(8,128)(2,1)S(1)} %copy-done.3), channel_id=1, source_target_pairs={{8,0},{16,8},{24,16},{9,1},{17,9},{25,17},{10,2},{18,10},{26,18},{... | collective-permute-start | bytes 2359304 | tf_op jit(solution)/shard_map/ppermute | solution.py:738
  23.6 0.0 collective-permute-done.4.pl_ref
  23.6 1.3 %collective-permute-start.5 = (bf16[2,4,64,128]{3,2,1,0:T(8,128)(2,1)S(1)}, bf16[2,4,64,128]{3,2,1,0:T(8,128)(2,1)S(1)}, u32[]{:S(2)}, u32[]{:S(2)}) collective-permute-start(bf16[2,4,64,128]{3,2,1,0:T(8,128)(2,1)S(1)} %get-tuple-element.52), channel_id=1, source_target_pairs={{1,0},{2,1},{3,2},{4,3},{5,4},{6,5},{7,6},{9,8},{10,9},{11,10},{12... | collective-permute-start | bytes 393224 | tf_op jit(solution)/shard_map/ppermute | solution.py:738
  24.9 6.7 %shard_map.39 = (bf16[24,128,384]{2,1,0:T(8,128)(2,1)S(1)}, f32[2,128,128]{2,1,0:T(8,128)S(1)}) custom-call(bf16[1536,1024]{1,0:T(8,128)(2,1)S(1)} %get-tuple-element.45.unit0_ref.start0_ref, bf16[1536,1024]{1,0:T(8,128)(2,1)S(1)} %get-tuple-element.46.unit1_ref.start1_ref), custom_call_target="tpu_custom_call" | custom-call | tf_op jit(solution)/shard_map/pallas_call | solution.py:236
  31.6 0.0 collective-permute-done.5.pr_ref
  31.7 0.0 collective-permute-done.2.xl_ref
  31.7 0.0 collective-permute-done.3.xr_ref
  31.7 6.2 %shard_map.41 = (bf16[1536,1024]{1,0:T(8,128)(2,1)S(1)}, bf16[1536,1024]{1,0:T(8,128)(2,1)S(1)}, bf16[24,128,384]{2,1,0:T(8,128)(2,1)S(1)}, f32[3,128,128]{2,1,0:T(8,128)S(1)}, bf16[832,128]{1,0:T(8,128)(2,1)S(1)}) custom-call(bf16[1536,1024]{1,0:T(8,128)(2,1)S(1)} %get-tuple-element.45.unit0_ref.start0_re, ...), custom_call_target="tpu_custom_call", output_to_operand_aliasing={{0}: (0, {}), {1}: (1, {}), {2}: (2, {})} | custom-call | tf_op jit(solution)/shard_map/pallas_call | solution.py:290
  37.9 0.4 collective-permute-done.be_ref
  38.3 0.1 shard_map.42
  38.4 4.5 %collective-permute-start.6 = (bf16[4,64,1024]{2,1,0:T(8,128)(2,1)S(1)}, bf16[4,64,1024]{2,1,0:T(8,128)(2,1)S(1)}, u32[]{:S(2)}, u32[]{:S(2)}) collective-permute-start(bf16[4,64,1024]{2,1,0:T(8,128)(2,1)S(1)} %get-tuple-element.55), channel_id=1, source_target_pairs={{0,1},{1,2},{2,3},{3,4},{4,5},{5,6},{6,7},{8,9},{9,10},{10,11},{11... | collective-permute-start | bytes 1572872 | tf_op jit(solution)/shard_map/ppermute | solution.py:738
  42.9 1.3 %collective-permute-start.7 = (bf16[4,64,1024]{2,1,0:T(8,128)(2,1)S(1)}, bf16[4,64,1024]{2,1,0:T(8,128)(2,1)S(1)}, u32[]{:S(2)}, u32[]{:S(2)}) collective-permute-start(bf16[4,64,1024]{2,1,0:T(8,128)(2,1)S(1)} %get-tuple-element.56), channel_id=1, source_target_pairs={{1,0},{2,1},{3,2},{4,3},{5,4},{6,5},{7,6},{9,8},{10,9},{11,10},{12... | collective-permute-start | bytes 1572872 | tf_op jit(solution)/shard_map/ppermute | solution.py:738
  44.2 1.3 %collective-permute-start.9 = (bf16[832,128]{1,0:T(8,128)(2,1)S(1)}, bf16[832,128]{1,0:T(8,128)(2,1)S(1)}, u32[]{:S(2)}, u32[]{:S(2)}) collective-permute-start(bf16[832,128]{1,0:T(8,128)(2,1)S(1)} %get-tuple-element.63), channel_id=1, source_target_pairs={{8,0},{16,8},{24,16},{9,1},{17,9},{25,17},{10,2},{18,10},{26,18},{... | collective-permute-start | bytes 638984 | tf_op jit(solution)/shard_map/ppermute | solution.py:738
  45.5 0.0 collective-permute-done.6.bl_ref
  45.5 3.1 %collective-permute-done.7.br_ref = bf16[4,64,1024]{2,1,0:T(8,128)(2,1)S(1)} collective-permute-done((bf16[4,64,1024]{2,1,0:T(8,128)(2,1)S(1)}, bf16[4,64,1024]{2,1,0:T(8,128)(2,1)S(1)}, u32[]{:S(2)}, u32[]{:S(2)}) %collective-permute-start.7) | collective-permute-done | bytes 524320 | tf_op jit(solution)/shard_map/ppermute | solution.py:738
  48.6 4.5 %shard_map.43 = (bf16[14,64,192]{2,1,0:T(8,128)(2,1)S(1)}, bf16[14,64,192]{2,1,0:T(8,128)(2,1)S(1)}, f32[3,64,128]{2,1,0:T(8,128)S(1)}, bf16[24,64,64]{2,1,0:T(8,128)(2,1)S(1)}, bf16[640,128]{1,0:T(8,128)(2,1)S(1)}) custom-call(bf16[4,64,1024]{2,1,0:T(8,128)(2,1)S(1)} %collective-permute-done.6.bl_ref, ...), custom_call_target="tpu_custom_call" | custom-call | flops 704643072 | bytes 1048576 | tf_op jit(solution)/shard_map/pallas_call | solution.py:403
  53.2 2.0 %collective-permute-done.1.bm_ref = bf16[6,64,1024]{2,1,0:T(8,128)(2,1)S(1)} collective-permute-done((bf16[6,64,1024]{2,1,0:T(8,128)(2,1)S(1)}, bf16[6,64,1024]{2,1,0:T(8,128)(2,1)S(1)}, u32[]{:S(2)}, u32[]{:S(2)}) %collective-permute-start.1) | collective-permute-done | bytes 786464 | tf_op jit(solution)/shard_map/ppermute | solution.py:738
  55.1 2.9 %shard_map.44 = (bf16[8,64,192]{2,1,0:T(8,128)(2,1)S(1)}, bf16[8,64,192]{2,1,0:T(8,128)(2,1)S(1)}, f32[2,64,128]{2,1,0:T(8,128)S(1)}, bf16[24,64,64]{2,1,0:T(8,1...) custom-call(bf16[10,64,1024]{2,1,0:T(8,128)(2,1)S(1)} %collective-permute-done.be_ref, ...), custom_call_target="tpu_custom_call" | custom-call | flops 402653184 | bytes 1048576 | tf_op jit(solution)/shard_map/pallas_call | solution.py:451
  58.0 5.0 %collective-permute-start.8 = (bf16[768,128]{1,0:T(8,128)(2,1)S(1)}, bf16[768,128]{1,0:T(8,128)(2,1)S(1)}, u32[]{:S(2)}, u32[]{:S(2)}) collective-permute-start(bf16[768,128]{1,0:T(8,128)(2,1)S(1)} %get-tuple-element.61), channel_id=1, source_target_pairs={{0,8},{8,16},{16,24},{1,9},{9,17},{17,25},{2,10},{10,18},{18,26},{... | collective-permute-start | bytes 589832 | tf_op jit(solution)/shard_map/ppermute | solution.py:738
  63.0 0.0 collective-permute-done.9.got_ref
  63.0 0.9 shard_map.45.z_ref
  64.0 2.0 %collective-permute-done.8.got_ref = bf16[768,128]{1,0:T(8,128)(2,1)S(1)} collective-permute-done((bf16[768,128]{1,0:T(8,128)(2,1)S(1)}, bf16[768,128]{1,0:T(8,128)(2,1)S(1)}, u32[]{:S(2)}, u32[]{:S(2)}) %collective-permute-start.8) | collective-permute-done | bytes 196640 | tf_op jit(solution)/shard_map/ppermute | solution.py:738
  66.0 2.6 %shard_map.46 = (f32[2,24,64,64]{3,2,1,0:T(8,128)S(1)}, bf16[2,24,64,64]{3,2,1,0:T(8,128)(2,1)S(1)}, f32[2,128,128]{2,1,0:T(8,128)S(1)}, bf16[640,128]{1,0:T(8,128)(2,1)S(1)}, bf16[576,128]{1,0:T(8,128)(2,1)S(1)}) custom-call(bf16[768,128]{1,0:T(8,128)(2,1)S(1)} %collective-permute-done.8.got_ref, f32[3,128,128]{2,1,0:T(8,128)S(1)} %get-tuple-element.54.after_ref.stat_ref, ...), custom_call_target="tpu_custom_call" | custom-call | flops 75497472 | bytes 1048576 | tf_op jit(solution)/shard_map/pallas_call | solution.py:536
  68.7 1.3 %collective-permute-start.10 = (bf16[640,128]{1,0:T(8,128)(2,1)S(1)}, bf16[640,128]{1,0:T(8,128)(2,1)S(1)}, u32[]{:S(2)}, u32[]{:S(2)}) collective-permute-start(bf16[640,128]{1,0:T(8,128)(2,1)S(1)} %get-tuple-element.70), channel_id=1, source_target_pairs={{8,0},{16,8},{24,16},{9,1},{17,9},{25,17},{10,2},{18,10},{26,18},{... | collective-permute-start | bytes 491528 | tf_op jit(solution)/shard_map/ppermute | solution.py:738
  70.0 5.0 %collective-permute-start.11 = (bf16[576,128]{1,0:T(8,128)(2,1)S(1)}, bf16[576,128]{1,0:T(8,128)(2,1)S(1)}, u32[]{:S(2)}, u32[]{:S(2)}) collective-permute-start(bf16[576,128]{1,0:T(8,128)(2,1)S(1)} %get-tuple-element.71), channel_id=1, source_target_pairs={{0,8},{8,16},{16,24},{1,9},{9,17},{17,25},{2,10},{10,18},{18,26},{... | collective-permute-start | bytes 442376 | tf_op jit(solution)/shard_map/ppermute | solution.py:738
  75.0 0.6 shard_map.47.z_ref
  75.6 2.0 %collective-permute-done.11.above_ref = bf16[576,128]{1,0:T(8,128)(2,1)S(1)} collective-permute-done((bf16[576,128]{1,0:T(8,128)(2,1)S(1)}, bf16[576,128]{1,0:T(8,128)(2,1)S(1)}, u32[]{:S(2)}, u32[]{:S(2)}) %collective-permute-start.11) | collective-permute-done | bytes 147488 | tf_op jit(solution)/shard_map/ppermute | solution.py:738
  77.6 0.0 collective-permute-done.10.below_ref
  77.6 2.0 %shard_map.48 = (f32[2,24,64,64]{3,2,1,0:T(8,128)S(1)}, bf16[2,24,64,64]{3,2,1,0:T(8,128)(2,1)S(1)}, bf16[576,128]{1,0:T(8,128)(2,1)S(1)}, bf16[512,128]{1,0:T(8,128)(2,1)S(1)}) custom-call(bf16[640,128]{1,0:T(8,128)(2,1)S(1)} %collective-permute-done.10.below_ref, bf16[576,128]{1,0:T(8,128)(2,1)S(1)} %collective-permute-done.11.above_ref, ...), custom_call_target="tpu_custom_call" | custom-call | flops 50331648 | bytes 1048576 | tf_op jit(solution)/shard_map/pallas_call | solution.py:611
  79.6 1.3 %collective-permute-start.12 = (bf16[576,128]{1,0:T(8,128)(2,1)S(1)}, bf16[576,128]{1,0:T(8,128)(2,1)S(1)}, u32[]{:S(2)}, u32[]{:S(2)}) collective-permute-start(bf16[576,128]{1,0:T(8,128)(2,1)S(1)} %get-tuple-element.75), channel_id=1, source_target_pairs={{8,0},{16,8},{24,16},{9,1},{17,9},{25,17},{10,2},{18,10},{26,18},{... | collective-permute-start | bytes 442376 | tf_op jit(solution)/shard_map/ppermute | solution.py:738
  80.9 6.0 %collective-permute-start.13 = (bf16[512,128]{1,0:T(8,128)(2,1)S(1)}, bf16[512,128]{1,0:T(8,128)(2,1)S(1)}, u32[]{:S(2)}, u32[]{:S(2)}) collective-permute-start(bf16[512,128]{1,0:T(8,128)(2,1)S(1)} %get-tuple-element.76), channel_id=1, source_target_pairs={{0,8},{8,16},{16,24},{1,9},{9,17},{17,25},{2,10},{10,18},{18,26},{... | collective-permute-start | bytes 393224 | tf_op jit(solution)/shard_map/ppermute | solution.py:738
  86.9 0.6 shard_map.49.z_ref
  87.5 1.9 %collective-permute-done.13.above_ref = bf16[512,128]{1,0:T(8,128)(2,1)S(1)} collective-permute-done((bf16[512,128]{1,0:T(8,128)(2,1)S(1)}, bf16[512,128]{1,0:T(8,128)(2,1)S(1)}, u32[]{:S(2)}, u32[]{:S(2)}) %collective-permute-start.13) | collective-permute-done | bytes 131104 | tf_op jit(solution)/shard_map/ppermute | solution.py:738
  89.4 0.0 collective-permute-done.12.below_ref
  89.4 2.0 %shard_map.50 = (f32[2,16,64,64]{3,2,1,0:T(8,128)S(1)}, f32[32,128]{1,0:T(8,128)S(1)}) custom-call(bf16[576,128]{1,0:T(8,128)(2,1)S(1)} %collective-permute-done.12.below_ref, bf16[512,128]{1,0:T(8,128)(2,1)S(1)} %collective-permute-done.13.above_ref, f32[24,128,64]{2,1,0:T(8,128)S(1)} %shard_map.49.z_ref, f32[2,24,64,64]{3,2,1,0:T(8,128)S(1)} %get-tuple-element.78.y_ref, ...), custom_call_target="tpu_custom_call" | custom-call | flops 50331648 | bytes 1048576 | tf_op jit(solution)/shard_map/pallas_call | solution.py:645
  91.4 2.3 %collective-permute-start.14 = (f32[32,128]{1,0:T(8,128)S(1)}, f32[32,128]{1,0:T(8,128)S(1)}, u32[]{:S(2)}, u32[]{:S(2)}) collective-permute-start(f32[32,128]{1,0:T(8,128)S(1)} %get-tuple-element.79), channel_id=1, source_target_pairs={{0,1},{1,0},{2,3},{3,2},{4,5},{5,4},{6,7},{7,6},{8,9},{9,8},{10,11... | collective-permute-start | bytes 49160 | tf_op jit(solution)/shard_map/ppermute | solution.py:726
  93.7 0.8 collective-permute-done.14
  94.5 5.8 %collective-permute-start.17 = (f32[32,128]{1,0:T(8,128)S(1)}, f32[32,128]{1,0:T(8,128)S(1)}, u32[]{:S(2)}, u32[]{:S(2)}) collective-permute-start(f32[32,128]{1,0:T(8,128)S(1)} %add.12), channel_id=1, source_target_pairs={{0,6},{1,7},{2,4},{3,5},{4,2},{5,3},{6,0},{7,1},{8,14},{9,15},{10,... | collective-permute-start | bytes 49160 | tf_op jit(solution)/shard_map/ppermute | solution.py:726
  100.3 1.4 %collective-permute-start.16 = (f32[32,128]{1,0:T(8,128)S(1)}, f32[32,128]{1,0:T(8,128)S(1)}, u32[]{:S(2)}, u32[]{:S(2)}) collective-permute-start(f32[32,128]{1,0:T(8,128)S(1)} %add.12), channel_id=1, source_target_pairs={{0,4},{1,5},{2,6},{3,7},{4,0},{5,1},{6,2},{7,3},{8,12},{9,13},{10,... | collective-permute-start | bytes 49160 | tf_op jit(solution)/shard_map/ppermute | solution.py:726
  101.7 0.1 collective-permute-start.15
  101.8 0.2 collective-permute-done.17
  102.0 2.9 %collective-permute-done.16 = f32[32,128]{1,0:T(8,128)S(1)} collective-permute-done((f32[32,128]{1,0:T(8,128)S(1)}, f32[32,128]{1,0:T(8,128)S(1)}, u32[]{:S(2)}, u32[]{:S(2)}) %collective-permute-start.16) | collective-permute-done | bytes 16416 | tf_op jit(solution)/shard_map/ppermute | solution.py:726
  105.0 0.5 collective-permute-done.15
  105.4 5.5 %collective-permute-start.20 = (f32[32,128]{1,0:T(8,128)S(1)}, f32[32,128]{1,0:T(8,128)S(1)}, u32[]{:S(2)}, u32[]{:S(2)}) collective-permute-start(f32[32,128]{1,0:T(8,128)S(1)} %add_add_fusion.refs_0_), channel_id=1, source_target_pairs={{0,24},{8,16},{16,8},{24,0},{1,25},{9,17},{17,9},{25,1},{2,26},{10... | collective-permute-start | bytes 49160 | tf_op jit(solution)/shard_map/ppermute | solution.py:726
  110.9 0.0 collective-permute-start.19
  111.0 1.1 collective-permute-start.18
  112.1 0.4 reshape.10.refs_4_
  112.4 0.2 collective-permute-done.20.refs_3_
  112.7 2.0 %collective-permute-done.19.refs_2_ = f32[32,128]{1,0:T(8,128)S(1)} collective-permute-done((f32[32,128]{1,0:T(8,128)S(1)}, f32[32,128]{1,0:T(8,128)S(1)}, u32[]{:S(2)}, u32[]{:S(2)}) %collective-permute-start.19) | collective-permute-done | bytes 16416 | tf_op jit(solution)/shard_map/ppermute | solution.py:726
  114.7 0.0 collective-permute-done.18.refs_1_
  114.7 3.5 %shard_map.51 = f32[32,4096]{1,0:T(8,128)} custom-call(f32[32,128]{1,0:T(8,128)S(1)} %add_add_fusion.refs_0_, f32[32,128]{1,0:T(8,128)S(1)} %collective-permute-done.18.refs_1_, f32[32,128]{1,0:T(8,128)S(1)} %collective-permute-done.19.refs_2_, f32[32,128]{1,0:T(8,128)S(1)} %collective-permute-done.20.refs_3_, f32[32,4096]{1,0:T(8,128)S(1)} %reshape.10.refs_4_), custom_call_target="tpu_custom_call" | custom-call | flops 16777216 | bytes 1048576 | tf_op jit(solution)/shard_map/pallas_call | solution.py:697
  (7 shorter events, 0.0 us)
Async XLA Ops:
  0.0 4.9 %copy-start.4 = (s32[2,16,64]{2,1,0:T(8,128)S(1)}, s32[2,16,64]{2,1,0:T(8,128)}, u32[]{:S(2)}) copy-start(s32[2,16,64]{2,1,0:T(8,128)} %tissue_ref.7) | copy-start | bytes 24580
  0.0 4.9 %copy-start = (bf16[2,16,64,1024]{3,2,1,0:T(8,128)(2,1)S(1)}, bf16[2,16,64,1024]{3,2,1,0:T(8,128)(2,1)}, u32[]{:S(2)}) copy-start(bf16[2,16,64,1024]{3,2,1,0:T(8,128)(2,1)} %last_ref.1) | copy-start | bytes 12582916
  3.6 3.2 %copy-start.2 = (bf16[6,64,1024]{2,1,0:T(8,128)(2,1)}, bf16[6,64,1024]{2,1,0:T(8,128)(2,1)S(1)}, u32[]{:S(2)}) copy-start(bf16[6,64,1024]{2,1,0:T(8,128)(2,1)S(1)} %get-tuple-element.44.after_ref) | copy-start | bytes 2359300
  3.6 34.7 %collective-permute-start = (bf16[10,64,1024]{2,1,0:T(8,128)(2,1)}, bf16[10,64,1024]{2,1,0:T(8,128)(2,1)S(1)}, u32[]{:S(2)}, u32[]{:S(2)}) collective-permute-start(bf16[10,64,1024]{2,1,0:T(8,128)(2,1)} %get-tuple-element.43.after_ref), channel_id=1, source_target_pairs={{8,0},{16,8},{24,16},{9,1},{17,9},{25,17},{10,2},{18,10},{26,18},{... | collective-permute-start | bytes 3932168 | tf_op jit(solution)/shard_map/ppermute | solution.py:738
  6.8 24.9 %collective-permute-start.2 = (bf16[2,4,64,1024]{3,2,1,0:T(8,128)(2,1)}, bf16[2,4,64,1024]{3,2,1,0:T(8,128)(2,1)S(1)}, u32[]{:S(2)}, u32[]{:S(2)}) collective-permute-start(bf16[2,4,64,1024]{3,2,1,0:T(8,128)(2,1)} %get-tuple-element.48), channel_id=1, source_target_pairs={{0,1},{1,2},{2,3},{3,4},{4,5},{5,6},{6,7},{8,9},{9,10},{10,11},{11... | collective-permute-start | bytes 3145736 | tf_op jit(solution)/shard_map/ppermute | solution.py:738
  9.2 22.5 %collective-permute-start.3 = (bf16[2,4,64,1024]{3,2,1,0:T(8,128)(2,1)}, bf16[2,4,64,1024]{3,2,1,0:T(8,128)(2,1)}, u32[]{:S(2)}, u32[]{:S(2)}) collective-permute-start(bf16[2,4,64,1024]{3,2,1,0:T(8,128)(2,1)} %get-tuple-element.49), channel_id=1, source_target_pairs={{1,0},{2,1},{3,2},{4,3},{5,4},{6,5},{7,6},{9,8},{10,9},{11,10},{12... | collective-permute-start | bytes 3145736 | tf_op jit(solution)/shard_map/ppermute | solution.py:738
  11.9 2.2 %copy-start.1 = (bf16[2,16,64,1024]{3,2,1,0:T(8,128)(2,1)S(1)}, bf16[2,16,64,1024]{3,2,1,0:T(8,128)(2,1)}, u32[]{:S(2)}) copy-start(bf16[2,16,64,1024]{3,2,1,0:T(8,128)(2,1)} %last_ref.1) | copy-start | bytes 12582916
  14.1 1.1 copy-start.3
  17.1 6.5 %collective-permute-start.4 = (bf16[2,4,64,128]{3,2,1,0:T(8,128)(2,1)S(1)}, bf16[2,4,64,128]{3,2,1,0:T(8,128)(2,1)S(1)}, u32[]{:S(2)}, u32[]{:S(2)}) collective-permute-start(bf16[2,4,64,128]{3,2,1,0:T(8,128)(2,1)S(1)} %get-tuple-element.51), channel_id=1, source_target_pairs={{0,1},{1,2},{2,3},{3,4},{4,5},{5,6},{6,7},{8,9},{9,10},{10,11},{11... | collective-permute-start | bytes 393224 | tf_op jit(solution)/shard_map/ppermute | solution.py:738
  22.3 32.8 %collective-permute-start.1 = (bf16[6,64,1024]{2,1,0:T(8,128)(2,1)S(1)}, bf16[6,64,1024]{2,1,0:T(8,128)(2,1)S(1)}, u32[]{:S(2)}, u32[]{:S(2)}) collective-permute-start(bf16[6,64,1024]{2,1,0:T(8,128)(2,1)S(1)} %copy-done.3), channel_id=1, source_target_pairs={{8,0},{16,8},{24,16},{9,1},{17,9},{25,17},{10,2},{18,10},{26,18},{... | collective-permute-start | bytes 2359304 | tf_op jit(solution)/shard_map/ppermute | solution.py:738
  23.6 8.0 %collective-permute-start.5 = (bf16[2,4,64,128]{3,2,1,0:T(8,128)(2,1)S(1)}, bf16[2,4,64,128]{3,2,1,0:T(8,128)(2,1)S(1)}, u32[]{:S(2)}, u32[]{:S(2)}) collective-permute-start(bf16[2,4,64,128]{3,2,1,0:T(8,128)(2,1)S(1)} %get-tuple-element.52), channel_id=1, source_target_pairs={{1,0},{2,1},{3,2},{4,3},{5,4},{6,5},{7,6},{9,8},{10,9},{11,10},{12... | collective-permute-start | bytes 393224 | tf_op jit(solution)/shard_map/ppermute | solution.py:738
  38.4 7.2 %collective-permute-start.6 = (bf16[4,64,1024]{2,1,0:T(8,128)(2,1)S(1)}, bf16[4,64,1024]{2,1,0:T(8,128)(2,1)S(1)}, u32[]{:S(2)}, u32[]{:S(2)}) collective-permute-start(bf16[4,64,1024]{2,1,0:T(8,128)(2,1)S(1)} %get-tuple-element.55), channel_id=1, source_target_pairs={{0,1},{1,2},{2,3},{3,4},{4,5},{5,6},{6,7},{8,9},{9,10},{10,11},{11... | collective-permute-start | bytes 1572872 | tf_op jit(solution)/shard_map/ppermute | solution.py:738
  42.9 5.7 %collective-permute-start.7 = (bf16[4,64,1024]{2,1,0:T(8,128)(2,1)S(1)}, bf16[4,64,1024]{2,1,0:T(8,128)(2,1)S(1)}, u32[]{:S(2)}, u32[]{:S(2)}) collective-permute-start(bf16[4,64,1024]{2,1,0:T(8,128)(2,1)S(1)} %get-tuple-element.56), channel_id=1, source_target_pairs={{1,0},{2,1},{3,2},{4,3},{5,4},{6,5},{7,6},{9,8},{10,9},{11,10},{12... | collective-permute-start | bytes 1572872 | tf_op jit(solution)/shard_map/ppermute | solution.py:738
  44.2 18.8 %collective-permute-start.9 = (bf16[832,128]{1,0:T(8,128)(2,1)S(1)}, bf16[832,128]{1,0:T(8,128)(2,1)S(1)}, u32[]{:S(2)}, u32[]{:S(2)}) collective-permute-start(bf16[832,128]{1,0:T(8,128)(2,1)S(1)} %get-tuple-element.63), channel_id=1, source_target_pairs={{8,0},{16,8},{24,16},{9,1},{17,9},{25,17},{10,2},{18,10},{26,18},{... | collective-permute-start | bytes 638984 | tf_op jit(solution)/shard_map/ppermute | solution.py:738
  58.0 8.0 %collective-permute-start.8 = (bf16[768,128]{1,0:T(8,128)(2,1)S(1)}, bf16[768,128]{1,0:T(8,128)(2,1)S(1)}, u32[]{:S(2)}, u32[]{:S(2)}) collective-permute-start(bf16[768,128]{1,0:T(8,128)(2,1)S(1)} %get-tuple-element.61), channel_id=1, source_target_pairs={{0,8},{8,16},{16,24},{1,9},{9,17},{17,25},{2,10},{10,18},{18,26},{... | collective-permute-start | bytes 589832 | tf_op jit(solution)/shard_map/ppermute | solution.py:738
  68.7 9.0 %collective-permute-start.10 = (bf16[640,128]{1,0:T(8,128)(2,1)S(1)}, bf16[640,128]{1,0:T(8,128)(2,1)S(1)}, u32[]{:S(2)}, u32[]{:S(2)}) collective-permute-start(bf16[640,128]{1,0:T(8,128)(2,1)S(1)} %get-tuple-element.70), channel_id=1, source_target_pairs={{8,0},{16,8},{24,16},{9,1},{17,9},{25,17},{10,2},{18,10},{26,18},{... | collective-permute-start | bytes 491528 | tf_op jit(solution)/shard_map/ppermute | solution.py:738
  70.0 7.7 %collective-permute-start.11 = (bf16[576,128]{1,0:T(8,128)(2,1)S(1)}, bf16[576,128]{1,0:T(8,128)(2,1)S(1)}, u32[]{:S(2)}, u32[]{:S(2)}) collective-permute-start(bf16[576,128]{1,0:T(8,128)(2,1)S(1)} %get-tuple-element.71), channel_id=1, source_target_pairs={{0,8},{8,16},{16,24},{1,9},{9,17},{17,25},{2,10},{10,18},{18,26},{... | collective-permute-start | bytes 442376 | tf_op jit(solution)/shard_map/ppermute | solution.py:738
  79.6 9.8 %collective-permute-start.12 = (bf16[576,128]{1,0:T(8,128)(2,1)S(1)}, bf16[576,128]{1,0:T(8,128)(2,1)S(1)}, u32[]{:S(2)}, u32[]{:S(2)}) collective-permute-start(bf16[576,128]{1,0:T(8,128)(2,1)S(1)} %get-tuple-element.75), channel_id=1, source_target_pairs={{8,0},{16,8},{24,16},{9,1},{17,9},{25,17},{10,2},{18,10},{26,18},{... | collective-permute-start | bytes 442376 | tf_op jit(solution)/shard_map/ppermute | solution.py:738
  80.9 8.5 %collective-permute-start.13 = (bf16[512,128]{1,0:T(8,128)(2,1)S(1)}, bf16[512,128]{1,0:T(8,128)(2,1)S(1)}, u32[]{:S(2)}, u32[]{:S(2)}) collective-permute-start(bf16[512,128]{1,0:T(8,128)(2,1)S(1)} %get-tuple-element.76), channel_id=1, source_target_pairs={{0,8},{8,16},{16,24},{1,9},{9,17},{17,25},{2,10},{10,18},{18,26},{... | collective-permute-start | bytes 393224 | tf_op jit(solution)/shard_map/ppermute | solution.py:738
  91.4 3.1 %collective-permute-start.14 = (f32[32,128]{1,0:T(8,128)S(1)}, f32[32,128]{1,0:T(8,128)S(1)}, u32[]{:S(2)}, u32[]{:S(2)}) collective-permute-start(f32[32,128]{1,0:T(8,128)S(1)} %get-tuple-element.79), channel_id=1, source_target_pairs={{0,1},{1,0},{2,3},{3,2},{4,5},{5,4},{6,7},{7,6},{8,9},{9,8},{10,11... | collective-permute-start | bytes 49160 | tf_op jit(solution)/shard_map/ppermute | solution.py:726
  94.5 7.5 %collective-permute-start.17 = (f32[32,128]{1,0:T(8,128)S(1)}, f32[32,128]{1,0:T(8,128)S(1)}, u32[]{:S(2)}, u32[]{:S(2)}) collective-permute-start(f32[32,128]{1,0:T(8,128)S(1)} %add.12), channel_id=1, source_target_pairs={{0,6},{1,7},{2,4},{3,5},{4,2},{5,3},{6,0},{7,1},{8,14},{9,15},{10,... | collective-permute-start | bytes 49160 | tf_op jit(solution)/shard_map/ppermute | solution.py:726
  100.3 4.7 %collective-permute-start.16 = (f32[32,128]{1,0:T(8,128)S(1)}, f32[32,128]{1,0:T(8,128)S(1)}, u32[]{:S(2)}, u32[]{:S(2)}) collective-permute-start(f32[32,128]{1,0:T(8,128)S(1)} %add.12), channel_id=1, source_target_pairs={{0,4},{1,5},{2,6},{3,7},{4,0},{5,1},{6,2},{7,3},{8,12},{9,13},{10,... | collective-permute-start | bytes 49160 | tf_op jit(solution)/shard_map/ppermute | solution.py:726
  101.7 3.7 %collective-permute-start.15 = (f32[32,128]{1,0:T(8,128)S(1)}, f32[32,128]{1,0:T(8,128)S(1)}, u32[]{:S(2)}, u32[]{:S(2)}) collective-permute-start(f32[32,128]{1,0:T(8,128)S(1)} %add.12), channel_id=1, source_target_pairs={{0,2},{1,3},{2,0},{3,1},{4,6},{5,7},{6,4},{7,5},{8,10},{9,11},{10,... | collective-permute-start | bytes 49160 | tf_op jit(solution)/shard_map/ppermute | solution.py:726
  105.4 7.2 %collective-permute-start.20 = (f32[32,128]{1,0:T(8,128)S(1)}, f32[32,128]{1,0:T(8,128)S(1)}, u32[]{:S(2)}, u32[]{:S(2)}) collective-permute-start(f32[32,128]{1,0:T(8,128)S(1)} %add_add_fusion.refs_0_), channel_id=1, source_target_pairs={{0,24},{8,16},{16,8},{24,0},{1,25},{9,17},{17,9},{25,1},{2,26},{10... | collective-permute-start | bytes 49160 | tf_op jit(solution)/shard_map/ppermute | solution.py:726
  110.9 3.7 %collective-permute-start.19 = (f32[32,128]{1,0:T(8,128)S(1)}, f32[32,128]{1,0:T(8,128)S(1)}, u32[]{:S(2)}, u32[]{:S(2)}) collective-permute-start(f32[32,128]{1,0:T(8,128)S(1)} %add_add_fusion.refs_0_), channel_id=1, source_target_pairs={{0,16},{8,24},{16,0},{24,8},{1,17},{9,25},{17,1},{25,9},{2,18},{10... | collective-permute-start | bytes 49160 | tf_op jit(solution)/shard_map/ppermute | solution.py:726
  111.0 3.7 %collective-permute-start.18 = (f32[32,128]{1,0:T(8,128)S(1)}, f32[32,128]{1,0:T(8,128)S(1)}, u32[]{:S(2)}, u32[]{:S(2)}) collective-permute-start(f32[32,128]{1,0:T(8,128)S(1)} %add_add_fusion.refs_0_), channel_id=1, source_target_pairs={{0,8},{8,0},{16,24},{24,16},{1,9},{9,1},{17,25},{25,17},{2,10},{10... | collective-permute-start | bytes 49160 | tf_op jit(solution)/shard_map/ppermute | solution.py:726

commit v3 on v2

--- a/solution.py
+++ b/solution.py
@@ -13,7 +13,7 @@
 AFFINITY_TEMP = 4.0
 
 GHOST = ITERS + 1
-EDGE = 5
+EDGE = 4
 TINY = 1e-30
 VMEM_BYTES = 16 * 1024 * 1024
 FLOOR = math.exp(-AFFINITY_TEMP)
@@ -80,7 +80,8 @@
     own = own_ref.shape[1]
     if GHOST <= e < GHOST + own:
         return own_ref[row, e - GHOST]
-    both = (left_ref[row, e] if e < GHOST else right_ref[row, e - GHOST - own]).astype(f32)
+    ref, at = (left_ref, e) if e < GHOST else (right_ref, e - GHOST - own)
+    both = ref[row, at, :, ref.shape[3] - 2 * RANK :].astype(f32)
     return both[:, :RANK] + both[:, RANK:]
 
 
@@ -99,102 +100,106 @@
     return jnp.where(zero, jnp.asarray(TINY, bf16), tile) * column.astype(bf16)
 
 
-def mark_row_kernel(x_ref, tissue_ref, edge_ref, middle_ref, tile_ref, mask_ref, sem_ref):
-    cols = x_ref.shape[1]
-    copies = [pltpu.make_async_copy(x_ref.at[0, c], tile_ref.at[c], sem_ref.at[c]) for c in range(cols)]
-    mask_copy = pltpu.make_async_copy(tissue_ref.at[0], mask_ref, sem_ref.at[cols])
-    mask_copy.start()
+def fetched(sources, slots, sems):
+    copies = [pltpu.make_async_copy(source, slot, sems.at[i]) for i, (source, slot) in enumerate(zip(sources, slots))]
     for copy in copies:
         copy.start()
-    mask_copy.wait()
+    return copies
+
+
+def in_hbm(*arrays):
+    return tuple(pltpu.with_memory_space_constraint(array, pltpu.HBM) for array in arrays)
+
+
+VMEM_SPEC = pl.BlockSpec(memory_space=pltpu.VMEM)
+HBM_SPEC = pl.BlockSpec(memory_space=pltpu.HBM)
+ANY_SPEC = pl.BlockSpec(memory_space=pl.ANY)
+
+
+def mark_edges_kernel(x_ref, tissue_ref, edge_ref, tile_ref, mask_ref, sems):
+    cols = x_ref.shape[1]
+    chosen = list(range(EDGE)) + list(range(cols - EDGE, cols))
+    sources = [tissue_ref.at[0]] + [x_ref.at[0, c] for c in chosen]
+    copies = fetched(sources, [mask_ref] + [tile_ref.at[i] for i in range(len(chosen))], sems)
+    copies[0].wait()
     mask = by_sublane(mask_ref[...])
-    for c in range(cols):
-        copies[c].wait()
-        tile = marked(tile_ref[c], mask[:, c : c + 1])
-        if c < EDGE:
-            edge_ref[c] = tile
-        elif c < cols - EDGE:
-            middle_ref[c - EDGE] = tile
-        else:
-            edge_ref[c - cols + 2 * EDGE] = tile
-
-
-def mark_row(x, tissue):
+    for i, c in enumerate(chosen):
+        copies[i + 1].wait()
+        edge_ref[i] = marked(tile_ref[i], mask[:, c : c + 1])
+
+
+def mark_edges(x, tissue):
     rows, cols, patch, width = x.shape
-    vmem = pl.BlockSpec(memory_space=pltpu.VMEM)
-    hbm = pl.BlockSpec(memory_space=pltpu.HBM)
+    shape = (2 * EDGE, patch, width)
     return pl.pallas_call(
-        mark_row_kernel,
-        in_specs=[hbm, hbm],
-        out_specs=[vmem] * 2,
-        out_shape=(
-            sds((2 * EDGE, patch, width), bf16),
-            sds((cols - 2 * EDGE, patch, width), bf16),
-        ),
+        mark_edges_kernel,
+        in_specs=[HBM_SPEC, HBM_SPEC],
+        out_specs=VMEM_SPEC,
+        out_shape=sds(shape, bf16),
         scratch_shapes=[
-            pltpu.VMEM((cols, patch, width), bf16),
+            pltpu.VMEM(shape, bf16),
             pltpu.VMEM((cols, patch), jnp.int32),
-            pltpu.SemaphoreType.DMA((cols + 1,)),
+            pltpu.SemaphoreType.DMA((2 * EDGE + 1,)),
         ],
         compiler_params=pltpu.CompilerParams(vmem_limit_bytes=VMEM_BYTES),
-    )(pltpu.with_memory_space_constraint(x, pltpu.HBM), pltpu.with_memory_space_constraint(tissue, pltpu.HBM))
-
-
-def mark_ends_kernel(first_ref, last_ref, tissue_ref, after_ref, left_ref, right_ref):
-    rows, count, patch, width = first_ref.shape
-    cols = tissue_ref.shape[1]
-    for row in range(rows):
-        mask = by_sublane(tissue_ref[row])
-        for c in range(count):
-            left_ref[row, c] = marked(first_ref[row, c], mask[:, c : c + 1])
-            at = cols - count + c
-            right_ref[row, c] = marked(last_ref[row, c], mask[:, at : at + 1])
-
-
-def mark_ends(x, tissue, after):
+    )(*in_hbm(x, tissue))
+
+
+def mark_rest_kernel(x_ref, tissue_ref, probe_ref, after_ref, left_ref, right_ref, middle_ref, tile_ref, sems):
+    rows, cols, patch, width = x_ref.shape
+    ends = [(row, c) for row in range(rows) for c in list(range(GHOST)) + list(range(cols - GHOST, cols))]
+    chosen = ends + [(0, c) for c in range(EDGE, cols - EDGE)]
+    copies = fetched([x_ref.at[row, c] for row, c in chosen], [tile_ref.at[i] for i in range(len(chosen))], sems)
+    masks = [by_sublane(tissue_ref[row]) for row in range(rows)]
+    for i, (row, c) in enumerate(chosen):
+        copies[i].wait()
+        tile = marked(tile_ref[i], masks[row][:, c : c + 1])
+        if i >= len(ends):
+            middle_ref[c - EDGE] = tile
+            continue
+        side_ref, at = (left_ref, c) if c < GHOST else (right_ref, c - cols + GHOST)
+        side_ref[row, at, :, :width] = tile
+        side_ref[row, at, :, width:] = jnp.concatenate(pair_of(probe_ref[row, c]), axis=1)
+
+
+def mark_rest(x, tissue, probe, after):
     rows, cols, patch, width = x.shape
-    shape = (rows, GHOST, patch, width)
+    side = sds((rows, GHOST, patch, width + 2 * RANK), bf16)
+    count = 2 * rows * GHOST + cols - 2 * EDGE
     return pl.pallas_call(
-        mark_ends_kernel,
-        grid=(1,),
-        in_specs=[
-            pl.BlockSpec(shape, lambda i: (0, 0, 0, 0)),
-            pl.BlockSpec(shape, lambda i: (0, cols // GHOST - 1, 0, 0)),
-            pl.BlockSpec((rows, cols, patch), lambda i: (0, 0, 0)),
-            pl.BlockSpec(memory_space=pl.ANY),
-        ],
-        out_specs=[pl.BlockSpec(shape, lambda i: (0, 0, 0, 0))] * 2,
-        out_shape=(sds(shape, bf16), sds(shape, bf16)),
+        mark_rest_kernel,
+        in_specs=[HBM_SPEC, VMEM_SPEC, VMEM_SPEC, ANY_SPEC],
+        out_specs=[VMEM_SPEC] * 3,
+        out_shape=(side, side, sds((cols - 2 * EDGE, patch, width), bf16)),
+        scratch_shapes=[pltpu.VMEM((count, patch, width), bf16), pltpu.SemaphoreType.DMA((count,))],
         compiler_params=pltpu.CompilerParams(vmem_limit_bytes=VMEM_BYTES),
-    )(x, x, tissue, after)
-
-
-def units_kernel(n, x_ref, tissue_ref, probe_ref, after_ref, unit0_ref, unit1_ref, left_ref, right_ref):
+    )(*in_hbm(x), tissue, probe, after)
+
+
+def units_kernel(n, x_ref, tissue_ref, after_ref, unit0_ref, unit1_ref, tile_ref, sems):
     rows, cols, patch, width = x_ref.shape
-    for row, unit_ref in ((0, unit0_ref), (1, unit1_ref)):
-        mask = by_sublane(tissue_ref[row]).astype(bf16)
-        for c in range(cols):
-            unit, _ = unit_and_mask(x_ref[row, c])
-            at = (GHOST + c) * patch
-            unit_ref[at : at + patch, :] = unit * mask[:, c : c + 1]
-        for c in range(GHOST):
-            left_ref[row, c] = jnp.concatenate(pair_of(probe_ref[row, c]), axis=1)
-            right_ref[row, c] = jnp.concatenate(pair_of(probe_ref[row, cols - GHOST + c]), axis=1)
-
-
-def own_units(x, tissue, probe, after):
+    chosen = [(row, c) for row in range(rows) for c in range(cols)]
+    copies = fetched([x_ref.at[row, c] for row, c in chosen], [tile_ref.at[i] for i in range(len(chosen))], sems)
+    masks = [by_sublane(tissue_ref[row]).astype(bf16) for row in range(rows)]
+    for i, (row, c) in enumerate(chosen):
+        copies[i].wait()
+        unit, _ = unit_and_mask(tile_ref[i])
+        at = (GHOST + c) * patch
+        (unit0_ref, unit1_ref)[row][at : at + patch, :] = unit * masks[row][:, c : c + 1]
+
+
+def own_units(x, tissue, after):
     rows, cols, patch, width = x.shape
     n = cols + 2 * GHOST
-    vmem = pl.BlockSpec(memory_space=pltpu.VMEM)
-    side = sds((rows, GHOST, patch, 2 * RANK), bf16)
     unit = sds((n * patch, width), bf16)
     return pl.pallas_call(
         functools.partial(units_kernel, n),
-        in_specs=[vmem, vmem, vmem, pl.BlockSpec(memory_space=pl.ANY)],
-        out_specs=[vmem] * 4,
-        out_shape=(unit, unit, side, side),
+        in_specs=[HBM_SPEC, VMEM_SPEC, ANY_SPEC],
+        out_specs=[VMEM_SPEC] * 2,
+        out_shape=(unit, unit),
+        scratch_shapes=[pltpu.VMEM((rows * cols, patch, width), bf16), pltpu.SemaphoreType.DMA((rows * cols,))],
         compiler_params=pltpu.CompilerParams(vmem_limit_bytes=VMEM_BYTES),
-    )(x, tissue, probe, after)
+    )(*in_hbm(x), tissue, after)
 
 
 def bands(ranges, patch, unit0_ref, unit1_ref, m_ref, degree, diagonal):
@@ -206,8 +211,8 @@
 
     def band(e, carry):
         degree, diagonal = carry
-        around = pl.ds(pl.multiple_of((e - 1) * patch, patch), 3 * patch)
-        here = pl.ds(pl.multiple_of(e * patch, patch), patch)
+        around = slice((e - 1) * patch, (e + 2) * patch)
+        here = slice(e * patch, (e + 1) * patch)
         left = jnp.concatenate([unit0_ref[here, :], unit1_ref[here, :]], axis=0)
         right = jnp.concatenate([unit0_ref[around, :], unit1_ref[around, :]], axis=0)
         weights = affinity_of(left, right)
@@ -220,7 +225,8 @@
 
     carry = (degree, diagonal)
     for low, high in ranges:
-        carry = lax.fori_loop(low, high, band, carry)
+        for e in range(low, high):
+            carry = band(e, carry)
     return carry
 
 
@@ -242,10 +248,11 @@
 
 def outside_kernel(
     n,
-    start0_ref, start1_ref, some_ref, xl_ref, xr_ref, tissue_ref, sum_ref, pl_ref, p_ref, pr_ref,
-    unit0_ref, unit1_ref, m_ref, stat_ref, pay_ref,
+    start0_ref, start1_ref, some_ref, tissue_ref, sum_ref, xl_ref, p_ref, xr_ref, after_ref,
+    unit0_ref, unit1_ref, m_ref, stat_ref, pay_ref, pl_ref, pr_ref,
 ):
-    rows, count, patch, width = xl_ref.shape
+    rows, count, patch, _ = xl_ref.shape
+    width = unit0_ref.shape[1]
     cols = n - 2 * count
     both = rows * patch
     lane = iota((patch, 128), 1)
@@ -256,11 +263,11 @@
         mask = jnp.zeros((patch, 128), f32)
         for e in range(n):
             if e < count:
-                unit, column = unit_and_mask(xl_ref[row, e])
+                unit, column = unit_and_mask(xl_ref[row, e, :, :width])
             elif e < count + cols:
                 unit, column = None, own_mask[:, e - count : e - count + 1]
             else:
-                unit, column = unit_and_mask(xr_ref[row, e - count - cols])
+                unit, column = unit_and_mask(xr_ref[row, e - count - cols, :, :width])
             mask = at_lane(lane, e, column, mask)
             if unit is not None:
                 unit_ref[e * patch : (e + 1) * patch, :] = unit
@@ -275,24 +282,29 @@
     half = patch // 2
     tail = (n - 2) * half
     for e in range(1, n - 1):
-        pay_ref[(e - 1) * half : e * half, :] = packed(panel_at((pl_ref, p_ref, pr_ref), 0, e)).astype(bf16)
+        pay_ref[(e - 1) * half : e * half, :] = packed(panel_at((xl_ref, p_ref, xr_ref), 0, e)).astype(bf16)
     pay_ref[tail : tail + patch, :], pay_ref[tail + patch :, :] = pair_of(degree[:patch])
+    pl_ref[...] = xl_ref[:, :, :, width:]
+    pr_ref[...] = xr_ref[:, :, :, width:]
 
 
 def payload_rows(columns, patch):
     return columns * patch // 2 + 2 * patch
 
 
-def outside_affinity(unit0, unit1, m, xl, xr, tissue, sums, panel):
+def outside_affinity(unit0, unit1, m, tissue, sums, panel, after):
     n, both, _ = m.shape
     payload = sds((payload_rows(n - 2, both // 2), 2 * RANK), bf16)
+    side = sds(panel[0].shape[:3] + (2 * RANK,), bf16)
     unit = sds(unit0.shape, bf16)
     return pl.pallas_call(
         functools.partial(outside_kernel, n),
-        out_shape=(unit, unit, sds(m.shape, bf16), sds((3, both, 128), f32), payload),
+        in_specs=[VMEM_SPEC] * 8 + [ANY_SPEC],
+        out_specs=[VMEM_SPEC] * 7,
+        out_shape=(unit, unit, sds(m.shape, bf16), sds((3, both, 128), f32), payload, side, side),
         input_output_aliases={0: 0, 1: 1, 2: 2},
         compiler_params=pltpu.CompilerParams(vmem_limit_bytes=VMEM_BYTES),
-    )(unit0, unit1, m, xl, xr, tissue, sums, *panel)
+    )(unit0, unit1, m, tissue, sums, *panel, after)
 
 
 def cut_kernel(be_ref, after_ref, left_ref, right_ref):
@@ -740,21 +752,21 @@
 
 def local(features, tissue, probe):
     tile_rows, tile_cols, patches, width = features.shape
-    edges, middle = mark_row(features, tissue)
+    edges = mark_edges(features, tissue)
     below_edges = passed_along(edges, "row", -1)
-    below_middle = passed_along(middle, "row", -1)
     own_panel = probe.reshape(tile_rows, tile_cols, patches, RANK)
-    unit0, unit1, probe_left, probe_right = own_units(features, tissue, own_panel, middle)
-    left_end, right_end = mark_ends(features, tissue, edges)
+    left_end, right_end, middle = mark_rest(features, tissue, own_panel, edges)
     from_left = passed_along(right_end, "col", 1)
     from_right = passed_along(left_end, "col", -1)
-    probe_left, probe_right = passed_along(probe_right, "col", 1), passed_along(probe_left, "col", -1)
-    panel = (probe_left, own_panel, probe_right)
+    below_middle = passed_along(middle, "row", -1)
+    unit0, unit1 = own_units(features, tissue, left_end)
     m, sums = inside_affinity(unit0, unit1, patches)
-    _, u1, m, stat, payload = outside_affinity(unit0, unit1, m, from_left, from_right, tissue, sums, panel)
+    below_left, below_right = cut(below_edges, sums)
+    panel = (from_left, own_panel, from_right)
+    _, u1, m, stat, payload, *sides = outside_affinity(unit0, unit1, m, tissue, sums, panel, below_left)
+    panel = (sides[0], own_panel, sides[1])
+    below_left, below_right = passed_along(below_right, "col", 1), passed_along(below_left, "col", -1)
     got_below = passed_along(payload, "row", -1)
-    below_left, below_right = cut(below_edges, stat)
-    below_left, below_right = passed_along(below_right, "col", 1), passed_along(below_left, "col", -1)
     va, wa, sa, ua, paya = edge_affinity(below_left, below_edges, below_right, u1, stat, panel)
     vb, wb, sums, u0, t, payload = middle_affinity(below_edges, below_middle, u1, stat, panel, sa, ua, wa, paya)
     got_above = passed_along(payload, "row", 1)

time: 119 us -> 112 us (0.941)
  waiting for transfers between devices: 18.1 us -> 34.4 us
  starting transfers between devices: 54.7 us -> 39.5 us
  Pallas kernels: 39.9 us -> 35.7 us
  local copies, waits for them, and re-layouts: 5.14 us -> 1.82 us
    ppermute x14 -> x12, waiting for transfers between devices: 11.4 us -> 26.9 us  [passed_along(): return lax.ppermute(shard, axis, pairs)]
    ppermute x14 -> x12, starting transfers between devices: 38.5 us -> 28.3 us  [passed_along(): return lax.ppermute(shard, axis, pairs)]
    ppermute x7, starting transfers between devices: 16.2 us -> 11.2 us  [summed_parts(): lax.ppermute(gram, axis, [(i, i ^ p) for i in range(size)])]
    unnamed x10 -> x2, local copies, waits for them, and re-layouts: 3.33 us -> 0.01 us
    pallas_call x1, Pallas kernels: 6.73 us -> 3.49 us  [inside_affinity(): pl.pallas_call(functools.partial(inside_kernel, n), out_shape=(sds((n, bo...]
  transfers between devices with their start and end apart: 21 -> 19, of which waited for: 12 -> 12; matrix products, arithmetic and copies ran while one was open for 2% -> 2% of each run, Pallas kernels for 22% -> 21%
where the time goes in v3:
time: 112 us
  starting transfers between devices  39.5 us (35%)
  Pallas kernels  35.7 us (32%)
  waiting for transfers between devices  34.4 us (31%)
  local copies, waits for them, and re-layouts  1.82 us (2%)
    ppermute x12, starting transfers between devices, passed_along(): return lax.ppermute(shard, axis, pairs)  28.3 us
    ppermute x12, waiting for transfers between devices, passed_along(): return lax.ppermute(shard, axis, pairs)  26.9 us
    ppermute x7, starting transfers between devices, summed_parts(): lax.ppermute(gram, axis, [(i, i ^ p) for i in range(size)])  11.2 us
    ppermute x7, waiting for transfers between devices, summed_parts(): lax.ppermute(gram, axis, [(i, i ^ p) for i in range(size)])  7.5 us
    pallas_call x1, Pallas kernels, own_units(): pl.pallas_call(functools.partial(units_kernel, n), in_specs=[HBM_SPEC, VM...  5.44 us
    pallas_call x1, Pallas kernels, edge_affinity(): kernel_call(functools.partial(edge_kernel, n), (sds((count, patch, 3 * pa...  3.99 us
    pallas_call x1, Pallas kernels, finish(): kernel_call(functools.partial(finish_kernel, factor, len(parts)), sds(y.s...  3.5 us
    pallas_call x1, Pallas kernels, inside_affinity(): pl.pallas_call(functools.partial(inside_kernel, n), out_shape=(sds((n, bo...  3.49 us
  transfers between devices with their start and end apart: 19, of which 12 were waited for; matrix products, arithmetic and copies ran while one was open for 2% of the time, Pallas kernels for 21%

profile of v3, /device:TPU:0, one launch (start us, length us, event | category | flops | bytes accessed | tf_op | source)
XLA Modules:
  0.0 111.7 jit_solution(10499078926614807205)
XLA Ops:
  0.0 1.6 %shard_map.37.after_ref = bf16[8,64,1024]{2,1,0:T(8,128)(2,1)S(1)} custom-call(bf16[2,16,64,1024]{3,2,1,0:T(8,128)(2,1)} %x_ref.5, s32[2,16,64]{2,1,0:T(8,128)} %tissue_ref.7), custom_call_target="tpu_custom_call" | custom-call | tf_op jit(solution)/shard_map/pallas_call | solution.py:134
  1.7 0.0 copy-start
  1.7 1.3 %collective-permute-start = (bf16[8,64,1024]{2,1,0:T(8,128)(2,1)S(1)}, bf16[8,64,1024]{2,1,0:T(8,128)(2,1)S(1)}, u32[]{:S(2)}, u32[]{:S(2)}) collective-permute-start(bf16[8,64,1024]{2,1,0:T(8,128)(2,1)S(1)} %shard_map.37.after_ref), channel_id=1, source_target_pairs={{8,0},{16,8},{24,16},{9,1},{17,9},{25,17},{10,2},{18,10},{26,18},{... | collective-permute-start | bytes 3145736 | tf_op jit(solution)/shard_map/ppermute | solution.py:750
  3.0 1.5 %reshape.9.probe_ref.p_ref = f32[2,16,64,64]{3,2,1,0:T(8,128)S(1)} reshape(f32[2,16,4096]{2,1,0:T(8,128)} %param.5) | data formatting | bytes 1048576 | tf_op jit(solution)/shard_map/reshape | solution.py:757
  4.4 0.0 copy-done
  4.4 3.1 %shard_map.38 = (bf16[2,4,64,1152]{3,2,1,0:T(8,128)(2,1)S(1)}, bf16[2,4,64,1152]{3,2,1,0:T(8,128)(2,1)S(1)}, bf16[8,64,1024]{2,1,0:T(8,128)(2,1)S(1)}) custom-call(bf16[2,16,64,1024]{3,2,1,0:T(8,128)(2,1)} %x_ref.5, s32[2,16,64]{2,1,0:T(8,128)S(1)} %copy-done, f32[2,16,64,64]{3,2,1,0:T(8,128)S(1)} %reshape.9.probe_ref.p_ref, ...), custom_call_target="tpu_custom_call" | custom-call | tf_op jit(solution)/shard_map/pallas_call | solution.py:169
  7.6 2.4 %collective-permute-start.2 = (bf16[2,4,64,1152]{3,2,1,0:T(8,128)(2,1)S(1)}, bf16[2,4,64,1152]{3,2,1,0:T(8,128)(2,1)S(1)}, u32[]{:S(2)}, u32[]{:S(2)}) collective-permute-start(bf16[2,4,64,1152]{3,2,1,0:T(8,128)(2,1)S(1)} %get-tuple-element.48), channel_id=1, source_target_pairs={{0,1},{1,2},{2,3},{3,4},{4,5},{5,6},{6,7},{8,9},{9,10},{10,11},{11... | collective-permute-start | bytes 3538952 | tf_op jit(solution)/shard_map/ppermute | solution.py:750
  10.0 1.3 %collective-permute-start.3 = (bf16[2,4,64,1152]{3,2,1,0:T(8,128)(2,1)S(1)}, bf16[2,4,64,1152]{3,2,1,0:T(8,128)(2,1)S(1)}, u32[]{:S(2)}, u32[]{:S(2)}) collective-permute-start(bf16[2,4,64,1152]{3,2,1,0:T(8,128)(2,1)S(1)} %get-tuple-element.43.after_ref), channel_id=1, source_target_pairs={{1,0},{2,1},{3,2},{4,3},{5,4},{6,5},{7,6},{9,8},{10,9},{11,10},{12... | collective-permute-start | bytes 3538952 | tf_op jit(solution)/shard_map/ppermute | solution.py:750
  11.3 1.3 %collective-permute-start.1 = (bf16[8,64,1024]{2,1,0:T(8,128)(2,1)S(1)}, bf16[8,64,1024]{2,1,0:T(8,128)(2,1)S(1)}, u32[]{:S(2)}, u32[]{:S(2)}) collective-permute-start(bf16[8,64,1024]{2,1,0:T(8,128)(2,1)S(1)} %get-tuple-element.42), channel_id=1, source_target_pairs={{8,0},{16,8},{24,16},{9,1},{17,9},{25,17},{10,2},{18,10},{26,18},{... | collective-permute-start | bytes 3145736 | tf_op jit(solution)/shard_map/ppermute | solution.py:750
  12.6 5.4 %shard_map.39 = (bf16[1536,1024]{1,0:T(8,128)(2,1)S(1)}, bf16[1536,1024]{1,0:T(8,128)(2,1)S(1)}) custom-call(bf16[2,16,64,1024]{3,2,1,0:T(8,128)(2,1)} %x_ref.5, s32[2,16,64]{2,1,0:T(8,128)S(1)} %copy-done, bf16[2,4,64,1152]{3,2,1,0:T(8,128)(2,1)S(1)} %get-tuple-element.43.after_ref), custom_call_target="tpu_custom_call" | custom-call | tf_op jit(solution)/shard_map/pallas_call | solution.py:195
  18.1 3.5 %shard_map.40 = (bf16[24,128,384]{2,1,0:T(8,128)(2,1)S(1)}, f32[2,128,128]{2,1,0:T(8,128)S(1)}) custom-call(bf16[1536,1024]{1,0:T(8,128)(2,1)S(1)} %get-tuple-element.44.unit0_ref.start0_ref, bf16[1536,1024]{1,0:T(8,128)(2,1)S(1)} %get-tuple-element.45.unit1_ref.start1_ref), custom_call_target="tpu_custom_call" | custom-call | tf_op jit(solution)/shard_map/pallas_call | solution.py:242
  21.6 8.9 %collective-permute-done.be_ref = bf16[8,64,1024]{2,1,0:T(8,128)(2,1)S(1)} collective-permute-done((bf16[8,64,1024]{2,1,0:T(8,128)(2,1)S(1)}, bf16[8,64,1024]{2,1,0:T(8,128)(2,1)S(1)}, u32[]{:S(2)}, u32[]{:S(2)}) %collective-permute-start) | collective-permute-done | bytes 1048608 | tf_op jit(solution)/shard_map/ppermute | solution.py:750
  30.5 0.1 shard_map.41
  30.6 1.3 %collective-permute-start.4 = (bf16[4,64,1024]{2,1,0:T(8,128)(2,1)S(1)}, bf16[4,64,1024]{2,1,0:T(8,128)(2,1)S(1)}, u32[]{:S(2)}, u32[]{:S(2)}) collective-permute-start(bf16[4,64,1024]{2,1,0:T(8,128)(2,1)S(1)} %get-tuple-element.54), channel_id=1, source_target_pairs={{0,1},{1,2},{2,3},{3,4},{4,5},{5,6},{6,7},{8,9},{9,10},{10,11},{11... | collective-permute-start | bytes 1572872 | tf_op jit(solution)/shard_map/ppermute | solution.py:750
  31.9 1.3 %collective-permute-start.5 = (bf16[4,64,1024]{2,1,0:T(8,128)(2,1)S(1)}, bf16[4,64,1024]{2,1,0:T(8,128)(2,1)S(1)}, u32[]{:S(2)}, u32[]{:S(2)}) collective-permute-start(bf16[4,64,1024]{2,1,0:T(8,128)(2,1)S(1)} %get-tuple-element.49.after_ref), channel_id=1, source_target_pairs={{1,0},{2,1},{3,2},{4,3},{5,4},{6,5},{7,6},{9,8},{10,9},{11,10},{12... | collective-permute-start | bytes 1572872 | tf_op jit(solution)/shard_map/ppermute | solution.py:750
  33.2 0.0 collective-permute-done.2.xl_ref
  33.2 0.0 collective-permute-done.3.xr_ref
  33.2 2.4 %shard_map.42 = (bf16[1536,1024]{1,0:T(8,128)(2,1)S(1)}, bf16[1536,1024]{1,0:T(8,128)(2,1)S(1)}, bf16[24,128,384]{2,1,0:T(8,128)(2,1)S(1)}, f32[3,128,128]{2,1,0...) custom-call(bf16[1536,1024]{1,0:T(8,128)(2,1)S(1)} %get-tuple-elemen, ...), custom_call_target="tpu_custom_call", output_to_operand_aliasing={{0}: (0, {}), {1}: (1, {}), {2}: (2, {})} | custom-call | tf_op jit(solution)/shard_map/pallas_call | solution.py:300
  35.7 1.5 %collective-permute-start.7 = (bf16[832,128]{1,0:T(8,128)(2,1)S(1)}, bf16[832,128]{1,0:T(8,128)(2,1)S(1)}, u32[]{:S(2)}, u32[]{:S(2)}) collective-permute-start(bf16[832,128]{1,0:T(8,128)(2,1)S(1)} %get-tuple-element.61), channel_id=1, source_target_pairs={{8,0},{16,8},{24,16},{9,1},{17,9},{25,17},{10,2},{18,10},{26,18},{... | collective-permute-start | bytes 638984 | tf_op jit(solution)/shard_map/ppermute | solution.py:750
  37.2 0.0 collective-permute-done.4.bl_ref
  37.2 0.9 collective-permute-done.5.br_ref
  38.0 4.0 %shard_map.43 = (bf16[12,64,192]{2,1,0:T(8,128)(2,1)S(1)}, bf16[12,64,192]{2,1,0:T(8,128)(2,1)S(1)}, f32[3,64,128]{2,1,0:T(8,128)S(1)}, bf16[24,64,64]{2,1,0:T(8,128)(2,1)S(1)}, bf16[640,128]{1,0:T(8,128)(2,1)S(1)}) custom-call(bf16[4,64,1024]{2,1,0:T(8,128)(2,1)S(1)} %collective-permute-done.4.bl_ref, bf16[8,64,1024]{2,1,0:T(8,128)(2,1)S(1)} %collective-permute-done.be_ref, ...), custom_call_target="tpu_custom_call" | custom-call | flops 603979776 | bytes 1048576 | tf_op jit(solution)/shard_map/pallas_call | solution.py:415
  42.0 10.9 %collective-permute-done.1.bm_ref = bf16[8,64,1024]{2,1,0:T(8,128)(2,1)S(1)} collective-permute-done((bf16[8,64,1024]{2,1,0:T(8,128)(2,1)S(1)}, bf16[8,64,1024]{2,1,0:T(8,128)(2,1)S(1)}, u32[]{:S(2)}, u32[]{:S(2)}) %collective-permute-start.1) | collective-permute-done | bytes 1048608 | tf_op jit(solution)/shard_map/ppermute | solution.py:750
  53.0 3.2 %shard_map.44 = (bf16[10,64,192]{2,1,0:T(8,128)(2,1)S(1)}, bf16[10,64,192]{2,1,0:T(8,128)(2,1)S(1)}, f32[2,64,128]{2,1,0:T(8,128)S(1)}, bf16[24,64,64]{2,1,0:T(8...) custom-call(bf16[8,64,1024]{2,1,0:T(8,128)(2,1)S(1)} %collective-permute-done.be_ref, ...), custom_call_target="tpu_custom_call" | custom-call | flops 503316480 | bytes 1048576 | tf_op jit(solution)/shard_map/pallas_call | solution.py:463
  56.2 4.9 %collective-permute-start.6 = (bf16[768,128]{1,0:T(8,128)(2,1)S(1)}, bf16[768,128]{1,0:T(8,128)(2,1)S(1)}, u32[]{:S(2)}, u32[]{:S(2)}) collective-permute-start(bf16[768,128]{1,0:T(8,128)(2,1)S(1)} %get-tuple-element.59), channel_id=1, source_target_pairs={{0,8},{8,16},{16,24},{1,9},{9,17},{17,25},{2,10},{10,18},{18,26},{... | collective-permute-start | bytes 589832 | tf_op jit(solution)/shard_map/ppermute | solution.py:750
  61.1 0.0 collective-permute-done.7.got_ref
  61.1 0.9 shard_map.45.z_ref
  62.0 2.2 %collective-permute-done.6.got_ref = bf16[768,128]{1,0:T(8,128)(2,1)S(1)} collective-permute-done((bf16[768,128]{1,0:T(8,128)(2,1)S(1)}, bf16[768,128]{1,0:T(8,128)(2,1)S(1)}, u32[]{:S(2)}, u32[]{:S(2)}) %collective-permute-start.6) | collective-permute-done | bytes 196640 | tf_op jit(solution)/shard_map/ppermute | solution.py:750
  64.2 2.6 %shard_map.46 = (f32[2,24,64,64]{3,2,1,0:T(8,128)S(1)}, bf16[2,24,64,64]{3,2,1,0:T(8,128)(2,1)S(1)}, f32[2,128,128]{2,1,0:T(8,128)S(1)}, bf16[640,128]{1,0:T(8,128)(2,1)S(1)}, bf16[576,128]{1,0:T(8,128)(2,1)S(1)}) custom-call(bf16[768,128]{1,0:T(8,128)(2,1)S(1)} %collective-permute-done.6.got_ref, f32[3,128,128]{2,1,0:T(8,128)S(1)} %get-tuple-element.51.stat_ref, ...), custom_call_target="tpu_custom_call" | custom-call | flops 75497472 | bytes 1048576 | tf_op jit(solution)/shard_map/pallas_call | solution.py:548
  66.9 1.3 %collective-permute-start.8 = (bf16[640,128]{1,0:T(8,128)(2,1)S(1)}, bf16[640,128]{1,0:T(8,128)(2,1)S(1)}, u32[]{:S(2)}, u32[]{:S(2)}) collective-permute-start(bf16[640,128]{1,0:T(8,128)(2,1)S(1)} %get-tuple-element.68), channel_id=1, source_target_pairs={{8,0},{16,8},{24,16},{9,1},{17,9},{25,17},{10,2},{18,10},{26,18},{... | collective-permute-start | bytes 491528 | tf_op jit(solution)/shard_map/ppermute | solution.py:750
  68.2 5.0 %collective-permute-start.9 = (bf16[576,128]{1,0:T(8,128)(2,1)S(1)}, bf16[576,128]{1,0:T(8,128)(2,1)S(1)}, u32[]{:S(2)}, u32[]{:S(2)}) collective-permute-start(bf16[576,128]{1,0:T(8,128)(2,1)S(1)} %get-tuple-element.69), channel_id=1, source_target_pairs={{0,8},{8,16},{16,24},{1,9},{9,17},{17,25},{2,10},{10,18},{18,26},{... | collective-permute-start | bytes 442376 | tf_op jit(solution)/shard_map/ppermute | solution.py:750
  73.2 0.6 shard_map.47.z_ref
  73.8 2.0 %collective-permute-done.9.above_ref = bf16[576,128]{1,0:T(8,128)(2,1)S(1)} collective-permute-done((bf16[576,128]{1,0:T(8,128)(2,1)S(1)}, bf16[576,128]{1,0:T(8,128)(2,1)S(1)}, u32[]{:S(2)}, u32[]{:S(2)}) %collective-permute-start.9) | collective-permute-done | bytes 147488 | tf_op jit(solution)/shard_map/ppermute | solution.py:750
  75.8 0.2 collective-permute-done.8.below_ref
  76.0 2.0 %shard_map.48 = (f32[2,24,64,64]{3,2,1,0:T(8,128)S(1)}, bf16[2,24,64,64]{3,2,1,0:T(8,128)(2,1)S(1)}, bf16[576,128]{1,0:T(8,128)(2,1)S(1)}, bf16[512,128]{1,0:T(8,128)(2,1)S(1)}) custom-call(bf16[640,128]{1,0:T(8,128)(2,1)S(1)} %collective-permute-done.8.below_ref, bf16[576,128]{1,0:T(8,128)(2,1)S(1)} %collective-permute-done.9.above_ref, ...), custom_call_target="tpu_custom_call" | custom-call | flops 50331648 | bytes 1048576 | tf_op jit(solution)/shard_map/pallas_call | solution.py:623
  78.0 1.3 %collective-permute-start.10 = (bf16[576,128]{1,0:T(8,128)(2,1)S(1)}, bf16[576,128]{1,0:T(8,128)(2,1)S(1)}, u32[]{:S(2)}, u32[]{:S(2)}) collective-permute-start(bf16[576,128]{1,0:T(8,128)(2,1)S(1)} %get-tuple-element.73), channel_id=1, source_target_pairs={{8,0},{16,8},{24,16},{9,1},{17,9},{25,17},{10,2},{18,10},{26,18},{... | collective-permute-start | bytes 442376 | tf_op jit(solution)/shard_map/ppermute | solution.py:750
  79.3 5.5 %collective-permute-start.11 = (bf16[512,128]{1,0:T(8,128)(2,1)S(1)}, bf16[512,128]{1,0:T(8,128)(2,1)S(1)}, u32[]{:S(2)}, u32[]{:S(2)}) collective-permute-start(bf16[512,128]{1,0:T(8,128)(2,1)S(1)} %get-tuple-element.74), channel_id=1, source_target_pairs={{0,8},{8,16},{16,24},{1,9},{9,17},{17,25},{2,10},{10,18},{18,26},{... | collective-permute-start | bytes 393224 | tf_op jit(solution)/shard_map/ppermute | solution.py:750
  84.8 0.6 shard_map.49.z_ref
  85.4 1.7 %collective-permute-done.11.above_ref = bf16[512,128]{1,0:T(8,128)(2,1)S(1)} collective-permute-done((bf16[512,128]{1,0:T(8,128)(2,1)S(1)}, bf16[512,128]{1,0:T(8,128)(2,1)S(1)}, u32[]{:S(2)}, u32[]{:S(2)}) %collective-permute-start.11) | collective-permute-done | bytes 131104 | tf_op jit(solution)/shard_map/ppermute | solution.py:750
  87.1 0.0 collective-permute-done.10.below_ref
  87.1 2.0 %shard_map.50 = (f32[2,16,64,64]{3,2,1,0:T(8,128)S(1)}, f32[32,128]{1,0:T(8,128)S(1)}) custom-call(bf16[576,128]{1,0:T(8,128)(2,1)S(1)} %collective-permute-done.10.below_ref, bf16[512,128]{1,0:T(8,128)(2,1)S(1)} %collective-permute-done.11.above_ref, f32[24,128,64]{2,1,0:T(8,128)S(1)} %shard_map.49.z_ref, f32[2,24,64,64]{3,2,1,0:T(8,128)S(1)} %get-tuple-element.76.y_ref, ...), custom_call_target="tpu_custom_call" | custom-call | flops 50331648 | bytes 1048576 | tf_op jit(solution)/shard_map/pallas_call | solution.py:657
  89.1 0.0 collective-permute-start.12
  89.1 1.2 %collective-permute-done.12 = f32[32,128]{1,0:T(8,128)S(1)} collective-permute-done((f32[32,128]{1,0:T(8,128)S(1)}, f32[32,128]{1,0:T(8,128)S(1)}, u32[]{:S(2)}, u32[]{:S(2)}) %collective-permute-start.12) | collective-permute-done | bytes 16416 | tf_op jit(solution)/shard_map/ppermute | solution.py:738
  90.3 3.6 %collective-permute-start.15 = (f32[32,128]{1,0:T(8,128)S(1)}, f32[32,128]{1,0:T(8,128)S(1)}, u32[]{:S(2)}, u32[]{:S(2)}) collective-permute-start(f32[32,128]{1,0:T(8,128)S(1)} %add.12), channel_id=1, source_target_pairs={{0,6},{1,7},{2,4},{3,5},{4,2},{5,3},{6,0},{7,1},{8,14},{9,15},{10,... | collective-permute-start | bytes 49160 | tf_op jit(solution)/shard_map/ppermute | solution.py:738
  93.9 0.0 collective-permute-start.14
  93.9 0.8 collective-permute-start.13
  94.7 1.1 %collective-permute-done.15 = f32[32,128]{1,0:T(8,128)S(1)} collective-permute-done((f32[32,128]{1,0:T(8,128)S(1)}, f32[32,128]{1,0:T(8,128)S(1)}, u32[]{:S(2)}, u32[]{:S(2)}) %collective-permute-start.15) | collective-permute-done | bytes 16416 | tf_op jit(solution)/shard_map/ppermute | solution.py:738
  95.9 2.7 %collective-permute-done.14 = f32[32,128]{1,0:T(8,128)S(1)} collective-permute-done((f32[32,128]{1,0:T(8,128)S(1)}, f32[32,128]{1,0:T(8,128)S(1)}, u32[]{:S(2)}, u32[]{:S(2)}) %collective-permute-start.14) | collective-permute-done | bytes 16416 | tf_op jit(solution)/shard_map/ppermute | solution.py:738
  98.6 0.0 collective-permute-done.13
  98.6 5.9 %collective-permute-start.18 = (f32[32,128]{1,0:T(8,128)S(1)}, f32[32,128]{1,0:T(8,128)S(1)}, u32[]{:S(2)}, u32[]{:S(2)}) collective-permute-start(f32[32,128]{1,0:T(8,128)S(1)} %add_add_fusion.refs_0_), channel_id=1, source_target_pairs={{0,24},{8,16},{16,8},{24,0},{1,25},{9,17},{17,9},{25,1},{2,26},{10... | collective-permute-start | bytes 49160 | tf_op jit(solution)/shard_map/ppermute | solution.py:738
  104.4 0.0 collective-permute-start.17
  104.5 0.9 collective-permute-start.16
  105.4 0.4 reshape.10.refs_4_
  105.7 0.4 collective-permute-done.18.refs_3_
  106.2 2.0 %collective-permute-done.17.refs_2_ = f32[32,128]{1,0:T(8,128)S(1)} collective-permute-done((f32[32,128]{1,0:T(8,128)S(1)}, f32[32,128]{1,0:T(8,128)S(1)}, u32[]{:S(2)}, u32[]{:S(2)}) %collective-permute-start.17) | collective-permute-done | bytes 16416 | tf_op jit(solution)/shard_map/ppermute | solution.py:738
  108.2 0.0 collective-permute-done.16.refs_1_
  108.2 3.5 %shard_map.51 = f32[32,4096]{1,0:T(8,128)} custom-call(f32[32,128]{1,0:T(8,128)S(1)} %add_add_fusion.refs_0_, f32[32,128]{1,0:T(8,128)S(1)} %collective-permute-done.16.refs_1_, f32[32,128]{1,0:T(8,128)S(1)} %collective-permute-done.17.refs_2_, f32[32,128]{1,0:T(8,128)S(1)} %collective-permute-done.18.refs_3_, f32[32,4096]{1,0:T(8,128)S(1)} %reshape.10.refs_4_), custom_call_target="tpu_custom_call" | custom-call | flops 16777216 | bytes 1048576 | tf_op jit(solution)/shard_map/pallas_call | solution.py:709
  (2 shorter events, 0.0 us)
Async XLA Ops:
  1.7 2.8 %copy-start = (s32[2,16,64]{2,1,0:T(8,128)S(1)}, s32[2,16,64]{2,1,0:T(8,128)}, u32[]{:S(2)}) copy-start(s32[2,16,64]{2,1,0:T(8,128)} %tissue_ref.7) | copy-start | bytes 24580
  1.7 28.8 %collective-permute-start = (bf16[8,64,1024]{2,1,0:T(8,128)(2,1)S(1)}, bf16[8,64,1024]{2,1,0:T(8,128)(2,1)S(1)}, u32[]{:S(2)}, u32[]{:S(2)}) collective-permute-start(bf16[8,64,1024]{2,1,0:T(8,128)(2,1)S(1)} %shard_map.37.after_ref), channel_id=1, source_target_pairs={{8,0},{16,8},{24,16},{9,1},{17,9},{25,17},{10,2},{18,10},{26,18},{... | collective-permute-start | bytes 3145736 | tf_op jit(solution)/shard_map/ppermute | solution.py:750
  7.6 25.6 %collective-permute-start.2 = (bf16[2,4,64,1152]{3,2,1,0:T(8,128)(2,1)S(1)}, bf16[2,4,64,1152]{3,2,1,0:T(8,128)(2,1)S(1)}, u32[]{:S(2)}, u32[]{:S(2)}) collective-permute-start(bf16[2,4,64,1152]{3,2,1,0:T(8,128)(2,1)S(1)} %get-tuple-element.48), channel_id=1, source_target_pairs={{0,1},{1,2},{2,3},{3,4},{4,5},{5,6},{6,7},{8,9},{9,10},{10,11},{11... | collective-permute-start | bytes 3538952 | tf_op jit(solution)/shard_map/ppermute | solution.py:750
  10.0 23.2 %collective-permute-start.3 = (bf16[2,4,64,1152]{3,2,1,0:T(8,128)(2,1)S(1)}, bf16[2,4,64,1152]{3,2,1,0:T(8,128)(2,1)S(1)}, u32[]{:S(2)}, u32[]{:S(2)}) collective-permute-start(bf16[2,4,64,1152]{3,2,1,0:T(8,128)(2,1)S(1)} %get-tuple-element.43.after_ref), channel_id=1, source_target_pairs={{1,0},{2,1},{3,2},{4,3},{5,4},{6,5},{7,6},{9,8},{10,9},{11,10},{12... | collective-permute-start | bytes 3538952 | tf_op jit(solution)/shard_map/ppermute | solution.py:750
  11.3 41.7 %collective-permute-start.1 = (bf16[8,64,1024]{2,1,0:T(8,128)(2,1)S(1)}, bf16[8,64,1024]{2,1,0:T(8,128)(2,1)S(1)}, u32[]{:S(2)}, u32[]{:S(2)}) collective-permute-start(bf16[8,64,1024]{2,1,0:T(8,128)(2,1)S(1)} %get-tuple-element.42), channel_id=1, source_target_pairs={{8,0},{16,8},{24,16},{9,1},{17,9},{25,17},{10,2},{18,10},{26,18},{... | collective-permute-start | bytes 3145736 | tf_op jit(solution)/shard_map/ppermute | solution.py:750
  30.6 6.6 %collective-permute-start.4 = (bf16[4,64,1024]{2,1,0:T(8,128)(2,1)S(1)}, bf16[4,64,1024]{2,1,0:T(8,128)(2,1)S(1)}, u32[]{:S(2)}, u32[]{:S(2)}) collective-permute-start(bf16[4,64,1024]{2,1,0:T(8,128)(2,1)S(1)} %get-tuple-element.54), channel_id=1, source_target_pairs={{0,1},{1,2},{2,3},{3,4},{4,5},{5,6},{6,7},{8,9},{9,10},{10,11},{11... | collective-permute-start | bytes 1572872 | tf_op jit(solution)/shard_map/ppermute | solution.py:750
  31.9 6.1 %collective-permute-start.5 = (bf16[4,64,1024]{2,1,0:T(8,128)(2,1)S(1)}, bf16[4,64,1024]{2,1,0:T(8,128)(2,1)S(1)}, u32[]{:S(2)}, u32[]{:S(2)}) collective-permute-start(bf16[4,64,1024]{2,1,0:T(8,128)(2,1)S(1)} %get-tuple-element.49.after_ref), channel_id=1, source_target_pairs={{1,0},{2,1},{3,2},{4,3},{5,4},{6,5},{7,6},{9,8},{10,9},{11,10},{12... | collective-permute-start | bytes 1572872 | tf_op jit(solution)/shard_map/ppermute | solution.py:750
  35.7 25.4 %collective-permute-start.7 = (bf16[832,128]{1,0:T(8,128)(2,1)S(1)}, bf16[832,128]{1,0:T(8,128)(2,1)S(1)}, u32[]{:S(2)}, u32[]{:S(2)}) collective-permute-start(bf16[832,128]{1,0:T(8,128)(2,1)S(1)} %get-tuple-element.61), channel_id=1, source_target_pairs={{8,0},{16,8},{24,16},{9,1},{17,9},{25,17},{10,2},{18,10},{26,18},{... | collective-permute-start | bytes 638984 | tf_op jit(solution)/shard_map/ppermute | solution.py:750
  56.2 8.0 %collective-permute-start.6 = (bf16[768,128]{1,0:T(8,128)(2,1)S(1)}, bf16[768,128]{1,0:T(8,128)(2,1)S(1)}, u32[]{:S(2)}, u32[]{:S(2)}) collective-permute-start(bf16[768,128]{1,0:T(8,128)(2,1)S(1)} %get-tuple-element.59), channel_id=1, source_target_pairs={{0,8},{8,16},{16,24},{1,9},{9,17},{17,25},{2,10},{10,18},{18,26},{... | collective-permute-start | bytes 589832 | tf_op jit(solution)/shard_map/ppermute | solution.py:750
  66.9 9.2 %collective-permute-start.8 = (bf16[640,128]{1,0:T(8,128)(2,1)S(1)}, bf16[640,128]{1,0:T(8,128)(2,1)S(1)}, u32[]{:S(2)}, u32[]{:S(2)}) collective-permute-start(bf16[640,128]{1,0:T(8,128)(2,1)S(1)} %get-tuple-element.68), channel_id=1, source_target_pairs={{8,0},{16,8},{24,16},{9,1},{17,9},{25,17},{10,2},{18,10},{26,18},{... | collective-permute-start | bytes 491528 | tf_op jit(solution)/shard_map/ppermute | solution.py:750
  68.2 7.7 %collective-permute-start.9 = (bf16[576,128]{1,0:T(8,128)(2,1)S(1)}, bf16[576,128]{1,0:T(8,128)(2,1)S(1)}, u32[]{:S(2)}, u32[]{:S(2)}) collective-permute-start(bf16[576,128]{1,0:T(8,128)(2,1)S(1)} %get-tuple-element.69), channel_id=1, source_target_pairs={{0,8},{8,16},{16,24},{1,9},{9,17},{17,25},{2,10},{10,18},{18,26},{... | collective-permute-start | bytes 442376 | tf_op jit(solution)/shard_map/ppermute | solution.py:750
  78.0 9.1 %collective-permute-start.10 = (bf16[576,128]{1,0:T(8,128)(2,1)S(1)}, bf16[576,128]{1,0:T(8,128)(2,1)S(1)}, u32[]{:S(2)}, u32[]{:S(2)}) collective-permute-start(bf16[576,128]{1,0:T(8,128)(2,1)S(1)} %get-tuple-element.73), channel_id=1, source_target_pairs={{8,0},{16,8},{24,16},{9,1},{17,9},{25,17},{10,2},{18,10},{26,18},{... | collective-permute-start | bytes 442376 | tf_op jit(solution)/shard_map/ppermute | solution.py:750
  79.3 7.8 %collective-permute-start.11 = (bf16[512,128]{1,0:T(8,128)(2,1)S(1)}, bf16[512,128]{1,0:T(8,128)(2,1)S(1)}, u32[]{:S(2)}, u32[]{:S(2)}) collective-permute-start(bf16[512,128]{1,0:T(8,128)(2,1)S(1)} %get-tuple-element.74), channel_id=1, source_target_pairs={{0,8},{8,16},{16,24},{1,9},{9,17},{17,25},{2,10},{10,18},{18,26},{... | collective-permute-start | bytes 393224 | tf_op jit(solution)/shard_map/ppermute | solution.py:750
  89.1 1.2 %collective-permute-start.12 = (f32[32,128]{1,0:T(8,128)S(1)}, f32[32,128]{1,0:T(8,128)S(1)}, u32[]{:S(2)}, u32[]{:S(2)}) collective-permute-start(f32[32,128]{1,0:T(8,128)S(1)} %get-tuple-element.77), channel_id=1, source_target_pairs={{0,1},{1,0},{2,3},{3,2},{4,5},{5,4},{6,7},{7,6},{8,9},{9,8},{10,11... | collective-permute-start | bytes 49160 | tf_op jit(solution)/shard_map/ppermute | solution.py:738
  90.3 5.5 %collective-permute-start.15 = (f32[32,128]{1,0:T(8,128)S(1)}, f32[32,128]{1,0:T(8,128)S(1)}, u32[]{:S(2)}, u32[]{:S(2)}) collective-permute-start(f32[32,128]{1,0:T(8,128)S(1)} %add.12), channel_id=1, source_target_pairs={{0,6},{1,7},{2,4},{3,5},{4,2},{5,3},{6,0},{7,1},{8,14},{9,15},{10,... | collective-permute-start | bytes 49160 | tf_op jit(solution)/shard_map/ppermute | solution.py:738
  93.9 4.6 %collective-permute-start.14 = (f32[32,128]{1,0:T(8,128)S(1)}, f32[32,128]{1,0:T(8,128)S(1)}, u32[]{:S(2)}, u32[]{:S(2)}) collective-permute-start(f32[32,128]{1,0:T(8,128)S(1)} %add.12), channel_id=1, source_target_pairs={{0,4},{1,5},{2,6},{3,7},{4,0},{5,1},{6,2},{7,3},{8,12},{9,13},{10,... | collective-permute-start | bytes 49160 | tf_op jit(solution)/shard_map/ppermute | solution.py:738
  93.9 4.6 %collective-permute-start.13 = (f32[32,128]{1,0:T(8,128)S(1)}, f32[32,128]{1,0:T(8,128)S(1)}, u32[]{:S(2)}, u32[]{:S(2)}) collective-permute-start(f32[32,128]{1,0:T(8,128)S(1)} %add.12), channel_id=1, source_target_pairs={{0,2},{1,3},{2,0},{3,1},{4,6},{5,7},{6,4},{7,5},{8,10},{9,11},{10,... | collective-permute-start | bytes 49160 | tf_op jit(solution)/shard_map/ppermute | solution.py:738
  98.6 7.6 %collective-permute-start.18 = (f32[32,128]{1,0:T(8,128)S(1)}, f32[32,128]{1,0:T(8,128)S(1)}, u32[]{:S(2)}, u32[]{:S(2)}) collective-permute-start(f32[32,128]{1,0:T(8,128)S(1)} %add_add_fusion.refs_0_), channel_id=1, source_target_pairs={{0,24},{8,16},{16,8},{24,0},{1,25},{9,17},{17,9},{25,1},{2,26},{10... | collective-permute-start | bytes 49160 | tf_op jit(solution)/shard_map/ppermute | solution.py:738
  104.4 3.7 %collective-permute-start.17 = (f32[32,128]{1,0:T(8,128)S(1)}, f32[32,128]{1,0:T(8,128)S(1)}, u32[]{:S(2)}, u32[]{:S(2)}) collective-permute-start(f32[32,128]{1,0:T(8,128)S(1)} %add_add_fusion.refs_0_), channel_id=1, source_target_pairs={{0,16},{8,24},{16,0},{24,8},{1,17},{9,25},{17,1},{25,9},{2,18},{10... | collective-permute-start | bytes 49160 | tf_op jit(solution)/shard_map/ppermute | solution.py:738
  104.5 3.7 %collective-permute-start.16 = (f32[32,128]{1,0:T(8,128)S(1)}, f32[32,128]{1,0:T(8,128)S(1)}, u32[]{:S(2)}, u32[]{:S(2)}) collective-permute-start(f32[32,128]{1,0:T(8,128)S(1)} %add_add_fusion.refs_0_), channel_id=1, source_target_pairs={{0,8},{8,0},{16,24},{24,16},{1,9},{9,1},{17,25},{25,17},{2,10},{10... | collective-permute-start | bytes 49160 | tf_op jit(solution)/shard_map/ppermute | solution.py:738

commit v4 on v3

--- a/solution.py
+++ b/solution.py
@@ -24,13 +24,12 @@
 bf16 = jnp.bfloat16
 
 
-def kernel_call(body, out_shape, scratch=(), cost=0):
+def kernel_call(body, out_shape, scratch=()):
     return pl.pallas_call(
         body,
         out_shape=out_shape,
         scratch_shapes=list(scratch),
         compiler_params=pltpu.CompilerParams(vmem_limit_bytes=VMEM_BYTES),
-        cost_estimate=pl.CostEstimate(flops=cost, bytes_accessed=1 << 20, transcendentals=0),
     )
 
 
@@ -324,58 +323,16 @@
     )(be, after)
 
 
-def cross_columns(patch, columns, sources, own_ref, unit_ref, v_ref, w_ref, sums):
-    lane = iota((patch, 128), 1)
-    down_sum, up_sum, mask = sums
-    needed = sorted({c for e in columns for c in (e - 1, e, e + 1)})
-    for c in needed:
-        ref, index = sources[c]
-        unit, column = unit_and_mask(ref[index])
-        unit_ref[c * patch : (c + 1) * patch, :] = unit
-        mask = at_lane(lane, c, column, mask)
-    for place, e in enumerate(columns):
-        around = slice((e - 1) * patch, (e + 2) * patch)
-        here = slice(e * patch, (e + 1) * patch)
-        down = affinity_of(own_ref[here, :], unit_ref[around, :])
-        up = affinity_of(unit_ref[here, :], own_ref[around, :])
-        v_ref[place] = down.astype(bf16)
-        w_ref[place] = up.astype(bf16)
-        down_sum = at_lane(lane, e, jnp.sum(down, axis=1, keepdims=True), down_sum)
-        up_sum = at_lane(lane, e, jnp.sum(up, axis=1, keepdims=True), up_sum)
-    return down_sum, up_sum, mask
-
-
-def edge_columns(n):
-    return list(range(1, GHOST + EDGE - 1)) + list(range(n - GHOST - EDGE + 1, n - 1))
-
-
-def middle_columns(n):
-    return list(range(GHOST + EDGE - 1, n - GHOST - EDGE + 1))
-
-
-def inner(columns, low, high):
-    return [e for e in columns if low <= e < high and e - 1 in columns and e + 1 in columns]
-
-
-def place_of(n):
-    edge, middle = edge_columns(n), middle_columns(n)
-    return {e: (0, i) for i, e in enumerate(edge)} | {e: (1, i) for i, e in enumerate(middle)}
-
-
-def below_sources(n, bl_ref, be_ref, bm_ref, br_ref):
-    sources = {}
-    for c in range(n):
-        if c < GHOST:
-            sources[c] = (bl_ref, c)
-        elif c < GHOST + EDGE:
-            sources[c] = (be_ref, c - GHOST)
-        elif c < n - GHOST - EDGE:
-            sources[c] = (bm_ref, c - GHOST - EDGE)
-        elif c < n - GHOST:
-            sources[c] = (be_ref, c - (n - GHOST) + 2 * EDGE)
-        else:
-            sources[c] = (br_ref, c - (n - GHOST))
-    return sources
+def stages(n):
+    middle = list(range(GHOST + EDGE, n - GHOST - EDGE))
+    ends = [c for c in range(n) if c not in middle]
+    arrived, seen, steps = set(), set(), []
+    for tiles in (ends, middle):
+        arrived |= set(tiles)
+        columns = [e for e in range(1, n - 1) if {e - 1, e, e + 1} <= arrived and e not in seen]
+        seen |= set(columns)
+        steps.append((tiles, columns))
+    return steps
 
 
 def scale_of(stat_ref, sums):
@@ -385,178 +342,189 @@
     return stat_ref[2, patch:] * lax.rsqrt(degree)
 
 
-def products(columns, where, ups, u_ref, pay_ref, first):
-    half = u_ref.shape[1] // 2
+def pair_source(e, tiles):
+    some = next(iter(tiles.values()))
+    near = [tiles.get(c, jnp.zeros_like(some)) for c in range(e - 1, e + 3)]
+    return jnp.concatenate(near, axis=0)
+
+
+def pairs_of(columns):
+    return sorted({e - (e + 1) % 2 for e in columns})
+
+
+def pair_products(columns, block_ref, tiles):
+    results = {}
+    for e in pairs_of(columns):
+        product = jnp.dot(block_ref[e // 2], pair_source(e, tiles), preferred_element_type=f32)
+        patch = product.shape[0] // 2
+        results[e], results[e + 1] = product[:patch], product[patch:]
+    return results
+
+
+def products(columns, up_ref, tiles, pay_ref, first):
+    half = up_ref.shape[1] // 4
+    results = pair_products(columns, up_ref, tiles)
     for e in columns:
-        which, i = where[e]
-        source = u_ref[e - 1 : e + 2].reshape(3 * u_ref.shape[1], RANK)
-        product = jnp.dot(ups[which][i], source, preferred_element_type=f32)
-        pay_ref[(e - first) * half : (e - first + 1) * half, :] = packed(product).astype(bf16)
-
-
-def edge_kernel(n, bl_ref, be_ref, br_ref, u1_ref, stat_ref, pl_ref, p_ref, pr_ref, v_ref, w_ref, sum_ref, u0_ref, pay_ref, unit_ref):
-    patch = be_ref.shape[1]
-    sources = below_sources(n, bl_ref, be_ref, None, br_ref)
-    columns = edge_columns(n)
-    empty = jnp.zeros((patch, 128), f32)
-    sums = cross_columns(patch, columns, sources, u1_ref, unit_ref, v_ref, w_ref, (empty, empty, empty))
-    for i in range(3):
-        sum_ref[i] = sums[i]
+        pay_ref[(e - first) * half : (e - first + 1) * half, :] = packed(results[e]).astype(bf16)
+
+
+def cross_kernel(n, stage, *refs):
+    steps = stages(n)
+    tiles, columns = steps[stage]
+    count = 3 if stage == 0 else 1
+    pieces, (own_ref, stat_ref, pl_ref, p_ref, pr_ref) = refs[:count], refs[count : count + 5]
+    refs = refs[count + 5 :]
+    patch = pieces[0].shape[1]
+    lane = iota((patch, 128), 1)
+    if stage == 0:
+        v_ref, w_ref, sum_ref, u0_ref, pay_ref, unit_ref = refs
+        empty = jnp.zeros((patch, 128), f32)
+        down_sum, up_sum, mask = empty, empty, empty
+    else:
+        before, (v_ref, w_ref, sum_ref, u0_ref, pay_ref, unit_ref) = refs[:6], refs[6:12]
+        down_sum, up_sum, mask = (before[2][i] for i in range(3))
+    sources = [(ref, i) for ref in pieces for i in range(ref.shape[0])]
+    for c, (ref, i) in zip(tiles, sources):
+        unit, column = unit_and_mask(ref[i])
+        unit_ref[c * patch : (c + 1) * patch, :] = unit
+        mask = at_lane(lane, c, column, mask)
+    shape = (2 * patch, 4 * patch)
+    apart = iota(shape, 1) // patch - iota(shape, 0) // patch
+    beside = (apart >= 0) & (apart <= 2)
+    for e in pairs_of(columns):
+        around = slice((e - 1) * patch, (e + 3) * patch)
+        here = slice(e * patch, (e + 2) * patch)
+        down = jnp.where(beside, affinity_of(own_ref[here, :], unit_ref[around, :]), 0.0)
+        up = jnp.where(beside, affinity_of(unit_ref[here, :], own_ref[around, :]), 0.0)
+        v_ref[e // 2] = down.astype(bf16)
+        w_ref[e // 2] = up.astype(bf16)
+        down = jnp.sum(down, axis=1, keepdims=True)
+        up = jnp.sum(up, axis=1, keepdims=True)
+        for i in range(2):
+            span = slice(i * patch, (i + 1) * patch)
+            down_sum = at_lane(lane, e + i, down[span], down_sum)
+            up_sum = at_lane(lane, e + i, up[span], up_sum)
+    sums = (down_sum, up_sum, mask)
     scale = scale_of(stat_ref, sums)
     for e in columns:
         u0_ref[e] = (scale[:, e : e + 1] * panel_at((pl_ref, p_ref, pr_ref), 1, e)).astype(bf16)
-    products(inner(columns, 2, n - 2), place_of(n), (w_ref, None), u0_ref, pay_ref, 2)
-
-
-def edge_affinity(bl, be, br, u1, stat, panel):
-    _, patch, width = be.shape
+    inner, known = [], []
+    for last in (stage - 1, stage):
+        known = [e for _, reached in steps[: last + 1] for e in reached]
+        inner.append({e for e in range(2, n - 2) if {e - 1, e, e + 1} <= set(known)})
+    fresh = sorted(inner[1] - inner[0])
+    near = {c for e in fresh for c in (e - 1, e, e + 1)}
+    products(fresh, w_ref, {e: u0_ref[e] for e in near}, pay_ref, 2)
+    if stage < len(steps) - 1:
+        for i in range(3):
+            sum_ref[i] = sums[i]
+        return
+    shared = up_sum - FLOOR * absent_near(stat_ref[2, patch:], 3 * patch)
+    sum_ref[0], sum_ref[1], sum_ref[2] = shared, mask, scale
+    tail = (n - 4) * patch // 2
+    pay_ref[tail : tail + patch, :], pay_ref[tail + patch :, :] = pair_of(shared)
+
+
+def cross_affinity(stage, pieces, u1, stat, panel, before=()):
+    patch, width = pieces[0].shape[1:]
     n = u1.shape[0] // patch
-    count = len(edge_columns(n))
-    return kernel_call(
-        functools.partial(edge_kernel, n),
-        (
-            sds((count, patch, 3 * patch), bf16),
-            sds((count, patch, 3 * patch), bf16),
+    given = len(pieces) + 5
+    return pl.pallas_call(
+        functools.partial(cross_kernel, n, stage),
+        out_shape=(
+            sds((n // 2 - 1, 2 * patch, 4 * patch), bf16),
+            sds((n // 2 - 1, 2 * patch, 4 * patch), bf16),
             sds((3, patch, 128), f32),
             sds((n, patch, RANK), bf16),
-            sds(((n - 4) * patch // 2, 2 * RANK), bf16),
+            sds((payload_rows(n - 4, patch), 2 * RANK), bf16),
+            sds((n * patch, width), bf16),
         ),
-        [pltpu.VMEM((n * patch, width), bf16)],
-        cost=4 * count * patch * 3 * patch * width,
-    )(bl, be, br, u1, stat, *panel)
-
-
-def middle_kernel(
-    n,
-    be_ref, bm_ref, u1_ref, stat_ref, pl_ref, p_ref, pr_ref, sa_ref, ua_ref, wa_ref, paya_ref,
-    v_ref, w_ref, sum_ref, u0_ref, t_ref, pay_ref,
-    unit_ref,
-):
-    patch = be_ref.shape[1]
-    half = patch // 2
-    sources = below_sources(n, None, be_ref, bm_ref, None)
-    columns = middle_columns(n)
-    before = tuple(sa_ref[i] for i in range(3))
-    sums = cross_columns(patch, columns, sources, u1_ref, unit_ref, v_ref, w_ref, before)
-    scale = scale_of(stat_ref, sums)
-    t_ref[...] = scale
-    shared = sums[1] - FLOOR * absent_near(stat_ref[2, patch:], 3 * patch)
-    sum_ref[0] = shared
-    sum_ref[1] = sums[2]
-    edges = edge_columns(n)
-    for e in edges:
-        u0_ref[e] = ua_ref[e]
-    for e in columns:
-        u0_ref[e] = (scale[:, e : e + 1] * panel_at((pl_ref, p_ref, pr_ref), 1, e)).astype(bf16)
-    done = inner(edges, 2, n - 2)
-    for e in done:
-        pay_ref[(e - 2) * half : (e - 1) * half, :] = paya_ref[(e - 2) * half : (e - 1) * half, :]
-    products([e for e in range(2, n - 2) if e not in done], place_of(n), (wa_ref, w_ref), u0_ref, pay_ref, 2)
-    tail = (n - 4) * half
-    pay_ref[tail : tail + patch, :], pay_ref[tail + patch :, :] = pair_of(shared)
-
-
-def middle_affinity(be, bm, u1, stat, panel, sa, ua, wa, paya):
-    _, patch, width = be.shape
-    n = u1.shape[0] // patch
-    count = len(middle_columns(n))
-    return kernel_call(
-        functools.partial(middle_kernel, n),
-        (
-            sds((count, patch, 3 * patch), bf16),
-            sds((count, patch, 3 * patch), bf16),
-            sds((2, patch, 128), f32),
-            sds((n, patch, RANK), bf16),
-            sds((patch, 128), f32),
-            sds((payload_rows(n - 4, patch), 2 * RANK), bf16),
-        ),
-        [pltpu.VMEM((n * patch, width), bf16)],
-        cost=4 * count * patch * 3 * patch * width,
-    )(be, bm, u1, stat, *panel, sa, ua, wa, paya)
-
-
-def before_first_kernel(n, got_ref, sum_ref, u0_ref, m_ref, va_ref, vb_ref, z_ref, u2_ref):
+        input_output_aliases={given + i: i for i in range(len(before))},
+        compiler_params=pltpu.CompilerParams(vmem_limit_bytes=VMEM_BYTES),
+    )(*pieces, u1, stat, *panel, *before)
+
+
+def before_first_kernel(n, got_ref, sum_ref, stat_ref, u0_ref, m_ref, v_ref, z_ref, t_ref, gain_ref, own_ref, u2_ref):
     patch = u0_ref.shape[1]
     half = patch // 2
-    both = 2 * patch
-    where = place_of(n)
     tail = (n - 2) * half
     partial = got_ref[tail : tail + patch, :].astype(f32) + got_ref[tail + patch :, :].astype(f32)
-    scale = sum_ref[1] * lax.rsqrt(1.0 + partial + sum_ref[0])
+    below_scale = sum_ref[1] * lax.rsqrt(1.0 + partial + sum_ref[0])
+    scale = sum_ref[2]
+    gain = 1.0 + scale * scale * stat_ref[1, patch:]
+    upper = stat_ref[1, :patch]
     for e in range(1, n - 1):
         theirs = unpacked(got_ref[(e - 1) * half : e * half, :].astype(f32))
-        u2_ref[e] = (scale[:, e : e + 1] * theirs).astype(bf16)
+        u2_ref[e] = (below_scale[:, e : e + 1] * theirs).astype(bf16)
+    lower = pair_products(range(2, n - 2), v_ref, {e: u2_ref[e] for e in range(1, n - 1)})
     for e in range(2, n - 2):
-        which, i = where[e]
         own = u0_ref[e - 1 : e + 2].reshape(3 * patch, RANK)
         total = jnp.dot(m_ref[e, :, 3 * patch :], own, preferred_element_type=f32)
-        below = u2_ref[e - 1 : e + 2].reshape(3 * patch, RANK)
-        lower = jnp.dot((va_ref, vb_ref)[which][i], below, preferred_element_type=f32)
         z_ref[e, :patch] = total[:patch]
-        z_ref[e, patch:] = total[patch:] + lower
-
-
-def before_first(got, sums, u0, m, va, vb):
+        z_ref[e, patch:] = total[patch:] + lower[e]
+        for ref, table in ((t_ref, scale), (gain_ref, gain), (own_ref, upper)):
+            ref[e] = jnp.broadcast_to(table[:, e : e + 1], (patch, RANK))
+
+
+def before_first(got, sums, stat, u0, m, v):
     n, patch, _ = u0.shape
+    spread = sds((n, patch, RANK), f32)
     return kernel_call(
         functools.partial(before_first_kernel, n),
-        sds((n, 2 * patch, RANK), f32),
+        (sds((n, 2 * patch, RANK), f32), spread, spread, spread),
         [pltpu.VMEM((n, patch, RANK), bf16)],
-        cost=2 * n * 2 * patch * 3 * patch * RANK,
-    )(got, sums, u0, m, va, vb)
+    )(got, sums, stat, u0, m, v)
 
 
 def first_kernel(
     n,
-    got_ref, stat_ref, t_ref, z_ref, pl_ref, p_ref, pr_ref, m_ref, wa_ref, wb_ref,
-    y_ref, u_ref, tt_ref, up_ref, down_ref,
+    got_ref, stat_ref, t1_ref, gain1_ref, own_ref, z_ref, pl_ref, p_ref, pr_ref, m_ref, w_ref,
+    y_ref, u_ref, t0_ref, gain0_ref, up_ref, down_ref,
     start_ref,
 ):
     panel = (pl_ref, p_ref, pr_ref)
-    patch = t_ref.shape[0]
+    patch = t1_ref.shape[1]
     half = patch // 2
     tail = (n - 4) * half
     partial = got_ref[tail : tail + patch, :].astype(f32) + got_ref[tail + patch :, :].astype(f32)
-    upper_scale = stat_ref[2, :patch] * lax.rsqrt(1.0 + stat_ref[0, :patch] + partial)
-    scale = jnp.concatenate([upper_scale, t_ref[...]], axis=0)
-    gain = 1.0 + scale * scale * stat_ref[1]
-    tt_ref[0] = scale
-    tt_ref[1] = gain
+    scale = stat_ref[2, :patch] * lax.rsqrt(1.0 + stat_ref[0, :patch] + partial)
     for e in range(1, n - 1):
-        start_ref[e] = (upper_scale[:, e : e + 1] * panel_at(panel, 0, e)).astype(bf16)
+        t = jnp.broadcast_to(scale[:, e : e + 1], (patch, RANK))
+        t0_ref[e] = t
+        start_ref[e] = (t * panel_at(panel, 0, e)).astype(bf16)
     for e in range(2, n - 2):
         own = start_ref[e - 1 : e + 2].reshape(3 * patch, RANK)
         total = z_ref[e] + jnp.dot(m_ref[e, :, : 3 * patch], own, preferred_element_type=f32)
-        upper = unpacked(got_ref[(e - 2) * half : (e - 1) * half, :].astype(f32))
-        for row in range(2):
-            span = slice(row * patch, (row + 1) * patch)
-            piece = total[span] + upper if row == 0 else total[span]
-            t = scale[span, e : e + 1]
-            image = panel_at(panel, row, e) * gain[span, e : e + 1] + t * piece
+        upper = total[:patch] + unpacked(got_ref[(e - 2) * half : (e - 1) * half, :].astype(f32))
+        gain = 1.0 + t0_ref[e] * t0_ref[e] * own_ref[e]
+        gain0_ref[e] = gain
+        for row, piece, t, g in ((0, upper, t0_ref[e], gain), (1, total[patch:], t1_ref[e], gain1_ref[e])):
+            image = panel_at(panel, row, e) * g + t * piece
             y_ref[row, e] = image
             scaled = t * image
             u_ref[row, e] = scaled.astype(bf16)
             if row == 0:
                 up_ref[(e - 2) * half : (e - 1) * half, :] = packed(scaled).astype(bf16)
-    products(range(3, n - 3), place_of(n), (wa_ref, wb_ref), u_ref.at[1], down_ref, 3)
-
-
-def first_iteration(got, stat, t, z, panel, m, wa, wb):
+    products(range(3, n - 3), w_ref, {e: u_ref[1, e] for e in range(2, n - 2)}, down_ref, 3)
+
+
+def first_iteration(got, stat, t1, gain1, own, z, panel, m, w):
     n, both, _ = z.shape
     patch = both // 2
     half = patch // 2
+    spread = sds((n, patch, RANK), f32)
     return kernel_call(
         functools.partial(first_kernel, n),
         (
             sds((2, n, patch, RANK), f32),
             sds((2, n, patch, RANK), bf16),
-            sds((2, both, 128), f32),
+            spread,
+            spread,
             sds(((n - 4) * half, 2 * RANK), bf16),
             sds(((n - 6) * half, 2 * RANK), bf16),
         ),
         [pltpu.VMEM((n, patch, RANK), bf16)],
-        cost=2 * n * both * 3 * patch * RANK,
-    )(got, stat, t, z, *panel, m, wa, wb)
+    )(got, stat, t1, gain1, own, z, *panel, m, w)
 
 
 def local_kernel(low, high, m_ref, u_ref, z_ref):
@@ -572,22 +540,15 @@
     return kernel_call(
         functools.partial(local_kernel, low, high),
         sds((n, both, RANK), f32),
-        cost=2 * n * both * 3 * both * RANK,
     )(m, u)
 
 
-def joined(e, low, where, downs, near, z_ref, above_ref, y_ref, scale, gain):
+def joined(e, low, lower, z_ref, above_ref, y_ref, scales, gains):
     patch = y_ref.shape[2]
     half = patch // 2
-    which, i = where[e]
-    below = jnp.concatenate([near[e - 1], near[e], near[e + 1]], axis=0)
-    lower = z_ref[e, patch:] + jnp.dot(downs[which][i], below, preferred_element_type=f32)
-    upper = z_ref[e, :patch] + unpacked(above_ref[(e - low) * half : (e - low + 1) * half, :].astype(f32))
-    images = []
-    for row, piece in ((0, upper), (1, lower)):
-        span = slice(row * patch, (row + 1) * patch)
-        images.append(y_ref[row, e] * gain[span, e : e + 1] + scale[span, e : e + 1] * piece)
-    return images
+    upper = unpacked(above_ref[(e - low) * half : (e - low + 1) * half, :].astype(f32))
+    pieces = (z_ref[e, :patch] + upper, z_ref[e, patch:] + lower[e])
+    return [y_ref[row, e] * gains[row][e] + scales[row][e] * pieces[row] for row in range(2)]
 
 
 def halo(n, low, half, below_ref):
@@ -598,26 +559,27 @@
 
 def middle_step_kernel(
     n, low,
-    below_ref, above_ref, z_ref, y_ref, tt_ref, va_ref, wa_ref, vb_ref, wb_ref,
+    below_ref, above_ref, z_ref, y_ref, t0_ref, t1_ref, gain0_ref, gain1_ref, v_ref, w_ref,
     new_ref, u_ref, up_ref, down_ref,
 ):
     patch = y_ref.shape[2]
     half = patch // 2
-    where = place_of(n)
-    scale, gain = tt_ref[0], tt_ref[1]
-    near = halo(n, low, half, below_ref)
+    scales, gains = (t0_ref, t1_ref), (gain0_ref, gain1_ref)
+    lower = pair_products(range(low, n - low), v_ref, halo(n, low, half, below_ref))
     for e in range(low, n - low):
-        images = joined(e, low, where, (va_ref, vb_ref), near, z_ref, above_ref, y_ref, scale, gain)
+        images = joined(e, low, lower, z_ref, above_ref, y_ref, scales, gains)
         for row in range(2):
             new_ref[row, e] = images[row]
-            scaled = scale[row * patch : (row + 1) * patch, e : e + 1] * images[row]
+            scaled = scales[row][e] * images[row]
             u_ref[row, e] = scaled.astype(bf16)
             if row == 0:
                 up_ref[(e - low) * half : (e - low + 1) * half, :] = packed(scaled).astype(bf16)
-    products(range(low + 1, n - low - 1), where, (wa_ref, wb_ref), u_ref.at[1], down_ref, low + 1)
-
-
-def middle_step(low, below, above, z, y, tt, va, wa, vb, wb):
+    products(
+        range(low + 1, n - low - 1), w_ref, {e: u_ref[1, e] for e in range(low, n - low)}, down_ref, low + 1
+    )
+
+
+def middle_step(low, below, above, z, y, spread, v, w):
     _, n, patch, _ = y.shape
     half = patch // 2
     return kernel_call(
@@ -628,18 +590,20 @@
             sds(((n - 2 * low) * half, 2 * RANK), bf16),
             sds(((n - 2 * low - 2) * half, 2 * RANK), bf16),
         ),
-        cost=8 * n * patch * patch * RANK,
-    )(below, above, z, y, tt, va, wa, vb, wb)
-
-
-def last_step_kernel(n, low, below_ref, above_ref, z_ref, y_ref, tt_ref, va_ref, vb_ref, new_ref, gram_ref, side_ref):
+    )(below, above, z, y, *spread, v, w)
+
+
+def last_step_kernel(
+    n, low,
+    below_ref, above_ref, z_ref, y_ref, t0_ref, t1_ref, gain0_ref, gain1_ref, v_ref,
+    new_ref, gram_ref, side_ref,
+):
     patch = y_ref.shape[2]
-    where = place_of(n)
-    scale, gain = tt_ref[0], tt_ref[1]
-    near = halo(n, low, patch // 2, below_ref)
+    scales, gains = (t0_ref, t1_ref), (gain0_ref, gain1_ref)
+    lower = pair_products(range(low, n - low), v_ref, halo(n, low, patch // 2, below_ref))
     wide = 2 * RANK
     for e in range(low, n - low):
-        images = joined(e, low, where, (va_ref, vb_ref), near, z_ref, above_ref, y_ref, scale, gain)
+        images = joined(e, low, lower, z_ref, above_ref, y_ref, scales, gains)
         for row in range(2):
             new_ref[row, e - low] = images[row]
         span = slice((e - low) * patch, (e - low + 1) * patch)
@@ -651,20 +615,19 @@
     gram_ref[...] = packed(gram[:RANK, :RANK] + gram[RANK:, RANK:])
 
 
-def last_step(low, below, above, z, y, tt, va, vb):
+def last_step(low, below, above, z, y, spread, v):
     _, n, patch, _ = y.shape
     cols = n - 2 * low
     return kernel_call(
         functools.partial(last_step_kernel, n, low),
         (sds((2, cols, patch, RANK), f32), sds((RANK // 2, 2 * RANK), f32)),
         [pltpu.VMEM((cols * patch, 4 * RANK), bf16)],
-        cost=8 * n * patch * patch * RANK,
-    )(below, above, z, y, tt, va, vb)
+    )(below, above, z, y, *spread, v)
 
 
 def inverse_factor(gram):
     size = gram.shape[0]
-    step = 4
+    step = 8
     row = iota((size, 2 * size), 0)
     lane = iota((size, 2 * size), 1)
     table = jnp.concatenate([gram, identity(size).astype(f32)], axis=1)
@@ -709,7 +672,6 @@
     return kernel_call(
         functools.partial(finish_kernel, factor, len(parts)),
         sds(y.shape, f32),
-        cost=2 * y.shape[0] * y.shape[1] * RANK,
     )(*parts, y)
 
 
@@ -767,18 +729,19 @@
     panel = (sides[0], own_panel, sides[1])
     below_left, below_right = passed_along(below_right, "col", 1), passed_along(below_left, "col", -1)
     got_below = passed_along(payload, "row", -1)
-    va, wa, sa, ua, paya = edge_affinity(below_left, below_edges, below_right, u1, stat, panel)
-    vb, wb, sums, u0, t, payload = middle_affinity(below_edges, below_middle, u1, stat, panel, sa, ua, wa, paya)
+    n = tile_cols + 2 * GHOST
+    cross = cross_affinity(0, (below_left, below_edges, below_right), u1, stat, panel)
+    v, w, sums, u0, payload, _ = cross_affinity(1, (below_middle,), u1, stat, panel, cross)
     got_above = passed_along(payload, "row", 1)
-    z = before_first(got_below, sums, u0, m, va, vb)
-    y, u, tt, up, down = first_iteration(got_above, stat, t, z, panel, m, wa, wb)
+    z, t1, gain1, own = before_first(got_below, sums, stat, u0, m, v)
+    y, u, t0, gain0, up, down = first_iteration(got_above, stat, t1, gain1, own, z, panel, m, w)
+    spread = (t0, t1, gain0, gain1)
     below, above = passed_along(up, "row", -1), passed_along(down, "row", 1)
-    n = tile_cols + 2 * GHOST
     z = local_products(3, n - 3, m, u)
-    y, u, up, down = middle_step(3, below, above, z, y, tt, va, wa, vb, wb)
+    y, u, up, down = middle_step(3, below, above, z, y, spread, v, w)
     below, above = passed_along(up, "row", -1), passed_along(down, "row", 1)
     z = local_products(4, n - 4, m, u)
-    y, gram = last_step(4, below, above, z, y, tt, va, vb)
+    y, gram = last_step(4, below, above, z, y, spread, v)
 
     parts = summed_parts(gram)
     flat = y.reshape(tile_rows * tile_cols, patches * RANK)

time: 112 us -> 107 us (0.955)
  Pallas kernels: 35.7 us -> 30.4 us
    pallas_call x1, Pallas kernels: 2.61 us -> 1.03 us  [first_iteration(): kernel_call(functools.partial(first_kernel, n), (sds((2, n, patch, RANK),...]
    pallas_call x3, Pallas kernels: 8.17 us -> 6.96 us  [the longest x2 5.55 us: cross_affinity(): pl.pallas_call(functools.partial(cross_kernel, n, stage), out_shape=(sds(...]
where the time goes in v4:
time: 107 us
  starting transfers between devices  39.3 us (37%)
  waiting for transfers between devices  35.1 us (33%)
  Pallas kernels  30.4 us (28%)
  local copies, waits for them, and re-layouts  1.82 us (2%)
    ppermute x12, starting transfers between devices, passed_along(): return lax.ppermute(shard, axis, pairs)  28.1 us
    ppermute x12, waiting for transfers between devices, passed_along(): return lax.ppermute(shard, axis, pairs)  27.6 us
    ppermute x7, starting transfers between devices, summed_parts(): lax.ppermute(gram, axis, [(i, i ^ p) for i in range(size)])  11.2 us
    ppermute x7, waiting for transfers between devices, summed_parts(): lax.ppermute(gram, axis, [(i, i ^ p) for i in range(size)])  7.49 us
    pallas_call x2, Pallas kernels, cross_affinity(): pl.pallas_call(functools.partial(cross_kernel, n, stage), out_shape=(sds(...  5.55 us
    pallas_call x1, Pallas kernels, own_units(): pl.pallas_call(functools.partial(units_kernel, n), in_specs=[HBM_SPEC, VM...  5.44 us
    pallas_call x1, Pallas kernels, inside_affinity(): pl.pallas_call(functools.partial(inside_kernel, n), out_shape=(sds((n, bo...  3.49 us
    pallas_call x1, Pallas kernels, mark_rest(): pl.pallas_call(mark_rest_kernel, in_specs=[HBM_SPEC, VMEM_SPEC, VMEM_SPEC...  3.13 us
  transfers between devices with their start and end apart: 19, of which 12 were waited for; matrix products, arithmetic and copies ran while one was open for 2% of the time, Pallas kernels for 21%

profile of v4, /device:TPU:0, one launch (start us, length us, event | category | flops | bytes accessed | tf_op | source)
XLA Modules:
  0.0 106.9 jit_solution(2591625383204254749)
XLA Ops:
  0.0 0.0 copy-start
  0.0 1.7 %shard_map.37.after_ref = bf16[8,64,1024]{2,1,0:T(8,128)(2,1)S(1)} custom-call(bf16[2,16,64,1024]{3,2,1,0:T(8,128)(2,1)} %x_ref.5, s32[2,16,64]{2,1,0:T(8,128)} %tissue_ref.7), custom_call_target="tpu_custom_call" | custom-call | tf_op jit(solution)/shard_map/pallas_call | solution.py:133
  1.7 1.3 %collective-permute-start.3 = (bf16[8,64,1024]{2,1,0:T(8,128)(2,1)S(1)}, bf16[8,64,1024]{2,1,0:T(8,128)(2,1)S(1)}, u32[]{:S(2)}, u32[]{:S(2)}) collective-permute-start(bf16[8,64,1024]{2,1,0:T(8,128)(2,1)S(1)} %shard_map.37.after_ref), channel_id=1, source_target_pairs={{8,0},{16,8},{24,16},{9,1},{17,9},{25,17},{10,2},{18,10},{26,18},{... | collective-permute-start | bytes 3145736 | tf_op jit(solution)/shard_map/ppermute | solution.py:712
  3.0 1.5 %reshape.9.probe_ref.p_ref.refs_6_.refs_4_ = f32[2,16,64,64]{3,2,1,0:T(8,128)S(1)} reshape(f32[2,16,4096]{2,1,0:T(8,128)} %param.5) | data formatting | bytes 1048576 | tf_op jit(solution)/shard_map/reshape | solution.py:719
  4.4 0.0 copy-done
  4.5 3.1 %shard_map.38 = (bf16[2,4,64,1152]{3,2,1,0:T(8,128)(2,1)S(1)}, bf16[2,4,64,1152]{3,2,1,0:T(8,128)(2,1)S(1)}, bf16[8,64,1024]{2,1,0:T(8,128)(2,1)S(1)}) custom-call(bf16[2,16,64,1024]{3,2,1,0:T(8,128)(2,1)} %x_ref.5, s32[2,16,64]{2,1,0:T(8,128)S(1)} %copy-done, f32[2,16,64,64]{3,2,1,0:T(8,128)S(1)} %reshape.9.probe_ref.p_ref.refs_6_.refs_4_, ...), custom_call_target="tpu_custom_call" | custom-call | tf_op jit(solution)/shard_map/pallas_call | solution.py:168
  7.6 2.4 %collective-permute-start.1 = (bf16[2,4,64,1152]{3,2,1,0:T(8,128)(2,1)S(1)}, bf16[2,4,64,1152]{3,2,1,0:T(8,128)(2,1)S(1)}, u32[]{:S(2)}, u32[]{:S(2)}) collective-permute-start(bf16[2,4,64,1152]{3,2,1,0:T(8,128)(2,1)S(1)} %get-tuple-element.53), channel_id=1, source_target_pairs={{0,1},{1,2},{2,3},{3,4},{4,5},{5,6},{6,7},{8,9},{9,10},{10,11},{11... | collective-permute-start | bytes 3538952 | tf_op jit(solution)/shard_map/ppermute | solution.py:712
  10.0 1.3 %collective-permute-start.2 = (bf16[2,4,64,1152]{3,2,1,0:T(8,128)(2,1)S(1)}, bf16[2,4,64,1152]{3,2,1,0:T(8,128)(2,1)S(1)}, u32[]{:S(2)}, u32[]{:S(2)}) collective-permute-start(bf16[2,4,64,1152]{3,2,1,0:T(8,128)(2,1)S(1)} %get-tuple-element.48.after_ref), channel_id=1, source_target_pairs={{1,0},{2,1},{3,2},{4,3},{5,4},{6,5},{7,6},{9,8},{10,9},{11,10},{12... | collective-permute-start | bytes 3538952 | tf_op jit(solution)/shard_map/ppermute | solution.py:712
  11.3 1.3 %collective-permute-start = (bf16[8,64,1024]{2,1,0:T(8,128)(2,1)S(1)}, bf16[8,64,1024]{2,1,0:T(8,128)(2,1)S(1)}, u32[]{:S(2)}, u32[]{:S(2)}) collective-permute-start(bf16[8,64,1024]{2,1,0:T(8,128)(2,1)S(1)} %get-tuple-element.47), channel_id=1, source_target_pairs={{8,0},{16,8},{24,16},{9,1},{17,9},{25,17},{10,2},{18,10},{26,18},{... | collective-permute-start | bytes 3145736 | tf_op jit(solution)/shard_map/ppermute | solution.py:712
  12.6 5.4 %shard_map.39 = (bf16[1536,1024]{1,0:T(8,128)(2,1)S(1)}, bf16[1536,1024]{1,0:T(8,128)(2,1)S(1)}) custom-call(bf16[2,16,64,1024]{3,2,1,0:T(8,128)(2,1)} %x_ref.5, s32[2,16,64]{2,1,0:T(8,128)S(1)} %copy-done, bf16[2,4,64,1152]{3,2,1,0:T(8,128)(2,1)S(1)} %get-tuple-element.48.after_ref), custom_call_target="tpu_custom_call" | custom-call | tf_op jit(solution)/shard_map/pallas_call | solution.py:194
  18.1 3.5 %shard_map.40 = (bf16[24,128,384]{2,1,0:T(8,128)(2,1)S(1)}, f32[2,128,128]{2,1,0:T(8,128)S(1)}) custom-call(bf16[1536,1024]{1,0:T(8,128)(2,1)S(1)} %get-tuple-element.49.unit0_ref.start0_ref, bf16[1536,1024]{1,0:T(8,128)(2,1)S(1)} %get-tuple-element.50.unit1_ref.start1_ref), custom_call_target="tpu_custom_call" | custom-call | tf_op jit(solution)/shard_map/pallas_call | solution.py:241
  21.6 8.9 %collective-permute-done.3.be_ref.refs_1_ = bf16[8,64,1024]{2,1,0:T(8,128)(2,1)S(1)} collective-permute-done((bf16[8,64,1024]{2,1,0:T(8,128)(2,1)S(1)}, bf16[8,64,1024]{2,1,0:T(8,128)(2,1)S(1)}, u32[]{:S(2)}, u32[]{:S(2)}) %collective-permute-start.3) | collective-permute-done | bytes 1048608 | tf_op jit(solution)/shard_map/ppermute | solution.py:712
  30.5 0.1 shard_map.41
  30.6 1.3 %collective-permute-start.4 = (bf16[4,64,1024]{2,1,0:T(8,128)(2,1)S(1)}, bf16[4,64,1024]{2,1,0:T(8,128)(2,1)S(1)}, u32[]{:S(2)}, u32[]{:S(2)}) collective-permute-start(bf16[4,64,1024]{2,1,0:T(8,128)(2,1)S(1)} %get-tuple-element.59), channel_id=1, source_target_pairs={{0,1},{1,2},{2,3},{3,4},{4,5},{5,6},{6,7},{8,9},{9,10},{10,11},{11... | collective-permute-start | bytes 1572872 | tf_op jit(solution)/shard_map/ppermute | solution.py:712
  31.9 1.3 %collective-permute-start.5 = (bf16[4,64,1024]{2,1,0:T(8,128)(2,1)S(1)}, bf16[4,64,1024]{2,1,0:T(8,128)(2,1)S(1)}, u32[]{:S(2)}, u32[]{:S(2)}) collective-permute-start(bf16[4,64,1024]{2,1,0:T(8,128)(2,1)S(1)} %get-tuple-element.54.after_ref), channel_id=1, source_target_pairs={{1,0},{2,1},{3,2},{4,3},{5,4},{6,5},{7,6},{9,8},{10,9},{11,10},{12... | collective-permute-start | bytes 1572872 | tf_op jit(solution)/shard_map/ppermute | solution.py:712
  33.2 0.0 collective-permute-done.1.xl_ref
  33.2 0.0 collective-permute-done.2.xr_ref
  33.2 2.4 %shard_map.42 = (bf16[1536,1024]{1,0:T(8,128)(2,1)S(1)}, bf16[1536,1024]{1,0:T(8,128)(2,1)S(1)}, bf16[24,128,384]{2,1,0:T(8,128)(2,1)S(1)}, f32[3,128,128]{2,1,0...) custom-call(bf16[1536,1024]{1,0:T(8,128)(2,1)S(1)} %get-tuple-elemen, ...), custom_call_target="tpu_custom_call", output_to_operand_aliasing={{0}: (0, {}), {1}: (1, {}), {2}: (2, {})} | custom-call | tf_op jit(solution)/shard_map/pallas_call | solution.py:299
  35.7 1.5 %collective-permute-start.7 = (bf16[832,128]{1,0:T(8,128)(2,1)S(1)}, bf16[832,128]{1,0:T(8,128)(2,1)S(1)}, u32[]{:S(2)}, u32[]{:S(2)}) collective-permute-start(bf16[832,128]{1,0:T(8,128)(2,1)S(1)} %get-tuple-element.67), channel_id=1, source_target_pairs={{8,0},{16,8},{24,16},{9,1},{17,9},{25,17},{10,2},{18,10},{26,18},{... | collective-permute-start | bytes 638984 | tf_op jit(solution)/shard_map/ppermute | solution.py:712
  37.2 0.0 collective-permute-done.4.refs_0_
  37.2 0.9 collective-permute-done.5.refs_2_
  38.1 3.0 %shard_map.43 = (bf16[11,128,256]{2,1,0:T(8,128)(2,1)S(1)}, bf16[11,128,256]{2,1,0:T(8,128)(2,1)S(1)}, f32[3,64,128]{2,1,0:T(8,128)S(1)}, bf16[24,64,64]{2,1,0:T...) custom-call(bf16[4,64,1024]{2,1,0:T(8,128)(2,1)S(1)} %collective-permute-done.4.refs_0_, ...), custom_call_target="tpu_custom_call" | custom-call | tf_op jit(solution)/shard_map/pallas_call | solution.py:432
  41.1 11.9 %collective-permute-done.refs_0_ = bf16[8,64,1024]{2,1,0:T(8,128)(2,1)S(1)} collective-permute-done((bf16[8,64,1024]{2,1,0:T(8,128)(2,1)S(1)}, bf16[8,64,1024]{2,1,0:T(8,128)(2,1)S(1)}, u32[]{:S(2)}, u32[]{:S(2)}) %collective-permute-start) | collective-permute-done | bytes 1048608 | tf_op jit(solution)/shard_map/ppermute | solution.py:712
  53.0 2.5 %shard_map.44 = (bf16[11,128,256]{2,1,0:T(8,128)(2,1)S(1)}, bf16[11,128,256]{2,1,0:T(8,128)(2,1)S(1)}, f32[3,64,128]{2,1,0:T(8,128)S(1)}, bf16[24,64,64]{2,1,0:T...) custom-call(bf16[8,64,1024]{2,1,0:T(8,128)(2,1)S(1)} %collective-per, ...), custom_call_target="tpu_custom_call", output_to_operand_aliasing={{0}: (6, {}), {1}: (7, {}), {2}: (8, {}), {3}: (9, {}), {4}... | custom-call | tf_op jit(solution)/shard_map/pallas_call | solution.py:432
  55.5 4.9 %collective-permute-start.6 = (bf16[768,128]{1,0:T(8,128)(2,1)S(1)}, bf16[768,128]{1,0:T(8,128)(2,1)S(1)}, u32[]{:S(2)}, u32[]{:S(2)}) collective-permute-start(bf16[768,128]{1,0:T(8,128)(2,1)S(1)} %get-tuple-element.66), channel_id=1, source_target_pairs={{0,8},{8,16},{16,24},{1,9},{9,17},{17,25},{2,10},{10,18},{18,26},{... | collective-permute-start | bytes 589832 | tf_op jit(solution)/shard_map/ppermute | solution.py:712
  60.4 0.0 collective-permute-done.7.got_ref
  60.4 1.4 %shard_map.45 = (f32[24,128,64]{2,1,0:T(8,128)S(1)}, f32[24,64,64]{2,1,0:T(8,128)S(1)}, f32[24,64,64]{2,1,0:T(8,128)S(1)}, f32[24,64,64]{2,1,0:T(8,128)S(1)}) custom-call(bf16[832,128]{1,0:T(8,128)(2,1)S(1)} %collective-permute-done.7.got_ref, f32[3,64,128]{2,1,0:T(8,128)S(1)} %get-tuple-element.68.sum_ref, ...), custom_call_target="tpu_custom_call" | custom-call | tf_op jit(solution)/shard_map/pallas_call | solution.py:472
  61.8 1.7 %collective-permute-done.6.got_ref = bf16[768,128]{1,0:T(8,128)(2,1)S(1)} collective-permute-done((bf16[768,128]{1,0:T(8,128)(2,1)S(1)}, bf16[768,128]{1,0:T(8,128)(2,1)S(1)}, u32[]{:S(2)}, u32[]{:S(2)}) %collective-permute-start.6) | collective-permute-done | bytes 196640 | tf_op jit(solution)/shard_map/ppermute | solution.py:712
  63.6 1.0 shard_map.46
  64.6 1.3 %collective-permute-start.8 = (bf16[640,128]{1,0:T(8,128)(2,1)S(1)}, bf16[640,128]{1,0:T(8,128)(2,1)S(1)}, u32[]{:S(2)}, u32[]{:S(2)}) collective-permute-start(bf16[640,128]{1,0:T(8,128)(2,1)S(1)} %get-tuple-element.77), channel_id=1, source_target_pairs={{8,0},{16,8},{24,16},{9,1},{17,9},{25,17},{10,2},{18,10},{26,18},{... | collective-permute-start | bytes 491528 | tf_op jit(solution)/shard_map/ppermute | solution.py:712
  65.9 5.0 %collective-permute-start.9 = (bf16[576,128]{1,0:T(8,128)(2,1)S(1)}, bf16[576,128]{1,0:T(8,128)(2,1)S(1)}, u32[]{:S(2)}, u32[]{:S(2)}) collective-permute-start(bf16[576,128]{1,0:T(8,128)(2,1)S(1)} %get-tuple-element.78), channel_id=1, source_target_pairs={{0,8},{8,16},{16,24},{1,9},{9,17},{17,25},{2,10},{10,18},{18,26},{... | collective-permute-start | bytes 442376 | tf_op jit(solution)/shard_map/ppermute | solution.py:712
  70.9 0.6 shard_map.47.z_ref
  71.6 2.0 %collective-permute-done.9.above_ref = bf16[576,128]{1,0:T(8,128)(2,1)S(1)} collective-permute-done((bf16[576,128]{1,0:T(8,128)(2,1)S(1)}, bf16[576,128]{1,0:T(8,128)(2,1)S(1)}, u32[]{:S(2)}, u32[]{:S(2)}) %collective-permute-start.9) | collective-permute-done | bytes 147488 | tf_op jit(solution)/shard_map/ppermute | solution.py:712
  73.6 0.2 collective-permute-done.8.below_ref
  73.8 1.1 shard_map.48
  74.9 1.3 %collective-permute-start.10 = (bf16[576,128]{1,0:T(8,128)(2,1)S(1)}, bf16[576,128]{1,0:T(8,128)(2,1)S(1)}, u32[]{:S(2)}, u32[]{:S(2)}) collective-permute-start(bf16[576,128]{1,0:T(8,128)(2,1)S(1)} %get-tuple-element.83), channel_id=1, source_target_pairs={{8,0},{16,8},{24,16},{9,1},{17,9},{25,17},{10,2},{18,10},{26,18},{... | collective-permute-start | bytes 442376 | tf_op jit(solution)/shard_map/ppermute | solution.py:712
  76.2 5.2 %collective-permute-start.11 = (bf16[512,128]{1,0:T(8,128)(2,1)S(1)}, bf16[512,128]{1,0:T(8,128)(2,1)S(1)}, u32[]{:S(2)}, u32[]{:S(2)}) collective-permute-start(bf16[512,128]{1,0:T(8,128)(2,1)S(1)} %get-tuple-element.84), channel_id=1, source_target_pairs={{0,8},{8,16},{16,24},{1,9},{9,17},{17,25},{2,10},{10,18},{18,26},{... | collective-permute-start | bytes 393224 | tf_op jit(solution)/shard_map/ppermute | solution.py:712
  81.4 0.6 shard_map.49.z_ref
  82.0 1.9 %collective-permute-done.11.above_ref = bf16[512,128]{1,0:T(8,128)(2,1)S(1)} collective-permute-done((bf16[512,128]{1,0:T(8,128)(2,1)S(1)}, bf16[512,128]{1,0:T(8,128)(2,1)S(1)}, u32[]{:S(2)}, u32[]{:S(2)}) %collective-permute-start.11) | collective-permute-done | bytes 131104 | tf_op jit(solution)/shard_map/ppermute | solution.py:712
  83.9 0.0 collective-permute-done.10.below_ref
  83.9 1.0 shard_map.50
  84.9 0.0 collective-permute-start.12
  84.9 1.2 %collective-permute-done.12 = f32[32,128]{1,0:T(8,128)S(1)} collective-permute-done((f32[32,128]{1,0:T(8,128)S(1)}, f32[32,128]{1,0:T(8,128)S(1)}, u32[]{:S(2)}, u32[]{:S(2)}) %collective-permute-start.12) | collective-permute-done | bytes 16416 | tf_op jit(solution)/shard_map/ppermute | solution.py:700
  86.1 3.6 %collective-permute-start.15 = (f32[32,128]{1,0:T(8,128)S(1)}, f32[32,128]{1,0:T(8,128)S(1)}, u32[]{:S(2)}, u32[]{:S(2)}) collective-permute-start(f32[32,128]{1,0:T(8,128)S(1)} %add.12), channel_id=1, source_target_pairs={{0,6},{1,7},{2,4},{3,5},{4,2},{5,3},{6,0},{7,1},{8,14},{9,15},{10,... | collective-permute-start | bytes 49160 | tf_op jit(solution)/shard_map/ppermute | solution.py:700
  89.7 0.0 collective-permute-start.14
  89.7 0.8 collective-permute-start.13
  90.5 1.1 %collective-permute-done.15 = f32[32,128]{1,0:T(8,128)S(1)} collective-permute-done((f32[32,128]{1,0:T(8,128)S(1)}, f32[32,128]{1,0:T(8,128)S(1)}, u32[]{:S(2)}, u32[]{:S(2)}) %collective-permute-start.15) | collective-permute-done | bytes 16416 | tf_op jit(solution)/shard_map/ppermute | solution.py:700
  91.6 2.7 %collective-permute-done.14 = f32[32,128]{1,0:T(8,128)S(1)} collective-permute-done((f32[32,128]{1,0:T(8,128)S(1)}, f32[32,128]{1,0:T(8,128)S(1)}, u32[]{:S(2)}, u32[]{:S(2)}) %collective-permute-start.14) | collective-permute-done | bytes 16416 | tf_op jit(solution)/shard_map/ppermute | solution.py:700
  94.3 0.0 collective-permute-done.13
  94.4 5.9 %collective-permute-start.18 = (f32[32,128]{1,0:T(8,128)S(1)}, f32[32,128]{1,0:T(8,128)S(1)}, u32[]{:S(2)}, u32[]{:S(2)}) collective-permute-start(f32[32,128]{1,0:T(8,128)S(1)} %add_add_fusion.refs_0_), channel_id=1, source_target_pairs={{0,24},{8,16},{16,8},{24,0},{1,25},{9,17},{17,9},{25,1},{2,26},{10... | collective-permute-start | bytes 49160 | tf_op jit(solution)/shard_map/ppermute | solution.py:700
  100.2 0.0 collective-permute-start.17
  100.2 0.9 collective-permute-start.16
  101.1 0.4 reshape.10.refs_4_
  101.5 0.5 collective-permute-done.18.refs_3_
  101.9 2.0 %collective-permute-done.17.refs_2_ = f32[32,128]{1,0:T(8,128)S(1)} collective-permute-done((f32[32,128]{1,0:T(8,128)S(1)}, f32[32,128]{1,0:T(8,128)S(1)}, u32[]{:S(2)}, u32[]{:S(2)}) %collective-permute-start.17) | collective-permute-done | bytes 16416 | tf_op jit(solution)/shard_map/ppermute | solution.py:700
  104.0 0.0 collective-permute-done.16.refs_1_
  104.0 2.9 %shard_map.51 = f32[32,4096]{1,0:T(8,128)} custom-call(f32[32,128]{1,0:T(8,128)S(1)} %add_add_fusion.refs_0_, f32[32,128]{1,0:T(8,128)S(1)} %collective-permute-done.16.refs_1_, f32[32,128]{1,0:T(8,128)S(1)} %collective-permute-done.17.refs_2_, f32[32,128]{1,0:T(8,128)S(1)} %collective-permute-done.18.refs_3_, f32[32,4096]{1,0:T(8,128)S(1)} %reshape.10.refs_4_), custom_call_target="tpu_custom_call" | custom-call | tf_op jit(solution)/shard_map/pallas_call | solution.py:672
  (2 shorter events, 0.0 us)
Async XLA Ops:
  0.0 4.5 %copy-start = (s32[2,16,64]{2,1,0:T(8,128)S(1)}, s32[2,16,64]{2,1,0:T(8,128)}, u32[]{:S(2)}) copy-start(s32[2,16,64]{2,1,0:T(8,128)} %tissue_ref.7) | copy-start | bytes 24580
  1.7 28.8 %collective-permute-start.3 = (bf16[8,64,1024]{2,1,0:T(8,128)(2,1)S(1)}, bf16[8,64,1024]{2,1,0:T(8,128)(2,1)S(1)}, u32[]{:S(2)}, u32[]{:S(2)}) collective-permute-start(bf16[8,64,1024]{2,1,0:T(8,128)(2,1)S(1)} %shard_map.37.after_ref), channel_id=1, source_target_pairs={{8,0},{16,8},{24,16},{9,1},{17,9},{25,17},{10,2},{18,10},{26,18},{... | collective-permute-start | bytes 3145736 | tf_op jit(solution)/shard_map/ppermute | solution.py:712
  7.6 25.6 %collective-permute-start.1 = (bf16[2,4,64,1152]{3,2,1,0:T(8,128)(2,1)S(1)}, bf16[2,4,64,1152]{3,2,1,0:T(8,128)(2,1)S(1)}, u32[]{:S(2)}, u32[]{:S(2)}) collective-permute-start(bf16[2,4,64,1152]{3,2,1,0:T(8,128)(2,1)S(1)} %get-tuple-element.53), channel_id=1, source_target_pairs={{0,1},{1,2},{2,3},{3,4},{4,5},{5,6},{6,7},{8,9},{9,10},{10,11},{11... | collective-permute-start | bytes 3538952 | tf_op jit(solution)/shard_map/ppermute | solution.py:712
  10.0 23.2 %collective-permute-start.2 = (bf16[2,4,64,1152]{3,2,1,0:T(8,128)(2,1)S(1)}, bf16[2,4,64,1152]{3,2,1,0:T(8,128)(2,1)S(1)}, u32[]{:S(2)}, u32[]{:S(2)}) collective-permute-start(bf16[2,4,64,1152]{3,2,1,0:T(8,128)(2,1)S(1)} %get-tuple-element.48.after_ref), channel_id=1, source_target_pairs={{1,0},{2,1},{3,2},{4,3},{5,4},{6,5},{7,6},{9,8},{10,9},{11,10},{12... | collective-permute-start | bytes 3538952 | tf_op jit(solution)/shard_map/ppermute | solution.py:712
  11.3 41.7 %collective-permute-start = (bf16[8,64,1024]{2,1,0:T(8,128)(2,1)S(1)}, bf16[8,64,1024]{2,1,0:T(8,128)(2,1)S(1)}, u32[]{:S(2)}, u32[]{:S(2)}) collective-permute-start(bf16[8,64,1024]{2,1,0:T(8,128)(2,1)S(1)} %get-tuple-element.47), channel_id=1, source_target_pairs={{8,0},{16,8},{24,16},{9,1},{17,9},{25,17},{10,2},{18,10},{26,18},{... | collective-permute-start | bytes 3145736 | tf_op jit(solution)/shard_map/ppermute | solution.py:712
  30.6 6.6 %collective-permute-start.4 = (bf16[4,64,1024]{2,1,0:T(8,128)(2,1)S(1)}, bf16[4,64,1024]{2,1,0:T(8,128)(2,1)S(1)}, u32[]{:S(2)}, u32[]{:S(2)}) collective-permute-start(bf16[4,64,1024]{2,1,0:T(8,128)(2,1)S(1)} %get-tuple-element.59), channel_id=1, source_target_pairs={{0,1},{1,2},{2,3},{3,4},{4,5},{5,6},{6,7},{8,9},{9,10},{10,11},{11... | collective-permute-start | bytes 1572872 | tf_op jit(solution)/shard_map/ppermute | solution.py:712
  31.9 6.1 %collective-permute-start.5 = (bf16[4,64,1024]{2,1,0:T(8,128)(2,1)S(1)}, bf16[4,64,1024]{2,1,0:T(8,128)(2,1)S(1)}, u32[]{:S(2)}, u32[]{:S(2)}) collective-permute-start(bf16[4,64,1024]{2,1,0:T(8,128)(2,1)S(1)} %get-tuple-element.54.after_ref), channel_id=1, source_target_pairs={{1,0},{2,1},{3,2},{4,3},{5,4},{6,5},{7,6},{9,8},{10,9},{11,10},{12... | collective-permute-start | bytes 1572872 | tf_op jit(solution)/shard_map/ppermute | solution.py:712
  35.7 24.7 %collective-permute-start.7 = (bf16[832,128]{1,0:T(8,128)(2,1)S(1)}, bf16[832,128]{1,0:T(8,128)(2,1)S(1)}, u32[]{:S(2)}, u32[]{:S(2)}) collective-permute-start(bf16[832,128]{1,0:T(8,128)(2,1)S(1)} %get-tuple-element.67), channel_id=1, source_target_pairs={{8,0},{16,8},{24,16},{9,1},{17,9},{25,17},{10,2},{18,10},{26,18},{... | collective-permute-start | bytes 638984 | tf_op jit(solution)/shard_map/ppermute | solution.py:712
  55.5 8.0 %collective-permute-start.6 = (bf16[768,128]{1,0:T(8,128)(2,1)S(1)}, bf16[768,128]{1,0:T(8,128)(2,1)S(1)}, u32[]{:S(2)}, u32[]{:S(2)}) collective-permute-start(bf16[768,128]{1,0:T(8,128)(2,1)S(1)} %get-tuple-element.66), channel_id=1, source_target_pairs={{0,8},{8,16},{16,24},{1,9},{9,17},{17,25},{2,10},{10,18},{18,26},{... | collective-permute-start | bytes 589832 | tf_op jit(solution)/shard_map/ppermute | solution.py:712
  64.6 9.2 %collective-permute-start.8 = (bf16[640,128]{1,0:T(8,128)(2,1)S(1)}, bf16[640,128]{1,0:T(8,128)(2,1)S(1)}, u32[]{:S(2)}, u32[]{:S(2)}) collective-permute-start(bf16[640,128]{1,0:T(8,128)(2,1)S(1)} %get-tuple-element.77), channel_id=1, source_target_pairs={{8,0},{16,8},{24,16},{9,1},{17,9},{25,17},{10,2},{18,10},{26,18},{... | collective-permute-start | bytes 491528 | tf_op jit(solution)/shard_map/ppermute | solution.py:712
  65.9 7.7 %collective-permute-start.9 = (bf16[576,128]{1,0:T(8,128)(2,1)S(1)}, bf16[576,128]{1,0:T(8,128)(2,1)S(1)}, u32[]{:S(2)}, u32[]{:S(2)}) collective-permute-start(bf16[576,128]{1,0:T(8,128)(2,1)S(1)} %get-tuple-element.78), channel_id=1, source_target_pairs={{0,8},{8,16},{16,24},{1,9},{9,17},{17,25},{2,10},{10,18},{18,26},{... | collective-permute-start | bytes 442376 | tf_op jit(solution)/shard_map/ppermute | solution.py:712
  74.9 9.1 %collective-permute-start.10 = (bf16[576,128]{1,0:T(8,128)(2,1)S(1)}, bf16[576,128]{1,0:T(8,128)(2,1)S(1)}, u32[]{:S(2)}, u32[]{:S(2)}) collective-permute-start(bf16[576,128]{1,0:T(8,128)(2,1)S(1)} %get-tuple-element.83), channel_id=1, source_target_pairs={{8,0},{16,8},{24,16},{9,1},{17,9},{25,17},{10,2},{18,10},{26,18},{... | collective-permute-start | bytes 442376 | tf_op jit(solution)/shard_map/ppermute | solution.py:712
  76.2 7.8 %collective-permute-start.11 = (bf16[512,128]{1,0:T(8,128)(2,1)S(1)}, bf16[512,128]{1,0:T(8,128)(2,1)S(1)}, u32[]{:S(2)}, u32[]{:S(2)}) collective-permute-start(bf16[512,128]{1,0:T(8,128)(2,1)S(1)} %get-tuple-element.84), channel_id=1, source_target_pairs={{0,8},{8,16},{16,24},{1,9},{9,17},{17,25},{2,10},{10,18},{18,26},{... | collective-permute-start | bytes 393224 | tf_op jit(solution)/shard_map/ppermute | solution.py:712
  84.9 1.2 %collective-permute-start.12 = (f32[32,128]{1,0:T(8,128)S(1)}, f32[32,128]{1,0:T(8,128)S(1)}, u32[]{:S(2)}, u32[]{:S(2)}) collective-permute-start(f32[32,128]{1,0:T(8,128)S(1)} %get-tuple-element.87), channel_id=1, source_target_pairs={{0,1},{1,0},{2,3},{3,2},{4,5},{5,4},{6,7},{7,6},{8,9},{9,8},{10,11... | collective-permute-start | bytes 49160 | tf_op jit(solution)/shard_map/ppermute | solution.py:700
  86.1 5.5 %collective-permute-start.15 = (f32[32,128]{1,0:T(8,128)S(1)}, f32[32,128]{1,0:T(8,128)S(1)}, u32[]{:S(2)}, u32[]{:S(2)}) collective-permute-start(f32[32,128]{1,0:T(8,128)S(1)} %add.12), channel_id=1, source_target_pairs={{0,6},{1,7},{2,4},{3,5},{4,2},{5,3},{6,0},{7,1},{8,14},{9,15},{10,... | collective-permute-start | bytes 49160 | tf_op jit(solution)/shard_map/ppermute | solution.py:700
  89.7 4.6 %collective-permute-start.14 = (f32[32,128]{1,0:T(8,128)S(1)}, f32[32,128]{1,0:T(8,128)S(1)}, u32[]{:S(2)}, u32[]{:S(2)}) collective-permute-start(f32[32,128]{1,0:T(8,128)S(1)} %add.12), channel_id=1, source_target_pairs={{0,4},{1,5},{2,6},{3,7},{4,0},{5,1},{6,2},{7,3},{8,12},{9,13},{10,... | collective-permute-start | bytes 49160 | tf_op jit(solution)/shard_map/ppermute | solution.py:700
  89.7 4.6 %collective-permute-start.13 = (f32[32,128]{1,0:T(8,128)S(1)}, f32[32,128]{1,0:T(8,128)S(1)}, u32[]{:S(2)}, u32[]{:S(2)}) collective-permute-start(f32[32,128]{1,0:T(8,128)S(1)} %add.12), channel_id=1, source_target_pairs={{0,2},{1,3},{2,0},{3,1},{4,6},{5,7},{6,4},{7,5},{8,10},{9,11},{10,... | collective-permute-start | bytes 49160 | tf_op jit(solution)/shard_map/ppermute | solution.py:700
  94.4 7.6 %collective-permute-start.18 = (f32[32,128]{1,0:T(8,128)S(1)}, f32[32,128]{1,0:T(8,128)S(1)}, u32[]{:S(2)}, u32[]{:S(2)}) collective-permute-start(f32[32,128]{1,0:T(8,128)S(1)} %add_add_fusion.refs_0_), channel_id=1, source_target_pairs={{0,24},{8,16},{16,8},{24,0},{1,25},{9,17},{17,9},{25,1},{2,26},{10... | collective-permute-start | bytes 49160 | tf_op jit(solution)/shard_map/ppermute | solution.py:700
  100.2 3.7 %collective-permute-start.17 = (f32[32,128]{1,0:T(8,128)S(1)}, f32[32,128]{1,0:T(8,128)S(1)}, u32[]{:S(2)}, u32[]{:S(2)}) collective-permute-start(f32[32,128]{1,0:T(8,128)S(1)} %add_add_fusion.refs_0_), channel_id=1, source_target_pairs={{0,16},{8,24},{16,0},{24,8},{1,17},{9,25},{17,1},{25,9},{2,18},{10... | collective-permute-start | bytes 49160 | tf_op jit(solution)/shard_map/ppermute | solution.py:700
  100.2 3.7 %collective-permute-start.16 = (f32[32,128]{1,0:T(8,128)S(1)}, f32[32,128]{1,0:T(8,128)S(1)}, u32[]{:S(2)}, u32[]{:S(2)}) collective-permute-start(f32[32,128]{1,0:T(8,128)S(1)} %add_add_fusion.refs_0_), channel_id=1, source_target_pairs={{0,8},{8,0},{16,24},{24,16},{1,9},{9,1},{17,25},{25,17},{2,10},{10... | collective-permute-start | bytes 49160 | tf_op jit(solution)/shard_map/ppermute | solution.py:700

commit v5 on v4

--- a/solution.py
+++ b/solution.py
@@ -74,19 +74,20 @@
     return jnp.concatenate([block[:, :RANK], block[:, RANK:]], axis=0)
 
 
-def panel_at(panel, row, e):
-    left_ref, own_ref, right_ref = panel
-    own = own_ref.shape[1]
-    if GHOST <= e < GHOST + own:
-        return own_ref[row, e - GHOST]
-    ref, at = (left_ref, e) if e < GHOST else (right_ref, e - GHOST - own)
-    both = ref[row, at, :, ref.shape[3] - 2 * RANK :].astype(f32)
-    return both[:, :RANK] + both[:, RANK:]
-
-
 def pair_of(values):
     high = values.astype(bf16)
     return high, (values - high.astype(f32)).astype(bf16)
+
+
+def four_of(values):
+    high, middle = pair_of(values)
+    low = (values - high.astype(f32) - middle.astype(f32)).astype(bf16)
+    return jnp.concatenate([high, middle, low, jnp.zeros_like(low)], axis=1)
+
+
+def whole_of(parts):
+    parts = parts.astype(f32)
+    return parts[:, :RANK] + parts[:, RANK : 2 * RANK] + parts[:, 2 * RANK : 3 * RANK]
 
 
 def by_sublane(tissue):
@@ -115,16 +116,46 @@
 ANY_SPEC = pl.BlockSpec(memory_space=pl.ANY)
 
 
+def folded_gram(side):
+    wide = 2 * RANK
+    gram = lax.dot_general(side, side, ATB, preferred_element_type=f32)
+    gram = gram[:wide] + gram[wide:]
+    gram = gram[:, :wide] + gram[:, wide:]
+    return packed(gram[:RANK, :RANK] + gram[RANK:, RANK:])
+
+
+def start_gram_kernel(probe_ref, gram_ref, flat_ref, sems):
+    rows, cols, width = probe_ref.shape
+    (copy,) = fetched([probe_ref], [flat_ref], sems)
+    copy.wait()
+    wide = 2 * RANK
+    spans = [slice(q * wide, (q + 1) * wide) for q in range(width // wide)]
+    side = jnp.concatenate([flat_ref[row, :, span] for row in range(rows) for span in spans], axis=0)
+    gram_ref[...] = folded_gram(jnp.concatenate(pair_of(side), axis=1))
+
+
+def start_gram(probe):
+    return pl.pallas_call(
+        start_gram_kernel,
+        in_specs=[HBM_SPEC],
+        out_specs=VMEM_SPEC,
+        out_shape=sds((RANK // 2, 2 * RANK), f32),
+        scratch_shapes=[pltpu.VMEM(probe.shape, f32), pltpu.SemaphoreType.DMA((1,))],
+        compiler_params=pltpu.CompilerParams(vmem_limit_bytes=VMEM_BYTES),
+    )(*in_hbm(probe))
+
+
 def mark_edges_kernel(x_ref, tissue_ref, edge_ref, tile_ref, mask_ref, sems):
     cols = x_ref.shape[1]
-    chosen = list(range(EDGE)) + list(range(cols - EDGE, cols))
-    sources = [tissue_ref.at[0]] + [x_ref.at[0, c] for c in chosen]
-    copies = fetched(sources, [mask_ref] + [tile_ref.at[i] for i in range(len(chosen))], sems)
+    sources = [tissue_ref.at[0], x_ref.at[0, :EDGE], x_ref.at[0, cols - EDGE :]]
+    copies = fetched(sources, [mask_ref, tile_ref.at[:EDGE], tile_ref.at[EDGE:]], sems)
     copies[0].wait()
     mask = by_sublane(mask_ref[...])
-    for i, c in enumerate(chosen):
-        copies[i + 1].wait()
-        edge_ref[i] = marked(tile_ref[i], mask[:, c : c + 1])
+    for side, first in ((0, 0), (1, cols - EDGE)):
+        copies[1 + side].wait()
+        for i in range(EDGE):
+            at = side * EDGE + i
+            edge_ref[at] = marked(tile_ref[at], mask[:, first + i : first + i + 1])
 
 
 def mark_edges(x, tissue):
@@ -138,67 +169,72 @@
         scratch_shapes=[
             pltpu.VMEM(shape, bf16),
             pltpu.VMEM((cols, patch), jnp.int32),
-            pltpu.SemaphoreType.DMA((2 * EDGE + 1,)),
+            pltpu.SemaphoreType.DMA((3,)),
         ],
         compiler_params=pltpu.CompilerParams(vmem_limit_bytes=VMEM_BYTES),
     )(*in_hbm(x, tissue))
 
 
-def mark_rest_kernel(x_ref, tissue_ref, probe_ref, after_ref, left_ref, right_ref, middle_ref, tile_ref, sems):
+def gate_kernel(count, *refs):
+    for x_ref, out_ref in zip(refs[:count], refs[len(refs) - count :]):
+        out_ref[...] = x_ref[...]
+
+
+def gate(arrays, after):
+    count = len(arrays)
+    return pl.pallas_call(
+        functools.partial(gate_kernel, count),
+        in_specs=[VMEM_SPEC] * count + [ANY_SPEC] * len(after),
+        out_specs=[VMEM_SPEC] * count,
+        out_shape=tuple(sds(x.shape, x.dtype) for x in arrays),
+        input_output_aliases={i: i for i in range(count)},
+        compiler_params=pltpu.CompilerParams(vmem_limit_bytes=VMEM_BYTES),
+    )(*arrays, *after)
+
+
+def units_kernel(
+    x_ref, tissue_ref, probe_ref, after_ref,
+    left_ref, right_ref, middle_ref, unit0_ref, unit1_ref,
+    tile_ref, sems,
+):
     rows, cols, patch, width = x_ref.shape
-    ends = [(row, c) for row in range(rows) for c in list(range(GHOST)) + list(range(cols - GHOST, cols))]
-    chosen = ends + [(0, c) for c in range(EDGE, cols - EDGE)]
-    copies = fetched([x_ref.at[row, c] for row, c in chosen], [tile_ref.at[i] for i in range(len(chosen))], sems)
+    run = GHOST
+    order = [(row, c) for row in range(rows) for c in (0, cols - run)]
+    order += [(row, c) for row in range(rows) for c in range(run, cols - run, run)]
+    copies = fetched([x_ref.at[row, c : c + run] for row, c in order], [tile_ref.at[i] for i in range(len(order))], sems)
     masks = [by_sublane(tissue_ref[row]) for row in range(rows)]
-    for i, (row, c) in enumerate(chosen):
+    for i, (row, first) in enumerate(order):
         copies[i].wait()
-        tile = marked(tile_ref[i], masks[row][:, c : c + 1])
-        if i >= len(ends):
-            middle_ref[c - EDGE] = tile
-            continue
-        side_ref, at = (left_ref, c) if c < GHOST else (right_ref, c - cols + GHOST)
-        side_ref[row, at, :, :width] = tile
-        side_ref[row, at, :, width:] = jnp.concatenate(pair_of(probe_ref[row, c]), axis=1)
-
-
-def mark_rest(x, tissue, probe, after):
+        for k in range(run):
+            c = first + k
+            tile, column = tile_ref[i, k], masks[row][:, c : c + 1]
+            unit, _ = unit_and_mask(tile)
+            at = (GHOST + c) * patch
+            (unit0_ref, unit1_ref)[row][at : at + patch, :] = unit * column.astype(bf16)
+            if first == 0 or first == cols - run:
+                side_ref = left_ref if first == 0 else right_ref
+                side_ref[row, k, :, :width] = marked(tile, column)
+                side_ref[row, k, :, width:] = four_of(probe_ref[row, c])
+            if row == 0 and EDGE <= c < cols - EDGE:
+                middle_ref[c - EDGE] = marked(tile, column)
+
+
+def own_units(x, tissue, probe, after):
     rows, cols, patch, width = x.shape
-    side = sds((rows, GHOST, patch, width + 2 * RANK), bf16)
-    count = 2 * rows * GHOST + cols - 2 * EDGE
+    n = cols + 2 * GHOST
+    side = sds((rows, GHOST, patch, width + 4 * RANK), bf16)
+    unit = sds((n * patch, width), bf16)
     return pl.pallas_call(
-        mark_rest_kernel,
+        units_kernel,
         in_specs=[HBM_SPEC, VMEM_SPEC, VMEM_SPEC, ANY_SPEC],
-        out_specs=[VMEM_SPEC] * 3,
-        out_shape=(side, side, sds((cols - 2 * EDGE, patch, width), bf16)),
-        scratch_shapes=[pltpu.VMEM((count, patch, width), bf16), pltpu.SemaphoreType.DMA((count,))],
+        out_specs=[VMEM_SPEC] * 5,
+        out_shape=(side, side, sds((cols - 2 * EDGE, patch, width), bf16), unit, unit),
+        scratch_shapes=[
+            pltpu.VMEM((rows * cols // GHOST, GHOST, patch, width), bf16),
+            pltpu.SemaphoreType.DMA((rows * cols // GHOST,)),
+        ],
         compiler_params=pltpu.CompilerParams(vmem_limit_bytes=VMEM_BYTES),
     )(*in_hbm(x), tissue, probe, after)
-
-
-def units_kernel(n, x_ref, tissue_ref, after_ref, unit0_ref, unit1_ref, tile_ref, sems):
-    rows, cols, patch, width = x_ref.shape
-    chosen = [(row, c) for row in range(rows) for c in range(cols)]
-    copies = fetched([x_ref.at[row, c] for row, c in chosen], [tile_ref.at[i] for i in range(len(chosen))], sems)
-    masks = [by_sublane(tissue_ref[row]).astype(bf16) for row in range(rows)]
-    for i, (row, c) in enumerate(chosen):
-        copies[i].wait()
-        unit, _ = unit_and_mask(tile_ref[i])
-        at = (GHOST + c) * patch
-        (unit0_ref, unit1_ref)[row][at : at + patch, :] = unit * masks[row][:, c : c + 1]
-
-
-def own_units(x, tissue, after):
-    rows, cols, patch, width = x.shape
-    n = cols + 2 * GHOST
-    unit = sds((n * patch, width), bf16)
-    return pl.pallas_call(
-        functools.partial(units_kernel, n),
-        in_specs=[HBM_SPEC, VMEM_SPEC, ANY_SPEC],
-        out_specs=[VMEM_SPEC] * 2,
-        out_shape=(unit, unit),
-        scratch_shapes=[pltpu.VMEM((rows * cols, patch, width), bf16), pltpu.SemaphoreType.DMA((rows * cols,))],
-        compiler_params=pltpu.CompilerParams(vmem_limit_bytes=VMEM_BYTES),
-    )(*in_hbm(x), tissue, after)
 
 
 def bands(ranges, patch, unit0_ref, unit1_ref, m_ref, degree, diagonal):
@@ -247,8 +283,8 @@
 
 def outside_kernel(
     n,
-    start0_ref, start1_ref, some_ref, tissue_ref, sum_ref, xl_ref, p_ref, xr_ref, after_ref,
-    unit0_ref, unit1_ref, m_ref, stat_ref, pay_ref, pl_ref, pr_ref,
+    start0_ref, start1_ref, some_ref, tissue_ref, sum_ref, xl_ref, xr_ref, after_ref,
+    unit0_ref, unit1_ref, m_ref, stat_ref,
 ):
     rows, count, patch, _ = xl_ref.shape
     width = unit0_ref.shape[1]
@@ -256,6 +292,11 @@
     both = rows * patch
     lane = iota((patch, 128), 1)
 
+    kept = slice(count * patch, (count + cols) * patch)
+    unit0_ref[kept, :] = start0_ref[kept, :]
+    unit1_ref[kept, :] = start1_ref[kept, :]
+    for e in range(count + 1, n - count - 1):
+        m_ref[e] = some_ref[e]
     masks = []
     for row, unit_ref in ((0, unit0_ref), (1, unit1_ref)):
         own_mask = by_sublane(tissue_ref[row])
@@ -278,32 +319,54 @@
     stat_ref[0] = degree
     stat_ref[1] = diagonal
     stat_ref[2] = mask
-    half = patch // 2
-    tail = (n - 2) * half
-    for e in range(1, n - 1):
-        pay_ref[(e - 1) * half : e * half, :] = packed(panel_at((xl_ref, p_ref, xr_ref), 0, e)).astype(bf16)
-    pay_ref[tail : tail + patch, :], pay_ref[tail + patch :, :] = pair_of(degree[:patch])
-    pl_ref[...] = xl_ref[:, :, :, width:]
-    pr_ref[...] = xr_ref[:, :, :, width:]
-
 
 def payload_rows(columns, patch):
     return columns * patch // 2 + 2 * patch
 
 
-def outside_affinity(unit0, unit1, m, tissue, sums, panel, after):
+def outside_affinity(unit0, unit1, m, tissue, sums, xl, xr, after):
     n, both, _ = m.shape
-    payload = sds((payload_rows(n - 2, both // 2), 2 * RANK), bf16)
-    side = sds(panel[0].shape[:3] + (2 * RANK,), bf16)
     unit = sds(unit0.shape, bf16)
     return pl.pallas_call(
         functools.partial(outside_kernel, n),
-        in_specs=[VMEM_SPEC] * 8 + [ANY_SPEC],
-        out_specs=[VMEM_SPEC] * 7,
-        out_shape=(unit, unit, sds(m.shape, bf16), sds((3, both, 128), f32), payload, side, side),
+        in_specs=[VMEM_SPEC] * 7 + [ANY_SPEC],
+        out_specs=[VMEM_SPEC] * 4,
+        out_shape=(unit, unit, sds(m.shape, bf16), sds((3, both, 128), f32)),
         input_output_aliases={0: 0, 1: 1, 2: 2},
         compiler_params=pltpu.CompilerParams(vmem_limit_bytes=VMEM_BYTES),
-    )(unit0, unit1, m, tissue, sums, *panel, after)
+    )(unit0, unit1, m, tissue, sums, xl, xr, after)
+
+
+def start_kernel(factor, count, *refs):
+    parts, (stat_ref, xl_ref, p_ref, xr_ref, panel_ref, pay_ref) = refs[:count], refs[count:]
+    rows, cols, patch, _ = p_ref.shape
+    n = cols + 2 * GHOST
+    half = patch // 2
+    width = xl_ref.shape[3] - 4 * RANK
+    inverse = factor * inverse_factor(unpacked(balanced([part[...] for part in parts])), True)
+    for row in range(rows):
+        tiles = [whole_of(xl_ref[row, c, :, width:]) for c in range(GHOST)]
+        tiles += [p_ref[row, c] for c in range(cols)]
+        tiles += [whole_of(xr_ref[row, c, :, width:]) for c in range(GHOST)]
+        turned = lax.dot_general(
+            jnp.concatenate(tiles, axis=0), inverse, ABT, precision=lax.Precision.HIGHEST, preferred_element_type=f32
+        )
+        for e in range(n):
+            tile = turned[e * patch : (e + 1) * patch]
+            panel_ref[row, e] = tile
+            if row == 0 and 0 < e < n - 1:
+                pay_ref[(e - 1) * half : e * half, :] = packed(tile).astype(bf16)
+    tail = (n - 2) * half
+    pay_ref[tail : tail + patch, :], pay_ref[tail + patch :, :] = pair_of(stat_ref[0, :patch])
+
+
+def start_panel(factor, parts, stat, xl, own_panel, xr):
+    rows, cols, patch, _ = own_panel.shape
+    n = cols + 2 * GHOST
+    return kernel_call(
+        functools.partial(start_kernel, factor, len(parts)),
+        (sds((rows, n, patch, RANK), f32), sds((payload_rows(n - 2, patch), 2 * RANK), bf16)),
+    )(*parts, stat, xl, own_panel, xr)
 
 
 def cut_kernel(be_ref, after_ref, left_ref, right_ref):
@@ -372,8 +435,8 @@
     steps = stages(n)
     tiles, columns = steps[stage]
     count = 3 if stage == 0 else 1
-    pieces, (own_ref, stat_ref, pl_ref, p_ref, pr_ref) = refs[:count], refs[count : count + 5]
-    refs = refs[count + 5 :]
+    pieces, (own_ref, stat_ref, p_ref) = refs[:count], refs[count : count + 3]
+    refs = refs[count + 3 :]
     patch = pieces[0].shape[1]
     lane = iota((patch, 128), 1)
     if stage == 0:
@@ -383,6 +446,18 @@
     else:
         before, (v_ref, w_ref, sum_ref, u0_ref, pay_ref, unit_ref) = refs[:6], refs[6:12]
         down_sum, up_sum, mask = (before[2][i] for i in range(3))
+        earlier = {e for _, reached in steps[:stage] for e in reached}
+        for e in pairs_of(earlier):
+            v_ref[e // 2] = before[0][e // 2]
+            w_ref[e // 2] = before[1][e // 2]
+        for e in sorted(earlier):
+            u0_ref[e] = before[3][e]
+        for e in sorted(e for e in earlier if e - 1 in earlier and e + 1 in earlier):
+            span = slice((e - 2) * patch // 2, (e - 1) * patch // 2)
+            pay_ref[span, :] = before[4][span, :]
+        for c in sorted({c for e in columns for c in (e - 1, e, e + 1)} - set(tiles)):
+            span = slice(c * patch, (c + 1) * patch)
+            unit_ref[span, :] = before[5][span, :]
     sources = [(ref, i) for ref in pieces for i in range(ref.shape[0])]
     for c, (ref, i) in zip(tiles, sources):
         unit, column = unit_and_mask(ref[i])
@@ -407,7 +482,7 @@
     sums = (down_sum, up_sum, mask)
     scale = scale_of(stat_ref, sums)
     for e in columns:
-        u0_ref[e] = (scale[:, e : e + 1] * panel_at((pl_ref, p_ref, pr_ref), 1, e)).astype(bf16)
+        u0_ref[e] = (scale[:, e : e + 1] * p_ref[1, e]).astype(bf16)
     inner, known = [], []
     for last in (stage - 1, stage):
         known = [e for _, reached in steps[: last + 1] for e in reached]
@@ -428,7 +503,7 @@
 def cross_affinity(stage, pieces, u1, stat, panel, before=()):
     patch, width = pieces[0].shape[1:]
     n = u1.shape[0] // patch
-    given = len(pieces) + 5
+    given = len(pieces) + 3
     return pl.pallas_call(
         functools.partial(cross_kernel, n, stage),
         out_shape=(
@@ -441,7 +516,7 @@
         ),
         input_output_aliases={given + i: i for i in range(len(before))},
         compiler_params=pltpu.CompilerParams(vmem_limit_bytes=VMEM_BYTES),
-    )(*pieces, u1, stat, *panel, *before)
+    )(*pieces, u1, stat, panel, *before)
 
 
 def before_first_kernel(n, got_ref, sum_ref, stat_ref, u0_ref, m_ref, v_ref, z_ref, t_ref, gain_ref, own_ref, u2_ref):
@@ -478,11 +553,10 @@
 
 def first_kernel(
     n,
-    got_ref, stat_ref, t1_ref, gain1_ref, own_ref, z_ref, pl_ref, p_ref, pr_ref, m_ref, w_ref,
+    got_ref, stat_ref, t1_ref, gain1_ref, own_ref, z_ref, p_ref, m_ref, w_ref,
     y_ref, u_ref, t0_ref, gain0_ref, up_ref, down_ref,
     start_ref,
 ):
-    panel = (pl_ref, p_ref, pr_ref)
     patch = t1_ref.shape[1]
     half = patch // 2
     tail = (n - 4) * half
@@ -491,7 +565,7 @@
     for e in range(1, n - 1):
         t = jnp.broadcast_to(scale[:, e : e + 1], (patch, RANK))
         t0_ref[e] = t
-        start_ref[e] = (t * panel_at(panel, 0, e)).astype(bf16)
+        start_ref[e] = (t * p_ref[0, e]).astype(bf16)
     for e in range(2, n - 2):
         own = start_ref[e - 1 : e + 2].reshape(3 * patch, RANK)
         total = z_ref[e] + jnp.dot(m_ref[e, :, : 3 * patch], own, preferred_element_type=f32)
@@ -499,7 +573,7 @@
         gain = 1.0 + t0_ref[e] * t0_ref[e] * own_ref[e]
         gain0_ref[e] = gain
         for row, piece, t, g in ((0, upper, t0_ref[e], gain), (1, total[patch:], t1_ref[e], gain1_ref[e])):
-            image = panel_at(panel, row, e) * g + t * piece
+            image = p_ref[row, e] * g + t * piece
             y_ref[row, e] = image
             scaled = t * image
             u_ref[row, e] = scaled.astype(bf16)
@@ -524,7 +598,7 @@
             sds(((n - 6) * half, 2 * RANK), bf16),
         ),
         [pltpu.VMEM((n, patch, RANK), bf16)],
-    )(got, stat, t1, gain1, own, z, *panel, m, w)
+    )(got, stat, t1, gain1, own, z, panel, m, w)
 
 
 def local_kernel(low, high, m_ref, u_ref, z_ref):
@@ -608,11 +682,7 @@
             new_ref[row, e - low] = images[row]
         span = slice((e - low) * patch, (e - low + 1) * patch)
         side_ref[span, :wide], side_ref[span, wide:] = pair_of(jnp.concatenate(images, axis=1))
-    side = side_ref[...]
-    gram = lax.dot_general(side, side, ATB, preferred_element_type=f32)
-    gram = gram[:wide] + gram[wide:]
-    gram = gram[:, :wide] + gram[:, wide:]
-    gram_ref[...] = packed(gram[:RANK, :RANK] + gram[RANK:, RANK:])
+    gram_ref[...] = folded_gram(side_ref[...])
 
 
 def last_step(low, below, above, z, y, spread, v):
@@ -625,8 +695,11 @@
     )(below, above, z, y, *spread, v)
 
 
-def inverse_factor(gram):
+def inverse_factor(gram, bounded=False):
     size = gram.shape[0]
+    least = 0.0
+    if bounded:
+        least = 1e-6 * jnp.sum(jnp.where(identity(size), gram, 0.0), axis=1, keepdims=True) + 1e-30
     step = 8
     row = iota((size, 2 * size), 0)
     lane = iota((size, 2 * size), 1)
@@ -635,21 +708,25 @@
         cols = [jnp.broadcast_to(table[:, k + i : k + i + 1], table.shape) for i in range(step)]
         lines = [table[k + i : k + i + 1, :] for i in range(step)]
         for i in range(step):
-            inverse = 1.0 / cols[i][k + i : k + i + 1, :]
+            pivot = cols[i][k + i : k + i + 1, :]
+            inverse = 1.0 / (jnp.maximum(pivot, least[k + i : k + i + 1, :]) if bounded else pivot)
             for j in range(i + 1, step):
                 lines[j] = lines[j] - lines[i] * (cols[i][k + j : k + j + 1, :] * inverse)
                 cols[j] = cols[j] - cols[i] * (cols[j][k + i : k + i + 1, :] * inverse)
             table = table - jnp.where(row > k + i, cols[i], 0.0) * (lines[i] * inverse)
     pivots = jnp.sum(jnp.where(row == lane, table, 0.0), axis=1, keepdims=True)
-    return table[:, size:] * lax.rsqrt(pivots)
+    return table[:, size:] * lax.rsqrt(jnp.maximum(pivots, least) if bounded else pivots)
+
+
+def balanced(parts):
+    while len(parts) > 1:
+        parts = [a + b for a, b in zip(parts[::2], parts[1::2])]
+    return parts[0]
 
 
 def finish_kernel(factor, count, *refs):
     parts, y_ref, out_ref = refs[:count], refs[count], refs[count + 1]
-    total = parts[0][...]
-    for part in parts[1:]:
-        total = total + part[...]
-    inverse = factor * inverse_factor(unpacked(total))
+    inverse = factor * inverse_factor(unpacked(balanced([part[...] for part in parts])))
     zero = jnp.zeros_like(inverse)
     both = jnp.concatenate(
         [jnp.concatenate([inverse, zero], axis=1), jnp.concatenate([zero, inverse], axis=1)], axis=0
@@ -675,35 +752,29 @@
     )(*parts, y)
 
 
-def exchange_stages():
-    stages = []
-    for axis in ("col", "row"):
-        size = lax.axis_size(axis)
-        bit = 1
-        if axis == "col":
-            stages.append((axis, size, [1]))
-            bit = 2
-        while bit < size:
-            if 2 * bit < size:
-                stages.append((axis, size, [bit, 2 * bit, 3 * bit]))
-                bit *= 4
-            else:
-                stages.append((axis, size, [bit]))
-                bit *= 2
+def exchange_stages(axis):
+    size = lax.axis_size(axis)
+    stages, bit = [], 1
+    if axis == "col":
+        stages.append([1])
+        bit = 2
+    while bit < size:
+        if 2 * bit < size:
+            stages.append([bit, 2 * bit, 3 * bit])
+            bit *= 4
+        else:
+            stages.append([bit])
+            bit *= 2
     return stages
 
 
-def summed_parts(gram):
-    stages = exchange_stages()
-    for place, (axis, size, partners) in enumerate(stages):
-        parts = [gram] + [
-            lax.ppermute(gram, axis, [(i, i ^ p) for i in range(size)]) for p in partners
-        ]
-        if place == len(stages) - 1:
-            return parts
-        gram = parts[0]
-        for part in parts[1:]:
-            gram = gram + part
+def summed_parts(gram, axis):
+    size = lax.axis_size(axis)
+    parts = [gram]
+    for partners in exchange_stages(axis):
+        gram = balanced(parts)
+        parts = [gram] + [lax.ppermute(gram, axis, [(i, i ^ p) for i in range(size)]) for p in partners]
+    return parts
 
 
 def passed_along(shard, axis, by):
@@ -714,19 +785,22 @@
 
 def local(features, tissue, probe):
     tile_rows, tile_cols, patches, width = features.shape
-    edges = mark_edges(features, tissue)
+    total = tile_rows * lax.axis_size("row") * tile_cols * lax.axis_size("col") * patches
+    factor = math.sqrt(float(total))
+    parts = summed_parts(start_gram(probe), "row")
+    (edges,) = gate((mark_edges(features, tissue),), parts[1:])
     below_edges = passed_along(edges, "row", -1)
+    parts = summed_parts(balanced(parts), "col")
     own_panel = probe.reshape(tile_rows, tile_cols, patches, RANK)
-    left_end, right_end, middle = mark_rest(features, tissue, own_panel, edges)
+    left_end, right_end, middle, unit0, unit1 = own_units(features, tissue, own_panel, edges)
+    left_end, right_end = gate((left_end, right_end), parts)
     from_left = passed_along(right_end, "col", 1)
     from_right = passed_along(left_end, "col", -1)
     below_middle = passed_along(middle, "row", -1)
-    unit0, unit1 = own_units(features, tissue, left_end)
     m, sums = inside_affinity(unit0, unit1, patches)
     below_left, below_right = cut(below_edges, sums)
-    panel = (from_left, own_panel, from_right)
-    _, u1, m, stat, payload, *sides = outside_affinity(unit0, unit1, m, tissue, sums, panel, below_left)
-    panel = (sides[0], own_panel, sides[1])
+    _, u1, m, stat = outside_affinity(unit0, unit1, m, tissue, sums, from_left, from_right, below_left)
+    panel, payload = start_panel(factor, parts, stat, from_left, own_panel, from_right)
     below_left, below_right = passed_along(below_right, "col", 1), passed_along(below_left, "col", -1)
     got_below = passed_along(payload, "row", -1)
     n = tile_cols + 2 * GHOST
@@ -743,10 +817,9 @@
     z = local_products(4, n - 4, m, u)
     y, gram = last_step(4, below, above, z, y, spread, v)
 
-    parts = summed_parts(gram)
+    parts = summed_parts(balanced(summed_parts(gram, "col")), "row")
     flat = y.reshape(tile_rows * tile_cols, patches * RANK)
-    total = tile_rows * lax.axis_size("row") * tile_cols * lax.axis_size("col") * patches
-    out = finish(math.sqrt(float(total)), parts, flat)
+    out = finish(factor, parts, flat)
     return out.reshape(tile_rows, tile_cols, patches * RANK)
 
 

time: 107 us -> 115 us (1.075)
  starting transfers between devices: 39.3 us -> 45.5 us
  Pallas kernels: 30.4 us -> 31.8 us
    ppermute x7 -> x14, starting transfers between devices: 11.2 us -> 20.3 us  [summed_parts(): lax.ppermute(gram, axis, [(i, i ^ p) for i in range(size)])]
    ppermute x7 -> x14, waiting for transfers between devices: 7.49 us -> 14.4 us  [summed_parts(): lax.ppermute(gram, axis, [(i, i ^ p) for i in range(size)])]
    ppermute x12, waiting for transfers between devices: 27.6 us -> 20.7 us  [passed_along(): return lax.ppermute(shard, axis, pairs)]
    ppermute x12, starting transfers between devices: 28.1 us -> 25.2 us  [passed_along(): return lax.ppermute(shard, axis, pairs)]
    pallas_call x2 -> x5, Pallas kernels: 8.56 us -> 9.28 us  [the longest x1 3.8 us: own_units(): pl.pallas_call(units_kernel, in_specs=[HBM_SPEC, VMEM_SPEC, VMEM_SPEC, AN...]
  transfers between devices with their start and end apart: 19 -> 26, of which waited for: 12 -> 13; matrix products, arithmetic and copies ran while one was open for 2% -> 2% of each run, Pallas kernels for 21% -> 21%
where the time goes in v5:
time: 115 us
  starting transfers between devices  45.5 us (40%)
  waiting for transfers between devices  35.2 us (31%)
  Pallas kernels  31.8 us (28%)
  local copies, waits for them, and re-layouts  1.82 us (2%)
    ppermute x12, starting transfers between devices, passed_along(): return lax.ppermute(shard, axis, pairs)  25.2 us
    ppermute x12, waiting for transfers between devices, passed_along(): return lax.ppermute(shard, axis, pairs)  20.7 us
    ppermute x14, starting transfers between devices, summed_parts(): lax.ppermute(gram, axis, [(i, i ^ p) for i in range(size)])  20.3 us
    ppermute x14, waiting for transfers between devices, summed_parts(): lax.ppermute(gram, axis, [(i, i ^ p) for i in range(size)])  14.4 us
    pallas_call x2, Pallas kernels, cross_affinity(): pl.pallas_call(functools.partial(cross_kernel, n, stage), out_shape=(sds(...  5.74 us
    pallas_call x1, Pallas kernels, own_units(): pl.pallas_call(units_kernel, in_specs=[HBM_SPEC, VMEM_SPEC, VMEM_SPEC, AN...  3.8 us
    pallas_call x1, Pallas kernels, inside_affinity(): pl.pallas_call(functools.partial(inside_kernel, n), out_shape=(sds((n, bo...  3.49 us
    pallas_call x1, Pallas kernels, start_panel(): kernel_call(functools.partial(start_kernel, factor, len(parts)), (sds((ro...  3.48 us
  transfers between devices with their start and end apart: 26, of which 13 were waited for; matrix products, arithmetic and copies ran while one was open for 2% of the time, Pallas kernels for 21%

profile of v5, /device:TPU:0, one launch (start us, length us, event | category | flops | bytes accessed | tf_op | source)
XLA Modules:
  0.0 114.6 jit_solution(15377828408017602478)
XLA Ops:
  0.0 1.5 %shard_map.38 = f32[32,128]{1,0:T(8,128)S(1)} custom-call(f32[2,16,4096]{2,1,0:T(8,128)} %probe_ref.1), custom_call_target="tpu_custom_call" | custom-call | tf_op jit(solution)/shard_map/pallas_call | solution.py:138
  1.5 3.0 %collective-permute-start = (f32[32,128]{1,0:T(8,128)S(1)}, f32[32,128]{1,0:T(8,128)S(1)}, u32[]{:S(2)}, u32[]{:S(2)}) collective-permute-start(f32[32,128]{1,0:T(8,128)S(1)} %shard_map.38), channel_id=1, source_target_pairs={{0,8},{8,0},{16,24},{24,16},{1,9},{9,1},{17,25},{25,17},{2,10},{10... | collective-permute-start | bytes 49160 | tf_op jit(solution)/shard_map/ppermute | solution.py:776
  4.5 1.5 %collective-permute-start.1 = (f32[32,128]{1,0:T(8,128)S(1)}, f32[32,128]{1,0:T(8,128)S(1)}, u32[]{:S(2)}, u32[]{:S(2)}) collective-permute-start(f32[32,128]{1,0:T(8,128)S(1)} %shard_map.38), channel_id=1, source_target_pairs={{0,16},{8,24},{16,0},{24,8},{1,17},{9,25},{17,1},{25,9},{2,18},{10... | collective-permute-start | bytes 49160 | tf_op jit(solution)/shard_map/ppermute | solution.py:776
  6.1 0.0 collective-permute-start.2
  6.1 1.4 %shard_map.37.refs_0_ = bf16[8,64,1024]{2,1,0:T(8,128)(2,1)S(1)} custom-call(bf16[2,16,64,1024]{3,2,1,0:T(8,128)(2,1)} %x_ref.3, s32[2,16,64]{2,1,0:T(8,128)} %tissue_ref.5), custom_call_target="tpu_custom_call" | custom-call | tf_op jit(solution)/shard_map/pallas_call | solution.py:164
  7.5 0.0 copy-start
  7.5 0.8 collective-permute-done.1.refs_2_
  8.3 2.4 %collective-permute-done.2.refs_3_ = f32[32,128]{1,0:T(8,128)S(1)} collective-permute-done((f32[32,128]{1,0:T(8,128)S(1)}, f32[32,128]{1,0:T(8,128)S(1)}, u32[]{:S(2)}, u32[]{:S(2)}) %collective-permute-start.2) | collective-permute-done | bytes 16416 | tf_op jit(solution)/shard_map/ppermute | solution.py:776
  10.7 0.1 shard_map.39.after_ref
  10.8 1.3 %collective-permute-start.10 = (bf16[8,64,1024]{2,1,0:T(8,128)(2,1)S(1)}, bf16[8,64,1024]{2,1,0:T(8,128)(2,1)S(1)}, u32[]{:S(2)}, u32[]{:S(2)}) collective-permute-start(bf16[8,64,1024]{2,1,0:T(8,128)(2,1)S(1)} %shard_map.39.after_ref), channel_id=1, source_target_pairs={{8,0},{16,8},{24,16},{9,1},{17,9},{25,17},{10,2},{18,10},{26,18},{... | collective-permute-start | bytes 3145736 | tf_op jit(solution)/shard_map/ppermute | solution.py:783
  12.2 0.1 collective-permute-start.4
  12.2 1.2 %collective-permute-done.4 = f32[32,128]{1,0:T(8,128)S(1)} collective-permute-done((f32[32,128]{1,0:T(8,128)S(1)}, f32[32,128]{1,0:T(8,128)S(1)}, u32[]{:S(2)}, u32[]{:S(2)}) %collective-permute-start.4) | collective-permute-done | bytes 16416 | tf_op jit(solution)/shard_map/ppermute | solution.py:776
  13.4 1.6 %collective-permute-start.5 = (f32[32,128]{1,0:T(8,128)S(1)}, f32[32,128]{1,0:T(8,128)S(1)}, u32[]{:S(2)}, u32[]{:S(2)}) collective-permute-start(f32[32,128]{1,0:T(8,128)S(1)} %add.27.refs_2_.refs_0_), channel_id=1, source_target_pairs={{0,2},{1,3},{2,0},{3,1},{4,6},{5,7},{6,4},{7,5},{8,10},{9,11},{10,... | collective-permute-start | bytes 49160 | tf_op jit(solution)/shard_map/ppermute | solution.py:776
  15.0 2.6 %collective-permute-start.6 = (f32[32,128]{1,0:T(8,128)S(1)}, f32[32,128]{1,0:T(8,128)S(1)}, u32[]{:S(2)}, u32[]{:S(2)}) collective-permute-start(f32[32,128]{1,0:T(8,128)S(1)} %add.27.refs_2_.refs_0_), channel_id=1, source_target_pairs={{0,4},{1,5},{2,6},{3,7},{4,0},{5,1},{6,2},{7,3},{8,12},{9,13},{10,... | collective-permute-start | bytes 49160 | tf_op jit(solution)/shard_map/ppermute | solution.py:776
  17.6 0.2 collective-permute-start.7
  17.8 1.5 %reshape.9.probe_ref.refs_6_ = f32[2,16,64,64]{3,2,1,0:T(8,128)S(1)} reshape(f32[2,16,4096]{2,1,0:T(8,128)} %probe_ref.1) | data formatting | bytes 1048576 | tf_op jit(solution)/shard_map/reshape | solution.py:794
  19.3 3.8 %shard_map.40 = (bf16[2,4,64,1280]{3,2,1,0:T(8,128)(2,1)S(1)}, bf16[2,4,64,1280]{3,2,1,0:T(8,128)(2,1)S(1)}, bf16[8,64,1024]{2,1,0:T(8,128)(2,1)S(1)}, bf16[1536...) custom-call(bf16[2,16,64,1024]{3,2,1,0:T(8,128)(2,1)} %x_ref.3, s32[2,16,64]{2,1,0:T(8,128)S(1)} %copy-done, ...), custom_call_target="tpu_custom_call" | custom-call | tf_op jit(solution)/shard_map/pallas_call | solution.py:227
  23.1 0.0 collective-permute-done.5.refs_3_.refs_1_
  23.1 0.0 collective-permute-done.7.refs_5_.refs_3_
  23.1 0.3 shard_map.42
  23.5 1.4 %collective-permute-start.8 = (bf16[2,4,64,1280]{3,2,1,0:T(8,128)(2,1)S(1)}, bf16[2,4,64,1280]{3,2,1,0:T(8,128)(2,1)S(1)}, u32[]{:S(2)}, u32[]{:S(2)}) collective-permute-start(bf16[2,4,64,1280]{3,2,1,0:T(8,128)(2,1)S(1)} %get-tuple-element.55), channel_id=1, source_target_pairs={{0,1},{1,2},{2,3},{3,4},{4,5},{5,6},{6,7},{8,9},{9,10},{10,11},{11... | collective-permute-start | bytes 3932168 | tf_op jit(solution)/shard_map/ppermute | solution.py:783
  24.8 1.3 %collective-permute-start.9 = (bf16[2,4,64,1280]{3,2,1,0:T(8,128)(2,1)S(1)}, bf16[2,4,64,1280]{3,2,1,0:T(8,128)(2,1)S(1)}, u32[]{:S(2)}, u32[]{:S(2)}) collective-permute-start(bf16[2,4,64,1280]{3,2,1,0:T(8,128)(2,1)S(1)} %get-tuple-element.56), channel_id=1, source_target_pairs={{1,0},{2,1},{3,2},{4,3},{5,4},{6,5},{7,6},{9,8},{10,9},{11,10},{12... | collective-permute-start | bytes 3932168 | tf_op jit(solution)/shard_map/ppermute | solution.py:783
  26.1 1.3 %collective-permute-start.3 = (bf16[8,64,1024]{2,1,0:T(8,128)(2,1)S(1)}, bf16[8,64,1024]{2,1,0:T(8,128)(2,1)S(1)}, u32[]{:S(2)}, u32[]{:S(2)}) collective-permute-start(bf16[8,64,1024]{2,1,0:T(8,128)(2,1)S(1)} %get-tuple-element.48), channel_id=1, source_target_pairs={{8,0},{16,8},{24,16},{9,1},{17,9},{25,17},{10,2},{18,10},{26,18},{... | collective-permute-start | bytes 3145736 | tf_op jit(solution)/shard_map/ppermute | solution.py:783
  27.4 3.5 %shard_map.41 = (bf16[24,128,384]{2,1,0:T(8,128)(2,1)S(1)}, f32[2,128,128]{2,1,0:T(8,128)S(1)}) custom-call(bf16[1536,1024]{1,0:T(8,128)(2,1)S(1)} %get-tuple-element.49.unit0_ref.start0_ref, bf16[1536,1024]{1,0:T(8,128)(2,1)S(1)} %get-tuple-element.50.unit1_ref.start1_ref), custom_call_target="tpu_custom_call" | custom-call | tf_op jit(solution)/shard_map/pallas_call | solution.py:277
  30.9 7.4 %collective-permute-done.10.be_ref.refs_1_ = bf16[8,64,1024]{2,1,0:T(8,128)(2,1)S(1)} collective-permute-done((bf16[8,64,1024]{2,1,0:T(8,128)(2,1)S(1)}, bf16[8,64,1024]{2,1,0:T(8,128)(2,1)S(1)}, u32[]{:S(2)}, u32[]{:S(2)}) %collective-permute-start.10) | collective-permute-done | bytes 1048608 | tf_op jit(solution)/shard_map/ppermute | solution.py:783
  38.3 0.1 shard_map.43
  38.4 1.3 %collective-permute-start.11 = (bf16[4,64,1024]{2,1,0:T(8,128)(2,1)S(1)}, bf16[4,64,1024]{2,1,0:T(8,128)(2,1)S(1)}, u32[]{:S(2)}, u32[]{:S(2)}) collective-permute-start(bf16[4,64,1024]{2,1,0:T(8,128)(2,1)S(1)} %get-tuple-element.61), channel_id=1, source_target_pairs={{0,1},{1,2},{2,3},{3,4},{4,5},{5,6},{6,7},{8,9},{9,10},{10,11},{11... | collective-permute-start | bytes 1572872 | tf_op jit(solution)/shard_map/ppermute | solution.py:783
  39.7 1.5 %collective-permute-start.12 = (bf16[4,64,1024]{2,1,0:T(8,128)(2,1)S(1)}, bf16[4,64,1024]{2,1,0:T(8,128)(2,1)S(1)}, u32[]{:S(2)}, u32[]{:S(2)}) collective-permute-start(bf16[4,64,1024]{2,1,0:T(8,128)(2,1)S(1)} %get-tuple-element.57.after_ref), channel_id=1, source_target_pairs={{1,0},{2,1},{3,2},{4,3},{5,4},{6,5},{7,6},{9,8},{10,9},{11,10},{12... | collective-permute-start | bytes 1572872 | tf_op jit(solution)/shard_map/ppermute | solution.py:783
  41.2 3.3 %shard_map.44 = (bf16[1536,1024]{1,0:T(8,128)(2,1)S(1)}, bf16[1536,1024]{1,0:T(8,128)(2,1)S(1)}, bf16[24,128,384]{2,1,0:T(8,128)(2,1)S(1)}, f32[3,128,128]{2,1,0:T(8,128)S(1)}) custom-call(bf16[1536,1024]{1,0:T(8,128)(2,1)S(1)} %get-tuple-element.49.unit0_ref.start0_ref, ...), custom_call_target="tpu_custom_call", output_to_operand_aliasing={{0}: (0, {}), {1}: (1, {}), {2}: (2, {})} | custom-call | tf_op jit(solution)/shard_map/pallas_call | solution.py:330
  44.5 3.5 %shard_map.45 = (f32[2,24,64,64]{3,2,1,0:T(8,128)S(1)}, bf16[832,128]{1,0:T(8,128)(2,1)S(1)}) custom-call(f32[32,128]{1,0:T(8,128)S(1)} %add.27.refs_2_.refs_0_, f32[32,128]{1,0:T(8,128)S(1)} %collective-permute-done.5.refs_3_.refs_1_, f32[32,128]{1,0:T(8,128)S(1)} %collective-permute-done.6.refs_4_.refs_2_, ...), custom_call_target="tpu_custom_call" | custom-call | tf_op jit(solution)/shard_map/pallas_call | solution.py:366
  48.0 1.3 %collective-permute-start.14 = (bf16[832,128]{1,0:T(8,128)(2,1)S(1)}, bf16[832,128]{1,0:T(8,128)(2,1)S(1)}, u32[]{:S(2)}, u32[]{:S(2)}) collective-permute-start(bf16[832,128]{1,0:T(8,128)(2,1)S(1)} %get-tuple-element.69), channel_id=1, source_target_pairs={{8,0},{16,8},{24,16},{9,1},{17,9},{25,17},{10,2},{18,10},{26,18},{... | collective-permute-start | bytes 638984 | tf_op jit(solution)/shard_map/ppermute | solution.py:783
  49.3 0.0 collective-permute-done.12.refs_2_
  49.4 3.0 %shard_map.46 = (bf16[11,128,256]{2,1,0:T(8,128)(2,1)S(1)}, bf16[11,128,256]{2,1,0:T(8,128)(2,1)S(1)}, f32[3,64,128]{2,1,0:T(8,128)S(1)}, bf16[24,64,64]{2,1,0:T...) custom-call(bf16[4,64,1024]{2,1,0:T(8,128)(2,1)S(1)} %collective-permute-done.11.refs_0_, ...), custom_call_target="tpu_custom_call" | custom-call | tf_op jit(solution)/shard_map/pallas_call | solution.py:507
  52.4 6.8 %collective-permute-done.3.refs_0_ = bf16[8,64,1024]{2,1,0:T(8,128)(2,1)S(1)} collective-permute-done((bf16[8,64,1024]{2,1,0:T(8,128)(2,1)S(1)}, bf16[8,64,1024]{2,1,0:T(8,128)(2,1)S(1)}, u32[]{:S(2)}, u32[]{:S(2)}) %collective-permute-start.3) | collective-permute-done | bytes 1048608 | tf_op jit(solution)/shard_map/ppermute | solution.py:783
  59.1 2.7 %shard_map.47 = (bf16[11,128,256]{2,1,0:T(8,128)(2,1)S(1)}, bf16[11,128,256]{2,1,0:T(8,128)(2,1)S(1)}, f32[3,64,128]{2,1,0:T(8,128)S(1)}, bf16[24,64,64]{2,1,0:T...) custom-call(bf16[8,64,1024]{2,1,0:T(8,128)(2,1)S(1)} %collective-per, ...), custom_call_target="tpu_custom_call", output_to_operand_aliasing={{0}: (4, {}), {1}: (5, {}), {2}: (6, {}), {3}: (7, {}), {4}... | custom-call | tf_op jit(solution)/shard_map/pallas_call | solution.py:507
  61.9 2.8 %collective-permute-start.13 = (bf16[768,128]{1,0:T(8,128)(2,1)S(1)}, bf16[768,128]{1,0:T(8,128)(2,1)S(1)}, u32[]{:S(2)}, u32[]{:S(2)}) collective-permute-start(bf16[768,128]{1,0:T(8,128)(2,1)S(1)} %get-tuple-element.68), channel_id=1, source_target_pairs={{0,8},{8,16},{16,24},{1,9},{9,17},{17,25},{2,10},{10,18},{18,26},{... | collective-permute-start | bytes 589832 | tf_op jit(solution)/shard_map/ppermute | solution.py:783
  64.7 1.4 %shard_map.48 = (f32[24,128,64]{2,1,0:T(8,128)S(1)}, f32[24,64,64]{2,1,0:T(8,128)S(1)}, f32[24,64,64]{2,1,0:T(8,128)S(1)}, f32[24,64,64]{2,1,0:T(8,128)S(1)}) custom-call(bf16[832,128]{1,0:T(8,128)(2,1)S(1)} %collective-permute-done.14.got_ref, f32[3,64,128]{2,1,0:T(8,128)S(1)} %get-tuple-element.70.sum_ref, ...), custom_call_target="tpu_custom_call" | custom-call | tf_op jit(solution)/shard_map/pallas_call | solution.py:547
  66.1 2.6 %collective-permute-done.13.got_ref = bf16[768,128]{1,0:T(8,128)(2,1)S(1)} collective-permute-done((bf16[768,128]{1,0:T(8,128)(2,1)S(1)}, bf16[768,128]{1,0:T(8,128)(2,1)S(1)}, u32[]{:S(2)}, u32[]{:S(2)}) %collective-permute-start.13) | collective-permute-done | bytes 196640 | tf_op jit(solution)/shard_map/ppermute | solution.py:783
  68.8 1.0 shard_map.49
  69.7 1.3 %collective-permute-start.15 = (bf16[640,128]{1,0:T(8,128)(2,1)S(1)}, bf16[640,128]{1,0:T(8,128)(2,1)S(1)}, u32[]{:S(2)}, u32[]{:S(2)}) collective-permute-start(bf16[640,128]{1,0:T(8,128)(2,1)S(1)} %get-tuple-element.79), channel_id=1, source_target_pairs={{8,0},{16,8},{24,16},{9,1},{17,9},{25,17},{10,2},{18,10},{26,18},{... | collective-permute-start | bytes 491528 | tf_op jit(solution)/shard_map/ppermute | solution.py:783
  71.0 5.0 %collective-permute-start.16 = (bf16[576,128]{1,0:T(8,128)(2,1)S(1)}, bf16[576,128]{1,0:T(8,128)(2,1)S(1)}, u32[]{:S(2)}, u32[]{:S(2)}) collective-permute-start(bf16[576,128]{1,0:T(8,128)(2,1)S(1)} %get-tuple-element.80), channel_id=1, source_target_pairs={{0,8},{8,16},{16,24},{1,9},{9,17},{17,25},{2,10},{10,18},{18,26},{... | collective-permute-start | bytes 442376 | tf_op jit(solution)/shard_map/ppermute | solution.py:783
  76.1 0.6 shard_map.50.z_ref
  76.7 2.0 %collective-permute-done.16.above_ref = bf16[576,128]{1,0:T(8,128)(2,1)S(1)} collective-permute-done((bf16[576,128]{1,0:T(8,128)(2,1)S(1)}, bf16[576,128]{1,0:T(8,128)(2,1)S(1)}, u32[]{:S(2)}, u32[]{:S(2)}) %collective-permute-start.16) | collective-permute-done | bytes 147488 | tf_op jit(solution)/shard_map/ppermute | solution.py:783
  78.7 1.1 shard_map.51
  79.8 1.3 %collective-permute-start.17 = (bf16[576,128]{1,0:T(8,128)(2,1)S(1)}, bf16[576,128]{1,0:T(8,128)(2,1)S(1)}, u32[]{:S(2)}, u32[]{:S(2)}) collective-permute-start(bf16[576,128]{1,0:T(8,128)(2,1)S(1)} %get-tuple-element.85), channel_id=1, source_target_pairs={{8,0},{16,8},{24,16},{9,1},{17,9},{25,17},{10,2},{18,10},{26,18},{... | collective-permute-start | bytes 442376 | tf_op jit(solution)/shard_map/ppermute | solution.py:783
  81.1 5.5 %collective-permute-start.18 = (bf16[512,128]{1,0:T(8,128)(2,1)S(1)}, bf16[512,128]{1,0:T(8,128)(2,1)S(1)}, u32[]{:S(2)}, u32[]{:S(2)}) collective-permute-start(bf16[512,128]{1,0:T(8,128)(2,1)S(1)} %get-tuple-element.86), channel_id=1, source_target_pairs={{0,8},{8,16},{16,24},{1,9},{9,17},{17,25},{2,10},{10,18},{18,26},{... | collective-permute-start | bytes 393224 | tf_op jit(solution)/shard_map/ppermute | solution.py:783
  86.6 0.6 shard_map.52.z_ref
  87.1 1.9 %collective-permute-done.18.above_ref = bf16[512,128]{1,0:T(8,128)(2,1)S(1)} collective-permute-done((bf16[512,128]{1,0:T(8,128)(2,1)S(1)}, bf16[512,128]{1,0:T(8,128)(2,1)S(1)}, u32[]{:S(2)}, u32[]{:S(2)}) %collective-permute-start.18) | collective-permute-done | bytes 131104 | tf_op jit(solution)/shard_map/ppermute | solution.py:783
  89.1 1.0 shard_map.53
  90.0 0.0 collective-permute-start.19
  90.1 1.2 %collective-permute-done.19 = f32[32,128]{1,0:T(8,128)S(1)} collective-permute-done((f32[32,128]{1,0:T(8,128)S(1)}, f32[32,128]{1,0:T(8,128)S(1)}, u32[]{:S(2)}, u32[]{:S(2)}) %collective-permute-start.19) | collective-permute-done | bytes 16416 | tf_op jit(solution)/shard_map/ppermute | solution.py:776
  91.3 3.9 %collective-permute-start.21 = (f32[32,128]{1,0:T(8,128)S(1)}, f32[32,128]{1,0:T(8,128)S(1)}, u32[]{:S(2)}, u32[]{:S(2)}) collective-permute-start(f32[32,128]{1,0:T(8,128)S(1)} %add.28), channel_id=1, source_target_pairs={{0,4},{1,5},{2,6},{3,7},{4,0},{5,1},{6,2},{7,3},{8,12},{9,13},{10,... | collective-permute-start | bytes 49160 | tf_op jit(solution)/shard_map/ppermute | solution.py:776
  95.2 0.1 collective-permute-start.22
  95.3 0.5 collective-permute-start.20
  95.8 1.3 %collective-permute-done.21 = f32[32,128]{1,0:T(8,128)S(1)} collective-permute-done((f32[32,128]{1,0:T(8,128)S(1)}, f32[32,128]{1,0:T(8,128)S(1)}, u32[]{:S(2)}, u32[]{:S(2)}) %collective-permute-start.21) | collective-permute-done | bytes 16416 | tf_op jit(solution)/shard_map/ppermute | solution.py:776
  97.1 3.6 %collective-permute-done.22 = f32[32,128]{1,0:T(8,128)S(1)} collective-permute-done((f32[32,128]{1,0:T(8,128)S(1)}, f32[32,128]{1,0:T(8,128)S(1)}, u32[]{:S(2)}, u32[]{:S(2)}) %collective-permute-start.22) | collective-permute-done | bytes 16416 | tf_op jit(solution)/shard_map/ppermute | solution.py:776
  100.7 0.0 collective-permute-done.20
  100.7 3.3 %collective-permute-start.23 = (f32[32,128]{1,0:T(8,128)S(1)}, f32[32,128]{1,0:T(8,128)S(1)}, u32[]{:S(2)}, u32[]{:S(2)}) collective-permute-start(f32[32,128]{1,0:T(8,128)S(1)} %add_add_fusion.refs_0_), channel_id=1, source_target_pairs={{0,8},{8,0},{16,24},{24,16},{1,9},{9,1},{17,25},{25,17},{2,10},{10... | collective-permute-start | bytes 49160 | tf_op jit(solution)/shard_map/ppermute | solution.py:776
  104.1 3.0 %collective-permute-start.24 = (f32[32,128]{1,0:T(8,128)S(1)}, f32[32,128]{1,0:T(8,128)S(1)}, u32[]{:S(2)}, u32[]{:S(2)}) collective-permute-start(f32[32,128]{1,0:T(8,128)S(1)} %add_add_fusion.refs_0_), channel_id=1, source_target_pairs={{0,16},{8,24},{16,0},{24,8},{1,17},{9,25},{17,1},{25,9},{2,18},{10... | collective-permute-start | bytes 49160 | tf_op jit(solution)/shard_map/ppermute | solution.py:776
  107.1 0.3 collective-permute-start.25
  107.4 0.4 reshape.10.refs_4_
  107.8 1.0 collective-permute-done.24.refs_2_
  108.8 2.9 %collective-permute-done.25.refs_3_ = f32[32,128]{1,0:T(8,128)S(1)} collective-permute-done((f32[32,128]{1,0:T(8,128)S(1)}, f32[32,128]{1,0:T(8,128)S(1)}, u32[]{:S(2)}, u32[]{:S(2)}) %collective-permute-start.25) | collective-permute-done | bytes 16416 | tf_op jit(solution)/shard_map/ppermute | solution.py:776
  111.7 2.9 %shard_map.54 = f32[32,4096]{1,0:T(8,128)} custom-call(f32[32,128]{1,0:T(8,128)S(1)} %add_add_fusion.refs_0_, f32[32,128]{1,0:T(8,128)S(1)} %collective-permute-done.23.refs_1_, f32[32,128]{1,0:T(8,128)S(1)} %collective-permute-done.24.refs_2_, f32[32,128]{1,0:T(8,128)S(1)} %collective-permute-done.25.refs_3_, f32[32,4096]{1,0:T(8,128)S(1)} %reshape.10.refs_4_), custom_call_target="tpu_custom_call" | custom-call | tf_op jit(solution)/shard_map/pallas_call | solution.py:749
  (14 shorter events, 0.1 us)
Async XLA Ops:
  1.5 5.9 %collective-permute-start = (f32[32,128]{1,0:T(8,128)S(1)}, f32[32,128]{1,0:T(8,128)S(1)}, u32[]{:S(2)}, u32[]{:S(2)}) collective-permute-start(f32[32,128]{1,0:T(8,128)S(1)} %shard_map.38), channel_id=1, source_target_pairs={{0,8},{8,0},{16,24},{24,16},{1,9},{9,1},{17,25},{25,17},{2,10},{10... | collective-permute-start | bytes 49160 | tf_op jit(solution)/shard_map/ppermute | solution.py:776
  4.5 3.7 %collective-permute-start.1 = (f32[32,128]{1,0:T(8,128)S(1)}, f32[32,128]{1,0:T(8,128)S(1)}, u32[]{:S(2)}, u32[]{:S(2)}) collective-permute-start(f32[32,128]{1,0:T(8,128)S(1)} %shard_map.38), channel_id=1, source_target_pairs={{0,16},{8,24},{16,0},{24,8},{1,17},{9,25},{17,1},{25,9},{2,18},{10... | collective-permute-start | bytes 49160 | tf_op jit(solution)/shard_map/ppermute | solution.py:776
  6.1 4.6 %collective-permute-start.2 = (f32[32,128]{1,0:T(8,128)S(1)}, f32[32,128]{1,0:T(8,128)S(1)}, u32[]{:S(2)}, u32[]{:S(2)}) collective-permute-start(f32[32,128]{1,0:T(8,128)S(1)} %shard_map.38), channel_id=1, source_target_pairs={{0,24},{8,16},{16,8},{24,0},{1,25},{9,17},{17,9},{25,1},{2,26},{10... | collective-permute-start | bytes 49160 | tf_op jit(solution)/shard_map/ppermute | solution.py:776
  7.5 11.8 %copy-start = (s32[2,16,64]{2,1,0:T(8,128)S(1)}, s32[2,16,64]{2,1,0:T(8,128)}, u32[]{:S(2)}) copy-start(s32[2,16,64]{2,1,0:T(8,128)} %tissue_ref.5) | copy-start | bytes 24580
  10.8 27.5 %collective-permute-start.10 = (bf16[8,64,1024]{2,1,0:T(8,128)(2,1)S(1)}, bf16[8,64,1024]{2,1,0:T(8,128)(2,1)S(1)}, u32[]{:S(2)}, u32[]{:S(2)}) collective-permute-start(bf16[8,64,1024]{2,1,0:T(8,128)(2,1)S(1)} %shard_map.39.after_ref), channel_id=1, source_target_pairs={{8,0},{16,8},{24,16},{9,1},{17,9},{25,17},{10,2},{18,10},{26,18},{... | collective-permute-start | bytes 3145736 | tf_op jit(solution)/shard_map/ppermute | solution.py:783
  12.2 1.2 %collective-permute-start.4 = (f32[32,128]{1,0:T(8,128)S(1)}, f32[32,128]{1,0:T(8,128)S(1)}, u32[]{:S(2)}, u32[]{:S(2)}) collective-permute-start(f32[32,128]{1,0:T(8,128)S(1)} %add_add_fusion.1), channel_id=1, source_target_pairs={{0,1},{1,0},{2,3},{3,2},{4,5},{5,4},{6,7},{7,6},{8,9},{9,8},{10,11... | collective-permute-start | bytes 49160 | tf_op jit(solution)/shard_map/ppermute | solution.py:776
  13.4 9.7 %collective-permute-start.5 = (f32[32,128]{1,0:T(8,128)S(1)}, f32[32,128]{1,0:T(8,128)S(1)}, u32[]{:S(2)}, u32[]{:S(2)}) collective-permute-start(f32[32,128]{1,0:T(8,128)S(1)} %add.27.refs_2_.refs_0_), channel_id=1, source_target_pairs={{0,2},{1,3},{2,0},{3,1},{4,6},{5,7},{6,4},{7,5},{8,10},{9,11},{10,... | collective-permute-start | bytes 49160 | tf_op jit(solution)/shard_map/ppermute | solution.py:776
  15.0 8.1 %collective-permute-start.6 = (f32[32,128]{1,0:T(8,128)S(1)}, f32[32,128]{1,0:T(8,128)S(1)}, u32[]{:S(2)}, u32[]{:S(2)}) collective-permute-start(f32[32,128]{1,0:T(8,128)S(1)} %add.27.refs_2_.refs_0_), channel_id=1, source_target_pairs={{0,4},{1,5},{2,6},{3,7},{4,0},{5,1},{6,2},{7,3},{8,12},{9,13},{10,... | collective-permute-start | bytes 49160 | tf_op jit(solution)/shard_map/ppermute | solution.py:776
  17.6 5.5 %collective-permute-start.7 = (f32[32,128]{1,0:T(8,128)S(1)}, f32[32,128]{1,0:T(8,128)S(1)}, u32[]{:S(2)}, u32[]{:S(2)}) collective-permute-start(f32[32,128]{1,0:T(8,128)S(1)} %add.27.refs_2_.refs_0_), channel_id=1, source_target_pairs={{0,6},{1,7},{2,4},{3,5},{4,2},{5,3},{6,0},{7,1},{8,14},{9,15},{10,... | collective-permute-start | bytes 49160 | tf_op jit(solution)/shard_map/ppermute | solution.py:776
  23.5 17.7 %collective-permute-start.8 = (bf16[2,4,64,1280]{3,2,1,0:T(8,128)(2,1)S(1)}, bf16[2,4,64,1280]{3,2,1,0:T(8,128)(2,1)S(1)}, u32[]{:S(2)}, u32[]{:S(2)}) collective-permute-start(bf16[2,4,64,1280]{3,2,1,0:T(8,128)(2,1)S(1)} %get-tuple-element.55), channel_id=1, source_target_pairs={{0,1},{1,2},{2,3},{3,4},{4,5},{5,6},{6,7},{8,9},{9,10},{10,11},{11... | collective-permute-start | bytes 3932168 | tf_op jit(solution)/shard_map/ppermute | solution.py:783
  24.8 16.4 %collective-permute-start.9 = (bf16[2,4,64,1280]{3,2,1,0:T(8,128)(2,1)S(1)}, bf16[2,4,64,1280]{3,2,1,0:T(8,128)(2,1)S(1)}, u32[]{:S(2)}, u32[]{:S(2)}) collective-permute-start(bf16[2,4,64,1280]{3,2,1,0:T(8,128)(2,1)S(1)} %get-tuple-element.56), channel_id=1, source_target_pairs={{1,0},{2,1},{3,2},{4,3},{5,4},{6,5},{7,6},{9,8},{10,9},{11,10},{12... | collective-permute-start | bytes 3932168 | tf_op jit(solution)/shard_map/ppermute | solution.py:783
  26.1 33.0 %collective-permute-start.3 = (bf16[8,64,1024]{2,1,0:T(8,128)(2,1)S(1)}, bf16[8,64,1024]{2,1,0:T(8,128)(2,1)S(1)}, u32[]{:S(2)}, u32[]{:S(2)}) collective-permute-start(bf16[8,64,1024]{2,1,0:T(8,128)(2,1)S(1)} %get-tuple-element.48), channel_id=1, source_target_pairs={{8,0},{16,8},{24,16},{9,1},{17,9},{25,17},{10,2},{18,10},{26,18},{... | collective-permute-start | bytes 3145736 | tf_op jit(solution)/shard_map/ppermute | solution.py:783
  38.4 11.0 %collective-permute-start.11 = (bf16[4,64,1024]{2,1,0:T(8,128)(2,1)S(1)}, bf16[4,64,1024]{2,1,0:T(8,128)(2,1)S(1)}, u32[]{:S(2)}, u32[]{:S(2)}) collective-permute-start(bf16[4,64,1024]{2,1,0:T(8,128)(2,1)S(1)} %get-tuple-element.61), channel_id=1, source_target_pairs={{0,1},{1,2},{2,3},{3,4},{4,5},{5,6},{6,7},{8,9},{9,10},{10,11},{11... | collective-permute-start | bytes 1572872 | tf_op jit(solution)/shard_map/ppermute | solution.py:783
  39.7 9.6 %collective-permute-start.12 = (bf16[4,64,1024]{2,1,0:T(8,128)(2,1)S(1)}, bf16[4,64,1024]{2,1,0:T(8,128)(2,1)S(1)}, u32[]{:S(2)}, u32[]{:S(2)}) collective-permute-start(bf16[4,64,1024]{2,1,0:T(8,128)(2,1)S(1)} %get-tuple-element.57.after_ref), channel_id=1, source_target_pairs={{1,0},{2,1},{3,2},{4,3},{5,4},{6,5},{7,6},{9,8},{10,9},{11,10},{12... | collective-permute-start | bytes 1572872 | tf_op jit(solution)/shard_map/ppermute | solution.py:783
  48.0 16.7 %collective-permute-start.14 = (bf16[832,128]{1,0:T(8,128)(2,1)S(1)}, bf16[832,128]{1,0:T(8,128)(2,1)S(1)}, u32[]{:S(2)}, u32[]{:S(2)}) collective-permute-start(bf16[832,128]{1,0:T(8,128)(2,1)S(1)} %get-tuple-element.69), channel_id=1, source_target_pairs={{8,0},{16,8},{24,16},{9,1},{17,9},{25,17},{10,2},{18,10},{26,18},{... | collective-permute-start | bytes 638984 | tf_op jit(solution)/shard_map/ppermute | solution.py:783
  61.9 6.9 %collective-permute-start.13 = (bf16[768,128]{1,0:T(8,128)(2,1)S(1)}, bf16[768,128]{1,0:T(8,128)(2,1)S(1)}, u32[]{:S(2)}, u32[]{:S(2)}) collective-permute-start(bf16[768,128]{1,0:T(8,128)(2,1)S(1)} %get-tuple-element.68), channel_id=1, source_target_pairs={{0,8},{8,16},{16,24},{1,9},{9,17},{17,25},{2,10},{10,18},{18,26},{... | collective-permute-start | bytes 589832 | tf_op jit(solution)/shard_map/ppermute | solution.py:783
  69.7 9.0 %collective-permute-start.15 = (bf16[640,128]{1,0:T(8,128)(2,1)S(1)}, bf16[640,128]{1,0:T(8,128)(2,1)S(1)}, u32[]{:S(2)}, u32[]{:S(2)}) collective-permute-start(bf16[640,128]{1,0:T(8,128)(2,1)S(1)} %get-tuple-element.79), channel_id=1, source_target_pairs={{8,0},{16,8},{24,16},{9,1},{17,9},{25,17},{10,2},{18,10},{26,18},{... | collective-permute-start | bytes 491528 | tf_op jit(solution)/shard_map/ppermute | solution.py:783
  71.0 7.7 %collective-permute-start.16 = (bf16[576,128]{1,0:T(8,128)(2,1)S(1)}, bf16[576,128]{1,0:T(8,128)(2,1)S(1)}, u32[]{:S(2)}, u32[]{:S(2)}) collective-permute-start(bf16[576,128]{1,0:T(8,128)(2,1)S(1)} %get-tuple-element.80), channel_id=1, source_target_pairs={{0,8},{8,16},{16,24},{1,9},{9,17},{17,25},{2,10},{10,18},{18,26},{... | collective-permute-start | bytes 442376 | tf_op jit(solution)/shard_map/ppermute | solution.py:783
  79.8 9.3 %collective-permute-start.17 = (bf16[576,128]{1,0:T(8,128)(2,1)S(1)}, bf16[576,128]{1,0:T(8,128)(2,1)S(1)}, u32[]{:S(2)}, u32[]{:S(2)}) collective-permute-start(bf16[576,128]{1,0:T(8,128)(2,1)S(1)} %get-tuple-element.85), channel_id=1, source_target_pairs={{8,0},{16,8},{24,16},{9,1},{17,9},{25,17},{10,2},{18,10},{26,18},{... | collective-permute-start | bytes 442376 | tf_op jit(solution)/shard_map/ppermute | solution.py:783
  81.1 8.0 %collective-permute-start.18 = (bf16[512,128]{1,0:T(8,128)(2,1)S(1)}, bf16[512,128]{1,0:T(8,128)(2,1)S(1)}, u32[]{:S(2)}, u32[]{:S(2)}) collective-permute-start(bf16[512,128]{1,0:T(8,128)(2,1)S(1)} %get-tuple-element.86), channel_id=1, source_target_pairs={{0,8},{8,16},{16,24},{1,9},{9,17},{17,25},{2,10},{10,18},{18,26},{... | collective-permute-start | bytes 393224 | tf_op jit(solution)/shard_map/ppermute | solution.py:783
  90.0 1.2 %collective-permute-start.19 = (f32[32,128]{1,0:T(8,128)S(1)}, f32[32,128]{1,0:T(8,128)S(1)}, u32[]{:S(2)}, u32[]{:S(2)}) collective-permute-start(f32[32,128]{1,0:T(8,128)S(1)} %get-tuple-element.89), channel_id=1, source_target_pairs={{0,1},{1,0},{2,3},{3,2},{4,5},{5,4},{6,7},{7,6},{8,9},{9,8},{10,11... | collective-permute-start | bytes 49160 | tf_op jit(solution)/shard_map/ppermute | solution.py:776
  91.3 5.8 %collective-permute-start.21 = (f32[32,128]{1,0:T(8,128)S(1)}, f32[32,128]{1,0:T(8,128)S(1)}, u32[]{:S(2)}, u32[]{:S(2)}) collective-permute-start(f32[32,128]{1,0:T(8,128)S(1)} %add.28), channel_id=1, source_target_pairs={{0,4},{1,5},{2,6},{3,7},{4,0},{5,1},{6,2},{7,3},{8,12},{9,13},{10,... | collective-permute-start | bytes 49160 | tf_op jit(solution)/shard_map/ppermute | solution.py:776
  95.2 5.5 %collective-permute-start.22 = (f32[32,128]{1,0:T(8,128)S(1)}, f32[32,128]{1,0:T(8,128)S(1)}, u32[]{:S(2)}, u32[]{:S(2)}) collective-permute-start(f32[32,128]{1,0:T(8,128)S(1)} %add.28), channel_id=1, source_target_pairs={{0,6},{1,7},{2,4},{3,5},{4,2},{5,3},{6,0},{7,1},{8,14},{9,15},{10,... | collective-permute-start | bytes 49160 | tf_op jit(solution)/shard_map/ppermute | solution.py:776
  95.3 5.4 %collective-permute-start.20 = (f32[32,128]{1,0:T(8,128)S(1)}, f32[32,128]{1,0:T(8,128)S(1)}, u32[]{:S(2)}, u32[]{:S(2)}) collective-permute-start(f32[32,128]{1,0:T(8,128)S(1)} %add.28), channel_id=1, source_target_pairs={{0,2},{1,3},{2,0},{3,1},{4,6},{5,7},{6,4},{7,5},{8,10},{9,11},{10,... | collective-permute-start | bytes 49160 | tf_op jit(solution)/shard_map/ppermute | solution.py:776
  100.7 7.1 %collective-permute-start.23 = (f32[32,128]{1,0:T(8,128)S(1)}, f32[32,128]{1,0:T(8,128)S(1)}, u32[]{:S(2)}, u32[]{:S(2)}) collective-permute-start(f32[32,128]{1,0:T(8,128)S(1)} %add_add_fusion.refs_0_), channel_id=1, source_target_pairs={{0,8},{8,0},{16,24},{24,16},{1,9},{9,1},{17,25},{25,17},{2,10},{10... | collective-permute-start | bytes 49160 | tf_op jit(solution)/shard_map/ppermute | solution.py:776
  104.1 4.7 %collective-permute-start.24 = (f32[32,128]{1,0:T(8,128)S(1)}, f32[32,128]{1,0:T(8,128)S(1)}, u32[]{:S(2)}, u32[]{:S(2)}) collective-permute-start(f32[32,128]{1,0:T(8,128)S(1)} %add_add_fusion.refs_0_), channel_id=1, source_target_pairs={{0,16},{8,24},{16,0},{24,8},{1,17},{9,25},{17,1},{25,9},{2,18},{10... | collective-permute-start | bytes 49160 | tf_op jit(solution)/shard_map/ppermute | solution.py:776
  107.1 4.6 %collective-permute-start.25 = (f32[32,128]{1,0:T(8,128)S(1)}, f32[32,128]{1,0:T(8,128)S(1)}, u32[]{:S(2)}, u32[]{:S(2)}) collective-permute-start(f32[32,128]{1,0:T(8,128)S(1)} %add_add_fusion.refs_0_), channel_id=1, source_target_pairs={{0,24},{8,16},{16,8},{24,0},{1,25},{9,17},{17,9},{25,1},{2,26},{10... | collective-permute-start | bytes 49160 | tf_op jit(solution)/shard_map/ppermute | solution.py:776

commit v6 on v5

--- a/solution.py
+++ b/solution.py
@@ -83,6 +83,30 @@
     high, middle = pair_of(values)
     low = (values - high.astype(f32) - middle.astype(f32)).astype(bf16)
     return jnp.concatenate([high, middle, low, jnp.zeros_like(low)], axis=1)
+
+
+def basis_rows(table):
+    parts = four_of(table)
+    return jnp.concatenate([parts[:, : 2 * RANK], packed(parts[:, 2 * RANK : 3 * RANK])], axis=0)
+
+
+def basis_of(rows):
+    rows = rows.astype(f32)
+    return rows[:RANK, :RANK] + rows[:RANK, RANK:] + unpacked(rows[RANK:])
+
+
+def turn_of(theirs, inverse):
+    return lax.dot_general(
+        theirs, inverse, ABT, precision=lax.Precision.HIGHEST, preferred_element_type=f32
+    )
+
+
+def turned(tiles, turn):
+    patch = tiles[0].shape[0]
+    stack = jnp.concatenate(tiles, axis=0).astype(bf16)
+    high, low = turn
+    result = jnp.dot(stack, high, preferred_element_type=f32) + jnp.dot(stack, low, preferred_element_type=f32)
+    return [result[i * patch : (i + 1) * patch] for i in range(len(tiles))]
 
 
 def whole_of(parts):
@@ -321,7 +345,7 @@
     stat_ref[2] = mask
 
 def payload_rows(columns, patch):
-    return columns * patch // 2 + 2 * patch
+    return columns * patch // 2 + patch // 2 + RANK * 3 // 2
 
 
 def outside_affinity(unit0, unit1, m, tissue, sums, xl, xr, after):
@@ -338,12 +362,14 @@
 
 
 def start_kernel(factor, count, *refs):
-    parts, (stat_ref, xl_ref, p_ref, xr_ref, panel_ref, pay_ref) = refs[:count], refs[count:]
+    parts, (stat_ref, xl_ref, p_ref, xr_ref, panel_ref, pay_ref, base_ref) = refs[:count], refs[count:]
     rows, cols, patch, _ = p_ref.shape
     n = cols + 2 * GHOST
     half = patch // 2
     width = xl_ref.shape[3] - 4 * RANK
-    inverse = factor * inverse_factor(unpacked(balanced([part[...] for part in parts])), True)
+    inverse, root = inverse_factor(unpacked(balanced([part[...] for part in parts])), True)
+    inverse, root = factor * inverse, root / factor
+    base_ref[0], base_ref[1] = inverse, root
     for row in range(rows):
         tiles = [whole_of(xl_ref[row, c, :, width:]) for c in range(GHOST)]
         tiles += [p_ref[row, c] for c in range(cols)]
@@ -357,7 +383,23 @@
             if row == 0 and 0 < e < n - 1:
                 pay_ref[(e - 1) * half : e * half, :] = packed(tile).astype(bf16)
     tail = (n - 2) * half
-    pay_ref[tail : tail + patch, :], pay_ref[tail + patch :, :] = pair_of(stat_ref[0, :patch])
+    put_tail(pay_ref, tail, stat_ref[0, :patch], root)
+
+
+def put_tail(pay_ref, tail, table, root):
+    half = table.shape[0] // 2
+    high, low = pair_of(jnp.where(iota(table.shape, 1) < 32, table, 0.0))
+    both = high.astype(f32) + pltpu.roll(low.astype(f32), 32, 1)
+    pay_ref[tail : tail + half, :] = (both[:half] + pltpu.roll(both[half:], 64, 1)).astype(bf16)
+    pay_ref[tail + half :, :] = basis_rows(root)
+
+
+def got_tail(got_ref, tail, patch):
+    half = patch // 2
+    both = got_ref[tail : tail + half, :].astype(f32)
+    upper = both + pltpu.roll(both, 96, 1)
+    lower = pltpu.roll(both, 64, 1) + pltpu.roll(both, 32, 1)
+    return jnp.concatenate([upper, lower], axis=0), basis_of(got_ref[tail + half :, :])
 
 
 def start_panel(factor, parts, stat, xl, own_panel, xr):
@@ -365,7 +407,11 @@
     n = cols + 2 * GHOST
     return kernel_call(
         functools.partial(start_kernel, factor, len(parts)),
-        (sds((rows, n, patch, RANK), f32), sds((payload_rows(n - 2, patch), 2 * RANK), bf16)),
+        (
+            sds((rows, n, patch, RANK), f32),
+            sds((payload_rows(n - 2, patch), 2 * RANK), bf16),
+            sds((2, RANK, RANK), f32),
+        ),
     )(*parts, stat, xl, own_panel, xr)
 
 
@@ -435,8 +481,8 @@
     steps = stages(n)
     tiles, columns = steps[stage]
     count = 3 if stage == 0 else 1
-    pieces, (own_ref, stat_ref, p_ref) = refs[:count], refs[count : count + 3]
-    refs = refs[count + 3 :]
+    pieces, (own_ref, stat_ref, p_ref, base_ref) = refs[:count], refs[count : count + 4]
+    refs = refs[count + 4 :]
     patch = pieces[0].shape[1]
     lane = iota((patch, 128), 1)
     if stage == 0:
@@ -497,13 +543,13 @@
     shared = up_sum - FLOOR * absent_near(stat_ref[2, patch:], 3 * patch)
     sum_ref[0], sum_ref[1], sum_ref[2] = shared, mask, scale
     tail = (n - 4) * patch // 2
-    pay_ref[tail : tail + patch, :], pay_ref[tail + patch :, :] = pair_of(shared)
-
-
-def cross_affinity(stage, pieces, u1, stat, panel, before=()):
+    put_tail(pay_ref, tail, shared, base_ref[1])
+
+
+def cross_affinity(stage, pieces, u1, stat, panel, base, before=()):
     patch, width = pieces[0].shape[1:]
     n = u1.shape[0] // patch
-    given = len(pieces) + 3
+    given = len(pieces) + 4
     return pl.pallas_call(
         functools.partial(cross_kernel, n, stage),
         out_shape=(
@@ -516,22 +562,27 @@
         ),
         input_output_aliases={given + i: i for i in range(len(before))},
         compiler_params=pltpu.CompilerParams(vmem_limit_bytes=VMEM_BYTES),
-    )(*pieces, u1, stat, panel, *before)
-
-
-def before_first_kernel(n, got_ref, sum_ref, stat_ref, u0_ref, m_ref, v_ref, z_ref, t_ref, gain_ref, own_ref, u2_ref):
+    )(*pieces, u1, stat, panel, base, *before)
+
+
+def before_first_kernel(
+    n,
+    got_ref, sum_ref, stat_ref, u0_ref, m_ref, v_ref, base_ref,
+    z_ref, t_ref, gain_ref, own_ref, turn_ref,
+):
     patch = u0_ref.shape[1]
     half = patch // 2
     tail = (n - 2) * half
-    partial = got_ref[tail : tail + patch, :].astype(f32) + got_ref[tail + patch :, :].astype(f32)
+    partial, theirs = got_tail(got_ref, tail, patch)
     below_scale = sum_ref[1] * lax.rsqrt(1.0 + partial + sum_ref[0])
     scale = sum_ref[2]
     gain = 1.0 + scale * scale * stat_ref[1, patch:]
     upper = stat_ref[1, :patch]
-    for e in range(1, n - 1):
-        theirs = unpacked(got_ref[(e - 1) * half : e * half, :].astype(f32))
-        u2_ref[e] = (below_scale[:, e : e + 1] * theirs).astype(bf16)
-    lower = pair_products(range(2, n - 2), v_ref, {e: u2_ref[e] for e in range(1, n - 1)})
+    turn = pair_of(turn_of(theirs, base_ref[0]))
+    turn_ref[0], turn_ref[1] = turn
+    tiles = [unpacked(got_ref[(e - 1) * half : e * half, :].astype(f32)) for e in range(1, n - 1)]
+    tiles = turned([below_scale[:, e : e + 1] * tile for e, tile in zip(range(1, n - 1), tiles)], turn)
+    lower = pair_products(range(2, n - 2), v_ref, {e: tile.astype(bf16) for e, tile in zip(range(1, n - 1), tiles)})
     for e in range(2, n - 2):
         own = u0_ref[e - 1 : e + 2].reshape(3 * patch, RANK)
         total = jnp.dot(m_ref[e, :, 3 * patch :], own, preferred_element_type=f32)
@@ -541,26 +592,28 @@
             ref[e] = jnp.broadcast_to(table[:, e : e + 1], (patch, RANK))
 
 
-def before_first(got, sums, stat, u0, m, v):
+def before_first(got, sums, stat, u0, m, v, base):
     n, patch, _ = u0.shape
     spread = sds((n, patch, RANK), f32)
     return kernel_call(
         functools.partial(before_first_kernel, n),
-        (sds((n, 2 * patch, RANK), f32), spread, spread, spread),
-        [pltpu.VMEM((n, patch, RANK), bf16)],
-    )(got, sums, stat, u0, m, v)
+        (sds((n, 2 * patch, RANK), f32), spread, spread, spread, sds((2, RANK, RANK), bf16)),
+    )(got, sums, stat, u0, m, v, base)
 
 
 def first_kernel(
     n,
-    got_ref, stat_ref, t1_ref, gain1_ref, own_ref, z_ref, p_ref, m_ref, w_ref,
-    y_ref, u_ref, t0_ref, gain0_ref, up_ref, down_ref,
+    got_ref, stat_ref, t1_ref, gain1_ref, own_ref, z_ref, p_ref, m_ref, w_ref, base_ref,
+    y_ref, u_ref, t0_ref, gain0_ref, up_ref, down_ref, turn_ref,
     start_ref,
 ):
     patch = t1_ref.shape[1]
     half = patch // 2
     tail = (n - 4) * half
-    partial = got_ref[tail : tail + patch, :].astype(f32) + got_ref[tail + patch :, :].astype(f32)
+    partial, theirs = got_tail(got_ref, tail, patch)
+    turn = pair_of(turn_of(theirs, base_ref[0]))
+    turn_ref[0], turn_ref[1] = turn
+    above = turned([unpacked(got_ref[(e - 2) * half : (e - 1) * half, :]) for e in range(2, n - 2)], turn)
     scale = stat_ref[2, :patch] * lax.rsqrt(1.0 + stat_ref[0, :patch] + partial)
     for e in range(1, n - 1):
         t = jnp.broadcast_to(scale[:, e : e + 1], (patch, RANK))
@@ -569,7 +622,7 @@
     for e in range(2, n - 2):
         own = start_ref[e - 1 : e + 2].reshape(3 * patch, RANK)
         total = z_ref[e] + jnp.dot(m_ref[e, :, : 3 * patch], own, preferred_element_type=f32)
-        upper = total[:patch] + unpacked(got_ref[(e - 2) * half : (e - 1) * half, :].astype(f32))
+        upper = total[:patch] + above[e - 2]
         gain = 1.0 + t0_ref[e] * t0_ref[e] * own_ref[e]
         gain0_ref[e] = gain
         for row, piece, t, g in ((0, upper, t0_ref[e], gain), (1, total[patch:], t1_ref[e], gain1_ref[e])):
@@ -582,7 +635,7 @@
     products(range(3, n - 3), w_ref, {e: u_ref[1, e] for e in range(2, n - 2)}, down_ref, 3)
 
 
-def first_iteration(got, stat, t1, gain1, own, z, panel, m, w):
+def first_iteration(got, stat, t1, gain1, own, z, panel, m, w, base):
     n, both, _ = z.shape
     patch = both // 2
     half = patch // 2
@@ -596,9 +649,10 @@
             spread,
             sds(((n - 4) * half, 2 * RANK), bf16),
             sds(((n - 6) * half, 2 * RANK), bf16),
+            sds((2, RANK, RANK), bf16),
         ),
         [pltpu.VMEM((n, patch, RANK), bf16)],
-    )(got, stat, t1, gain1, own, z, panel, m, w)
+    )(got, stat, t1, gain1, own, z, panel, m, w, base)
 
 
 def local_kernel(low, high, m_ref, u_ref, z_ref):
@@ -617,31 +671,30 @@
     )(m, u)
 
 
-def joined(e, low, lower, z_ref, above_ref, y_ref, scales, gains):
+def images_of(n, low, below_ref, above_ref, z_ref, y_ref, scales, gains, turns, v_ref):
     patch = y_ref.shape[2]
     half = patch // 2
-    upper = unpacked(above_ref[(e - low) * half : (e - low + 1) * half, :].astype(f32))
-    pieces = (z_ref[e, :patch] + upper, z_ref[e, patch:] + lower[e])
-    return [y_ref[row, e] * gains[row][e] + scales[row][e] * pieces[row] for row in range(2)]
-
-
-def halo(n, low, half, below_ref):
-    return {
-        e: unpacked(below_ref[(e - low + 1) * half : (e - low + 2) * half, :]) for e in range(low - 1, n - low + 1)
-    }
+    count = n - 2 * low
+    down, up = ((ref[0], ref[1]) for ref in turns)
+    near = turned([unpacked(below_ref[i * half : (i + 1) * half, :]) for i in range(count + 2)], down)
+    near = {low - 1 + i: tile.astype(bf16) for i, tile in enumerate(near)}
+    lower = pair_products(range(low, n - low), v_ref, near)
+    upper = turned([unpacked(above_ref[i * half : (i + 1) * half, :]) for i in range(count)], up)
+    for e in range(low, n - low):
+        pieces = (z_ref[e, :patch] + upper[e - low], z_ref[e, patch:] + lower[e])
+        yield e, [y_ref[row, e] * gains[row][e] + scales[row][e] * pieces[row] for row in range(2)]
 
 
 def middle_step_kernel(
     n, low,
-    below_ref, above_ref, z_ref, y_ref, t0_ref, t1_ref, gain0_ref, gain1_ref, v_ref, w_ref,
+    below_ref, above_ref, z_ref, y_ref, t0_ref, t1_ref, gain0_ref, gain1_ref, turn0_ref, turn1_ref, v_ref, w_ref,
     new_ref, u_ref, up_ref, down_ref,
 ):
     patch = y_ref.shape[2]
     half = patch // 2
     scales, gains = (t0_ref, t1_ref), (gain0_ref, gain1_ref)
-    lower = pair_products(range(low, n - low), v_ref, halo(n, low, half, below_ref))
-    for e in range(low, n - low):
-        images = joined(e, low, lower, z_ref, above_ref, y_ref, scales, gains)
+    turns = (turn0_ref, turn1_ref)
+    for e, images in images_of(n, low, below_ref, above_ref, z_ref, y_ref, scales, gains, turns, v_ref):
         for row in range(2):
             new_ref[row, e] = images[row]
             scaled = scales[row][e] * images[row]
@@ -669,15 +722,14 @@
 
 def last_step_kernel(
     n, low,
-    below_ref, above_ref, z_ref, y_ref, t0_ref, t1_ref, gain0_ref, gain1_ref, v_ref,
+    below_ref, above_ref, z_ref, y_ref, t0_ref, t1_ref, gain0_ref, gain1_ref, turn0_ref, turn1_ref, v_ref,
     new_ref, gram_ref, side_ref,
 ):
     patch = y_ref.shape[2]
     scales, gains = (t0_ref, t1_ref), (gain0_ref, gain1_ref)
-    lower = pair_products(range(low, n - low), v_ref, halo(n, low, patch // 2, below_ref))
     wide = 2 * RANK
-    for e in range(low, n - low):
-        images = joined(e, low, lower, z_ref, above_ref, y_ref, scales, gains)
+    turns = (turn0_ref, turn1_ref)
+    for e, images in images_of(n, low, below_ref, above_ref, z_ref, y_ref, scales, gains, turns, v_ref):
         for row in range(2):
             new_ref[row, e - low] = images[row]
         span = slice((e - low) * patch, (e - low + 1) * patch)
@@ -699,7 +751,7 @@
     size = gram.shape[0]
     least = 0.0
     if bounded:
-        least = 1e-6 * jnp.sum(jnp.where(identity(size), gram, 0.0), axis=1, keepdims=True) + 1e-30
+        least = 1e-6 * jnp.sum(jnp.where(identity(size), gram, 0.0), axis=1, keepdims=True) + 1e-16
     step = 8
     row = iota((size, 2 * size), 0)
     lane = iota((size, 2 * size), 1)
@@ -715,7 +767,12 @@
                 cols[j] = cols[j] - cols[i] * (cols[j][k + i : k + i + 1, :] * inverse)
             table = table - jnp.where(row > k + i, cols[i], 0.0) * (lines[i] * inverse)
     pivots = jnp.sum(jnp.where(row == lane, table, 0.0), axis=1, keepdims=True)
-    return table[:, size:] * lax.rsqrt(jnp.maximum(pivots, least) if bounded else pivots)
+    if not bounded:
+        return table[:, size:] * lax.rsqrt(pivots)
+    pivots = jnp.maximum(pivots, least)
+    row, lane = row[:, :size], lane[:, :size]
+    upper = jnp.where(lane > row, table[:, :size], jnp.where(lane == row, pivots, 0.0))
+    return table[:, size:] * lax.rsqrt(pivots), upper * lax.rsqrt(pivots)
 
 
 def balanced(parts):
@@ -724,9 +781,35 @@
     return parts[0]
 
 
+def joint_gram(parts, base_ref):
+    size = RANK // 2
+    turns = turn_of(jnp.concatenate([unpacked(part[size:, :]) for part in parts[1:]], axis=0), base_ref[0])
+    first = []
+    for i, part in enumerate(parts[1:]):
+        turn = turns[i * RANK : (i + 1) * RANK]
+        first.append(
+            jnp.dot(
+                unpacked(part[:size, :]), turn, precision=lax.Precision.HIGHEST, preferred_element_type=f32
+            )
+        )
+    others = lax.dot_general(
+        turns, jnp.concatenate(first, axis=0), ATB, precision=lax.Precision.HIGHEST, preferred_element_type=f32
+    )
+    return unpacked(parts[0][:size, :]) + others
+
+
+def joint_kernel(count, *refs):
+    refs[-1][: RANK // 2, :] = packed(joint_gram(refs[:count], refs[count]))
+    refs[-1][RANK // 2 :, :] = packed(refs[count][1])
+
+
+def joint(parts, base):
+    return kernel_call(functools.partial(joint_kernel, len(parts)), sds(parts[0].shape, f32))(*parts, base)
+
+
 def finish_kernel(factor, count, *refs):
-    parts, y_ref, out_ref = refs[:count], refs[count], refs[count + 1]
-    inverse = factor * inverse_factor(unpacked(balanced([part[...] for part in parts])))
+    parts, (base_ref, y_ref, out_ref) = refs[:count], refs[count:]
+    inverse = factor * inverse_factor(joint_gram(parts, base_ref))
     zero = jnp.zeros_like(inverse)
     both = jnp.concatenate(
         [jnp.concatenate([inverse, zero], axis=1), jnp.concatenate([zero, inverse], axis=1)], axis=0
@@ -745,11 +828,11 @@
         out_ref[:, q * wide : (q + 1) * wide] = out[q * tiles : (q + 1) * tiles]
 
 
-def finish(factor, parts, y):
+def finish(factor, parts, base, y):
     return kernel_call(
         functools.partial(finish_kernel, factor, len(parts)),
         sds(y.shape, f32),
-    )(*parts, y)
+    )(*parts, base, y)
 
 
 def exchange_stages(axis):
@@ -768,11 +851,11 @@
     return stages
 
 
-def summed_parts(gram, axis):
+def summed_parts(gram, axis, combine):
     size = lax.axis_size(axis)
     parts = [gram]
     for partners in exchange_stages(axis):
-        gram = balanced(parts)
+        gram = combine(parts) if len(parts) > 1 else gram
         parts = [gram] + [lax.ppermute(gram, axis, [(i, i ^ p) for i in range(size)]) for p in partners]
     return parts
 
@@ -787,10 +870,9 @@
     tile_rows, tile_cols, patches, width = features.shape
     total = tile_rows * lax.axis_size("row") * tile_cols * lax.axis_size("col") * patches
     factor = math.sqrt(float(total))
-    parts = summed_parts(start_gram(probe), "row")
-    (edges,) = gate((mark_edges(features, tissue),), parts[1:])
+    edges = mark_edges(features, tissue)
     below_edges = passed_along(edges, "row", -1)
-    parts = summed_parts(balanced(parts), "col")
+    parts = summed_parts(start_gram(probe), "col", balanced)
     own_panel = probe.reshape(tile_rows, tile_cols, patches, RANK)
     left_end, right_end, middle, unit0, unit1 = own_units(features, tissue, own_panel, edges)
     left_end, right_end = gate((left_end, right_end), parts)
@@ -800,16 +882,16 @@
     m, sums = inside_affinity(unit0, unit1, patches)
     below_left, below_right = cut(below_edges, sums)
     _, u1, m, stat = outside_affinity(unit0, unit1, m, tissue, sums, from_left, from_right, below_left)
-    panel, payload = start_panel(factor, parts, stat, from_left, own_panel, from_right)
+    panel, payload, base = start_panel(factor, parts, stat, from_left, own_panel, from_right)
     below_left, below_right = passed_along(below_right, "col", 1), passed_along(below_left, "col", -1)
     got_below = passed_along(payload, "row", -1)
     n = tile_cols + 2 * GHOST
-    cross = cross_affinity(0, (below_left, below_edges, below_right), u1, stat, panel)
-    v, w, sums, u0, payload, _ = cross_affinity(1, (below_middle,), u1, stat, panel, cross)
+    cross = cross_affinity(0, (below_left, below_edges, below_right), u1, stat, panel, base)
+    v, w, sums, u0, payload, _ = cross_affinity(1, (below_middle,), u1, stat, panel, base, cross)
     got_above = passed_along(payload, "row", 1)
-    z, t1, gain1, own = before_first(got_below, sums, stat, u0, m, v)
-    y, u, t0, gain0, up, down = first_iteration(got_above, stat, t1, gain1, own, z, panel, m, w)
-    spread = (t0, t1, gain0, gain1)
+    z, t1, gain1, own, turn0 = before_first(got_below, sums, stat, u0, m, v, base)
+    y, u, t0, gain0, up, down, turn1 = first_iteration(got_above, stat, t1, gain1, own, z, panel, m, w, base)
+    spread = (t0, t1, gain0, gain1, turn0, turn1)
     below, above = passed_along(up, "row", -1), passed_along(down, "row", 1)
     z = local_products(3, n - 3, m, u)
     y, u, up, down = middle_step(3, below, above, z, y, spread, v, w)
@@ -817,9 +899,11 @@
     z = local_products(4, n - 4, m, u)
     y, gram = last_step(4, below, above, z, y, spread, v)
 
-    parts = summed_parts(balanced(summed_parts(gram, "col")), "row")
+    gram = balanced(summed_parts(gram, "col", balanced))
+    root = jnp.concatenate([base[1, : RANK // 2], base[1, RANK // 2 :]], axis=1)
+    parts = summed_parts(jnp.concatenate([gram, root], axis=0), "row", lambda parts: joint(parts, base))
     flat = y.reshape(tile_rows * tile_cols, patches * RANK)
-    out = finish(factor, parts, flat)
+    out = finish(factor, parts, base, flat)
     return out.reshape(tile_rows, tile_cols, patches * RANK)
 
 

time: 115 us -> 112 us (0.974)
  waiting for transfers between devices: 35.2 us -> 29.4 us
  Pallas kernels: 31.8 us -> 33.4 us
    ppermute x12, starting transfers between devices: 25.2 us -> 29.4 us  [passed_along(): return lax.ppermute(shard, axis, pairs)]
    ppermute x14 -> x11, starting transfers between devices: 20.3 us -> 17.2 us  [summed_parts(): lax.ppermute(gram, axis, [(i, i ^ p) for i in range(size)])]
    ppermute x12, waiting for transfers between devices: 20.7 us -> 17.7 us  [passed_along(): return lax.ppermute(shard, axis, pairs)]
    ppermute x14 -> x11, waiting for transfers between devices: 14.4 us -> 11.7 us  [summed_parts(): lax.ppermute(gram, axis, [(i, i ^ p) for i in range(size)])]
  transfers between devices with their start and end apart: 26 -> 23, of which waited for: 13 -> 12; matrix products, arithmetic and copies ran while one was open for 2% -> 2% of each run, Pallas kernels for 21% -> 22%
where the time goes in v6:
time: 112 us; the launch traced here: 111 us
  starting transfers between devices  46.5 us (42%)
  Pallas kernels  33.4 us (30%)
  waiting for transfers between devices  29.4 us (26%)
  local copies, waits for them, and re-layouts  1.82 us (2%)
    ppermute x12, starting transfers between devices, passed_along(): return lax.ppermute(shard, axis, pairs)  29.4 us
    ppermute x12, waiting for transfers between devices, passed_along(): return lax.ppermute(shard, axis, pairs)  17.7 us
    ppermute x11, starting transfers between devices, summed_parts(): lax.ppermute(gram, axis, [(i, i ^ p) for i in range(size)])  17.2 us
    ppermute x11, waiting for transfers between devices, summed_parts(): lax.ppermute(gram, axis, [(i, i ^ p) for i in range(size)])  11.7 us
    pallas_call x2, Pallas kernels, cross_affinity(): pl.pallas_call(functools.partial(cross_kernel, n, stage), out_shape=(sds(...  5.69 us
    pallas_call x1, Pallas kernels, own_units(): pl.pallas_call(units_kernel, in_specs=[HBM_SPEC, VMEM_SPEC, VMEM_SPEC, AN...  3.8 us
    pallas_call x1, Pallas kernels, finish(): kernel_call(functools.partial(finish_kernel, factor, len(parts)), sds(y.s...  3.63 us
    pallas_call x1, Pallas kernels, inside_affinity(): pl.pallas_call(functools.partial(inside_kernel, n), out_shape=(sds((n, bo...  3.5 us
  transfers between devices with their start and end apart: 23, of which 12 were waited for; matrix products, arithmetic and copies ran while one was open for 2% of the time, Pallas kernels for 22%

profile of v6, /device:TPU:0, one launch (start us, length us, event | category | flops | bytes accessed | tf_op | source)
XLA Modules:
  0.0 111.4 jit_solution(612867302580422922)
XLA Ops:
  0.0 1.4 %shard_map.37.after_ref = bf16[8,64,1024]{2,1,0:T(8,128)(2,1)S(1)} custom-call(bf16[2,16,64,1024]{3,2,1,0:T(8,128)(2,1)} %x_ref.3, s32[2,16,64]{2,1,0:T(8,128)} %tissue_ref.5), custom_call_target="tpu_custom_call" | custom-call | tf_op jit(solution)/shard_map/pallas_call | solution.py:188
  1.4 0.0 copy-start
  1.4 1.3 %collective-permute-start.7 = (bf16[8,64,1024]{2,1,0:T(8,128)(2,1)S(1)}, bf16[8,64,1024]{2,1,0:T(8,128)(2,1)S(1)}, u32[]{:S(2)}, u32[]{:S(2)}) collective-permute-start(bf16[8,64,1024]{2,1,0:T(8,128)(2,1)S(1)} %shard_map.37.after_ref), channel_id=1, source_target_pairs={{8,0},{16,8},{24,16},{9,1},{17,9},{25,17},{10,2},{18,10},{26,18},{... | collective-permute-start | bytes 3145736 | tf_op jit(solution)/shard_map/ppermute | solution.py:866
  2.7 1.5 %shard_map.40 = f32[32,128]{1,0:T(8,128)S(1)} custom-call(f32[2,16,4096]{2,1,0:T(8,128)} %probe_ref.1), custom_call_target="tpu_custom_call" | custom-call | tf_op jit(solution)/shard_map/pallas_call | solution.py:162
  4.2 0.5 collective-permute-start.1
  4.7 0.8 collective-permute-done.1
  5.6 2.9 %collective-permute-start.2 = (f32[32,128]{1,0:T(8,128)S(1)}, f32[32,128]{1,0:T(8,128)S(1)}, u32[]{:S(2)}, u32[]{:S(2)}) collective-permute-start(f32[32,128]{1,0:T(8,128)S(1)} %add.15.refs_2_.refs_0_), channel_id=1, source_target_pairs={{0,2},{1,3},{2,0},{3,1},{4,6},{5,7},{6,4},{7,5},{8,10},{9,11},{10,... | collective-permute-start | bytes 49160 | tf_op jit(solution)/shard_map/ppermute | solution.py:859
  8.5 2.6 %collective-permute-start.3 = (f32[32,128]{1,0:T(8,128)S(1)}, f32[32,128]{1,0:T(8,128)S(1)}, u32[]{:S(2)}, u32[]{:S(2)}) collective-permute-start(f32[32,128]{1,0:T(8,128)S(1)} %add.15.refs_2_.refs_0_), channel_id=1, source_target_pairs={{0,4},{1,5},{2,6},{3,7},{4,0},{5,1},{6,2},{7,3},{8,12},{9,13},{10,... | collective-permute-start | bytes 49160 | tf_op jit(solution)/shard_map/ppermute | solution.py:859
  11.1 0.0 collective-permute-start.4
  11.1 1.5 %reshape.9.probe_ref.refs_6_ = f32[2,16,64,64]{3,2,1,0:T(8,128)S(1)} reshape(f32[2,16,4096]{2,1,0:T(8,128)} %probe_ref.1) | data formatting | bytes 1048576 | tf_op jit(solution)/shard_map/reshape | solution.py:876
  12.6 3.8 %shard_map.38 = (bf16[2,4,64,1280]{3,2,1,0:T(8,128)(2,1)S(1)}, bf16[2,4,64,1280]{3,2,1,0:T(8,128)(2,1)S(1)}, bf16[8,64,1024]{2,1,0:T(8,128)(2,1)S(1)}, bf16[1536...) custom-call(bf16[2,16,64,1024]{3,2,1,0:T(8,128)(2,1)} %x_ref.3, s32[2,16,64]{2,1,0:T(8,128)S(1)} %copy-done, ...), custom_call_target="tpu_custom_call" | custom-call | tf_op jit(solution)/shard_map/pallas_call | solution.py:251
  16.4 0.0 collective-permute-done.3.refs_4_.refs_2_
  16.4 0.2 collective-permute-done.4.refs_5_.refs_3_
  16.6 0.3 shard_map.41
  17.0 1.4 %collective-permute-start.5 = (bf16[2,4,64,1280]{3,2,1,0:T(8,128)(2,1)S(1)}, bf16[2,4,64,1280]{3,2,1,0:T(8,128)(2,1)S(1)}, u32[]{:S(2)}, u32[]{:S(2)}) collective-permute-start(bf16[2,4,64,1280]{3,2,1,0:T(8,128)(2,1)S(1)} %get-tuple-element.58), channel_id=1, source_target_pairs={{0,1},{1,2},{2,3},{3,4},{4,5},{5,6},{6,7},{8,9},{9,10},{10,11},{11... | collective-permute-start | bytes 3932168 | tf_op jit(solution)/shard_map/ppermute | solution.py:866
  18.3 1.3 %collective-permute-start.6 = (bf16[2,4,64,1280]{3,2,1,0:T(8,128)(2,1)S(1)}, bf16[2,4,64,1280]{3,2,1,0:T(8,128)(2,1)S(1)}, u32[]{:S(2)}, u32[]{:S(2)}) collective-permute-start(bf16[2,4,64,1280]{3,2,1,0:T(8,128)(2,1)S(1)} %get-tuple-element.59), channel_id=1, source_target_pairs={{1,0},{2,1},{3,2},{4,3},{5,4},{6,5},{7,6},{9,8},{10,9},{11,10},{12... | collective-permute-start | bytes 3932168 | tf_op jit(solution)/shard_map/ppermute | solution.py:866
  19.6 1.3 %collective-permute-start = (bf16[8,64,1024]{2,1,0:T(8,128)(2,1)S(1)}, bf16[8,64,1024]{2,1,0:T(8,128)(2,1)S(1)}, u32[]{:S(2)}, u32[]{:S(2)}) collective-permute-start(bf16[8,64,1024]{2,1,0:T(8,128)(2,1)S(1)} %get-tuple-element.51), channel_id=1, source_target_pairs={{8,0},{16,8},{24,16},{9,1},{17,9},{25,17},{10,2},{18,10},{26,18},{... | collective-permute-start | bytes 3145736 | tf_op jit(solution)/shard_map/ppermute | solution.py:866
  20.9 3.5 %shard_map.39 = (bf16[24,128,384]{2,1,0:T(8,128)(2,1)S(1)}, f32[2,128,128]{2,1,0:T(8,128)S(1)}) custom-call(bf16[1536,1024]{1,0:T(8,128)(2,1)S(1)} %get-tuple-element.52.unit0_ref.start0_ref, bf16[1536,1024]{1,0:T(8,128)(2,1)S(1)} %get-tuple-element.53.unit1_ref.start1_ref), custom_call_target="tpu_custom_call" | custom-call | tf_op jit(solution)/shard_map/pallas_call | solution.py:301
  24.4 5.8 %collective-permute-done.7.be_ref.refs_1_ = bf16[8,64,1024]{2,1,0:T(8,128)(2,1)S(1)} collective-permute-done((bf16[8,64,1024]{2,1,0:T(8,128)(2,1)S(1)}, bf16[8,64,1024]{2,1,0:T(8,128)(2,1)S(1)}, u32[]{:S(2)}, u32[]{:S(2)}) %collective-permute-start.7) | collective-permute-done | bytes 1048608 | tf_op jit(solution)/shard_map/ppermute | solution.py:866
  30.2 0.1 shard_map.42
  30.3 1.3 %collective-permute-start.9 = (bf16[4,64,1024]{2,1,0:T(8,128)(2,1)S(1)}, bf16[4,64,1024]{2,1,0:T(8,128)(2,1)S(1)}, u32[]{:S(2)}, u32[]{:S(2)}) collective-permute-start(bf16[4,64,1024]{2,1,0:T(8,128)(2,1)S(1)} %get-tuple-element.60.after_ref), channel_id=1, source_target_pairs={{1,0},{2,1},{3,2},{4,3},{5,4},{6,5},{7,6},{9,8},{10,9},{11,10},{12... | collective-permute-start | bytes 1572872 | tf_op jit(solution)/shard_map/ppermute | solution.py:866
  31.6 3.2 %collective-permute-start.8 = (bf16[4,64,1024]{2,1,0:T(8,128)(2,1)S(1)}, bf16[4,64,1024]{2,1,0:T(8,128)(2,1)S(1)}, u32[]{:S(2)}, u32[]{:S(2)}) collective-permute-start(bf16[4,64,1024]{2,1,0:T(8,128)(2,1)S(1)} %get-tuple-element.65), channel_id=1, source_target_pairs={{0,1},{1,2},{2,3},{3,4},{4,5},{5,6},{6,7},{8,9},{9,10},{10,11},{11... | collective-permute-start | bytes 1572872 | tf_op jit(solution)/shard_map/ppermute | solution.py:866
  34.8 0.0 collective-permute-done.5.xl_ref.refs_5_
  34.8 0.0 collective-permute-done.6.xr_ref.refs_7_
  34.8 3.3 %shard_map.43 = (bf16[1536,1024]{1,0:T(8,128)(2,1)S(1)}, bf16[1536,1024]{1,0:T(8,128)(2,1)S(1)}, bf16[24,128,384]{2,1,0:T(8,128)(2,1)S(1)}, f32[3,128,128]{2,1,0:T(8,128)S(1)}) custom-call(bf16[1536,1024]{1,0:T(8,128)(2,1)S(1)} %get-tuple-element.52.unit0_ref.start0_ref, ...), custom_call_target="tpu_custom_call", output_to_operand_aliasing={{0}: (0, {}), {1}: (1, {}), {2}: (2, {})} | custom-call | tf_op jit(solution)/shard_map/pallas_call | solution.py:354
  38.2 3.5 %shard_map.44 = (f32[2,24,64,64]{3,2,1,0:T(8,128)S(1)}, bf16[832,128]{1,0:T(8,128)(2,1)S(1)}, f32[2,64,64]{2,1,0:T(8,128)S(1)}) custom-call(f32[32,128]{1,0:T(8,128)S(1)} %add.15.refs_2_.refs_0_, f32[32,128]{1,0:T(8,128)S(1)} %collective-permute-done.2.refs_3_.refs_1_, f32[32,128]{1,0:T(8,128)S(1)} %collective-permute-done.3.refs_4_.refs_2_, ...), custom_call_target="tpu_custom_call" | custom-call | tf_op jit(solution)/shard_map/pallas_call | solution.py:408
  41.7 1.3 %collective-permute-start.11 = (bf16[832,128]{1,0:T(8,128)(2,1)S(1)}, bf16[832,128]{1,0:T(8,128)(2,1)S(1)}, u32[]{:S(2)}, u32[]{:S(2)}) collective-permute-start(bf16[832,128]{1,0:T(8,128)(2,1)S(1)} %get-tuple-element.73), channel_id=1, source_target_pairs={{8,0},{16,8},{24,16},{9,1},{17,9},{25,17},{10,2},{18,10},{26,18},{... | collective-permute-start | bytes 638984 | tf_op jit(solution)/shard_map/ppermute | solution.py:866
  43.0 0.0 collective-permute-done.9.refs_2_
  43.0 3.0 %shard_map.45 = (bf16[11,128,256]{2,1,0:T(8,128)(2,1)S(1)}, bf16[11,128,256]{2,1,0:T(8,128)(2,1)S(1)}, f32[3,64,128]{2,1,0:T(8,128)S(1)}, bf16[24,64,64]{2,1,0:T...) custom-call(bf16[4,64,1024]{2,1,0:T(8,128)(2,1)S(1)} %collective-permute-done.8.refs_0_, ...), custom_call_target="tpu_custom_call" | custom-call | tf_op jit(solution)/shard_map/pallas_call | solution.py:553
  46.0 6.5 %collective-permute-done.refs_0_ = bf16[8,64,1024]{2,1,0:T(8,128)(2,1)S(1)} collective-permute-done((bf16[8,64,1024]{2,1,0:T(8,128)(2,1)S(1)}, bf16[8,64,1024]{2,1,0:T(8,128)(2,1)S(1)}, u32[]{:S(2)}, u32[]{:S(2)}) %collective-permute-start) | collective-permute-done | bytes 1048608 | tf_op jit(solution)/shard_map/ppermute | solution.py:866
  52.5 2.7 %shard_map.46 = (bf16[11,128,256]{2,1,0:T(8,128)(2,1)S(1)}, bf16[11,128,256]{2,1,0:T(8,128)(2,1)S(1)}, f32[3,64,128]{2,1,0:T(8,128)S(1)}, bf16[24,64,64]{2,1,0:T...) custom-call(bf16[8,64,1024]{2,1,0:T(8,128)(2,1)S(1)} %collective-per, ...), custom_call_target="tpu_custom_call", output_to_operand_aliasing={{0}: (5, {}), {1}: (6, {}), {2}: (7, {}), {3}: (8, {}), {4}... | custom-call | tf_op jit(solution)/shard_map/pallas_call | solution.py:553
  55.2 4.8 %collective-permute-start.10 = (bf16[768,128]{1,0:T(8,128)(2,1)S(1)}, bf16[768,128]{1,0:T(8,128)(2,1)S(1)}, u32[]{:S(2)}, u32[]{:S(2)}) collective-permute-start(bf16[768,128]{1,0:T(8,128)(2,1)S(1)} %get-tuple-element.72), channel_id=1, source_target_pairs={{0,8},{8,16},{16,24},{1,9},{9,17},{17,25},{2,10},{10,18},{18,26},{... | collective-permute-start | bytes 589832 | tf_op jit(solution)/shard_map/ppermute | solution.py:866
  60.0 0.0 collective-permute-done.11.got_ref
  60.0 1.4 %shard_map.47 = (f32[24,128,64]{2,1,0:T(8,128)S(1)}, f32[24,64,64]{2,1,0:T(8,128)S(1)}, f32[24,64,64]{2,1,0:T(8,128)S(1)}, f32[24,64,64]{2,1,0:T(8,128)S(1)}, bf16[2,64,64]{2,1,0:T(8,128)(2,1)S(1)}) custom-call(bf16[832,128]{1,0:T(8,128)(2,1)S(1)} %collective-permute-done.11.got_ref, f32[3,64,128]{2,1,0:T(8,128)S(1)} %get-tuple-element.74.sum_ref, ...), custom_call_target="tpu_custom_call" | custom-call | tf_op jit(solution)/shard_map/pallas_call | solution.py:598
  61.4 1.5 %collective-permute-done.10.got_ref = bf16[768,128]{1,0:T(8,128)(2,1)S(1)} collective-permute-done((bf16[768,128]{1,0:T(8,128)(2,1)S(1)}, bf16[768,128]{1,0:T(8,128)(2,1)S(1)}, u32[]{:S(2)}, u32[]{:S(2)}) %collective-permute-start.10) | collective-permute-done | bytes 196640 | tf_op jit(solution)/shard_map/ppermute | solution.py:866
  62.9 1.3 %shard_map.48 = (f32[2,24,64,64]{3,2,1,0:T(8,128)S(1)}, bf16[2,24,64,64]{3,2,1,0:T(8,128)(2,1)S(1)}, f32[24,64,64]{2,1,0:T(8,128)S(1)}, f32[24,64,64]{2,1,0:T(8,...) custom-call(bf16[768,128]{1,0:T(8,128)(2,1)S(1)} %collective-permute-done.10.go, ...), custom_call_target="tpu_custom_call" | custom-call | tf_op jit(solution)/shard_map/pallas_call | solution.py:643
  64.3 1.3 %collective-permute-start.12 = (bf16[640,128]{1,0:T(8,128)(2,1)S(1)}, bf16[640,128]{1,0:T(8,128)(2,1)S(1)}, u32[]{:S(2)}, u32[]{:S(2)}) collective-permute-start(bf16[640,128]{1,0:T(8,128)(2,1)S(1)} %get-tuple-element.83), channel_id=1, source_target_pairs={{8,0},{16,8},{24,16},{9,1},{17,9},{25,17},{10,2},{18,10},{26,18},{... | collective-permute-start | bytes 491528 | tf_op jit(solution)/shard_map/ppermute | solution.py:866
  65.6 5.0 %collective-permute-start.13 = (bf16[576,128]{1,0:T(8,128)(2,1)S(1)}, bf16[576,128]{1,0:T(8,128)(2,1)S(1)}, u32[]{:S(2)}, u32[]{:S(2)}) collective-permute-start(bf16[576,128]{1,0:T(8,128)(2,1)S(1)} %get-tuple-element.84), channel_id=1, source_target_pairs={{0,8},{8,16},{16,24},{1,9},{9,17},{17,25},{2,10},{10,18},{18,26},{... | collective-permute-start | bytes 442376 | tf_op jit(solution)/shard_map/ppermute | solution.py:866
  70.6 0.6 shard_map.49.z_ref
  71.2 2.0 %collective-permute-done.13.above_ref = bf16[576,128]{1,0:T(8,128)(2,1)S(1)} collective-permute-done((bf16[576,128]{1,0:T(8,128)(2,1)S(1)}, bf16[576,128]{1,0:T(8,128)(2,1)S(1)}, u32[]{:S(2)}, u32[]{:S(2)}) %collective-permute-start.13) | collective-permute-done | bytes 147488 | tf_op jit(solution)/shard_map/ppermute | solution.py:866
  73.3 0.0 collective-permute-done.12.below_ref
  73.3 1.3 %shard_map.50 = (f32[2,24,64,64]{3,2,1,0:T(8,128)S(1)}, bf16[2,24,64,64]{3,2,1,0:T(8,128)(2,1)S(1)}, bf16[576,128]{1,0:T(8,128)(2,1)S(1)}, bf16[512,128]{1,0:T(8,128)(2,1)S(1)}) custom-call(bf16[640,128]{1,0:T(8,128)(2,1)S(1)} %collective-permute-done.12.below_ref, bf16[576,128]{1,0:T(8,128)(2,1)S(1)} %collective-permute-done.13.above_ref, ...), custom_call_target="tpu_custom_call" | custom-call | tf_op jit(solution)/shard_map/pallas_call | solution.py:712
  74.5 1.3 %collective-permute-start.14 = (bf16[576,128]{1,0:T(8,128)(2,1)S(1)}, bf16[576,128]{1,0:T(8,128)(2,1)S(1)}, u32[]{:S(2)}, u32[]{:S(2)}) collective-permute-start(bf16[576,128]{1,0:T(8,128)(2,1)S(1)} %get-tuple-element.91), channel_id=1, source_target_pairs={{8,0},{16,8},{24,16},{9,1},{17,9},{25,17},{10,2},{18,10},{26,18},{... | collective-permute-start | bytes 442376 | tf_op jit(solution)/shard_map/ppermute | solution.py:866
  75.8 5.9 %collective-permute-start.15 = (bf16[512,128]{1,0:T(8,128)(2,1)S(1)}, bf16[512,128]{1,0:T(8,128)(2,1)S(1)}, u32[]{:S(2)}, u32[]{:S(2)}) collective-permute-start(bf16[512,128]{1,0:T(8,128)(2,1)S(1)} %get-tuple-element.92), channel_id=1, source_target_pairs={{0,8},{8,16},{16,24},{1,9},{9,17},{17,25},{2,10},{10,18},{18,26},{... | collective-permute-start | bytes 393224 | tf_op jit(solution)/shard_map/ppermute | solution.py:866
  81.8 0.6 shard_map.51.z_ref
  82.3 1.9 %collective-permute-done.15.above_ref = bf16[512,128]{1,0:T(8,128)(2,1)S(1)} collective-permute-done((bf16[512,128]{1,0:T(8,128)(2,1)S(1)}, bf16[512,128]{1,0:T(8,128)(2,1)S(1)}, u32[]{:S(2)}, u32[]{:S(2)}) %collective-permute-start.15) | collective-permute-done | bytes 131104 | tf_op jit(solution)/shard_map/ppermute | solution.py:866
  84.3 0.0 collective-permute-done.14.below_ref
  84.3 1.4 %shard_map.52 = (f32[2,16,64,64]{3,2,1,0:T(8,128)S(1)}, f32[32,128]{1,0:T(8,128)S(1)}) custom-call(bf16[576,128]{1,0:T(8,128)(2,1)S(1)} %collective-permute-done.14.below_ref, bf16[512,128]{1,0:T(8,128)(2,1)S(1)} %collective-permute-done.15.above_ref, f32[24,128,64]{2,1,0:T(8,128)S(1)} %shard_map.51.z_ref, f32[2,24,64,64]{3,2,1,0:T(8,128)S(1)} %get-tuple-element.94.y_ref, ...), custom_call_target="tpu_custom_call" | custom-call | tf_op jit(solution)/shard_map/pallas_call | solution.py:743
  85.6 0.0 collective-permute-start.16
  85.7 1.2 %collective-permute-done.16 = f32[32,128]{1,0:T(8,128)S(1)} collective-permute-done((f32[32,128]{1,0:T(8,128)S(1)}, f32[32,128]{1,0:T(8,128)S(1)}, u32[]{:S(2)}, u32[]{:S(2)}) %collective-permute-start.16) | collective-permute-done | bytes 16416 | tf_op jit(solution)/shard_map/ppermute | solution.py:859
  86.8 1.6 %collective-permute-start.17 = (f32[32,128]{1,0:T(8,128)S(1)}, f32[32,128]{1,0:T(8,128)S(1)}, u32[]{:S(2)}, u32[]{:S(2)}) collective-permute-start(f32[32,128]{1,0:T(8,128)S(1)} %add.16), channel_id=1, source_target_pairs={{0,2},{1,3},{2,0},{3,1},{4,6},{5,7},{6,4},{7,5},{8,10},{9,11},{10,... | collective-permute-start | bytes 49160 | tf_op jit(solution)/shard_map/ppermute | solution.py:859
  88.4 2.6 %collective-permute-start.18 = (f32[32,128]{1,0:T(8,128)S(1)}, f32[32,128]{1,0:T(8,128)S(1)}, u32[]{:S(2)}, u32[]{:S(2)}) collective-permute-start(f32[32,128]{1,0:T(8,128)S(1)} %add.16), channel_id=1, source_target_pairs={{0,4},{1,5},{2,6},{3,7},{4,0},{5,1},{6,2},{7,3},{8,12},{9,13},{10,... | collective-permute-start | bytes 49160 | tf_op jit(solution)/shard_map/ppermute | solution.py:859
  91.0 0.2 collective-permute-start.19
  91.2 2.0 %collective-permute-done.18 = f32[32,128]{1,0:T(8,128)S(1)} collective-permute-done((f32[32,128]{1,0:T(8,128)S(1)}, f32[32,128]{1,0:T(8,128)S(1)}, u32[]{:S(2)}, u32[]{:S(2)}) %collective-permute-start.18) | collective-permute-done | bytes 16416 | tf_op jit(solution)/shard_map/ppermute | solution.py:859
  93.2 3.3 %collective-permute-done.19 = f32[32,128]{1,0:T(8,128)S(1)} collective-permute-done((f32[32,128]{1,0:T(8,128)S(1)}, f32[32,128]{1,0:T(8,128)S(1)}, u32[]{:S(2)}, u32[]{:S(2)}) %collective-permute-start.19) | collective-permute-done | bytes 16416 | tf_op jit(solution)/shard_map/ppermute | solution.py:859
  96.5 0.1 maximum_maximum_fusion.refs_0_
  96.6 3.4 %collective-permute-start.20 = (f32[64,128]{1,0:T(8,128)S(1)}, f32[64,128]{1,0:T(8,128)S(1)}, u32[]{:S(2)}, u32[]{:S(2)}) collective-permute-start(f32[64,128]{1,0:T(8,128)S(1)} %maximum_maximum_fusion.refs_0_), channel_id=1, source_target_pairs={{0,8},{8,0},{16,24},{24,16},{1,9},{9,1},{17,25},{25,17},{2,10},{10... | collective-permute-start | bytes 98312 | tf_op jit(solution)/shard_map/ppermute | solution.py:859
  100.0 3.0 %collective-permute-start.21 = (f32[64,128]{1,0:T(8,128)S(1)}, f32[64,128]{1,0:T(8,128)S(1)}, u32[]{:S(2)}, u32[]{:S(2)}) collective-permute-start(f32[64,128]{1,0:T(8,128)S(1)} %maximum_maximum_fusion.refs_0_), channel_id=1, source_target_pairs={{0,16},{8,24},{16,0},{24,8},{1,17},{9,25},{17,1},{25,9},{2,18},{10... | collective-permute-start | bytes 98312 | tf_op jit(solution)/shard_map/ppermute | solution.py:859
  103.0 0.3 collective-permute-start.22
  103.3 0.4 reshape.10.refs_5_
  103.7 0.0 collective-permute-done.20.refs_1_
  103.7 1.4 %collective-permute-done.21.refs_2_ = f32[64,128]{1,0:T(8,128)S(1)} collective-permute-done((f32[64,128]{1,0:T(8,128)S(1)}, f32[64,128]{1,0:T(8,128)S(1)}, u32[]{:S(2)}, u32[]{:S(2)}) %collective-permute-start.21) | collective-permute-done | bytes 32800 | tf_op jit(solution)/shard_map/ppermute | solution.py:859
  105.1 2.7 %collective-permute-done.22.refs_3_ = f32[64,128]{1,0:T(8,128)S(1)} collective-permute-done((f32[64,128]{1,0:T(8,128)S(1)}, f32[64,128]{1,0:T(8,128)S(1)}, u32[]{:S(2)}, u32[]{:S(2)}) %collective-permute-start.22) | collective-permute-done | bytes 32800 | tf_op jit(solution)/shard_map/ppermute | solution.py:859
  107.8 3.6 %shard_map.53 = f32[32,4096]{1,0:T(8,128)} custom-call(f32[64,128]{1,0:T(8,128)S(1)} %maximum_maximum_fusion.refs_0_, f32[64,128]{1,0:T(8,128)S(1)} %collective-permute-done.20.refs_1_, f32[64,128]{1,0:T(8,128)S(1)} %collective-permute-done.21.refs_2_, f32[64,128]{1,0:T(8,128)S(1)} %collective-permute-done.22.refs_3_, ...), custom_call_target="tpu_custom_call" | custom-call | tf_op jit(solution)/shard_map/pallas_call | solution.py:832
  (8 shorter events, 0.0 us)
Async XLA Ops:
  1.4 11.2 %copy-start = (s32[2,16,64]{2,1,0:T(8,128)S(1)}, s32[2,16,64]{2,1,0:T(8,128)}, u32[]{:S(2)}) copy-start(s32[2,16,64]{2,1,0:T(8,128)} %tissue_ref.5) | copy-start | bytes 24580
  1.4 28.8 %collective-permute-start.7 = (bf16[8,64,1024]{2,1,0:T(8,128)(2,1)S(1)}, bf16[8,64,1024]{2,1,0:T(8,128)(2,1)S(1)}, u32[]{:S(2)}, u32[]{:S(2)}) collective-permute-start(bf16[8,64,1024]{2,1,0:T(8,128)(2,1)S(1)} %shard_map.37.after_ref), channel_id=1, source_target_pairs={{8,0},{16,8},{24,16},{9,1},{17,9},{25,17},{10,2},{18,10},{26,18},{... | collective-permute-start | bytes 3145736 | tf_op jit(solution)/shard_map/ppermute | solution.py:866
  4.2 1.4 %collective-permute-start.1 = (f32[32,128]{1,0:T(8,128)S(1)}, f32[32,128]{1,0:T(8,128)S(1)}, u32[]{:S(2)}, u32[]{:S(2)}) collective-permute-start(f32[32,128]{1,0:T(8,128)S(1)} %shard_map.40), channel_id=1, source_target_pairs={{0,1},{1,0},{2,3},{3,2},{4,5},{5,4},{6,7},{7,6},{8,9},{9,8},{10,11... | collective-permute-start | bytes 49160 | tf_op jit(solution)/shard_map/ppermute | solution.py:859
  5.6 10.8 %collective-permute-start.2 = (f32[32,128]{1,0:T(8,128)S(1)}, f32[32,128]{1,0:T(8,128)S(1)}, u32[]{:S(2)}, u32[]{:S(2)}) collective-permute-start(f32[32,128]{1,0:T(8,128)S(1)} %add.15.refs_2_.refs_0_), channel_id=1, source_target_pairs={{0,2},{1,3},{2,0},{3,1},{4,6},{5,7},{6,4},{7,5},{8,10},{9,11},{10,... | collective-permute-start | bytes 49160 | tf_op jit(solution)/shard_map/ppermute | solution.py:859
  8.5 7.9 %collective-permute-start.3 = (f32[32,128]{1,0:T(8,128)S(1)}, f32[32,128]{1,0:T(8,128)S(1)}, u32[]{:S(2)}, u32[]{:S(2)}) collective-permute-start(f32[32,128]{1,0:T(8,128)S(1)} %add.15.refs_2_.refs_0_), channel_id=1, source_target_pairs={{0,4},{1,5},{2,6},{3,7},{4,0},{5,1},{6,2},{7,3},{8,12},{9,13},{10,... | collective-permute-start | bytes 49160 | tf_op jit(solution)/shard_map/ppermute | solution.py:859
  11.1 5.5 %collective-permute-start.4 = (f32[32,128]{1,0:T(8,128)S(1)}, f32[32,128]{1,0:T(8,128)S(1)}, u32[]{:S(2)}, u32[]{:S(2)}) collective-permute-start(f32[32,128]{1,0:T(8,128)S(1)} %add.15.refs_2_.refs_0_), channel_id=1, source_target_pairs={{0,6},{1,7},{2,4},{3,5},{4,2},{5,3},{6,0},{7,1},{8,14},{9,15},{10,... | collective-permute-start | bytes 49160 | tf_op jit(solution)/shard_map/ppermute | solution.py:859
  17.0 17.9 %collective-permute-start.5 = (bf16[2,4,64,1280]{3,2,1,0:T(8,128)(2,1)S(1)}, bf16[2,4,64,1280]{3,2,1,0:T(8,128)(2,1)S(1)}, u32[]{:S(2)}, u32[]{:S(2)}) collective-permute-start(bf16[2,4,64,1280]{3,2,1,0:T(8,128)(2,1)S(1)} %get-tuple-element.58), channel_id=1, source_target_pairs={{0,1},{1,2},{2,3},{3,4},{4,5},{5,6},{6,7},{8,9},{9,10},{10,11},{11... | collective-permute-start | bytes 3932168 | tf_op jit(solution)/shard_map/ppermute | solution.py:866
  18.3 16.5 %collective-permute-start.6 = (bf16[2,4,64,1280]{3,2,1,0:T(8,128)(2,1)S(1)}, bf16[2,4,64,1280]{3,2,1,0:T(8,128)(2,1)S(1)}, u32[]{:S(2)}, u32[]{:S(2)}) collective-permute-start(bf16[2,4,64,1280]{3,2,1,0:T(8,128)(2,1)S(1)} %get-tuple-element.59), channel_id=1, source_target_pairs={{1,0},{2,1},{3,2},{4,3},{5,4},{6,5},{7,6},{9,8},{10,9},{11,10},{12... | collective-permute-start | bytes 3932168 | tf_op jit(solution)/shard_map/ppermute | solution.py:866
  19.6 32.9 %collective-permute-start = (bf16[8,64,1024]{2,1,0:T(8,128)(2,1)S(1)}, bf16[8,64,1024]{2,1,0:T(8,128)(2,1)S(1)}, u32[]{:S(2)}, u32[]{:S(2)}) collective-permute-start(bf16[8,64,1024]{2,1,0:T(8,128)(2,1)S(1)} %get-tuple-element.51), channel_id=1, source_target_pairs={{8,0},{16,8},{24,16},{9,1},{17,9},{25,17},{10,2},{18,10},{26,18},{... | collective-permute-start | bytes 3145736 | tf_op jit(solution)/shard_map/ppermute | solution.py:866
  30.3 12.7 %collective-permute-start.9 = (bf16[4,64,1024]{2,1,0:T(8,128)(2,1)S(1)}, bf16[4,64,1024]{2,1,0:T(8,128)(2,1)S(1)}, u32[]{:S(2)}, u32[]{:S(2)}) collective-permute-start(bf16[4,64,1024]{2,1,0:T(8,128)(2,1)S(1)} %get-tuple-element.60.after_ref), channel_id=1, source_target_pairs={{1,0},{2,1},{3,2},{4,3},{5,4},{6,5},{7,6},{9,8},{10,9},{11,10},{12... | collective-permute-start | bytes 1572872 | tf_op jit(solution)/shard_map/ppermute | solution.py:866
  31.6 11.4 %collective-permute-start.8 = (bf16[4,64,1024]{2,1,0:T(8,128)(2,1)S(1)}, bf16[4,64,1024]{2,1,0:T(8,128)(2,1)S(1)}, u32[]{:S(2)}, u32[]{:S(2)}) collective-permute-start(bf16[4,64,1024]{2,1,0:T(8,128)(2,1)S(1)} %get-tuple-element.65), channel_id=1, source_target_pairs={{0,1},{1,2},{2,3},{3,4},{4,5},{5,6},{6,7},{8,9},{9,10},{10,11},{11... | collective-permute-start | bytes 1572872 | tf_op jit(solution)/shard_map/ppermute | solution.py:866
  41.7 18.3 %collective-permute-start.11 = (bf16[832,128]{1,0:T(8,128)(2,1)S(1)}, bf16[832,128]{1,0:T(8,128)(2,1)S(1)}, u32[]{:S(2)}, u32[]{:S(2)}) collective-permute-start(bf16[832,128]{1,0:T(8,128)(2,1)S(1)} %get-tuple-element.73), channel_id=1, source_target_pairs={{8,0},{16,8},{24,16},{9,1},{17,9},{25,17},{10,2},{18,10},{26,18},{... | collective-permute-start | bytes 638984 | tf_op jit(solution)/shard_map/ppermute | solution.py:866
  55.2 7.7 %collective-permute-start.10 = (bf16[768,128]{1,0:T(8,128)(2,1)S(1)}, bf16[768,128]{1,0:T(8,128)(2,1)S(1)}, u32[]{:S(2)}, u32[]{:S(2)}) collective-permute-start(bf16[768,128]{1,0:T(8,128)(2,1)S(1)} %get-tuple-element.72), channel_id=1, source_target_pairs={{0,8},{8,16},{16,24},{1,9},{9,17},{17,25},{2,10},{10,18},{18,26},{... | collective-permute-start | bytes 589832 | tf_op jit(solution)/shard_map/ppermute | solution.py:866
  64.3 9.0 %collective-permute-start.12 = (bf16[640,128]{1,0:T(8,128)(2,1)S(1)}, bf16[640,128]{1,0:T(8,128)(2,1)S(1)}, u32[]{:S(2)}, u32[]{:S(2)}) collective-permute-start(bf16[640,128]{1,0:T(8,128)(2,1)S(1)} %get-tuple-element.83), channel_id=1, source_target_pairs={{8,0},{16,8},{24,16},{9,1},{17,9},{25,17},{10,2},{18,10},{26,18},{... | collective-permute-start | bytes 491528 | tf_op jit(solution)/shard_map/ppermute | solution.py:866
  65.6 7.7 %collective-permute-start.13 = (bf16[576,128]{1,0:T(8,128)(2,1)S(1)}, bf16[576,128]{1,0:T(8,128)(2,1)S(1)}, u32[]{:S(2)}, u32[]{:S(2)}) collective-permute-start(bf16[576,128]{1,0:T(8,128)(2,1)S(1)} %get-tuple-element.84), channel_id=1, source_target_pairs={{0,8},{8,16},{16,24},{1,9},{9,17},{17,25},{2,10},{10,18},{18,26},{... | collective-permute-start | bytes 442376 | tf_op jit(solution)/shard_map/ppermute | solution.py:866
  74.5 9.7 %collective-permute-start.14 = (bf16[576,128]{1,0:T(8,128)(2,1)S(1)}, bf16[576,128]{1,0:T(8,128)(2,1)S(1)}, u32[]{:S(2)}, u32[]{:S(2)}) collective-permute-start(bf16[576,128]{1,0:T(8,128)(2,1)S(1)} %get-tuple-element.91), channel_id=1, source_target_pairs={{8,0},{16,8},{24,16},{9,1},{17,9},{25,17},{10,2},{18,10},{26,18},{... | collective-permute-start | bytes 442376 | tf_op jit(solution)/shard_map/ppermute | solution.py:866
  75.8 8.4 %collective-permute-start.15 = (bf16[512,128]{1,0:T(8,128)(2,1)S(1)}, bf16[512,128]{1,0:T(8,128)(2,1)S(1)}, u32[]{:S(2)}, u32[]{:S(2)}) collective-permute-start(bf16[512,128]{1,0:T(8,128)(2,1)S(1)} %get-tuple-element.92), channel_id=1, source_target_pairs={{0,8},{8,16},{16,24},{1,9},{9,17},{17,25},{2,10},{10,18},{18,26},{... | collective-permute-start | bytes 393224 | tf_op jit(solution)/shard_map/ppermute | solution.py:866
  85.6 1.2 %collective-permute-start.16 = (f32[32,128]{1,0:T(8,128)S(1)}, f32[32,128]{1,0:T(8,128)S(1)}, u32[]{:S(2)}, u32[]{:S(2)}) collective-permute-start(f32[32,128]{1,0:T(8,128)S(1)} %get-tuple-element.95), channel_id=1, source_target_pairs={{0,1},{1,0},{2,3},{3,2},{4,5},{5,4},{6,7},{7,6},{8,9},{9,8},{10,11... | collective-permute-start | bytes 49160 | tf_op jit(solution)/shard_map/ppermute | solution.py:859
  86.8 4.4 %collective-permute-start.17 = (f32[32,128]{1,0:T(8,128)S(1)}, f32[32,128]{1,0:T(8,128)S(1)}, u32[]{:S(2)}, u32[]{:S(2)}) collective-permute-start(f32[32,128]{1,0:T(8,128)S(1)} %add.16), channel_id=1, source_target_pairs={{0,2},{1,3},{2,0},{3,1},{4,6},{5,7},{6,4},{7,5},{8,10},{9,11},{10,... | collective-permute-start | bytes 49160 | tf_op jit(solution)/shard_map/ppermute | solution.py:859
  88.4 4.8 %collective-permute-start.18 = (f32[32,128]{1,0:T(8,128)S(1)}, f32[32,128]{1,0:T(8,128)S(1)}, u32[]{:S(2)}, u32[]{:S(2)}) collective-permute-start(f32[32,128]{1,0:T(8,128)S(1)} %add.16), channel_id=1, source_target_pairs={{0,4},{1,5},{2,6},{3,7},{4,0},{5,1},{6,2},{7,3},{8,12},{9,13},{10,... | collective-permute-start | bytes 49160 | tf_op jit(solution)/shard_map/ppermute | solution.py:859
  91.0 5.5 %collective-permute-start.19 = (f32[32,128]{1,0:T(8,128)S(1)}, f32[32,128]{1,0:T(8,128)S(1)}, u32[]{:S(2)}, u32[]{:S(2)}) collective-permute-start(f32[32,128]{1,0:T(8,128)S(1)} %add.16), channel_id=1, source_target_pairs={{0,6},{1,7},{2,4},{3,5},{4,2},{5,3},{6,0},{7,1},{8,14},{9,15},{10,... | collective-permute-start | bytes 49160 | tf_op jit(solution)/shard_map/ppermute | solution.py:859
  96.6 7.1 %collective-permute-start.20 = (f32[64,128]{1,0:T(8,128)S(1)}, f32[64,128]{1,0:T(8,128)S(1)}, u32[]{:S(2)}, u32[]{:S(2)}) collective-permute-start(f32[64,128]{1,0:T(8,128)S(1)} %maximum_maximum_fusion.refs_0_), channel_id=1, source_target_pairs={{0,8},{8,0},{16,24},{24,16},{1,9},{9,1},{17,25},{25,17},{2,10},{10... | collective-permute-start | bytes 98312 | tf_op jit(solution)/shard_map/ppermute | solution.py:859
  100.0 5.1 %collective-permute-start.21 = (f32[64,128]{1,0:T(8,128)S(1)}, f32[64,128]{1,0:T(8,128)S(1)}, u32[]{:S(2)}, u32[]{:S(2)}) collective-permute-start(f32[64,128]{1,0:T(8,128)S(1)} %maximum_maximum_fusion.refs_0_), channel_id=1, source_target_pairs={{0,16},{8,24},{16,0},{24,8},{1,17},{9,25},{17,1},{25,9},{2,18},{10... | collective-permute-start | bytes 98312 | tf_op jit(solution)/shard_map/ppermute | solution.py:859
  103.0 4.8 %collective-permute-start.22 = (f32[64,128]{1,0:T(8,128)S(1)}, f32[64,128]{1,0:T(8,128)S(1)}, u32[]{:S(2)}, u32[]{:S(2)}) collective-permute-start(f32[64,128]{1,0:T(8,128)S(1)} %maximum_maximum_fusion.refs_0_), channel_id=1, source_target_pairs={{0,24},{8,16},{16,8},{24,0},{1,25},{9,17},{17,9},{25,1},{2,26},{10... | collective-permute-start | bytes 98312 | tf_op jit(solution)/shard_map/ppermute | solution.py:859

commit v7 on v6

--- a/solution.py
+++ b/solution.py
@@ -369,6 +369,8 @@
     width = xl_ref.shape[3] - 4 * RANK
     inverse, root = inverse_factor(unpacked(balanced([part[...] for part in parts])), True)
     inverse, root = factor * inverse, root / factor
+    error = identity(RANK).astype(f32) - turn_of(root, inverse)
+    root = root + jnp.dot(error, root, precision=lax.Precision.HIGHEST, preferred_element_type=f32)
     base_ref[0], base_ref[1] = inverse, root
     for row in range(rows):
         tiles = [whole_of(xl_ref[row, c, :, width:]) for c in range(GHOST)]

time: 112 us -> 112 us (level)
  no operation moved by 1% of the time
where the time goes in v7:
time: 112 us; the launch traced here: 111 us
  starting transfers between devices  46.5 us (42%)
  Pallas kernels  33.5 us (30%)
  waiting for transfers between devices  29.3 us (26%)
  local copies, waits for them, and re-layouts  1.82 us (2%)
    ppermute x12, starting transfers between devices, passed_along(): return lax.ppermute(shard, axis, pairs)  29.3 us
    ppermute x12, waiting for transfers between devices, passed_along(): return lax.ppermute(shard, axis, pairs)  17.9 us
    ppermute x11, starting transfers between devices, summed_parts(): lax.ppermute(gram, axis, [(i, i ^ p) for i in range(size)])  17.2 us
    ppermute x11, waiting for transfers between devices, summed_parts(): lax.ppermute(gram, axis, [(i, i ^ p) for i in range(size)])  11.4 us
    pallas_call x2, Pallas kernels, cross_affinity(): pl.pallas_call(functools.partial(cross_kernel, n, stage), out_shape=(sds(...  5.69 us
    pallas_call x1, Pallas kernels, own_units(): pl.pallas_call(units_kernel, in_specs=[HBM_SPEC, VMEM_SPEC, VMEM_SPEC, AN...  3.8 us
    pallas_call x1, Pallas kernels, finish(): kernel_call(functools.partial(finish_kernel, factor, len(parts)), sds(y.s...  3.63 us
    pallas_call x1, Pallas kernels, start_panel(): kernel_call(functools.partial(start_kernel, factor, len(parts)), (sds((ro...  3.59 us
  transfers between devices with their start and end apart: 23, of which 12 were waited for; matrix products, arithmetic and copies ran while one was open for 2% of the time, Pallas kernels for 22%

profile of v7, /device:TPU:0, one launch (start us, length us, event | category | flops | bytes accessed | tf_op | source)
XLA Modules:
  0.0 111.4 jit_solution(15990516557369152896)
XLA Ops:
  0.0 1.4 %shard_map.37.after_ref = bf16[8,64,1024]{2,1,0:T(8,128)(2,1)S(1)} custom-call(bf16[2,16,64,1024]{3,2,1,0:T(8,128)(2,1)} %x_ref.3, s32[2,16,64]{2,1,0:T(8,128)} %tissue_ref.5), custom_call_target="tpu_custom_call" | custom-call | tf_op jit(solution)/shard_map/pallas_call | solution.py:188
  1.4 0.0 copy-start
  1.4 1.3 %collective-permute-start.7 = (bf16[8,64,1024]{2,1,0:T(8,128)(2,1)S(1)}, bf16[8,64,1024]{2,1,0:T(8,128)(2,1)S(1)}, u32[]{:S(2)}, u32[]{:S(2)}) collective-permute-start(bf16[8,64,1024]{2,1,0:T(8,128)(2,1)S(1)} %shard_map.37.after_ref), channel_id=1, source_target_pairs={{8,0},{16,8},{24,16},{9,1},{17,9},{25,17},{10,2},{18,10},{26,18},{... | collective-permute-start | bytes 3145736 | tf_op jit(solution)/shard_map/ppermute | solution.py:868
  2.7 1.5 %shard_map.40 = f32[32,128]{1,0:T(8,128)S(1)} custom-call(f32[2,16,4096]{2,1,0:T(8,128)} %probe_ref.1), custom_call_target="tpu_custom_call" | custom-call | tf_op jit(solution)/shard_map/pallas_call | solution.py:162
  4.2 0.5 collective-permute-start.1
  4.7 0.8 collective-permute-done.1
  5.6 2.9 %collective-permute-start.2 = (f32[32,128]{1,0:T(8,128)S(1)}, f32[32,128]{1,0:T(8,128)S(1)}, u32[]{:S(2)}, u32[]{:S(2)}) collective-permute-start(f32[32,128]{1,0:T(8,128)S(1)} %add.15.refs_2_.refs_0_), channel_id=1, source_target_pairs={{0,2},{1,3},{2,0},{3,1},{4,6},{5,7},{6,4},{7,5},{8,10},{9,11},{10,... | collective-permute-start | bytes 49160 | tf_op jit(solution)/shard_map/ppermute | solution.py:861
  8.5 2.6 %collective-permute-start.3 = (f32[32,128]{1,0:T(8,128)S(1)}, f32[32,128]{1,0:T(8,128)S(1)}, u32[]{:S(2)}, u32[]{:S(2)}) collective-permute-start(f32[32,128]{1,0:T(8,128)S(1)} %add.15.refs_2_.refs_0_), channel_id=1, source_target_pairs={{0,4},{1,5},{2,6},{3,7},{4,0},{5,1},{6,2},{7,3},{8,12},{9,13},{10,... | collective-permute-start | bytes 49160 | tf_op jit(solution)/shard_map/ppermute | solution.py:861
  11.1 0.0 collective-permute-start.4
  11.1 1.5 %reshape.9.probe_ref.refs_6_ = f32[2,16,64,64]{3,2,1,0:T(8,128)S(1)} reshape(f32[2,16,4096]{2,1,0:T(8,128)} %probe_ref.1) | data formatting | bytes 1048576 | tf_op jit(solution)/shard_map/reshape | solution.py:878
  12.6 3.8 %shard_map.38 = (bf16[2,4,64,1280]{3,2,1,0:T(8,128)(2,1)S(1)}, bf16[2,4,64,1280]{3,2,1,0:T(8,128)(2,1)S(1)}, bf16[8,64,1024]{2,1,0:T(8,128)(2,1)S(1)}, bf16[1536...) custom-call(bf16[2,16,64,1024]{3,2,1,0:T(8,128)(2,1)} %x_ref.3, s32[2,16,64]{2,1,0:T(8,128)S(1)} %copy-done, ...), custom_call_target="tpu_custom_call" | custom-call | tf_op jit(solution)/shard_map/pallas_call | solution.py:251
  16.4 0.0 collective-permute-done.3.refs_4_.refs_2_
  16.4 0.2 collective-permute-done.4.refs_5_.refs_3_
  16.6 0.3 shard_map.41
  17.0 1.4 %collective-permute-start.5 = (bf16[2,4,64,1280]{3,2,1,0:T(8,128)(2,1)S(1)}, bf16[2,4,64,1280]{3,2,1,0:T(8,128)(2,1)S(1)}, u32[]{:S(2)}, u32[]{:S(2)}) collective-permute-start(bf16[2,4,64,1280]{3,2,1,0:T(8,128)(2,1)S(1)} %get-tuple-element.58), channel_id=1, source_target_pairs={{0,1},{1,2},{2,3},{3,4},{4,5},{5,6},{6,7},{8,9},{9,10},{10,11},{11... | collective-permute-start | bytes 3932168 | tf_op jit(solution)/shard_map/ppermute | solution.py:868
  18.3 1.3 %collective-permute-start.6 = (bf16[2,4,64,1280]{3,2,1,0:T(8,128)(2,1)S(1)}, bf16[2,4,64,1280]{3,2,1,0:T(8,128)(2,1)S(1)}, u32[]{:S(2)}, u32[]{:S(2)}) collective-permute-start(bf16[2,4,64,1280]{3,2,1,0:T(8,128)(2,1)S(1)} %get-tuple-element.59), channel_id=1, source_target_pairs={{1,0},{2,1},{3,2},{4,3},{5,4},{6,5},{7,6},{9,8},{10,9},{11,10},{12... | collective-permute-start | bytes 3932168 | tf_op jit(solution)/shard_map/ppermute | solution.py:868
  19.6 1.3 %collective-permute-start = (bf16[8,64,1024]{2,1,0:T(8,128)(2,1)S(1)}, bf16[8,64,1024]{2,1,0:T(8,128)(2,1)S(1)}, u32[]{:S(2)}, u32[]{:S(2)}) collective-permute-start(bf16[8,64,1024]{2,1,0:T(8,128)(2,1)S(1)} %get-tuple-element.51), channel_id=1, source_target_pairs={{8,0},{16,8},{24,16},{9,1},{17,9},{25,17},{10,2},{18,10},{26,18},{... | collective-permute-start | bytes 3145736 | tf_op jit(solution)/shard_map/ppermute | solution.py:868
  20.9 3.5 %shard_map.39 = (bf16[24,128,384]{2,1,0:T(8,128)(2,1)S(1)}, f32[2,128,128]{2,1,0:T(8,128)S(1)}) custom-call(bf16[1536,1024]{1,0:T(8,128)(2,1)S(1)} %get-tuple-element.52.unit0_ref.start0_ref, bf16[1536,1024]{1,0:T(8,128)(2,1)S(1)} %get-tuple-element.53.unit1_ref.start1_ref), custom_call_target="tpu_custom_call" | custom-call | tf_op jit(solution)/shard_map/pallas_call | solution.py:301
  24.4 5.8 %collective-permute-done.7.be_ref.refs_1_ = bf16[8,64,1024]{2,1,0:T(8,128)(2,1)S(1)} collective-permute-done((bf16[8,64,1024]{2,1,0:T(8,128)(2,1)S(1)}, bf16[8,64,1024]{2,1,0:T(8,128)(2,1)S(1)}, u32[]{:S(2)}, u32[]{:S(2)}) %collective-permute-start.7) | collective-permute-done | bytes 1048608 | tf_op jit(solution)/shard_map/ppermute | solution.py:868
  30.2 0.1 shard_map.42
  30.3 1.3 %collective-permute-start.9 = (bf16[4,64,1024]{2,1,0:T(8,128)(2,1)S(1)}, bf16[4,64,1024]{2,1,0:T(8,128)(2,1)S(1)}, u32[]{:S(2)}, u32[]{:S(2)}) collective-permute-start(bf16[4,64,1024]{2,1,0:T(8,128)(2,1)S(1)} %get-tuple-element.60.after_ref), channel_id=1, source_target_pairs={{1,0},{2,1},{3,2},{4,3},{5,4},{6,5},{7,6},{9,8},{10,9},{11,10},{12... | collective-permute-start | bytes 1572872 | tf_op jit(solution)/shard_map/ppermute | solution.py:868
  31.6 3.2 %collective-permute-start.8 = (bf16[4,64,1024]{2,1,0:T(8,128)(2,1)S(1)}, bf16[4,64,1024]{2,1,0:T(8,128)(2,1)S(1)}, u32[]{:S(2)}, u32[]{:S(2)}) collective-permute-start(bf16[4,64,1024]{2,1,0:T(8,128)(2,1)S(1)} %get-tuple-element.65), channel_id=1, source_target_pairs={{0,1},{1,2},{2,3},{3,4},{4,5},{5,6},{6,7},{8,9},{9,10},{10,11},{11... | collective-permute-start | bytes 1572872 | tf_op jit(solution)/shard_map/ppermute | solution.py:868
  34.8 0.0 collective-permute-done.5.xl_ref.refs_5_
  34.8 0.0 collective-permute-done.6.xr_ref.refs_7_
  34.8 3.3 %shard_map.43 = (bf16[1536,1024]{1,0:T(8,128)(2,1)S(1)}, bf16[1536,1024]{1,0:T(8,128)(2,1)S(1)}, bf16[24,128,384]{2,1,0:T(8,128)(2,1)S(1)}, f32[3,128,128]{2,1,0:T(8,128)S(1)}) custom-call(bf16[1536,1024]{1,0:T(8,128)(2,1)S(1)} %get-tuple-element.52.unit0_ref.start0_ref, ...), custom_call_target="tpu_custom_call", output_to_operand_aliasing={{0}: (0, {}), {1}: (1, {}), {2}: (2, {})} | custom-call | tf_op jit(solution)/shard_map/pallas_call | solution.py:354
  38.2 3.6 %shard_map.44 = (f32[2,24,64,64]{3,2,1,0:T(8,128)S(1)}, bf16[832,128]{1,0:T(8,128)(2,1)S(1)}, f32[2,64,64]{2,1,0:T(8,128)S(1)}) custom-call(f32[32,128]{1,0:T(8,128)S(1)} %add.15.refs_2_.refs_0_, f32[32,128]{1,0:T(8,128)S(1)} %collective-permute-done.2.refs_3_.refs_1_, f32[32,128]{1,0:T(8,128)S(1)} %collective-permute-done.3.refs_4_.refs_2_, ...), custom_call_target="tpu_custom_call" | custom-call | tf_op jit(solution)/shard_map/pallas_call | solution.py:410
  41.8 1.3 %collective-permute-start.11 = (bf16[832,128]{1,0:T(8,128)(2,1)S(1)}, bf16[832,128]{1,0:T(8,128)(2,1)S(1)}, u32[]{:S(2)}, u32[]{:S(2)}) collective-permute-start(bf16[832,128]{1,0:T(8,128)(2,1)S(1)} %get-tuple-element.73), channel_id=1, source_target_pairs={{8,0},{16,8},{24,16},{9,1},{17,9},{25,17},{10,2},{18,10},{26,18},{... | collective-permute-start | bytes 638984 | tf_op jit(solution)/shard_map/ppermute | solution.py:868
  43.1 0.0 collective-permute-done.9.refs_2_
  43.1 0.0 collective-permute-done.8.refs_0_
  43.1 3.0 %shard_map.45 = (bf16[11,128,256]{2,1,0:T(8,128)(2,1)S(1)}, bf16[11,128,256]{2,1,0:T(8,128)(2,1)S(1)}, f32[3,64,128]{2,1,0:T(8,128)S(1)}, bf16[24,64,64]{2,1,0:T...) custom-call(bf16[4,64,1024]{2,1,0:T(8,128)(2,1)S(1)} %collective-permute-done.8.refs_0_, ...), custom_call_target="tpu_custom_call" | custom-call | tf_op jit(solution)/shard_map/pallas_call | solution.py:555
  46.1 6.3 %collective-permute-done.refs_0_ = bf16[8,64,1024]{2,1,0:T(8,128)(2,1)S(1)} collective-permute-done((bf16[8,64,1024]{2,1,0:T(8,128)(2,1)S(1)}, bf16[8,64,1024]{2,1,0:T(8,128)(2,1)S(1)}, u32[]{:S(2)}, u32[]{:S(2)}) %collective-permute-start) | collective-permute-done | bytes 1048608 | tf_op jit(solution)/shard_map/ppermute | solution.py:868
  52.4 2.7 %shard_map.46 = (bf16[11,128,256]{2,1,0:T(8,128)(2,1)S(1)}, bf16[11,128,256]{2,1,0:T(8,128)(2,1)S(1)}, f32[3,64,128]{2,1,0:T(8,128)S(1)}, bf16[24,64,64]{2,1,0:T...) custom-call(bf16[8,64,1024]{2,1,0:T(8,128)(2,1)S(1)} %collective-per, ...), custom_call_target="tpu_custom_call", output_to_operand_aliasing={{0}: (5, {}), {1}: (6, {}), {2}: (7, {}), {3}: (8, {}), {4}... | custom-call | tf_op jit(solution)/shard_map/pallas_call | solution.py:555
  55.1 4.8 %collective-permute-start.10 = (bf16[768,128]{1,0:T(8,128)(2,1)S(1)}, bf16[768,128]{1,0:T(8,128)(2,1)S(1)}, u32[]{:S(2)}, u32[]{:S(2)}) collective-permute-start(bf16[768,128]{1,0:T(8,128)(2,1)S(1)} %get-tuple-element.72), channel_id=1, source_target_pairs={{0,8},{8,16},{16,24},{1,9},{9,17},{17,25},{2,10},{10,18},{18,26},{... | collective-permute-start | bytes 589832 | tf_op jit(solution)/shard_map/ppermute | solution.py:868
  59.9 0.0 collective-permute-done.11.got_ref
  59.9 1.4 %shard_map.47 = (f32[24,128,64]{2,1,0:T(8,128)S(1)}, f32[24,64,64]{2,1,0:T(8,128)S(1)}, f32[24,64,64]{2,1,0:T(8,128)S(1)}, f32[24,64,64]{2,1,0:T(8,128)S(1)}, bf16[2,64,64]{2,1,0:T(8,128)(2,1)S(1)}) custom-call(bf16[832,128]{1,0:T(8,128)(2,1)S(1)} %collective-permute-done.11.got_ref, f32[3,64,128]{2,1,0:T(8,128)S(1)} %get-tuple-element.74.sum_ref, ...), custom_call_target="tpu_custom_call" | custom-call | tf_op jit(solution)/shard_map/pallas_call | solution.py:600
  61.3 1.5 %collective-permute-done.10.got_ref = bf16[768,128]{1,0:T(8,128)(2,1)S(1)} collective-permute-done((bf16[768,128]{1,0:T(8,128)(2,1)S(1)}, bf16[768,128]{1,0:T(8,128)(2,1)S(1)}, u32[]{:S(2)}, u32[]{:S(2)}) %collective-permute-start.10) | collective-permute-done | bytes 196640 | tf_op jit(solution)/shard_map/ppermute | solution.py:868
  62.8 1.3 %shard_map.48 = (f32[2,24,64,64]{3,2,1,0:T(8,128)S(1)}, bf16[2,24,64,64]{3,2,1,0:T(8,128)(2,1)S(1)}, f32[24,64,64]{2,1,0:T(8,128)S(1)}, f32[24,64,64]{2,1,0:T(8,...) custom-call(bf16[768,128]{1,0:T(8,128)(2,1)S(1)} %collective-permute-done.10.go, ...), custom_call_target="tpu_custom_call" | custom-call | tf_op jit(solution)/shard_map/pallas_call | solution.py:645
  64.2 1.3 %collective-permute-start.12 = (bf16[640,128]{1,0:T(8,128)(2,1)S(1)}, bf16[640,128]{1,0:T(8,128)(2,1)S(1)}, u32[]{:S(2)}, u32[]{:S(2)}) collective-permute-start(bf16[640,128]{1,0:T(8,128)(2,1)S(1)} %get-tuple-element.83), channel_id=1, source_target_pairs={{8,0},{16,8},{24,16},{9,1},{17,9},{25,17},{10,2},{18,10},{26,18},{... | collective-permute-start | bytes 491528 | tf_op jit(solution)/shard_map/ppermute | solution.py:868
  65.5 5.0 %collective-permute-start.13 = (bf16[576,128]{1,0:T(8,128)(2,1)S(1)}, bf16[576,128]{1,0:T(8,128)(2,1)S(1)}, u32[]{:S(2)}, u32[]{:S(2)}) collective-permute-start(bf16[576,128]{1,0:T(8,128)(2,1)S(1)} %get-tuple-element.84), channel_id=1, source_target_pairs={{0,8},{8,16},{16,24},{1,9},{9,17},{17,25},{2,10},{10,18},{18,26},{... | collective-permute-start | bytes 442376 | tf_op jit(solution)/shard_map/ppermute | solution.py:868
  70.5 0.6 shard_map.49.z_ref
  71.1 2.4 %collective-permute-done.13.above_ref = bf16[576,128]{1,0:T(8,128)(2,1)S(1)} collective-permute-done((bf16[576,128]{1,0:T(8,128)(2,1)S(1)}, bf16[576,128]{1,0:T(8,128)(2,1)S(1)}, u32[]{:S(2)}, u32[]{:S(2)}) %collective-permute-start.13) | collective-permute-done | bytes 147488 | tf_op jit(solution)/shard_map/ppermute | solution.py:868
  73.5 1.3 %shard_map.50 = (f32[2,24,64,64]{3,2,1,0:T(8,128)S(1)}, bf16[2,24,64,64]{3,2,1,0:T(8,128)(2,1)S(1)}, bf16[576,128]{1,0:T(8,128)(2,1)S(1)}, bf16[512,128]{1,0:T(8,128)(2,1)S(1)}) custom-call(bf16[640,128]{1,0:T(8,128)(2,1)S(1)} %collective-permute-done.12.below_ref, bf16[576,128]{1,0:T(8,128)(2,1)S(1)} %collective-permute-done.13.above_ref, ...), custom_call_target="tpu_custom_call" | custom-call | tf_op jit(solution)/shard_map/pallas_call | solution.py:714
  74.8 1.3 %collective-permute-start.14 = (bf16[576,128]{1,0:T(8,128)(2,1)S(1)}, bf16[576,128]{1,0:T(8,128)(2,1)S(1)}, u32[]{:S(2)}, u32[]{:S(2)}) collective-permute-start(bf16[576,128]{1,0:T(8,128)(2,1)S(1)} %get-tuple-element.91), channel_id=1, source_target_pairs={{8,0},{16,8},{24,16},{9,1},{17,9},{25,17},{10,2},{18,10},{26,18},{... | collective-permute-start | bytes 442376 | tf_op jit(solution)/shard_map/ppermute | solution.py:868
  76.1 5.8 %collective-permute-start.15 = (bf16[512,128]{1,0:T(8,128)(2,1)S(1)}, bf16[512,128]{1,0:T(8,128)(2,1)S(1)}, u32[]{:S(2)}, u32[]{:S(2)}) collective-permute-start(bf16[512,128]{1,0:T(8,128)(2,1)S(1)} %get-tuple-element.92), channel_id=1, source_target_pairs={{0,8},{8,16},{16,24},{1,9},{9,17},{17,25},{2,10},{10,18},{18,26},{... | collective-permute-start | bytes 393224 | tf_op jit(solution)/shard_map/ppermute | solution.py:868
  82.0 0.6 shard_map.51.z_ref
  82.6 1.9 %collective-permute-done.15.above_ref = bf16[512,128]{1,0:T(8,128)(2,1)S(1)} collective-permute-done((bf16[512,128]{1,0:T(8,128)(2,1)S(1)}, bf16[512,128]{1,0:T(8,128)(2,1)S(1)}, u32[]{:S(2)}, u32[]{:S(2)}) %collective-permute-start.15) | collective-permute-done | bytes 131104 | tf_op jit(solution)/shard_map/ppermute | solution.py:868
  84.5 0.0 collective-permute-done.14.below_ref
  84.5 1.4 %shard_map.52 = (f32[2,16,64,64]{3,2,1,0:T(8,128)S(1)}, f32[32,128]{1,0:T(8,128)S(1)}) custom-call(bf16[576,128]{1,0:T(8,128)(2,1)S(1)} %collective-permute-done.14.below_ref, bf16[512,128]{1,0:T(8,128)(2,1)S(1)} %collective-permute-done.15.above_ref, f32[24,128,64]{2,1,0:T(8,128)S(1)} %shard_map.51.z_ref, f32[2,24,64,64]{3,2,1,0:T(8,128)S(1)} %get-tuple-element.94.y_ref, ...), custom_call_target="tpu_custom_call" | custom-call | tf_op jit(solution)/shard_map/pallas_call | solution.py:745
  85.8 0.0 collective-permute-start.16
  85.9 1.2 %collective-permute-done.16 = f32[32,128]{1,0:T(8,128)S(1)} collective-permute-done((f32[32,128]{1,0:T(8,128)S(1)}, f32[32,128]{1,0:T(8,128)S(1)}, u32[]{:S(2)}, u32[]{:S(2)}) %collective-permute-start.16) | collective-permute-done | bytes 16416 | tf_op jit(solution)/shard_map/ppermute | solution.py:861
  87.1 1.6 %collective-permute-start.17 = (f32[32,128]{1,0:T(8,128)S(1)}, f32[32,128]{1,0:T(8,128)S(1)}, u32[]{:S(2)}, u32[]{:S(2)}) collective-permute-start(f32[32,128]{1,0:T(8,128)S(1)} %add.16), channel_id=1, source_target_pairs={{0,2},{1,3},{2,0},{3,1},{4,6},{5,7},{6,4},{7,5},{8,10},{9,11},{10,... | collective-permute-start | bytes 49160 | tf_op jit(solution)/shard_map/ppermute | solution.py:861
  88.6 2.4 %collective-permute-start.18 = (f32[32,128]{1,0:T(8,128)S(1)}, f32[32,128]{1,0:T(8,128)S(1)}, u32[]{:S(2)}, u32[]{:S(2)}) collective-permute-start(f32[32,128]{1,0:T(8,128)S(1)} %add.16), channel_id=1, source_target_pairs={{0,4},{1,5},{2,6},{3,7},{4,0},{5,1},{6,2},{7,3},{8,12},{9,13},{10,... | collective-permute-start | bytes 49160 | tf_op jit(solution)/shard_map/ppermute | solution.py:861
  91.0 0.4 collective-permute-start.19
  91.4 0.0 collective-permute-done.17
  91.4 2.1 %collective-permute-done.18 = f32[32,128]{1,0:T(8,128)S(1)} collective-permute-done((f32[32,128]{1,0:T(8,128)S(1)}, f32[32,128]{1,0:T(8,128)S(1)}, u32[]{:S(2)}, u32[]{:S(2)}) %collective-permute-start.18) | collective-permute-done | bytes 16416 | tf_op jit(solution)/shard_map/ppermute | solution.py:861
  93.5 3.0 %collective-permute-done.19 = f32[32,128]{1,0:T(8,128)S(1)} collective-permute-done((f32[32,128]{1,0:T(8,128)S(1)}, f32[32,128]{1,0:T(8,128)S(1)}, u32[]{:S(2)}, u32[]{:S(2)}) %collective-permute-start.19) | collective-permute-done | bytes 16416 | tf_op jit(solution)/shard_map/ppermute | solution.py:861
  96.5 0.1 maximum_maximum_fusion.refs_0_
  96.6 3.4 %collective-permute-start.20 = (f32[64,128]{1,0:T(8,128)S(1)}, f32[64,128]{1,0:T(8,128)S(1)}, u32[]{:S(2)}, u32[]{:S(2)}) collective-permute-start(f32[64,128]{1,0:T(8,128)S(1)} %maximum_maximum_fusion.refs_0_), channel_id=1, source_target_pairs={{0,8},{8,0},{16,24},{24,16},{1,9},{9,1},{17,25},{25,17},{2,10},{10... | collective-permute-start | bytes 98312 | tf_op jit(solution)/shard_map/ppermute | solution.py:861
  100.0 3.0 %collective-permute-start.21 = (f32[64,128]{1,0:T(8,128)S(1)}, f32[64,128]{1,0:T(8,128)S(1)}, u32[]{:S(2)}, u32[]{:S(2)}) collective-permute-start(f32[64,128]{1,0:T(8,128)S(1)} %maximum_maximum_fusion.refs_0_), channel_id=1, source_target_pairs={{0,16},{8,24},{16,0},{24,8},{1,17},{9,25},{17,1},{25,9},{2,18},{10... | collective-permute-start | bytes 98312 | tf_op jit(solution)/shard_map/ppermute | solution.py:861
  103.0 0.3 collective-permute-start.22
  103.3 0.4 reshape.10.refs_5_
  103.7 1.4 %collective-permute-done.21.refs_2_ = f32[64,128]{1,0:T(8,128)S(1)} collective-permute-done((f32[64,128]{1,0:T(8,128)S(1)}, f32[64,128]{1,0:T(8,128)S(1)}, u32[]{:S(2)}, u32[]{:S(2)}) %collective-permute-start.21) | collective-permute-done | bytes 32800 | tf_op jit(solution)/shard_map/ppermute | solution.py:861
  105.1 2.7 %collective-permute-done.22.refs_3_ = f32[64,128]{1,0:T(8,128)S(1)} collective-permute-done((f32[64,128]{1,0:T(8,128)S(1)}, f32[64,128]{1,0:T(8,128)S(1)}, u32[]{:S(2)}, u32[]{:S(2)}) %collective-permute-start.22) | collective-permute-done | bytes 32800 | tf_op jit(solution)/shard_map/ppermute | solution.py:861
  107.8 3.6 %shard_map.53 = f32[32,4096]{1,0:T(8,128)} custom-call(f32[64,128]{1,0:T(8,128)S(1)} %maximum_maximum_fusion.refs_0_, f32[64,128]{1,0:T(8,128)S(1)} %collective-permute-done.20.refs_1_, f32[64,128]{1,0:T(8,128)S(1)} %collective-permute-done.21.refs_2_, f32[64,128]{1,0:T(8,128)S(1)} %collective-permute-done.22.refs_3_, ...), custom_call_target="tpu_custom_call" | custom-call | tf_op jit(solution)/shard_map/pallas_call | solution.py:834
  (8 shorter events, 0.0 us)
Async XLA Ops:
  1.4 11.2 %copy-start = (s32[2,16,64]{2,1,0:T(8,128)S(1)}, s32[2,16,64]{2,1,0:T(8,128)}, u32[]{:S(2)}) copy-start(s32[2,16,64]{2,1,0:T(8,128)} %tissue_ref.5) | copy-start | bytes 24580
  1.4 28.8 %collective-permute-start.7 = (bf16[8,64,1024]{2,1,0:T(8,128)(2,1)S(1)}, bf16[8,64,1024]{2,1,0:T(8,128)(2,1)S(1)}, u32[]{:S(2)}, u32[]{:S(2)}) collective-permute-start(bf16[8,64,1024]{2,1,0:T(8,128)(2,1)S(1)} %shard_map.37.after_ref), channel_id=1, source_target_pairs={{8,0},{16,8},{24,16},{9,1},{17,9},{25,17},{10,2},{18,10},{26,18},{... | collective-permute-start | bytes 3145736 | tf_op jit(solution)/shard_map/ppermute | solution.py:868
  4.2 1.4 %collective-permute-start.1 = (f32[32,128]{1,0:T(8,128)S(1)}, f32[32,128]{1,0:T(8,128)S(1)}, u32[]{:S(2)}, u32[]{:S(2)}) collective-permute-start(f32[32,128]{1,0:T(8,128)S(1)} %shard_map.40), channel_id=1, source_target_pairs={{0,1},{1,0},{2,3},{3,2},{4,5},{5,4},{6,7},{7,6},{8,9},{9,8},{10,11... | collective-permute-start | bytes 49160 | tf_op jit(solution)/shard_map/ppermute | solution.py:861
  5.6 10.8 %collective-permute-start.2 = (f32[32,128]{1,0:T(8,128)S(1)}, f32[32,128]{1,0:T(8,128)S(1)}, u32[]{:S(2)}, u32[]{:S(2)}) collective-permute-start(f32[32,128]{1,0:T(8,128)S(1)} %add.15.refs_2_.refs_0_), channel_id=1, source_target_pairs={{0,2},{1,3},{2,0},{3,1},{4,6},{5,7},{6,4},{7,5},{8,10},{9,11},{10,... | collective-permute-start | bytes 49160 | tf_op jit(solution)/shard_map/ppermute | solution.py:861
  8.5 7.9 %collective-permute-start.3 = (f32[32,128]{1,0:T(8,128)S(1)}, f32[32,128]{1,0:T(8,128)S(1)}, u32[]{:S(2)}, u32[]{:S(2)}) collective-permute-start(f32[32,128]{1,0:T(8,128)S(1)} %add.15.refs_2_.refs_0_), channel_id=1, source_target_pairs={{0,4},{1,5},{2,6},{3,7},{4,0},{5,1},{6,2},{7,3},{8,12},{9,13},{10,... | collective-permute-start | bytes 49160 | tf_op jit(solution)/shard_map/ppermute | solution.py:861
  11.1 5.5 %collective-permute-start.4 = (f32[32,128]{1,0:T(8,128)S(1)}, f32[32,128]{1,0:T(8,128)S(1)}, u32[]{:S(2)}, u32[]{:S(2)}) collective-permute-start(f32[32,128]{1,0:T(8,128)S(1)} %add.15.refs_2_.refs_0_), channel_id=1, source_target_pairs={{0,6},{1,7},{2,4},{3,5},{4,2},{5,3},{6,0},{7,1},{8,14},{9,15},{10,... | collective-permute-start | bytes 49160 | tf_op jit(solution)/shard_map/ppermute | solution.py:861
  17.0 17.9 %collective-permute-start.5 = (bf16[2,4,64,1280]{3,2,1,0:T(8,128)(2,1)S(1)}, bf16[2,4,64,1280]{3,2,1,0:T(8,128)(2,1)S(1)}, u32[]{:S(2)}, u32[]{:S(2)}) collective-permute-start(bf16[2,4,64,1280]{3,2,1,0:T(8,128)(2,1)S(1)} %get-tuple-element.58), channel_id=1, source_target_pairs={{0,1},{1,2},{2,3},{3,4},{4,5},{5,6},{6,7},{8,9},{9,10},{10,11},{11... | collective-permute-start | bytes 3932168 | tf_op jit(solution)/shard_map/ppermute | solution.py:868
  18.3 16.5 %collective-permute-start.6 = (bf16[2,4,64,1280]{3,2,1,0:T(8,128)(2,1)S(1)}, bf16[2,4,64,1280]{3,2,1,0:T(8,128)(2,1)S(1)}, u32[]{:S(2)}, u32[]{:S(2)}) collective-permute-start(bf16[2,4,64,1280]{3,2,1,0:T(8,128)(2,1)S(1)} %get-tuple-element.59), channel_id=1, source_target_pairs={{1,0},{2,1},{3,2},{4,3},{5,4},{6,5},{7,6},{9,8},{10,9},{11,10},{12... | collective-permute-start | bytes 3932168 | tf_op jit(solution)/shard_map/ppermute | solution.py:868
  19.6 32.8 %collective-permute-start = (bf16[8,64,1024]{2,1,0:T(8,128)(2,1)S(1)}, bf16[8,64,1024]{2,1,0:T(8,128)(2,1)S(1)}, u32[]{:S(2)}, u32[]{:S(2)}) collective-permute-start(bf16[8,64,1024]{2,1,0:T(8,128)(2,1)S(1)} %get-tuple-element.51), channel_id=1, source_target_pairs={{8,0},{16,8},{24,16},{9,1},{17,9},{25,17},{10,2},{18,10},{26,18},{... | collective-permute-start | bytes 3145736 | tf_op jit(solution)/shard_map/ppermute | solution.py:868
  30.3 12.8 %collective-permute-start.9 = (bf16[4,64,1024]{2,1,0:T(8,128)(2,1)S(1)}, bf16[4,64,1024]{2,1,0:T(8,128)(2,1)S(1)}, u32[]{:S(2)}, u32[]{:S(2)}) collective-permute-start(bf16[4,64,1024]{2,1,0:T(8,128)(2,1)S(1)} %get-tuple-element.60.after_ref), channel_id=1, source_target_pairs={{1,0},{2,1},{3,2},{4,3},{5,4},{6,5},{7,6},{9,8},{10,9},{11,10},{12... | collective-permute-start | bytes 1572872 | tf_op jit(solution)/shard_map/ppermute | solution.py:868
  31.6 11.5 %collective-permute-start.8 = (bf16[4,64,1024]{2,1,0:T(8,128)(2,1)S(1)}, bf16[4,64,1024]{2,1,0:T(8,128)(2,1)S(1)}, u32[]{:S(2)}, u32[]{:S(2)}) collective-permute-start(bf16[4,64,1024]{2,1,0:T(8,128)(2,1)S(1)} %get-tuple-element.65), channel_id=1, source_target_pairs={{0,1},{1,2},{2,3},{3,4},{4,5},{5,6},{6,7},{8,9},{9,10},{10,11},{11... | collective-permute-start | bytes 1572872 | tf_op jit(solution)/shard_map/ppermute | solution.py:868
  41.8 18.1 %collective-permute-start.11 = (bf16[832,128]{1,0:T(8,128)(2,1)S(1)}, bf16[832,128]{1,0:T(8,128)(2,1)S(1)}, u32[]{:S(2)}, u32[]{:S(2)}) collective-permute-start(bf16[832,128]{1,0:T(8,128)(2,1)S(1)} %get-tuple-element.73), channel_id=1, source_target_pairs={{8,0},{16,8},{24,16},{9,1},{17,9},{25,17},{10,2},{18,10},{26,18},{... | collective-permute-start | bytes 638984 | tf_op jit(solution)/shard_map/ppermute | solution.py:868
  55.1 7.7 %collective-permute-start.10 = (bf16[768,128]{1,0:T(8,128)(2,1)S(1)}, bf16[768,128]{1,0:T(8,128)(2,1)S(1)}, u32[]{:S(2)}, u32[]{:S(2)}) collective-permute-start(bf16[768,128]{1,0:T(8,128)(2,1)S(1)} %get-tuple-element.72), channel_id=1, source_target_pairs={{0,8},{8,16},{16,24},{1,9},{9,17},{17,25},{2,10},{10,18},{18,26},{... | collective-permute-start | bytes 589832 | tf_op jit(solution)/shard_map/ppermute | solution.py:868
  64.2 9.4 %collective-permute-start.12 = (bf16[640,128]{1,0:T(8,128)(2,1)S(1)}, bf16[640,128]{1,0:T(8,128)(2,1)S(1)}, u32[]{:S(2)}, u32[]{:S(2)}) collective-permute-start(bf16[640,128]{1,0:T(8,128)(2,1)S(1)} %get-tuple-element.83), channel_id=1, source_target_pairs={{8,0},{16,8},{24,16},{9,1},{17,9},{25,17},{10,2},{18,10},{26,18},{... | collective-permute-start | bytes 491528 | tf_op jit(solution)/shard_map/ppermute | solution.py:868
  65.5 8.1 %collective-permute-start.13 = (bf16[576,128]{1,0:T(8,128)(2,1)S(1)}, bf16[576,128]{1,0:T(8,128)(2,1)S(1)}, u32[]{:S(2)}, u32[]{:S(2)}) collective-permute-start(bf16[576,128]{1,0:T(8,128)(2,1)S(1)} %get-tuple-element.84), channel_id=1, source_target_pairs={{0,8},{8,16},{16,24},{1,9},{9,17},{17,25},{2,10},{10,18},{18,26},{... | collective-permute-start | bytes 442376 | tf_op jit(solution)/shard_map/ppermute | solution.py:868
  74.8 9.7 %collective-permute-start.14 = (bf16[576,128]{1,0:T(8,128)(2,1)S(1)}, bf16[576,128]{1,0:T(8,128)(2,1)S(1)}, u32[]{:S(2)}, u32[]{:S(2)}) collective-permute-start(bf16[576,128]{1,0:T(8,128)(2,1)S(1)} %get-tuple-element.91), channel_id=1, source_target_pairs={{8,0},{16,8},{24,16},{9,1},{17,9},{25,17},{10,2},{18,10},{26,18},{... | collective-permute-start | bytes 442376 | tf_op jit(solution)/shard_map/ppermute | solution.py:868
  76.1 8.4 %collective-permute-start.15 = (bf16[512,128]{1,0:T(8,128)(2,1)S(1)}, bf16[512,128]{1,0:T(8,128)(2,1)S(1)}, u32[]{:S(2)}, u32[]{:S(2)}) collective-permute-start(bf16[512,128]{1,0:T(8,128)(2,1)S(1)} %get-tuple-element.92), channel_id=1, source_target_pairs={{0,8},{8,16},{16,24},{1,9},{9,17},{17,25},{2,10},{10,18},{18,26},{... | collective-permute-start | bytes 393224 | tf_op jit(solution)/shard_map/ppermute | solution.py:868
  85.8 1.2 %collective-permute-start.16 = (f32[32,128]{1,0:T(8,128)S(1)}, f32[32,128]{1,0:T(8,128)S(1)}, u32[]{:S(2)}, u32[]{:S(2)}) collective-permute-start(f32[32,128]{1,0:T(8,128)S(1)} %get-tuple-element.95), channel_id=1, source_target_pairs={{0,1},{1,0},{2,3},{3,2},{4,5},{5,4},{6,7},{7,6},{8,9},{9,8},{10,11... | collective-permute-start | bytes 49160 | tf_op jit(solution)/shard_map/ppermute | solution.py:861
  87.1 4.4 %collective-permute-start.17 = (f32[32,128]{1,0:T(8,128)S(1)}, f32[32,128]{1,0:T(8,128)S(1)}, u32[]{:S(2)}, u32[]{:S(2)}) collective-permute-start(f32[32,128]{1,0:T(8,128)S(1)} %add.16), channel_id=1, source_target_pairs={{0,2},{1,3},{2,0},{3,1},{4,6},{5,7},{6,4},{7,5},{8,10},{9,11},{10,... | collective-permute-start | bytes 49160 | tf_op jit(solution)/shard_map/ppermute | solution.py:861
  88.6 4.9 %collective-permute-start.18 = (f32[32,128]{1,0:T(8,128)S(1)}, f32[32,128]{1,0:T(8,128)S(1)}, u32[]{:S(2)}, u32[]{:S(2)}) collective-permute-start(f32[32,128]{1,0:T(8,128)S(1)} %add.16), channel_id=1, source_target_pairs={{0,4},{1,5},{2,6},{3,7},{4,0},{5,1},{6,2},{7,3},{8,12},{9,13},{10,... | collective-permute-start | bytes 49160 | tf_op jit(solution)/shard_map/ppermute | solution.py:861
  91.0 5.5 %collective-permute-start.19 = (f32[32,128]{1,0:T(8,128)S(1)}, f32[32,128]{1,0:T(8,128)S(1)}, u32[]{:S(2)}, u32[]{:S(2)}) collective-permute-start(f32[32,128]{1,0:T(8,128)S(1)} %add.16), channel_id=1, source_target_pairs={{0,6},{1,7},{2,4},{3,5},{4,2},{5,3},{6,0},{7,1},{8,14},{9,15},{10,... | collective-permute-start | bytes 49160 | tf_op jit(solution)/shard_map/ppermute | solution.py:861
  96.6 7.1 %collective-permute-start.20 = (f32[64,128]{1,0:T(8,128)S(1)}, f32[64,128]{1,0:T(8,128)S(1)}, u32[]{:S(2)}, u32[]{:S(2)}) collective-permute-start(f32[64,128]{1,0:T(8,128)S(1)} %maximum_maximum_fusion.refs_0_), channel_id=1, source_target_pairs={{0,8},{8,0},{16,24},{24,16},{1,9},{9,1},{17,25},{25,17},{2,10},{10... | collective-permute-start | bytes 98312 | tf_op jit(solution)/shard_map/ppermute | solution.py:861
  100.0 5.1 %collective-permute-start.21 = (f32[64,128]{1,0:T(8,128)S(1)}, f32[64,128]{1,0:T(8,128)S(1)}, u32[]{:S(2)}, u32[]{:S(2)}) collective-permute-start(f32[64,128]{1,0:T(8,128)S(1)} %maximum_maximum_fusion.refs_0_), channel_id=1, source_target_pairs={{0,16},{8,24},{16,0},{24,8},{1,17},{9,25},{17,1},{25,9},{2,18},{10... | collective-permute-start | bytes 98312 | tf_op jit(solution)/shard_map/ppermute | solution.py:861
  103.0 4.8 %collective-permute-start.22 = (f32[64,128]{1,0:T(8,128)S(1)}, f32[64,128]{1,0:T(8,128)S(1)}, u32[]{:S(2)}, u32[]{:S(2)}) collective-permute-start(f32[64,128]{1,0:T(8,128)S(1)} %maximum_maximum_fusion.refs_0_), channel_id=1, source_target_pairs={{0,24},{8,16},{16,8},{24,0},{1,25},{9,17},{17,9},{25,1},{2,26},{10... | collective-permute-start | bytes 98312 | tf_op jit(solution)/shard_map/ppermute | solution.py:861

commit v8 on v7

--- a/solution.py
+++ b/solution.py
@@ -216,15 +216,41 @@
     )(*arrays, *after)
 
 
-def units_kernel(
-    x_ref, tissue_ref, probe_ref, after_ref,
-    left_ref, right_ref, middle_ref, unit0_ref, unit1_ref,
-    tile_ref, sems,
-):
+def ends_kernel(x_ref, tissue_ref, probe_ref, left_ref, right_ref, tile_ref, sems):
+    rows, cols, patch, width = x_ref.shape
+    order = [(row, c) for row in range(rows) for c in (0, cols - GHOST)]
+    sources = [x_ref.at[row, c : c + GHOST] for row, c in order]
+    copies = fetched(sources, [tile_ref.at[i] for i in range(len(order))], sems)
+    masks = [by_sublane(tissue_ref[row]) for row in range(rows)]
+    for i, (row, first) in enumerate(order):
+        copies[i].wait()
+        side_ref = right_ref if first else left_ref
+        for k in range(GHOST):
+            c = first + k
+            side_ref[row, k, :, :width] = marked(tile_ref[i, k], masks[row][:, c : c + 1])
+            side_ref[row, k, :, width:] = four_of(probe_ref[row, c])
+
+
+def mark_ends(x, tissue, probe):
+    rows, cols, patch, width = x.shape
+    side = sds((rows, GHOST, patch, width + 4 * RANK), bf16)
+    return pl.pallas_call(
+        ends_kernel,
+        in_specs=[HBM_SPEC, VMEM_SPEC, VMEM_SPEC],
+        out_specs=[VMEM_SPEC] * 2,
+        out_shape=(side, side),
+        scratch_shapes=[
+            pltpu.VMEM((2 * rows, GHOST, patch, width), bf16),
+            pltpu.SemaphoreType.DMA((2 * rows,)),
+        ],
+        compiler_params=pltpu.CompilerParams(vmem_limit_bytes=VMEM_BYTES),
+    )(*in_hbm(x), tissue, probe)
+
+
+def units_kernel(x_ref, tissue_ref, after_ref, middle_ref, unit0_ref, unit1_ref, tile_ref, sems):
     rows, cols, patch, width = x_ref.shape
     run = GHOST
-    order = [(row, c) for row in range(rows) for c in (0, cols - run)]
-    order += [(row, c) for row in range(rows) for c in range(run, cols - run, run)]
+    order = [(row, c) for row in range(rows) for c in range(0, cols, run)]
     copies = fetched([x_ref.at[row, c : c + run] for row, c in order], [tile_ref.at[i] for i in range(len(order))], sems)
     masks = [by_sublane(tissue_ref[row]) for row in range(rows)]
     for i, (row, first) in enumerate(order):
@@ -235,30 +261,25 @@
             unit, _ = unit_and_mask(tile)
             at = (GHOST + c) * patch
             (unit0_ref, unit1_ref)[row][at : at + patch, :] = unit * column.astype(bf16)
-            if first == 0 or first == cols - run:
-                side_ref = left_ref if first == 0 else right_ref
-                side_ref[row, k, :, :width] = marked(tile, column)
-                side_ref[row, k, :, width:] = four_of(probe_ref[row, c])
             if row == 0 and EDGE <= c < cols - EDGE:
                 middle_ref[c - EDGE] = marked(tile, column)
 
 
-def own_units(x, tissue, probe, after):
+def own_units(x, tissue, after):
     rows, cols, patch, width = x.shape
     n = cols + 2 * GHOST
-    side = sds((rows, GHOST, patch, width + 4 * RANK), bf16)
     unit = sds((n * patch, width), bf16)
     return pl.pallas_call(
         units_kernel,
-        in_specs=[HBM_SPEC, VMEM_SPEC, VMEM_SPEC, ANY_SPEC],
-        out_specs=[VMEM_SPEC] * 5,
-        out_shape=(side, side, sds((cols - 2 * EDGE, patch, width), bf16), unit, unit),
+        in_specs=[HBM_SPEC, VMEM_SPEC, ANY_SPEC],
+        out_specs=[VMEM_SPEC] * 3,
+        out_shape=(sds((cols - 2 * EDGE, patch, width), bf16), unit, unit),
         scratch_shapes=[
             pltpu.VMEM((rows * cols // GHOST, GHOST, patch, width), bf16),
             pltpu.SemaphoreType.DMA((rows * cols // GHOST,)),
         ],
         compiler_params=pltpu.CompilerParams(vmem_limit_bytes=VMEM_BYTES),
-    )(*in_hbm(x), tissue, probe, after)
+    )(*in_hbm(x), tissue, after)
 
 
 def bands(ranges, patch, unit0_ref, unit1_ref, m_ref, degree, diagonal):
@@ -876,8 +897,8 @@
     below_edges = passed_along(edges, "row", -1)
     parts = summed_parts(start_gram(probe), "col", balanced)
     own_panel = probe.reshape(tile_rows, tile_cols, patches, RANK)
-    left_end, right_end, middle, unit0, unit1 = own_units(features, tissue, own_panel, edges)
-    left_end, right_end = gate((left_end, right_end), parts)
+    left_end, right_end = gate(mark_ends(features, tissue, own_panel), parts)
+    middle, unit0, unit1 = own_units(features, tissue, left_end)
     from_left = passed_along(right_end, "col", 1)
     from_right = passed_along(left_end, "col", -1)
     below_middle = passed_along(middle, "row", -1)

time: 112 us -> 109 us (0.973)
  waiting for transfers between devices: 29.3 us -> 27 us
  starting transfers between devices: 46.5 us -> 44.7 us
  Pallas kernels: 33.5 us -> 34.7 us
    ppermute x12, starting transfers between devices: 29.3 us -> 27.2 us  [passed_along(): return lax.ppermute(shard, axis, pairs)]
    ppermute x11, waiting for transfers between devices: 11.4 us -> 9.49 us  [summed_parts(): lax.ppermute(gram, axis, [(i, i ^ p) for i in range(size)])]
    pallas_call x1 -> x2, Pallas kernels: 3.8 us -> 5 us  [the longest x1 3.31 us: own_units(): pl.pallas_call(units_kernel, in_specs=[HBM_SPEC, VMEM_SPEC, ANY_SPEC], ou...]
  transfers between devices with their start and end apart: 23 -> 23, of which waited for: 12 -> 12; matrix products, arithmetic and copies ran while one was open for 2% -> 2% of each run, Pallas kernels for 22% -> 24%
where the time goes in v8:
time: 109 us
  starting transfers between devices  44.7 us (41%)
  Pallas kernels  34.7 us (32%)
  waiting for transfers between devices  27 us (25%)
  local copies, waits for them, and re-layouts  1.82 us (2%)
    ppermute x12, starting transfers between devices, passed_along(): return lax.ppermute(shard, axis, pairs)  27.2 us
    ppermute x11, starting transfers between devices, summed_parts(): lax.ppermute(gram, axis, [(i, i ^ p) for i in range(size)])  17.5 us
    ppermute x12, waiting for transfers between devices, passed_along(): return lax.ppermute(shard, axis, pairs)  17.5 us
    ppermute x11, waiting for transfers between devices, summed_parts(): lax.ppermute(gram, axis, [(i, i ^ p) for i in range(size)])  9.49 us
    pallas_call x2, Pallas kernels, cross_affinity(): pl.pallas_call(functools.partial(cross_kernel, n, stage), out_shape=(sds(...  5.7 us
    pallas_call x1, Pallas kernels, finish(): kernel_call(functools.partial(finish_kernel, factor, len(parts)), sds(y.s...  3.63 us
    pallas_call x1, Pallas kernels, start_panel(): kernel_call(functools.partial(start_kernel, factor, len(parts)), (sds((ro...  3.59 us
    pallas_call x1, Pallas kernels, inside_affinity(): pl.pallas_call(functools.partial(inside_kernel, n), out_shape=(sds((n, bo...  3.49 us
  transfers between devices with their start and end apart: 23, of which 12 were waited for; matrix products, arithmetic and copies ran while one was open for 2% of the time, Pallas kernels for 24%

profile of v8, /device:TPU:0, one launch (start us, length us, event | category | flops | bytes accessed | tf_op | source)
XLA Modules:
  0.0 108.5 jit_solution(5193779586900461819)
XLA Ops:
  0.0 1.4 %shard_map.42 = bf16[8,64,1024]{2,1,0:T(8,128)(2,1)S(1)} custom-call(bf16[2,16,64,1024]{3,2,1,0:T(8,128)(2,1)} %x_ref.5, s32[2,16,64]{2,1,0:T(8,128)} %tissue_ref.7), custom_call_target="tpu_custom_call" | custom-call | tf_op jit(solution)/shard_map/pallas_call | solution.py:188
  1.4 0.0 copy-start
  1.4 1.3 %collective-permute-start.7 = (bf16[8,64,1024]{2,1,0:T(8,128)(2,1)S(1)}, bf16[8,64,1024]{2,1,0:T(8,128)(2,1)S(1)}, u32[]{:S(2)}, u32[]{:S(2)}) collective-permute-start(bf16[8,64,1024]{2,1,0:T(8,128)(2,1)S(1)} %shard_map.42), channel_id=1, source_target_pairs={{8,0},{16,8},{24,16},{9,1},{17,9},{25,17},{10,2},{18,10},{26,18},{... | collective-permute-start | bytes 3145736 | tf_op jit(solution)/shard_map/ppermute | solution.py:889
  2.7 1.5 %shard_map.38 = f32[32,128]{1,0:T(8,128)S(1)} custom-call(f32[2,16,4096]{2,1,0:T(8,128)} %probe_ref.1), custom_call_target="tpu_custom_call" | custom-call | tf_op jit(solution)/shard_map/pallas_call | solution.py:162
  4.2 0.5 collective-permute-start
  4.7 0.8 collective-permute-done
  5.6 4.9 %collective-permute-start.3 = (f32[32,128]{1,0:T(8,128)S(1)}, f32[32,128]{1,0:T(8,128)S(1)}, u32[]{:S(2)}, u32[]{:S(2)}) collective-permute-start(f32[32,128]{1,0:T(8,128)S(1)} %add.15.refs_2_.refs_0_), channel_id=1, source_target_pairs={{0,6},{1,7},{2,4},{3,5},{4,2},{5,3},{6,0},{7,1},{8,14},{9,15},{10,... | collective-permute-start | bytes 49160 | tf_op jit(solution)/shard_map/ppermute | solution.py:882
  10.5 0.0 collective-permute-start.2
  10.5 0.6 collective-permute-start.1
  11.2 1.5 %reshape.9.probe_ref.refs_6_ = f32[2,16,64,64]{3,2,1,0:T(8,128)S(1)} reshape(f32[2,16,4096]{2,1,0:T(8,128)} %probe_ref.1) | data formatting | bytes 1048576 | tf_op jit(solution)/shard_map/reshape | solution.py:899
  12.6 1.7 %shard_map.37 = (bf16[2,4,64,1280]{3,2,1,0:T(8,128)(2,1)S(1)}, bf16[2,4,64,1280]{3,2,1,0:T(8,128)(2,1)S(1)}) custom-call(bf16[2,16,64,1024]{3,2,1,0:T(8,128)(2,1)} %x_ref.5, s32[2,16,64]{2,1,0:T(8,128)S(1)} %copy-done, f32[2,16,64,64]{3,2,1,0:T(8,128)S(1)} %reshape.9.probe_ref.refs_6_), custom_call_target="tpu_custom_call" | custom-call | tf_op jit(solution)/shard_map/pallas_call | solution.py:237
  14.3 0.0 collective-permute-done.3.refs_5_.refs_3_
  14.3 0.8 collective-permute-done.2.refs_4_.refs_2_
  15.2 0.0 collective-permute-done.1.refs_3_.refs_1_
  15.2 0.3 shard_map.39
  15.5 1.4 %collective-permute-start.5 = (bf16[2,4,64,1280]{3,2,1,0:T(8,128)(2,1)S(1)}, bf16[2,4,64,1280]{3,2,1,0:T(8,128)(2,1)S(1)}, u32[]{:S(2)}, u32[]{:S(2)}) collective-permute-start(bf16[2,4,64,1280]{3,2,1,0:T(8,128)(2,1)S(1)} %get-tuple-element.59), channel_id=1, source_target_pairs={{0,1},{1,2},{2,3},{3,4},{4,5},{5,6},{6,7},{8,9},{9,10},{10,11},{11... | collective-permute-start | bytes 3932168 | tf_op jit(solution)/shard_map/ppermute | solution.py:889
  16.9 1.3 %collective-permute-start.6 = (bf16[2,4,64,1280]{3,2,1,0:T(8,128)(2,1)S(1)}, bf16[2,4,64,1280]{3,2,1,0:T(8,128)(2,1)S(1)}, u32[]{:S(2)}, u32[]{:S(2)}) collective-permute-start(bf16[2,4,64,1280]{3,2,1,0:T(8,128)(2,1)S(1)} %get-tuple-element.53.after_ref), channel_id=1, source_target_pairs={{1,0},{2,1},{3,2},{4,3},{5,4},{6,5},{7,6},{9,8},{10,9},{11,10},{12... | collective-permute-start | bytes 3932168 | tf_op jit(solution)/shard_map/ppermute | solution.py:889
  18.2 3.3 %shard_map.40 = (bf16[8,64,1024]{2,1,0:T(8,128)(2,1)S(1)}, bf16[1536,1024]{1,0:T(8,128)(2,1)S(1)}, bf16[1536,1024]{1,0:T(8,128)(2,1)S(1)}) custom-call(bf16[2,16,64,1024]{3,2,1,0:T(8,128)(2,1)} %x_ref.5, s32[2,16,64]{2,1,0:T(8,128)S(1)} %copy-done, bf16[2,4,64,1280]{3,2,1,0:T(8,128)(2,1)S(1)} %get-tuple-element.53.after_ref), custom_call_target="tpu_custom_call" | custom-call | tf_op jit(solution)/shard_map/pallas_call | solution.py:272
  21.5 1.3 %collective-permute-start.4 = (bf16[8,64,1024]{2,1,0:T(8,128)(2,1)S(1)}, bf16[8,64,1024]{2,1,0:T(8,128)(2,1)S(1)}, u32[]{:S(2)}, u32[]{:S(2)}) collective-permute-start(bf16[8,64,1024]{2,1,0:T(8,128)(2,1)S(1)} %get-tuple-element.54), channel_id=1, source_target_pairs={{8,0},{16,8},{24,16},{9,1},{17,9},{25,17},{10,2},{18,10},{26,18},{... | collective-permute-start | bytes 3145736 | tf_op jit(solution)/shard_map/ppermute | solution.py:889
  22.8 3.5 %shard_map.41 = (bf16[24,128,384]{2,1,0:T(8,128)(2,1)S(1)}, f32[2,128,128]{2,1,0:T(8,128)S(1)}) custom-call(bf16[1536,1024]{1,0:T(8,128)(2,1)S(1)} %get-tuple-element.55.unit0_ref.start0_ref, bf16[1536,1024]{1,0:T(8,128)(2,1)S(1)} %get-tuple-element.56.unit1_ref.start1_ref), custom_call_target="tpu_custom_call" | custom-call | tf_op jit(solution)/shard_map/pallas_call | solution.py:322
  26.3 3.6 %collective-permute-done.7.be_ref.refs_1_ = bf16[8,64,1024]{2,1,0:T(8,128)(2,1)S(1)} collective-permute-done((bf16[8,64,1024]{2,1,0:T(8,128)(2,1)S(1)}, bf16[8,64,1024]{2,1,0:T(8,128)(2,1)S(1)}, u32[]{:S(2)}, u32[]{:S(2)}) %collective-permute-start.7) | collective-permute-done | bytes 1048608 | tf_op jit(solution)/shard_map/ppermute | solution.py:889
  29.9 0.1 shard_map.43
  30.0 1.3 %collective-permute-start.8 = (bf16[4,64,1024]{2,1,0:T(8,128)(2,1)S(1)}, bf16[4,64,1024]{2,1,0:T(8,128)(2,1)S(1)}, u32[]{:S(2)}, u32[]{:S(2)}) collective-permute-start(bf16[4,64,1024]{2,1,0:T(8,128)(2,1)S(1)} %get-tuple-element.65), channel_id=1, source_target_pairs={{0,1},{1,2},{2,3},{3,4},{4,5},{5,6},{6,7},{8,9},{9,10},{10,11},{11... | collective-permute-start | bytes 1572872 | tf_op jit(solution)/shard_map/ppermute | solution.py:889
  31.3 1.5 %collective-permute-start.9 = (bf16[4,64,1024]{2,1,0:T(8,128)(2,1)S(1)}, bf16[4,64,1024]{2,1,0:T(8,128)(2,1)S(1)}, u32[]{:S(2)}, u32[]{:S(2)}) collective-permute-start(bf16[4,64,1024]{2,1,0:T(8,128)(2,1)S(1)} %get-tuple-element.60.after_ref), channel_id=1, source_target_pairs={{1,0},{2,1},{3,2},{4,3},{5,4},{6,5},{7,6},{9,8},{10,9},{11,10},{12... | collective-permute-start | bytes 1572872 | tf_op jit(solution)/shard_map/ppermute | solution.py:889
  32.8 0.0 collective-permute-done.5.xl_ref.refs_5_
  32.8 0.0 collective-permute-done.6.xr_ref.refs_7_
  32.8 3.3 %shard_map.44 = (bf16[1536,1024]{1,0:T(8,128)(2,1)S(1)}, bf16[1536,1024]{1,0:T(8,128)(2,1)S(1)}, bf16[24,128,384]{2,1,0:T(8,128)(2,1)S(1)}, f32[3,128,128]{2,1,0:T(8,128)S(1)}) custom-call(bf16[1536,1024]{1,0:T(8,128)(2,1)S(1)} %get-tuple-element.55.unit0_ref.start0_ref, ...), custom_call_target="tpu_custom_call", output_to_operand_aliasing={{0}: (0, {}), {1}: (1, {}), {2}: (2, {})} | custom-call | tf_op jit(solution)/shard_map/pallas_call | solution.py:375
  36.2 3.6 %shard_map.45 = (f32[2,24,64,64]{3,2,1,0:T(8,128)S(1)}, bf16[832,128]{1,0:T(8,128)(2,1)S(1)}, f32[2,64,64]{2,1,0:T(8,128)S(1)}) custom-call(f32[32,128]{1,0:T(8,128)S(1)} %add.15.refs_2_.refs_0_, f32[32,128]{1,0:T(8,128)S(1)} %collective-permute-done.1.refs_3_.refs_1_, f32[32,128]{1,0:T(8,128)S(1)} %collective-permute-done.2.refs_4_.refs_2_, ...), custom_call_target="tpu_custom_call" | custom-call | tf_op jit(solution)/shard_map/pallas_call | solution.py:431
  39.8 1.3 %collective-permute-start.11 = (bf16[832,128]{1,0:T(8,128)(2,1)S(1)}, bf16[832,128]{1,0:T(8,128)(2,1)S(1)}, u32[]{:S(2)}, u32[]{:S(2)}) collective-permute-start(bf16[832,128]{1,0:T(8,128)(2,1)S(1)} %get-tuple-element.73), channel_id=1, source_target_pairs={{8,0},{16,8},{24,16},{9,1},{17,9},{25,17},{10,2},{18,10},{26,18},{... | collective-permute-start | bytes 638984 | tf_op jit(solution)/shard_map/ppermute | solution.py:889
  41.1 0.0 collective-permute-done.8.refs_0_
  41.1 3.0 %shard_map.46 = (bf16[11,128,256]{2,1,0:T(8,128)(2,1)S(1)}, bf16[11,128,256]{2,1,0:T(8,128)(2,1)S(1)}, f32[3,64,128]{2,1,0:T(8,128)S(1)}, bf16[24,64,64]{2,1,0:T...) custom-call(bf16[4,64,1024]{2,1,0:T(8,128)(2,1)S(1)} %collective-permute-done.8.refs_0_, ...), custom_call_target="tpu_custom_call" | custom-call | tf_op jit(solution)/shard_map/pallas_call | solution.py:576
  44.1 8.3 %collective-permute-done.4.refs_0_ = bf16[8,64,1024]{2,1,0:T(8,128)(2,1)S(1)} collective-permute-done((bf16[8,64,1024]{2,1,0:T(8,128)(2,1)S(1)}, bf16[8,64,1024]{2,1,0:T(8,128)(2,1)S(1)}, u32[]{:S(2)}, u32[]{:S(2)}) %collective-permute-start.4) | collective-permute-done | bytes 1048608 | tf_op jit(solution)/shard_map/ppermute | solution.py:889
  52.4 2.7 %shard_map.47 = (bf16[11,128,256]{2,1,0:T(8,128)(2,1)S(1)}, bf16[11,128,256]{2,1,0:T(8,128)(2,1)S(1)}, f32[3,64,128]{2,1,0:T(8,128)S(1)}, bf16[24,64,64]{2,1,0:T...) custom-call(bf16[8,64,1024]{2,1,0:T(8,128)(2,1)S(1)} %collective-per, ...), custom_call_target="tpu_custom_call", output_to_operand_aliasing={{0}: (5, {}), {1}: (6, {}), {2}: (7, {}), {3}: (8, {}), {4}... | custom-call | tf_op jit(solution)/shard_map/pallas_call | solution.py:576
  55.1 4.8 %collective-permute-start.10 = (bf16[768,128]{1,0:T(8,128)(2,1)S(1)}, bf16[768,128]{1,0:T(8,128)(2,1)S(1)}, u32[]{:S(2)}, u32[]{:S(2)}) collective-permute-start(bf16[768,128]{1,0:T(8,128)(2,1)S(1)} %get-tuple-element.72), channel_id=1, source_target_pairs={{0,8},{8,16},{16,24},{1,9},{9,17},{17,25},{2,10},{10,18},{18,26},{... | collective-permute-start | bytes 589832 | tf_op jit(solution)/shard_map/ppermute | solution.py:889
  59.8 0.0 collective-permute-done.11.got_ref
  59.8 1.4 %shard_map.48 = (f32[24,128,64]{2,1,0:T(8,128)S(1)}, f32[24,64,64]{2,1,0:T(8,128)S(1)}, f32[24,64,64]{2,1,0:T(8,128)S(1)}, f32[24,64,64]{2,1,0:T(8,128)S(1)}, bf16[2,64,64]{2,1,0:T(8,128)(2,1)S(1)}) custom-call(bf16[832,128]{1,0:T(8,128)(2,1)S(1)} %collective-permute-done.11.got_ref, f32[3,64,128]{2,1,0:T(8,128)S(1)} %get-tuple-element.74.sum_ref, ...), custom_call_target="tpu_custom_call" | custom-call | tf_op jit(solution)/shard_map/pallas_call | solution.py:621
  61.3 1.7 %collective-permute-done.10.got_ref = bf16[768,128]{1,0:T(8,128)(2,1)S(1)} collective-permute-done((bf16[768,128]{1,0:T(8,128)(2,1)S(1)}, bf16[768,128]{1,0:T(8,128)(2,1)S(1)}, u32[]{:S(2)}, u32[]{:S(2)}) %collective-permute-start.10) | collective-permute-done | bytes 196640 | tf_op jit(solution)/shard_map/ppermute | solution.py:889
  62.9 1.3 %shard_map.49 = (f32[2,24,64,64]{3,2,1,0:T(8,128)S(1)}, bf16[2,24,64,64]{3,2,1,0:T(8,128)(2,1)S(1)}, f32[24,64,64]{2,1,0:T(8,128)S(1)}, f32[24,64,64]{2,1,0:T(8,...) custom-call(bf16[768,128]{1,0:T(8,128)(2,1)S(1)} %collective-permute-done.10.go, ...), custom_call_target="tpu_custom_call" | custom-call | tf_op jit(solution)/shard_map/pallas_call | solution.py:666
  64.3 1.3 %collective-permute-start.12 = (bf16[640,128]{1,0:T(8,128)(2,1)S(1)}, bf16[640,128]{1,0:T(8,128)(2,1)S(1)}, u32[]{:S(2)}, u32[]{:S(2)}) collective-permute-start(bf16[640,128]{1,0:T(8,128)(2,1)S(1)} %get-tuple-element.83), channel_id=1, source_target_pairs={{8,0},{16,8},{24,16},{9,1},{17,9},{25,17},{10,2},{18,10},{26,18},{... | collective-permute-start | bytes 491528 | tf_op jit(solution)/shard_map/ppermute | solution.py:889
  65.6 5.0 %collective-permute-start.13 = (bf16[576,128]{1,0:T(8,128)(2,1)S(1)}, bf16[576,128]{1,0:T(8,128)(2,1)S(1)}, u32[]{:S(2)}, u32[]{:S(2)}) collective-permute-start(bf16[576,128]{1,0:T(8,128)(2,1)S(1)} %get-tuple-element.84), channel_id=1, source_target_pairs={{0,8},{8,16},{16,24},{1,9},{9,17},{17,25},{2,10},{10,18},{18,26},{... | collective-permute-start | bytes 442376 | tf_op jit(solution)/shard_map/ppermute | solution.py:889
  70.6 0.6 shard_map.50.z_ref
  71.2 2.0 %collective-permute-done.13.above_ref = bf16[576,128]{1,0:T(8,128)(2,1)S(1)} collective-permute-done((bf16[576,128]{1,0:T(8,128)(2,1)S(1)}, bf16[576,128]{1,0:T(8,128)(2,1)S(1)}, u32[]{:S(2)}, u32[]{:S(2)}) %collective-permute-start.13) | collective-permute-done | bytes 147488 | tf_op jit(solution)/shard_map/ppermute | solution.py:889
  73.3 1.3 %shard_map.51 = (f32[2,24,64,64]{3,2,1,0:T(8,128)S(1)}, bf16[2,24,64,64]{3,2,1,0:T(8,128)(2,1)S(1)}, bf16[576,128]{1,0:T(8,128)(2,1)S(1)}, bf16[512,128]{1,0:T(8,128)(2,1)S(1)}) custom-call(bf16[640,128]{1,0:T(8,128)(2,1)S(1)} %collective-permute-done.12.below_ref, bf16[576,128]{1,0:T(8,128)(2,1)S(1)} %collective-permute-done.13.above_ref, ...), custom_call_target="tpu_custom_call" | custom-call | tf_op jit(solution)/shard_map/pallas_call | solution.py:735
  74.6 1.3 %collective-permute-start.14 = (bf16[576,128]{1,0:T(8,128)(2,1)S(1)}, bf16[576,128]{1,0:T(8,128)(2,1)S(1)}, u32[]{:S(2)}, u32[]{:S(2)}) collective-permute-start(bf16[576,128]{1,0:T(8,128)(2,1)S(1)} %get-tuple-element.91), channel_id=1, source_target_pairs={{8,0},{16,8},{24,16},{9,1},{17,9},{25,17},{10,2},{18,10},{26,18},{... | collective-permute-start | bytes 442376 | tf_op jit(solution)/shard_map/ppermute | solution.py:889
  75.9 5.5 %collective-permute-start.15 = (bf16[512,128]{1,0:T(8,128)(2,1)S(1)}, bf16[512,128]{1,0:T(8,128)(2,1)S(1)}, u32[]{:S(2)}, u32[]{:S(2)}) collective-permute-start(bf16[512,128]{1,0:T(8,128)(2,1)S(1)} %get-tuple-element.92), channel_id=1, source_target_pairs={{0,8},{8,16},{16,24},{1,9},{9,17},{17,25},{2,10},{10,18},{18,26},{... | collective-permute-start | bytes 393224 | tf_op jit(solution)/shard_map/ppermute | solution.py:889
  81.3 0.6 shard_map.52.z_ref
  81.9 1.9 %collective-permute-done.15.above_ref = bf16[512,128]{1,0:T(8,128)(2,1)S(1)} collective-permute-done((bf16[512,128]{1,0:T(8,128)(2,1)S(1)}, bf16[512,128]{1,0:T(8,128)(2,1)S(1)}, u32[]{:S(2)}, u32[]{:S(2)}) %collective-permute-start.15) | collective-permute-done | bytes 131104 | tf_op jit(solution)/shard_map/ppermute | solution.py:889
  83.8 0.0 collective-permute-done.14.below_ref
  83.8 1.4 %shard_map.53 = (f32[2,16,64,64]{3,2,1,0:T(8,128)S(1)}, f32[32,128]{1,0:T(8,128)S(1)}) custom-call(bf16[576,128]{1,0:T(8,128)(2,1)S(1)} %collective-permute-done.14.below_ref, bf16[512,128]{1,0:T(8,128)(2,1)S(1)} %collective-permute-done.15.above_ref, f32[24,128,64]{2,1,0:T(8,128)S(1)} %shard_map.52.z_ref, f32[2,24,64,64]{3,2,1,0:T(8,128)S(1)} %get-tuple-element.94.y_ref, ...), custom_call_target="tpu_custom_call" | custom-call | tf_op jit(solution)/shard_map/pallas_call | solution.py:766
  85.2 0.0 collective-permute-start.16
  85.2 1.2 %collective-permute-done.16 = f32[32,128]{1,0:T(8,128)S(1)} collective-permute-done((f32[32,128]{1,0:T(8,128)S(1)}, f32[32,128]{1,0:T(8,128)S(1)}, u32[]{:S(2)}, u32[]{:S(2)}) %collective-permute-start.16) | collective-permute-done | bytes 16416 | tf_op jit(solution)/shard_map/ppermute | solution.py:882
  86.4 4.0 %collective-permute-start.19 = (f32[32,128]{1,0:T(8,128)S(1)}, f32[32,128]{1,0:T(8,128)S(1)}, u32[]{:S(2)}, u32[]{:S(2)}) collective-permute-start(f32[32,128]{1,0:T(8,128)S(1)} %add.16), channel_id=1, source_target_pairs={{0,6},{1,7},{2,4},{3,5},{4,2},{5,3},{6,0},{7,1},{8,14},{9,15},{10,... | collective-permute-start | bytes 49160 | tf_op jit(solution)/shard_map/ppermute | solution.py:882
  90.4 0.0 collective-permute-start.18
  90.4 0.6 collective-permute-start.17
  91.1 1.1 collective-permute-done.19
  92.2 2.9 %collective-permute-done.18 = f32[32,128]{1,0:T(8,128)S(1)} collective-permute-done((f32[32,128]{1,0:T(8,128)S(1)}, f32[32,128]{1,0:T(8,128)S(1)}, u32[]{:S(2)}, u32[]{:S(2)}) %collective-permute-start.18) | collective-permute-done | bytes 16416 | tf_op jit(solution)/shard_map/ppermute | solution.py:882
  95.1 0.0 collective-permute-done.17
  95.1 0.1 maximum_maximum_fusion.refs_0_
  95.2 5.8 %collective-permute-start.22 = (f32[64,128]{1,0:T(8,128)S(1)}, f32[64,128]{1,0:T(8,128)S(1)}, u32[]{:S(2)}, u32[]{:S(2)}) collective-permute-start(f32[64,128]{1,0:T(8,128)S(1)} %maximum_maximum_fusion.refs_0_), channel_id=1, source_target_pairs={{0,24},{8,16},{16,8},{24,0},{1,25},{9,17},{17,9},{25,1},{2,26},{10... | collective-permute-start | bytes 98312 | tf_op jit(solution)/shard_map/ppermute | solution.py:882
  101.0 0.9 collective-permute-start.20
  101.9 0.4 reshape.10.refs_5_
  102.2 0.6 collective-permute-done.22.refs_3_
  102.9 2.0 %collective-permute-done.21.refs_2_ = f32[64,128]{1,0:T(8,128)S(1)} collective-permute-done((f32[64,128]{1,0:T(8,128)S(1)}, f32[64,128]{1,0:T(8,128)S(1)}, u32[]{:S(2)}, u32[]{:S(2)}) %collective-permute-start.21) | collective-permute-done | bytes 32800 | tf_op jit(solution)/shard_map/ppermute | solution.py:882
  104.9 3.6 %shard_map.54 = f32[32,4096]{1,0:T(8,128)} custom-call(f32[64,128]{1,0:T(8,128)S(1)} %maximum_maximum_fusion.refs_0_, f32[64,128]{1,0:T(8,128)S(1)} %collective-permute-done.20.refs_1_, f32[64,128]{1,0:T(8,128)S(1)} %collective-permute-done.21.refs_2_, f32[64,128]{1,0:T(8,128)S(1)} %collective-permute-done.22.refs_3_, ...), custom_call_target="tpu_custom_call" | custom-call | tf_op jit(solution)/shard_map/pallas_call | solution.py:855
  (9 shorter events, 0.0 us)
Async XLA Ops:
  1.4 11.3 %copy-start = (s32[2,16,64]{2,1,0:T(8,128)S(1)}, s32[2,16,64]{2,1,0:T(8,128)}, u32[]{:S(2)}) copy-start(s32[2,16,64]{2,1,0:T(8,128)} %tissue_ref.7) | copy-start | bytes 24580
  1.4 28.5 %collective-permute-start.7 = (bf16[8,64,1024]{2,1,0:T(8,128)(2,1)S(1)}, bf16[8,64,1024]{2,1,0:T(8,128)(2,1)S(1)}, u32[]{:S(2)}, u32[]{:S(2)}) collective-permute-start(bf16[8,64,1024]{2,1,0:T(8,128)(2,1)S(1)} %shard_map.42), channel_id=1, source_target_pairs={{8,0},{16,8},{24,16},{9,1},{17,9},{25,17},{10,2},{18,10},{26,18},{... | collective-permute-start | bytes 3145736 | tf_op jit(solution)/shard_map/ppermute | solution.py:889
  4.2 1.4 %collective-permute-start = (f32[32,128]{1,0:T(8,128)S(1)}, f32[32,128]{1,0:T(8,128)S(1)}, u32[]{:S(2)}, u32[]{:S(2)}) collective-permute-start(f32[32,128]{1,0:T(8,128)S(1)} %shard_map.38), channel_id=1, source_target_pairs={{0,1},{1,0},{2,3},{3,2},{4,5},{5,4},{6,7},{7,6},{8,9},{9,8},{10,11... | collective-permute-start | bytes 49160 | tf_op jit(solution)/shard_map/ppermute | solution.py:882
  5.6 8.7 %collective-permute-start.3 = (f32[32,128]{1,0:T(8,128)S(1)}, f32[32,128]{1,0:T(8,128)S(1)}, u32[]{:S(2)}, u32[]{:S(2)}) collective-permute-start(f32[32,128]{1,0:T(8,128)S(1)} %add.15.refs_2_.refs_0_), channel_id=1, source_target_pairs={{0,6},{1,7},{2,4},{3,5},{4,2},{5,3},{6,0},{7,1},{8,14},{9,15},{10,... | collective-permute-start | bytes 49160 | tf_op jit(solution)/shard_map/ppermute | solution.py:882
  10.5 4.6 %collective-permute-start.2 = (f32[32,128]{1,0:T(8,128)S(1)}, f32[32,128]{1,0:T(8,128)S(1)}, u32[]{:S(2)}, u32[]{:S(2)}) collective-permute-start(f32[32,128]{1,0:T(8,128)S(1)} %add.15.refs_2_.refs_0_), channel_id=1, source_target_pairs={{0,4},{1,5},{2,6},{3,7},{4,0},{5,1},{6,2},{7,3},{8,12},{9,13},{10,... | collective-permute-start | bytes 49160 | tf_op jit(solution)/shard_map/ppermute | solution.py:882
  10.5 4.6 %collective-permute-start.1 = (f32[32,128]{1,0:T(8,128)S(1)}, f32[32,128]{1,0:T(8,128)S(1)}, u32[]{:S(2)}, u32[]{:S(2)}) collective-permute-start(f32[32,128]{1,0:T(8,128)S(1)} %add.15.refs_2_.refs_0_), channel_id=1, source_target_pairs={{0,2},{1,3},{2,0},{3,1},{4,6},{5,7},{6,4},{7,5},{8,10},{9,11},{10,... | collective-permute-start | bytes 49160 | tf_op jit(solution)/shard_map/ppermute | solution.py:882
  15.5 17.3 %collective-permute-start.5 = (bf16[2,4,64,1280]{3,2,1,0:T(8,128)(2,1)S(1)}, bf16[2,4,64,1280]{3,2,1,0:T(8,128)(2,1)S(1)}, u32[]{:S(2)}, u32[]{:S(2)}) collective-permute-start(bf16[2,4,64,1280]{3,2,1,0:T(8,128)(2,1)S(1)} %get-tuple-element.59), channel_id=1, source_target_pairs={{0,1},{1,2},{2,3},{3,4},{4,5},{5,6},{6,7},{8,9},{9,10},{10,11},{11... | collective-permute-start | bytes 3932168 | tf_op jit(solution)/shard_map/ppermute | solution.py:889
  16.9 15.9 %collective-permute-start.6 = (bf16[2,4,64,1280]{3,2,1,0:T(8,128)(2,1)S(1)}, bf16[2,4,64,1280]{3,2,1,0:T(8,128)(2,1)S(1)}, u32[]{:S(2)}, u32[]{:S(2)}) collective-permute-start(bf16[2,4,64,1280]{3,2,1,0:T(8,128)(2,1)S(1)} %get-tuple-element.53.after_ref), channel_id=1, source_target_pairs={{1,0},{2,1},{3,2},{4,3},{5,4},{6,5},{7,6},{9,8},{10,9},{11,10},{12... | collective-permute-start | bytes 3932168 | tf_op jit(solution)/shard_map/ppermute | solution.py:889
  21.5 30.9 %collective-permute-start.4 = (bf16[8,64,1024]{2,1,0:T(8,128)(2,1)S(1)}, bf16[8,64,1024]{2,1,0:T(8,128)(2,1)S(1)}, u32[]{:S(2)}, u32[]{:S(2)}) collective-permute-start(bf16[8,64,1024]{2,1,0:T(8,128)(2,1)S(1)} %get-tuple-element.54), channel_id=1, source_target_pairs={{8,0},{16,8},{24,16},{9,1},{17,9},{25,17},{10,2},{18,10},{26,18},{... | collective-permute-start | bytes 3145736 | tf_op jit(solution)/shard_map/ppermute | solution.py:889
  30.0 11.1 %collective-permute-start.8 = (bf16[4,64,1024]{2,1,0:T(8,128)(2,1)S(1)}, bf16[4,64,1024]{2,1,0:T(8,128)(2,1)S(1)}, u32[]{:S(2)}, u32[]{:S(2)}) collective-permute-start(bf16[4,64,1024]{2,1,0:T(8,128)(2,1)S(1)} %get-tuple-element.65), channel_id=1, source_target_pairs={{0,1},{1,2},{2,3},{3,4},{4,5},{5,6},{6,7},{8,9},{9,10},{10,11},{11... | collective-permute-start | bytes 1572872 | tf_op jit(solution)/shard_map/ppermute | solution.py:889
  31.3 9.8 %collective-permute-start.9 = (bf16[4,64,1024]{2,1,0:T(8,128)(2,1)S(1)}, bf16[4,64,1024]{2,1,0:T(8,128)(2,1)S(1)}, u32[]{:S(2)}, u32[]{:S(2)}) collective-permute-start(bf16[4,64,1024]{2,1,0:T(8,128)(2,1)S(1)} %get-tuple-element.60.after_ref), channel_id=1, source_target_pairs={{1,0},{2,1},{3,2},{4,3},{5,4},{6,5},{7,6},{9,8},{10,9},{11,10},{12... | collective-permute-start | bytes 1572872 | tf_op jit(solution)/shard_map/ppermute | solution.py:889
  39.8 20.1 %collective-permute-start.11 = (bf16[832,128]{1,0:T(8,128)(2,1)S(1)}, bf16[832,128]{1,0:T(8,128)(2,1)S(1)}, u32[]{:S(2)}, u32[]{:S(2)}) collective-permute-start(bf16[832,128]{1,0:T(8,128)(2,1)S(1)} %get-tuple-element.73), channel_id=1, source_target_pairs={{8,0},{16,8},{24,16},{9,1},{17,9},{25,17},{10,2},{18,10},{26,18},{... | collective-permute-start | bytes 638984 | tf_op jit(solution)/shard_map/ppermute | solution.py:889
  55.1 7.9 %collective-permute-start.10 = (bf16[768,128]{1,0:T(8,128)(2,1)S(1)}, bf16[768,128]{1,0:T(8,128)(2,1)S(1)}, u32[]{:S(2)}, u32[]{:S(2)}) collective-permute-start(bf16[768,128]{1,0:T(8,128)(2,1)S(1)} %get-tuple-element.72), channel_id=1, source_target_pairs={{0,8},{8,16},{16,24},{1,9},{9,17},{17,25},{2,10},{10,18},{18,26},{... | collective-permute-start | bytes 589832 | tf_op jit(solution)/shard_map/ppermute | solution.py:889
  64.3 9.0 %collective-permute-start.12 = (bf16[640,128]{1,0:T(8,128)(2,1)S(1)}, bf16[640,128]{1,0:T(8,128)(2,1)S(1)}, u32[]{:S(2)}, u32[]{:S(2)}) collective-permute-start(bf16[640,128]{1,0:T(8,128)(2,1)S(1)} %get-tuple-element.83), channel_id=1, source_target_pairs={{8,0},{16,8},{24,16},{9,1},{17,9},{25,17},{10,2},{18,10},{26,18},{... | collective-permute-start | bytes 491528 | tf_op jit(solution)/shard_map/ppermute | solution.py:889
  65.6 7.7 %collective-permute-start.13 = (bf16[576,128]{1,0:T(8,128)(2,1)S(1)}, bf16[576,128]{1,0:T(8,128)(2,1)S(1)}, u32[]{:S(2)}, u32[]{:S(2)}) collective-permute-start(bf16[576,128]{1,0:T(8,128)(2,1)S(1)} %get-tuple-element.84), channel_id=1, source_target_pairs={{0,8},{8,16},{16,24},{1,9},{9,17},{17,25},{2,10},{10,18},{18,26},{... | collective-permute-start | bytes 442376 | tf_op jit(solution)/shard_map/ppermute | solution.py:889
  74.6 9.3 %collective-permute-start.14 = (bf16[576,128]{1,0:T(8,128)(2,1)S(1)}, bf16[576,128]{1,0:T(8,128)(2,1)S(1)}, u32[]{:S(2)}, u32[]{:S(2)}) collective-permute-start(bf16[576,128]{1,0:T(8,128)(2,1)S(1)} %get-tuple-element.91), channel_id=1, source_target_pairs={{8,0},{16,8},{24,16},{9,1},{17,9},{25,17},{10,2},{18,10},{26,18},{... | collective-permute-start | bytes 442376 | tf_op jit(solution)/shard_map/ppermute | solution.py:889
  75.9 8.0 %collective-permute-start.15 = (bf16[512,128]{1,0:T(8,128)(2,1)S(1)}, bf16[512,128]{1,0:T(8,128)(2,1)S(1)}, u32[]{:S(2)}, u32[]{:S(2)}) collective-permute-start(bf16[512,128]{1,0:T(8,128)(2,1)S(1)} %get-tuple-element.92), channel_id=1, source_target_pairs={{0,8},{8,16},{16,24},{1,9},{9,17},{17,25},{2,10},{10,18},{18,26},{... | collective-permute-start | bytes 393224 | tf_op jit(solution)/shard_map/ppermute | solution.py:889
  85.2 1.2 %collective-permute-start.16 = (f32[32,128]{1,0:T(8,128)S(1)}, f32[32,128]{1,0:T(8,128)S(1)}, u32[]{:S(2)}, u32[]{:S(2)}) collective-permute-start(f32[32,128]{1,0:T(8,128)S(1)} %get-tuple-element.95), channel_id=1, source_target_pairs={{0,1},{1,0},{2,3},{3,2},{4,5},{5,4},{6,7},{7,6},{8,9},{9,8},{10,11... | collective-permute-start | bytes 49160 | tf_op jit(solution)/shard_map/ppermute | solution.py:882
  86.4 5.8 %collective-permute-start.19 = (f32[32,128]{1,0:T(8,128)S(1)}, f32[32,128]{1,0:T(8,128)S(1)}, u32[]{:S(2)}, u32[]{:S(2)}) collective-permute-start(f32[32,128]{1,0:T(8,128)S(1)} %add.16), channel_id=1, source_target_pairs={{0,6},{1,7},{2,4},{3,5},{4,2},{5,3},{6,0},{7,1},{8,14},{9,15},{10,... | collective-permute-start | bytes 49160 | tf_op jit(solution)/shard_map/ppermute | solution.py:882
  90.4 4.6 %collective-permute-start.18 = (f32[32,128]{1,0:T(8,128)S(1)}, f32[32,128]{1,0:T(8,128)S(1)}, u32[]{:S(2)}, u32[]{:S(2)}) collective-permute-start(f32[32,128]{1,0:T(8,128)S(1)} %add.16), channel_id=1, source_target_pairs={{0,4},{1,5},{2,6},{3,7},{4,0},{5,1},{6,2},{7,3},{8,12},{9,13},{10,... | collective-permute-start | bytes 49160 | tf_op jit(solution)/shard_map/ppermute | solution.py:882
  90.4 4.6 %collective-permute-start.17 = (f32[32,128]{1,0:T(8,128)S(1)}, f32[32,128]{1,0:T(8,128)S(1)}, u32[]{:S(2)}, u32[]{:S(2)}) collective-permute-start(f32[32,128]{1,0:T(8,128)S(1)} %add.16), channel_id=1, source_target_pairs={{0,2},{1,3},{2,0},{3,1},{4,6},{5,7},{6,4},{7,5},{8,10},{9,11},{10,... | collective-permute-start | bytes 49160 | tf_op jit(solution)/shard_map/ppermute | solution.py:882
  95.2 7.7 %collective-permute-start.22 = (f32[64,128]{1,0:T(8,128)S(1)}, f32[64,128]{1,0:T(8,128)S(1)}, u32[]{:S(2)}, u32[]{:S(2)}) collective-permute-start(f32[64,128]{1,0:T(8,128)S(1)} %maximum_maximum_fusion.refs_0_), channel_id=1, source_target_pairs={{0,24},{8,16},{16,8},{24,0},{1,25},{9,17},{17,9},{25,1},{2,26},{10... | collective-permute-start | bytes 98312 | tf_op jit(solution)/shard_map/ppermute | solution.py:882
  101.0 3.9 %collective-permute-start.21 = (f32[64,128]{1,0:T(8,128)S(1)}, f32[64,128]{1,0:T(8,128)S(1)}, u32[]{:S(2)}, u32[]{:S(2)}) collective-permute-start(f32[64,128]{1,0:T(8,128)S(1)} %maximum_maximum_fusion.refs_0_), channel_id=1, source_target_pairs={{0,16},{8,24},{16,0},{24,8},{1,17},{9,25},{17,1},{25,9},{2,18},{10... | collective-permute-start | bytes 98312 | tf_op jit(solution)/shard_map/ppermute | solution.py:882
  101.0 3.9 %collective-permute-start.20 = (f32[64,128]{1,0:T(8,128)S(1)}, f32[64,128]{1,0:T(8,128)S(1)}, u32[]{:S(2)}, u32[]{:S(2)}) collective-permute-start(f32[64,128]{1,0:T(8,128)S(1)} %maximum_maximum_fusion.refs_0_), channel_id=1, source_target_pairs={{0,8},{8,0},{16,24},{24,16},{1,9},{9,1},{17,25},{25,17},{2,10},{10... | collective-permute-start | bytes 98312 | tf_op jit(solution)/shard_map/ppermute | solution.py:882

commit v9 on v8

--- a/solution.py
+++ b/solution.py
@@ -898,7 +898,7 @@
     parts = summed_parts(start_gram(probe), "col", balanced)
     own_panel = probe.reshape(tile_rows, tile_cols, patches, RANK)
     left_end, right_end = gate(mark_ends(features, tissue, own_panel), parts)
-    middle, unit0, unit1 = own_units(features, tissue, left_end)
+    middle, unit0, unit1 = own_units(features, tissue, edges)
     from_left = passed_along(right_end, "col", 1)
     from_right = passed_along(left_end, "col", -1)
     below_middle = passed_along(middle, "row", -1)

time: 109 us -> 109 us (level)
  no operation moved by 1% of the time
where the time goes in v9:
time: 109 us
  starting transfers between devices  44.7 us (41%)
  Pallas kernels  34.7 us (32%)
  waiting for transfers between devices  27 us (25%)
  local copies, waits for them, and re-layouts  1.82 us (2%)
    ppermute x12, starting transfers between devices, passed_along(): return lax.ppermute(shard, axis, pairs)  27.2 us
    ppermute x11, starting transfers between devices, summed_parts(): lax.ppermute(gram, axis, [(i, i ^ p) for i in range(size)])  17.5 us
    ppermute x12, waiting for transfers between devices, passed_along(): return lax.ppermute(shard, axis, pairs)  17.5 us
    ppermute x11, waiting for transfers between devices, summed_parts(): lax.ppermute(gram, axis, [(i, i ^ p) for i in range(size)])  9.49 us
    pallas_call x2, Pallas kernels, cross_affinity(): pl.pallas_call(functools.partial(cross_kernel, n, stage), out_shape=(sds(...  5.7 us
    pallas_call x1, Pallas kernels, finish(): kernel_call(functools.partial(finish_kernel, factor, len(parts)), sds(y.s...  3.63 us
    pallas_call x1, Pallas kernels, start_panel(): kernel_call(functools.partial(start_kernel, factor, len(parts)), (sds((ro...  3.59 us
    pallas_call x1, Pallas kernels, inside_affinity(): pl.pallas_call(functools.partial(inside_kernel, n), out_shape=(sds((n, bo...  3.49 us
  transfers between devices with their start and end apart: 23, of which 12 were waited for; matrix products, arithmetic and copies ran while one was open for 2% of the time, Pallas kernels for 24%

profile of v9, /device:TPU:0, one launch (start us, length us, event | category | flops | bytes accessed | tf_op | source)
XLA Modules:
  0.0 108.5 jit_solution(6253547456492238170)
XLA Ops:
  0.0 1.4 %shard_map.37.after_ref = bf16[8,64,1024]{2,1,0:T(8,128)(2,1)S(1)} custom-call(bf16[2,16,64,1024]{3,2,1,0:T(8,128)(2,1)} %x_ref.5, s32[2,16,64]{2,1,0:T(8,128)} %tissue_ref.7), custom_call_target="tpu_custom_call" | custom-call | tf_op jit(solution)/shard_map/pallas_call | solution.py:188
  1.4 0.0 copy-start
  1.4 1.3 %collective-permute-start.7 = (bf16[8,64,1024]{2,1,0:T(8,128)(2,1)S(1)}, bf16[8,64,1024]{2,1,0:T(8,128)(2,1)S(1)}, u32[]{:S(2)}, u32[]{:S(2)}) collective-permute-start(bf16[8,64,1024]{2,1,0:T(8,128)(2,1)S(1)} %shard_map.37.after_ref), channel_id=1, source_target_pairs={{8,0},{16,8},{24,16},{9,1},{17,9},{25,17},{10,2},{18,10},{26,18},{... | collective-permute-start | bytes 3145736 | tf_op jit(solution)/shard_map/ppermute | solution.py:889
  2.7 1.5 %shard_map.41 = f32[32,128]{1,0:T(8,128)S(1)} custom-call(f32[2,16,4096]{2,1,0:T(8,128)} %probe_ref.1), custom_call_target="tpu_custom_call" | custom-call | tf_op jit(solution)/shard_map/pallas_call | solution.py:162
  4.2 0.5 collective-permute-start.1
  4.7 0.8 collective-permute-done.1
  5.6 4.9 %collective-permute-start.4 = (f32[32,128]{1,0:T(8,128)S(1)}, f32[32,128]{1,0:T(8,128)S(1)}, u32[]{:S(2)}, u32[]{:S(2)}) collective-permute-start(f32[32,128]{1,0:T(8,128)S(1)} %add.15.refs_2_.refs_0_), channel_id=1, source_target_pairs={{0,6},{1,7},{2,4},{3,5},{4,2},{5,3},{6,0},{7,1},{8,14},{9,15},{10,... | collective-permute-start | bytes 49160 | tf_op jit(solution)/shard_map/ppermute | solution.py:882
  10.5 0.0 collective-permute-start.3
  10.5 0.6 collective-permute-start.2
  11.2 1.5 %reshape.9.probe_ref.refs_6_ = f32[2,16,64,64]{3,2,1,0:T(8,128)S(1)} reshape(f32[2,16,4096]{2,1,0:T(8,128)} %probe_ref.1) | data formatting | bytes 1048576 | tf_op jit(solution)/shard_map/reshape | solution.py:899
  12.6 1.7 %shard_map.40 = (bf16[2,4,64,1280]{3,2,1,0:T(8,128)(2,1)S(1)}, bf16[2,4,64,1280]{3,2,1,0:T(8,128)(2,1)S(1)}) custom-call(bf16[2,16,64,1024]{3,2,1,0:T(8,128)(2,1)} %x_ref.5, s32[2,16,64]{2,1,0:T(8,128)S(1)} %copy-done, f32[2,16,64,64]{3,2,1,0:T(8,128)S(1)} %reshape.9.probe_ref.refs_6_), custom_call_target="tpu_custom_call" | custom-call | tf_op jit(solution)/shard_map/pallas_call | solution.py:237
  14.3 0.0 collective-permute-done.4.refs_5_.refs_3_
  14.3 0.8 collective-permute-done.3.refs_4_.refs_2_
  15.2 0.0 collective-permute-done.2.refs_3_.refs_1_
  15.2 0.3 shard_map.42
  15.5 1.4 %collective-permute-start.5 = (bf16[2,4,64,1280]{3,2,1,0:T(8,128)(2,1)S(1)}, bf16[2,4,64,1280]{3,2,1,0:T(8,128)(2,1)S(1)}, u32[]{:S(2)}, u32[]{:S(2)}) collective-permute-start(bf16[2,4,64,1280]{3,2,1,0:T(8,128)(2,1)S(1)} %get-tuple-element.58), channel_id=1, source_target_pairs={{0,1},{1,2},{2,3},{3,4},{4,5},{5,6},{6,7},{8,9},{9,10},{10,11},{11... | collective-permute-start | bytes 3932168 | tf_op jit(solution)/shard_map/ppermute | solution.py:889
  16.9 1.3 %collective-permute-start.6 = (bf16[2,4,64,1280]{3,2,1,0:T(8,128)(2,1)S(1)}, bf16[2,4,64,1280]{3,2,1,0:T(8,128)(2,1)S(1)}, u32[]{:S(2)}, u32[]{:S(2)}) collective-permute-start(bf16[2,4,64,1280]{3,2,1,0:T(8,128)(2,1)S(1)} %get-tuple-element.59), channel_id=1, source_target_pairs={{1,0},{2,1},{3,2},{4,3},{5,4},{6,5},{7,6},{9,8},{10,9},{11,10},{12... | collective-permute-start | bytes 3932168 | tf_op jit(solution)/shard_map/ppermute | solution.py:889
  18.2 3.3 %shard_map.38 = (bf16[8,64,1024]{2,1,0:T(8,128)(2,1)S(1)}, bf16[1536,1024]{1,0:T(8,128)(2,1)S(1)}, bf16[1536,1024]{1,0:T(8,128)(2,1)S(1)}) custom-call(bf16[2,16,64,1024]{3,2,1,0:T(8,128)(2,1)} %x_ref.5, s32[2,16,64]{2,1,0:T(8,128)S(1)} %copy-done, bf16[8,64,1024]{2,1,0:T(8,128)(2,1)S(1)} %shard_map.37.after_ref), custom_call_target="tpu_custom_call" | custom-call | tf_op jit(solution)/shard_map/pallas_call | solution.py:272
  21.5 1.3 %collective-permute-start = (bf16[8,64,1024]{2,1,0:T(8,128)(2,1)S(1)}, bf16[8,64,1024]{2,1,0:T(8,128)(2,1)S(1)}, u32[]{:S(2)}, u32[]{:S(2)}) collective-permute-start(bf16[8,64,1024]{2,1,0:T(8,128)(2,1)S(1)} %get-tuple-element.51), channel_id=1, source_target_pairs={{8,0},{16,8},{24,16},{9,1},{17,9},{25,17},{10,2},{18,10},{26,18},{... | collective-permute-start | bytes 3145736 | tf_op jit(solution)/shard_map/ppermute | solution.py:889
  22.8 3.5 %shard_map.39 = (bf16[24,128,384]{2,1,0:T(8,128)(2,1)S(1)}, f32[2,128,128]{2,1,0:T(8,128)S(1)}) custom-call(bf16[1536,1024]{1,0:T(8,128)(2,1)S(1)} %get-tuple-element.52.unit0_ref.start0_ref, bf16[1536,1024]{1,0:T(8,128)(2,1)S(1)} %get-tuple-element.53.unit1_ref.start1_ref), custom_call_target="tpu_custom_call" | custom-call | tf_op jit(solution)/shard_map/pallas_call | solution.py:322
  26.3 3.6 %collective-permute-done.7.be_ref.refs_1_ = bf16[8,64,1024]{2,1,0:T(8,128)(2,1)S(1)} collective-permute-done((bf16[8,64,1024]{2,1,0:T(8,128)(2,1)S(1)}, bf16[8,64,1024]{2,1,0:T(8,128)(2,1)S(1)}, u32[]{:S(2)}, u32[]{:S(2)}) %collective-permute-start.7) | collective-permute-done | bytes 1048608 | tf_op jit(solution)/shard_map/ppermute | solution.py:889
  29.9 0.1 shard_map.43
  30.0 1.3 %collective-permute-start.8 = (bf16[4,64,1024]{2,1,0:T(8,128)(2,1)S(1)}, bf16[4,64,1024]{2,1,0:T(8,128)(2,1)S(1)}, u32[]{:S(2)}, u32[]{:S(2)}) collective-permute-start(bf16[4,64,1024]{2,1,0:T(8,128)(2,1)S(1)} %get-tuple-element.65), channel_id=1, source_target_pairs={{0,1},{1,2},{2,3},{3,4},{4,5},{5,6},{6,7},{8,9},{9,10},{10,11},{11... | collective-permute-start | bytes 1572872 | tf_op jit(solution)/shard_map/ppermute | solution.py:889
  31.3 1.5 %collective-permute-start.9 = (bf16[4,64,1024]{2,1,0:T(8,128)(2,1)S(1)}, bf16[4,64,1024]{2,1,0:T(8,128)(2,1)S(1)}, u32[]{:S(2)}, u32[]{:S(2)}) collective-permute-start(bf16[4,64,1024]{2,1,0:T(8,128)(2,1)S(1)} %get-tuple-element.60.after_ref), channel_id=1, source_target_pairs={{1,0},{2,1},{3,2},{4,3},{5,4},{6,5},{7,6},{9,8},{10,9},{11,10},{12... | collective-permute-start | bytes 1572872 | tf_op jit(solution)/shard_map/ppermute | solution.py:889
  32.8 0.0 collective-permute-done.5.xl_ref.refs_5_
  32.8 0.0 collective-permute-done.6.xr_ref.refs_7_
  32.8 3.3 %shard_map.44 = (bf16[1536,1024]{1,0:T(8,128)(2,1)S(1)}, bf16[1536,1024]{1,0:T(8,128)(2,1)S(1)}, bf16[24,128,384]{2,1,0:T(8,128)(2,1)S(1)}, f32[3,128,128]{2,1,0:T(8,128)S(1)}) custom-call(bf16[1536,1024]{1,0:T(8,128)(2,1)S(1)} %get-tuple-element.52.unit0_ref.start0_ref, ...), custom_call_target="tpu_custom_call", output_to_operand_aliasing={{0}: (0, {}), {1}: (1, {}), {2}: (2, {})} | custom-call | tf_op jit(solution)/shard_map/pallas_call | solution.py:375
  36.2 3.6 %shard_map.45 = (f32[2,24,64,64]{3,2,1,0:T(8,128)S(1)}, bf16[832,128]{1,0:T(8,128)(2,1)S(1)}, f32[2,64,64]{2,1,0:T(8,128)S(1)}) custom-call(f32[32,128]{1,0:T(8,128)S(1)} %add.15.refs_2_.refs_0_, f32[32,128]{1,0:T(8,128)S(1)} %collective-permute-done.2.refs_3_.refs_1_, f32[32,128]{1,0:T(8,128)S(1)} %collective-permute-done.3.refs_4_.refs_2_, ...), custom_call_target="tpu_custom_call" | custom-call | tf_op jit(solution)/shard_map/pallas_call | solution.py:431
  39.8 1.3 %collective-permute-start.11 = (bf16[832,128]{1,0:T(8,128)(2,1)S(1)}, bf16[832,128]{1,0:T(8,128)(2,1)S(1)}, u32[]{:S(2)}, u32[]{:S(2)}) collective-permute-start(bf16[832,128]{1,0:T(8,128)(2,1)S(1)} %get-tuple-element.73), channel_id=1, source_target_pairs={{8,0},{16,8},{24,16},{9,1},{17,9},{25,17},{10,2},{18,10},{26,18},{... | collective-permute-start | bytes 638984 | tf_op jit(solution)/shard_map/ppermute | solution.py:889
  41.1 0.0 collective-permute-done.8.refs_0_
  41.1 3.0 %shard_map.46 = (bf16[11,128,256]{2,1,0:T(8,128)(2,1)S(1)}, bf16[11,128,256]{2,1,0:T(8,128)(2,1)S(1)}, f32[3,64,128]{2,1,0:T(8,128)S(1)}, bf16[24,64,64]{2,1,0:T...) custom-call(bf16[4,64,1024]{2,1,0:T(8,128)(2,1)S(1)} %collective-permute-done.8.refs_0_, ...), custom_call_target="tpu_custom_call" | custom-call | tf_op jit(solution)/shard_map/pallas_call | solution.py:576
  44.1 8.3 %collective-permute-done.refs_0_ = bf16[8,64,1024]{2,1,0:T(8,128)(2,1)S(1)} collective-permute-done((bf16[8,64,1024]{2,1,0:T(8,128)(2,1)S(1)}, bf16[8,64,1024]{2,1,0:T(8,128)(2,1)S(1)}, u32[]{:S(2)}, u32[]{:S(2)}) %collective-permute-start) | collective-permute-done | bytes 1048608 | tf_op jit(solution)/shard_map/ppermute | solution.py:889
  52.4 2.7 %shard_map.47 = (bf16[11,128,256]{2,1,0:T(8,128)(2,1)S(1)}, bf16[11,128,256]{2,1,0:T(8,128)(2,1)S(1)}, f32[3,64,128]{2,1,0:T(8,128)S(1)}, bf16[24,64,64]{2,1,0:T...) custom-call(bf16[8,64,1024]{2,1,0:T(8,128)(2,1)S(1)} %collective-per, ...), custom_call_target="tpu_custom_call", output_to_operand_aliasing={{0}: (5, {}), {1}: (6, {}), {2}: (7, {}), {3}: (8, {}), {4}... | custom-call | tf_op jit(solution)/shard_map/pallas_call | solution.py:576
  55.1 4.8 %collective-permute-start.10 = (bf16[768,128]{1,0:T(8,128)(2,1)S(1)}, bf16[768,128]{1,0:T(8,128)(2,1)S(1)}, u32[]{:S(2)}, u32[]{:S(2)}) collective-permute-start(bf16[768,128]{1,0:T(8,128)(2,1)S(1)} %get-tuple-element.72), channel_id=1, source_target_pairs={{0,8},{8,16},{16,24},{1,9},{9,17},{17,25},{2,10},{10,18},{18,26},{... | collective-permute-start | bytes 589832 | tf_op jit(solution)/shard_map/ppermute | solution.py:889
  59.8 0.0 collective-permute-done.11.got_ref
  59.8 1.4 %shard_map.48 = (f32[24,128,64]{2,1,0:T(8,128)S(1)}, f32[24,64,64]{2,1,0:T(8,128)S(1)}, f32[24,64,64]{2,1,0:T(8,128)S(1)}, f32[24,64,64]{2,1,0:T(8,128)S(1)}, bf16[2,64,64]{2,1,0:T(8,128)(2,1)S(1)}) custom-call(bf16[832,128]{1,0:T(8,128)(2,1)S(1)} %collective-permute-done.11.got_ref, f32[3,64,128]{2,1,0:T(8,128)S(1)} %get-tuple-element.74.sum_ref, ...), custom_call_target="tpu_custom_call" | custom-call | tf_op jit(solution)/shard_map/pallas_call | solution.py:621
  61.3 1.7 %collective-permute-done.10.got_ref = bf16[768,128]{1,0:T(8,128)(2,1)S(1)} collective-permute-done((bf16[768,128]{1,0:T(8,128)(2,1)S(1)}, bf16[768,128]{1,0:T(8,128)(2,1)S(1)}, u32[]{:S(2)}, u32[]{:S(2)}) %collective-permute-start.10) | collective-permute-done | bytes 196640 | tf_op jit(solution)/shard_map/ppermute | solution.py:889
  62.9 1.3 %shard_map.49 = (f32[2,24,64,64]{3,2,1,0:T(8,128)S(1)}, bf16[2,24,64,64]{3,2,1,0:T(8,128)(2,1)S(1)}, f32[24,64,64]{2,1,0:T(8,128)S(1)}, f32[24,64,64]{2,1,0:T(8,...) custom-call(bf16[768,128]{1,0:T(8,128)(2,1)S(1)} %collective-permute-done.10.go, ...), custom_call_target="tpu_custom_call" | custom-call | tf_op jit(solution)/shard_map/pallas_call | solution.py:666
  64.3 1.3 %collective-permute-start.12 = (bf16[640,128]{1,0:T(8,128)(2,1)S(1)}, bf16[640,128]{1,0:T(8,128)(2,1)S(1)}, u32[]{:S(2)}, u32[]{:S(2)}) collective-permute-start(bf16[640,128]{1,0:T(8,128)(2,1)S(1)} %get-tuple-element.83), channel_id=1, source_target_pairs={{8,0},{16,8},{24,16},{9,1},{17,9},{25,17},{10,2},{18,10},{26,18},{... | collective-permute-start | bytes 491528 | tf_op jit(solution)/shard_map/ppermute | solution.py:889
  65.6 5.0 %collective-permute-start.13 = (bf16[576,128]{1,0:T(8,128)(2,1)S(1)}, bf16[576,128]{1,0:T(8,128)(2,1)S(1)}, u32[]{:S(2)}, u32[]{:S(2)}) collective-permute-start(bf16[576,128]{1,0:T(8,128)(2,1)S(1)} %get-tuple-element.84), channel_id=1, source_target_pairs={{0,8},{8,16},{16,24},{1,9},{9,17},{17,25},{2,10},{10,18},{18,26},{... | collective-permute-start | bytes 442376 | tf_op jit(solution)/shard_map/ppermute | solution.py:889
  70.6 0.6 shard_map.50.z_ref
  71.2 2.0 %collective-permute-done.13.above_ref = bf16[576,128]{1,0:T(8,128)(2,1)S(1)} collective-permute-done((bf16[576,128]{1,0:T(8,128)(2,1)S(1)}, bf16[576,128]{1,0:T(8,128)(2,1)S(1)}, u32[]{:S(2)}, u32[]{:S(2)}) %collective-permute-start.13) | collective-permute-done | bytes 147488 | tf_op jit(solution)/shard_map/ppermute | solution.py:889
  73.3 1.3 %shard_map.51 = (f32[2,24,64,64]{3,2,1,0:T(8,128)S(1)}, bf16[2,24,64,64]{3,2,1,0:T(8,128)(2,1)S(1)}, bf16[576,128]{1,0:T(8,128)(2,1)S(1)}, bf16[512,128]{1,0:T(8,128)(2,1)S(1)}) custom-call(bf16[640,128]{1,0:T(8,128)(2,1)S(1)} %collective-permute-done.12.below_ref, bf16[576,128]{1,0:T(8,128)(2,1)S(1)} %collective-permute-done.13.above_ref, ...), custom_call_target="tpu_custom_call" | custom-call | tf_op jit(solution)/shard_map/pallas_call | solution.py:735
  74.6 1.3 %collective-permute-start.14 = (bf16[576,128]{1,0:T(8,128)(2,1)S(1)}, bf16[576,128]{1,0:T(8,128)(2,1)S(1)}, u32[]{:S(2)}, u32[]{:S(2)}) collective-permute-start(bf16[576,128]{1,0:T(8,128)(2,1)S(1)} %get-tuple-element.91), channel_id=1, source_target_pairs={{8,0},{16,8},{24,16},{9,1},{17,9},{25,17},{10,2},{18,10},{26,18},{... | collective-permute-start | bytes 442376 | tf_op jit(solution)/shard_map/ppermute | solution.py:889
  75.9 5.5 %collective-permute-start.15 = (bf16[512,128]{1,0:T(8,128)(2,1)S(1)}, bf16[512,128]{1,0:T(8,128)(2,1)S(1)}, u32[]{:S(2)}, u32[]{:S(2)}) collective-permute-start(bf16[512,128]{1,0:T(8,128)(2,1)S(1)} %get-tuple-element.92), channel_id=1, source_target_pairs={{0,8},{8,16},{16,24},{1,9},{9,17},{17,25},{2,10},{10,18},{18,26},{... | collective-permute-start | bytes 393224 | tf_op jit(solution)/shard_map/ppermute | solution.py:889
  81.3 0.6 shard_map.52.z_ref
  81.9 1.9 %collective-permute-done.15.above_ref = bf16[512,128]{1,0:T(8,128)(2,1)S(1)} collective-permute-done((bf16[512,128]{1,0:T(8,128)(2,1)S(1)}, bf16[512,128]{1,0:T(8,128)(2,1)S(1)}, u32[]{:S(2)}, u32[]{:S(2)}) %collective-permute-start.15) | collective-permute-done | bytes 131104 | tf_op jit(solution)/shard_map/ppermute | solution.py:889
  83.8 0.0 collective-permute-done.14.below_ref
  83.8 1.4 %shard_map.53 = (f32[2,16,64,64]{3,2,1,0:T(8,128)S(1)}, f32[32,128]{1,0:T(8,128)S(1)}) custom-call(bf16[576,128]{1,0:T(8,128)(2,1)S(1)} %collective-permute-done.14.below_ref, bf16[512,128]{1,0:T(8,128)(2,1)S(1)} %collective-permute-done.15.above_ref, f32[24,128,64]{2,1,0:T(8,128)S(1)} %shard_map.52.z_ref, f32[2,24,64,64]{3,2,1,0:T(8,128)S(1)} %get-tuple-element.94.y_ref, ...), custom_call_target="tpu_custom_call" | custom-call | tf_op jit(solution)/shard_map/pallas_call | solution.py:766
  85.2 0.0 collective-permute-start.16
  85.2 1.2 %collective-permute-done.16 = f32[32,128]{1,0:T(8,128)S(1)} collective-permute-done((f32[32,128]{1,0:T(8,128)S(1)}, f32[32,128]{1,0:T(8,128)S(1)}, u32[]{:S(2)}, u32[]{:S(2)}) %collective-permute-start.16) | collective-permute-done | bytes 16416 | tf_op jit(solution)/shard_map/ppermute | solution.py:882
  86.4 4.0 %collective-permute-start.19 = (f32[32,128]{1,0:T(8,128)S(1)}, f32[32,128]{1,0:T(8,128)S(1)}, u32[]{:S(2)}, u32[]{:S(2)}) collective-permute-start(f32[32,128]{1,0:T(8,128)S(1)} %add.16), channel_id=1, source_target_pairs={{0,6},{1,7},{2,4},{3,5},{4,2},{5,3},{6,0},{7,1},{8,14},{9,15},{10,... | collective-permute-start | bytes 49160 | tf_op jit(solution)/shard_map/ppermute | solution.py:882
  90.4 0.0 collective-permute-start.18
  90.4 0.6 collective-permute-start.17
  91.1 1.1 collective-permute-done.19
  92.2 2.9 %collective-permute-done.18 = f32[32,128]{1,0:T(8,128)S(1)} collective-permute-done((f32[32,128]{1,0:T(8,128)S(1)}, f32[32,128]{1,0:T(8,128)S(1)}, u32[]{:S(2)}, u32[]{:S(2)}) %collective-permute-start.18) | collective-permute-done | bytes 16416 | tf_op jit(solution)/shard_map/ppermute | solution.py:882
  95.1 0.0 collective-permute-done.17
  95.1 0.1 maximum_maximum_fusion.refs_0_
  95.2 5.8 %collective-permute-start.22 = (f32[64,128]{1,0:T(8,128)S(1)}, f32[64,128]{1,0:T(8,128)S(1)}, u32[]{:S(2)}, u32[]{:S(2)}) collective-permute-start(f32[64,128]{1,0:T(8,128)S(1)} %maximum_maximum_fusion.refs_0_), channel_id=1, source_target_pairs={{0,24},{8,16},{16,8},{24,0},{1,25},{9,17},{17,9},{25,1},{2,26},{10... | collective-permute-start | bytes 98312 | tf_op jit(solution)/shard_map/ppermute | solution.py:882
  101.0 0.9 collective-permute-start.20
  101.9 0.4 reshape.10.refs_5_
  102.2 0.6 collective-permute-done.22.refs_3_
  102.9 2.0 %collective-permute-done.21.refs_2_ = f32[64,128]{1,0:T(8,128)S(1)} collective-permute-done((f32[64,128]{1,0:T(8,128)S(1)}, f32[64,128]{1,0:T(8,128)S(1)}, u32[]{:S(2)}, u32[]{:S(2)}) %collective-permute-start.21) | collective-permute-done | bytes 32800 | tf_op jit(solution)/shard_map/ppermute | solution.py:882
  104.9 3.6 %shard_map.54 = f32[32,4096]{1,0:T(8,128)} custom-call(f32[64,128]{1,0:T(8,128)S(1)} %maximum_maximum_fusion.refs_0_, f32[64,128]{1,0:T(8,128)S(1)} %collective-permute-done.20.refs_1_, f32[64,128]{1,0:T(8,128)S(1)} %collective-permute-done.21.refs_2_, f32[64,128]{1,0:T(8,128)S(1)} %collective-permute-done.22.refs_3_, ...), custom_call_target="tpu_custom_call" | custom-call | tf_op jit(solution)/shard_map/pallas_call | solution.py:855
  (9 shorter events, 0.0 us)
Async XLA Ops:
  1.4 11.3 %copy-start = (s32[2,16,64]{2,1,0:T(8,128)S(1)}, s32[2,16,64]{2,1,0:T(8,128)}, u32[]{:S(2)}) copy-start(s32[2,16,64]{2,1,0:T(8,128)} %tissue_ref.7) | copy-start | bytes 24580
  1.4 28.5 %collective-permute-start.7 = (bf16[8,64,1024]{2,1,0:T(8,128)(2,1)S(1)}, bf16[8,64,1024]{2,1,0:T(8,128)(2,1)S(1)}, u32[]{:S(2)}, u32[]{:S(2)}) collective-permute-start(bf16[8,64,1024]{2,1,0:T(8,128)(2,1)S(1)} %shard_map.37.after_ref), channel_id=1, source_target_pairs={{8,0},{16,8},{24,16},{9,1},{17,9},{25,17},{10,2},{18,10},{26,18},{... | collective-permute-start | bytes 3145736 | tf_op jit(solution)/shard_map/ppermute | solution.py:889
  4.2 1.4 %collective-permute-start.1 = (f32[32,128]{1,0:T(8,128)S(1)}, f32[32,128]{1,0:T(8,128)S(1)}, u32[]{:S(2)}, u32[]{:S(2)}) collective-permute-start(f32[32,128]{1,0:T(8,128)S(1)} %shard_map.41), channel_id=1, source_target_pairs={{0,1},{1,0},{2,3},{3,2},{4,5},{5,4},{6,7},{7,6},{8,9},{9,8},{10,11... | collective-permute-start | bytes 49160 | tf_op jit(solution)/shard_map/ppermute | solution.py:882
  5.6 8.7 %collective-permute-start.4 = (f32[32,128]{1,0:T(8,128)S(1)}, f32[32,128]{1,0:T(8,128)S(1)}, u32[]{:S(2)}, u32[]{:S(2)}) collective-permute-start(f32[32,128]{1,0:T(8,128)S(1)} %add.15.refs_2_.refs_0_), channel_id=1, source_target_pairs={{0,6},{1,7},{2,4},{3,5},{4,2},{5,3},{6,0},{7,1},{8,14},{9,15},{10,... | collective-permute-start | bytes 49160 | tf_op jit(solution)/shard_map/ppermute | solution.py:882
  10.5 4.6 %collective-permute-start.3 = (f32[32,128]{1,0:T(8,128)S(1)}, f32[32,128]{1,0:T(8,128)S(1)}, u32[]{:S(2)}, u32[]{:S(2)}) collective-permute-start(f32[32,128]{1,0:T(8,128)S(1)} %add.15.refs_2_.refs_0_), channel_id=1, source_target_pairs={{0,4},{1,5},{2,6},{3,7},{4,0},{5,1},{6,2},{7,3},{8,12},{9,13},{10,... | collective-permute-start | bytes 49160 | tf_op jit(solution)/shard_map/ppermute | solution.py:882
  10.5 4.6 %collective-permute-start.2 = (f32[32,128]{1,0:T(8,128)S(1)}, f32[32,128]{1,0:T(8,128)S(1)}, u32[]{:S(2)}, u32[]{:S(2)}) collective-permute-start(f32[32,128]{1,0:T(8,128)S(1)} %add.15.refs_2_.refs_0_), channel_id=1, source_target_pairs={{0,2},{1,3},{2,0},{3,1},{4,6},{5,7},{6,4},{7,5},{8,10},{9,11},{10,... | collective-permute-start | bytes 49160 | tf_op jit(solution)/shard_map/ppermute | solution.py:882
  15.5 17.3 %collective-permute-start.5 = (bf16[2,4,64,1280]{3,2,1,0:T(8,128)(2,1)S(1)}, bf16[2,4,64,1280]{3,2,1,0:T(8,128)(2,1)S(1)}, u32[]{:S(2)}, u32[]{:S(2)}) collective-permute-start(bf16[2,4,64,1280]{3,2,1,0:T(8,128)(2,1)S(1)} %get-tuple-element.58), channel_id=1, source_target_pairs={{0,1},{1,2},{2,3},{3,4},{4,5},{5,6},{6,7},{8,9},{9,10},{10,11},{11... | collective-permute-start | bytes 3932168 | tf_op jit(solution)/shard_map/ppermute | solution.py:889
  16.9 15.9 %collective-permute-start.6 = (bf16[2,4,64,1280]{3,2,1,0:T(8,128)(2,1)S(1)}, bf16[2,4,64,1280]{3,2,1,0:T(8,128)(2,1)S(1)}, u32[]{:S(2)}, u32[]{:S(2)}) collective-permute-start(bf16[2,4,64,1280]{3,2,1,0:T(8,128)(2,1)S(1)} %get-tuple-element.59), channel_id=1, source_target_pairs={{1,0},{2,1},{3,2},{4,3},{5,4},{6,5},{7,6},{9,8},{10,9},{11,10},{12... | collective-permute-start | bytes 3932168 | tf_op jit(solution)/shard_map/ppermute | solution.py:889
  21.5 30.9 %collective-permute-start = (bf16[8,64,1024]{2,1,0:T(8,128)(2,1)S(1)}, bf16[8,64,1024]{2,1,0:T(8,128)(2,1)S(1)}, u32[]{:S(2)}, u32[]{:S(2)}) collective-permute-start(bf16[8,64,1024]{2,1,0:T(8,128)(2,1)S(1)} %get-tuple-element.51), channel_id=1, source_target_pairs={{8,0},{16,8},{24,16},{9,1},{17,9},{25,17},{10,2},{18,10},{26,18},{... | collective-permute-start | bytes 3145736 | tf_op jit(solution)/shard_map/ppermute | solution.py:889
  30.0 11.1 %collective-permute-start.8 = (bf16[4,64,1024]{2,1,0:T(8,128)(2,1)S(1)}, bf16[4,64,1024]{2,1,0:T(8,128)(2,1)S(1)}, u32[]{:S(2)}, u32[]{:S(2)}) collective-permute-start(bf16[4,64,1024]{2,1,0:T(8,128)(2,1)S(1)} %get-tuple-element.65), channel_id=1, source_target_pairs={{0,1},{1,2},{2,3},{3,4},{4,5},{5,6},{6,7},{8,9},{9,10},{10,11},{11... | collective-permute-start | bytes 1572872 | tf_op jit(solution)/shard_map/ppermute | solution.py:889
  31.3 9.8 %collective-permute-start.9 = (bf16[4,64,1024]{2,1,0:T(8,128)(2,1)S(1)}, bf16[4,64,1024]{2,1,0:T(8,128)(2,1)S(1)}, u32[]{:S(2)}, u32[]{:S(2)}) collective-permute-start(bf16[4,64,1024]{2,1,0:T(8,128)(2,1)S(1)} %get-tuple-element.60.after_ref), channel_id=1, source_target_pairs={{1,0},{2,1},{3,2},{4,3},{5,4},{6,5},{7,6},{9,8},{10,9},{11,10},{12... | collective-permute-start | bytes 1572872 | tf_op jit(solution)/shard_map/ppermute | solution.py:889
  39.8 20.1 %collective-permute-start.11 = (bf16[832,128]{1,0:T(8,128)(2,1)S(1)}, bf16[832,128]{1,0:T(8,128)(2,1)S(1)}, u32[]{:S(2)}, u32[]{:S(2)}) collective-permute-start(bf16[832,128]{1,0:T(8,128)(2,1)S(1)} %get-tuple-element.73), channel_id=1, source_target_pairs={{8,0},{16,8},{24,16},{9,1},{17,9},{25,17},{10,2},{18,10},{26,18},{... | collective-permute-start | bytes 638984 | tf_op jit(solution)/shard_map/ppermute | solution.py:889
  55.1 7.9 %collective-permute-start.10 = (bf16[768,128]{1,0:T(8,128)(2,1)S(1)}, bf16[768,128]{1,0:T(8,128)(2,1)S(1)}, u32[]{:S(2)}, u32[]{:S(2)}) collective-permute-start(bf16[768,128]{1,0:T(8,128)(2,1)S(1)} %get-tuple-element.72), channel_id=1, source_target_pairs={{0,8},{8,16},{16,24},{1,9},{9,17},{17,25},{2,10},{10,18},{18,26},{... | collective-permute-start | bytes 589832 | tf_op jit(solution)/shard_map/ppermute | solution.py:889
  64.3 9.0 %collective-permute-start.12 = (bf16[640,128]{1,0:T(8,128)(2,1)S(1)}, bf16[640,128]{1,0:T(8,128)(2,1)S(1)}, u32[]{:S(2)}, u32[]{:S(2)}) collective-permute-start(bf16[640,128]{1,0:T(8,128)(2,1)S(1)} %get-tuple-element.83), channel_id=1, source_target_pairs={{8,0},{16,8},{24,16},{9,1},{17,9},{25,17},{10,2},{18,10},{26,18},{... | collective-permute-start | bytes 491528 | tf_op jit(solution)/shard_map/ppermute | solution.py:889
  65.6 7.7 %collective-permute-start.13 = (bf16[576,128]{1,0:T(8,128)(2,1)S(1)}, bf16[576,128]{1,0:T(8,128)(2,1)S(1)}, u32[]{:S(2)}, u32[]{:S(2)}) collective-permute-start(bf16[576,128]{1,0:T(8,128)(2,1)S(1)} %get-tuple-element.84), channel_id=1, source_target_pairs={{0,8},{8,16},{16,24},{1,9},{9,17},{17,25},{2,10},{10,18},{18,26},{... | collective-permute-start | bytes 442376 | tf_op jit(solution)/shard_map/ppermute | solution.py:889
  74.6 9.3 %collective-permute-start.14 = (bf16[576,128]{1,0:T(8,128)(2,1)S(1)}, bf16[576,128]{1,0:T(8,128)(2,1)S(1)}, u32[]{:S(2)}, u32[]{:S(2)}) collective-permute-start(bf16[576,128]{1,0:T(8,128)(2,1)S(1)} %get-tuple-element.91), channel_id=1, source_target_pairs={{8,0},{16,8},{24,16},{9,1},{17,9},{25,17},{10,2},{18,10},{26,18},{... | collective-permute-start | bytes 442376 | tf_op jit(solution)/shard_map/ppermute | solution.py:889
  75.9 8.0 %collective-permute-start.15 = (bf16[512,128]{1,0:T(8,128)(2,1)S(1)}, bf16[512,128]{1,0:T(8,128)(2,1)S(1)}, u32[]{:S(2)}, u32[]{:S(2)}) collective-permute-start(bf16[512,128]{1,0:T(8,128)(2,1)S(1)} %get-tuple-element.92), channel_id=1, source_target_pairs={{0,8},{8,16},{16,24},{1,9},{9,17},{17,25},{2,10},{10,18},{18,26},{... | collective-permute-start | bytes 393224 | tf_op jit(solution)/shard_map/ppermute | solution.py:889
  85.2 1.2 %collective-permute-start.16 = (f32[32,128]{1,0:T(8,128)S(1)}, f32[32,128]{1,0:T(8,128)S(1)}, u32[]{:S(2)}, u32[]{:S(2)}) collective-permute-start(f32[32,128]{1,0:T(8,128)S(1)} %get-tuple-element.95), channel_id=1, source_target_pairs={{0,1},{1,0},{2,3},{3,2},{4,5},{5,4},{6,7},{7,6},{8,9},{9,8},{10,11... | collective-permute-start | bytes 49160 | tf_op jit(solution)/shard_map/ppermute | solution.py:882
  86.4 5.8 %collective-permute-start.19 = (f32[32,128]{1,0:T(8,128)S(1)}, f32[32,128]{1,0:T(8,128)S(1)}, u32[]{:S(2)}, u32[]{:S(2)}) collective-permute-start(f32[32,128]{1,0:T(8,128)S(1)} %add.16), channel_id=1, source_target_pairs={{0,6},{1,7},{2,4},{3,5},{4,2},{5,3},{6,0},{7,1},{8,14},{9,15},{10,... | collective-permute-start | bytes 49160 | tf_op jit(solution)/shard_map/ppermute | solution.py:882
  90.4 4.6 %collective-permute-start.18 = (f32[32,128]{1,0:T(8,128)S(1)}, f32[32,128]{1,0:T(8,128)S(1)}, u32[]{:S(2)}, u32[]{:S(2)}) collective-permute-start(f32[32,128]{1,0:T(8,128)S(1)} %add.16), channel_id=1, source_target_pairs={{0,4},{1,5},{2,6},{3,7},{4,0},{5,1},{6,2},{7,3},{8,12},{9,13},{10,... | collective-permute-start | bytes 49160 | tf_op jit(solution)/shard_map/ppermute | solution.py:882
  90.4 4.6 %collective-permute-start.17 = (f32[32,128]{1,0:T(8,128)S(1)}, f32[32,128]{1,0:T(8,128)S(1)}, u32[]{:S(2)}, u32[]{:S(2)}) collective-permute-start(f32[32,128]{1,0:T(8,128)S(1)} %add.16), channel_id=1, source_target_pairs={{0,2},{1,3},{2,0},{3,1},{4,6},{5,7},{6,4},{7,5},{8,10},{9,11},{10,... | collective-permute-start | bytes 49160 | tf_op jit(solution)/shard_map/ppermute | solution.py:882
  95.2 7.7 %collective-permute-start.22 = (f32[64,128]{1,0:T(8,128)S(1)}, f32[64,128]{1,0:T(8,128)S(1)}, u32[]{:S(2)}, u32[]{:S(2)}) collective-permute-start(f32[64,128]{1,0:T(8,128)S(1)} %maximum_maximum_fusion.refs_0_), channel_id=1, source_target_pairs={{0,24},{8,16},{16,8},{24,0},{1,25},{9,17},{17,9},{25,1},{2,26},{10... | collective-permute-start | bytes 98312 | tf_op jit(solution)/shard_map/ppermute | solution.py:882
  101.0 3.9 %collective-permute-start.21 = (f32[64,128]{1,0:T(8,128)S(1)}, f32[64,128]{1,0:T(8,128)S(1)}, u32[]{:S(2)}, u32[]{:S(2)}) collective-permute-start(f32[64,128]{1,0:T(8,128)S(1)} %maximum_maximum_fusion.refs_0_), channel_id=1, source_target_pairs={{0,16},{8,24},{16,0},{24,8},{1,17},{9,25},{17,1},{25,9},{2,18},{10... | collective-permute-start | bytes 98312 | tf_op jit(solution)/shard_map/ppermute | solution.py:882
  101.0 3.9 %collective-permute-start.20 = (f32[64,128]{1,0:T(8,128)S(1)}, f32[64,128]{1,0:T(8,128)S(1)}, u32[]{:S(2)}, u32[]{:S(2)}) collective-permute-start(f32[64,128]{1,0:T(8,128)S(1)} %maximum_maximum_fusion.refs_0_), channel_id=1, source_target_pairs={{0,8},{8,0},{16,24},{24,16},{1,9},{9,1},{17,25},{25,17},{2,10},{10... | collective-permute-start | bytes 98312 | tf_op jit(solution)/shard_map/ppermute | solution.py:882
